TPU v7x, 32 devices: a whole 2x2x4 slice. The times are simulated.
32 devices in a mesh: head: 4 (over y, x), blk: 8 (over z, core).
Axes of the slice: x: 2, y: 2, z: 4, core: 2. Of those that a mesh axis runs over, the one named last changes fastest.
Arguments:
- tokens: bfloat16 [4096, 1024], P(('head', 'blk')), may hold values from -6 to 6
- attn_gain: bfloat16 [1024], P(('head', 'blk')), may hold values from 0.25 to 1.75
- w_qkv: bfloat16 [1024, 3072], P(('head', 'blk')), may hold values from -0.1875 to 0.1875
- w_attn_out: bfloat16 [1024, 1024], P(('head', 'blk')), may hold values from -4 to 4
- mlp_gain: bfloat16 [1024], P(('head', 'blk')), may hold values from 0.25 to 1.75
- w_in: bfloat16 [1024, 5248], P(('head', 'blk')), may hold values from -0.1875 to 0.1875
- w_mlp_out: bfloat16 [2624, 1024], P(None, ('head', 'blk')), may hold values from -0.125 to 0.125
- doc_lengths: int32 [32], replicated, may hold values from 1 to 1024, 4096 in all
- cotangent: bfloat16 [4096, 1024], P(('head', 'blk')), may hold values from -6 to 6
Outputs:
- output: bfloat16 [4096, 1024], P(('head', 'blk'))
- input_grad: float32 [4096, 1024], P(('head', 'blk'))
- attn_gain_grad: float32 [1024], P(('head', 'blk'))
- w_qkv_grad: float32 [1024, 3072], P(('head', 'blk'))
- w_attn_out_grad: float32 [1024, 1024], P(('head', 'blk'))
- mlp_gain_grad: float32 [1024], P(('head', 'blk'))
- w_in_grad: float32 [1024, 5248], P(('head', 'blk'))
- w_mlp_out_grad: float32 [2624, 1024], P(None, ('head', 'blk'))
Inputs may be any that keep to these rules, and one draw needn't show every extreme that they name: `doc_lengths`: document lengths in stream order; they sum to 4096, and the longest is exactly 1024.
All inputs are finite; a program needn't handle non-finite values.
Results may differ from a plain program's by a relative error of at most 0.023.
Values may be sent and summed in bfloat16 or wider, within the bound.
A program may use at most 192 MiB of HBM per device.

v0:
```python
from functools import partial

import jax
import jax.numpy as jnp
from jax import lax
from jax.sharding import PartitionSpec as P

HEAD_DIM = 64


norm_eps = 1e-05
rope_base = 160000.0
neg_large = -1e30


def from_behind(value, axis, by):
    devices = lax.axis_size(axis)
    return lax.ppermute(value, axis, [(i, (i + by) % devices) for i in range(devices)])


def layer_norm(values, gain):
    center = values - jnp.mean(values, axis=-1, keepdims=True)
    spread = jnp.mean(center * center, axis=-1, keepdims=True)
    return center * lax.rsqrt(spread + norm_eps) * gain


def rope_tables(places, head_size):
    half = head_size // 2
    freqs = rope_base ** (-(jnp.arange(half, dtype=jnp.float32) * 2.0) / head_size)
    angles = places.astype(jnp.float32)[:, None] * freqs[None, :]
    angles = jnp.concatenate([angles, angles], axis=1)
    return (jnp.cos(angles), jnp.sin(angles))


def rotate(values, cosine, sine):
    count = values.shape[0]
    head_size = cosine.shape[1]
    half = head_size // 2
    split = values.reshape(count, -1, head_size)
    turned = jnp.concatenate([-split[..., half:], split[..., :half]], axis=-1)
    return (split * cosine[:, None, :] + turned * sine[:, None, :]).reshape(count, -1)


def rotate_pair(query, keys, cosine, sine):
    return (rotate(query, cosine, sine), rotate(keys, cosine, sine))


def doc_numbers(places, ends, lengths):
    passed = places[:, None] >= ends[None, :]
    numbers = jnp.sum(passed.astype(jnp.int32), axis=1)
    offset = jnp.sum(jnp.where(passed, lengths[None, :], 0), axis=1)
    return (numbers, places - offset)


def gelu_gate(lifted):
    half = lifted.shape[1] // 2
    return jax.nn.gelu(lifted[:, :half], approximate=False) * lifted[:, half:]


def tile_scores(query, keys):
    heads = query.shape[1] // HEAD_DIM
    query_split = query.reshape(query.shape[0], heads, HEAD_DIM)
    key_split = keys.reshape(keys.shape[0], heads, HEAD_DIM)
    return jnp.einsum(
        "qhd,khd->hqk", query_split, key_split, preferred_element_type=jnp.float32
    ) * HEAD_DIM ** (-0.5)


def unchanged(state):
    return state


def forward_tile(state, query, keys, values, mask):
    top, total, running = state
    count = query.shape[0]
    heads = top.shape[0]
    scores = tile_scores(query, keys)
    filled = jnp.where(mask[None], scores, neg_large)
    new_top = jnp.maximum(top, jnp.max(filled, axis=-1))
    weights = jnp.where(mask[None], jnp.exp(scores - new_top[:, :, None]), 0.0)
    factor = jnp.exp(top - new_top)
    new_total = total * factor + jnp.sum(weights, axis=-1)
    mixed = jnp.einsum(
        "hqk,khd->qhd",
        weights.astype(jnp.bfloat16),
        values.reshape(-1, heads, HEAD_DIM),
        preferred_element_type=jnp.float32,
    )
    new_running = running.reshape(count, heads, HEAD_DIM) * factor.T[:, :, None] + mixed
    return (new_top, new_total, new_running.reshape(count, heads * HEAD_DIM))


def backward_tile(carry, query, keys, values, mask, norm_log, grad_out, delta):
    query_grad, run_grads = carry
    count = query.shape[0]
    columns = keys.shape[0]
    heads = norm_log.shape[0]
    scores = tile_scores(query, keys)
    probs = jnp.where(mask[None], jnp.exp(scores - norm_log[:, :, None]), 0.0)
    grad_split = grad_out.reshape(count, heads, HEAD_DIM)
    value_split = values.reshape(columns, heads, HEAD_DIM)
    grad_values = jnp.einsum(
        "hqk,qhd->khd", probs.astype(jnp.bfloat16), grad_split, preferred_element_type=jnp.float32
    )
    grad_probs = jnp.einsum(
        "qhd,khd->hqk", grad_split, value_split, preferred_element_type=jnp.float32
    )
    grad_scores = (probs * (grad_probs - delta[:, :, None])).astype(jnp.bfloat16)
    grad_query = jnp.einsum(
        "hqk,khd->qhd",
        grad_scores,
        keys.reshape(columns, heads, HEAD_DIM),
        preferred_element_type=jnp.float32,
    ) * HEAD_DIM ** (-0.5)
    grad_keys = jnp.einsum(
        "hqk,qhd->khd",
        grad_scores,
        query.reshape(count, heads, HEAD_DIM),
        preferred_element_type=jnp.float32,
    ) * HEAD_DIM ** (-0.5)
    added = jnp.stack([grad_keys.reshape(columns, -1), grad_values.reshape(columns, -1)])
    return (query_grad + grad_query.reshape(count, -1), run_grads + added)


def per_device(
    tokens, attn_gain, w_qkv, w_attn_out, mlp_gain, w_in, w_mlp_out, doc_lengths, cotangent
):
    own_rows = tokens.shape[0]
    width = tokens.shape[1]
    head_count = lax.axis_size("head")
    cycle_count = lax.axis_size("blk")
    head_place = lax.axis_index("head")
    cycle_place = lax.axis_index("blk")
    group_rows = head_count * own_rows
    block_runs = min(head_count, max(1, 512 // own_rows))
    block_count = head_count // block_runs
    block_rows = block_runs * own_rows
    doc_ends = jnp.cumsum(doc_lengths)
    counter = jnp.arange(own_rows, dtype=jnp.int32)
    own_places = (head_place * cycle_count + cycle_place) * own_rows + counter
    unused_docs, own_positions = doc_numbers(own_places, doc_ends, doc_lengths)
    cosine, sine = rope_tables(own_positions, HEAD_DIM)
    run_numbers = jnp.arange(head_count, dtype=jnp.int32)
    query_places = (
        (run_numbers[:, None] * cycle_count + cycle_place) * own_rows + counter[None, :]
    ).reshape(group_rows)
    query_docs, unused_positions = doc_numbers(query_places, doc_ends, doc_lengths)
    params = (
        lax.all_gather(attn_gain, ("head", "blk"), axis=0, tiled=True),
        lax.all_gather(w_qkv, ("head", "blk"), axis=0, tiled=True),
        lax.all_gather(w_attn_out, ("head", "blk"), axis=0, tiled=True),
        lax.all_gather(mlp_gain, ("head", "blk"), axis=0, tiled=True),
        lax.all_gather(w_in, ("head", "blk"), axis=0, tiled=True),
        lax.all_gather(w_mlp_out, ("head", "blk"), axis=1, tiled=True),
    )
    gain_one, full_qkv, full_attn_out, gain_two, full_in, full_mlp_out = params
    inputs = tokens.astype(jnp.float32)
    normed_one, norm_one_pull = jax.vjp(layer_norm, inputs, gain_one.astype(jnp.float32))
    normed_low = normed_one.astype(jnp.bfloat16)
    projected = jnp.dot(normed_low, full_qkv, preferred_element_type=jnp.float32)
    turned, rope_pull = jax.vjp(
        partial(rotate_pair, cosine=cosine, sine=sine),
        projected[:, :width],
        projected[:, width : 2 * width],
    )
    stacked = jnp.stack(
        [
            turned[0].astype(jnp.bfloat16),
            turned[1].astype(jnp.bfloat16),
            projected[:, 2 * width :].astype(jnp.bfloat16),
        ]
    )
    regrouped = lax.all_to_all(stacked, "head", split_axis=2, concat_axis=1, tiled=True)
    query_heads = regrouped[0]
    key_heads = regrouped[1]
    value_heads = regrouped[2]
    head_width = query_heads.shape[1]
    heads_here = head_width // HEAD_DIM

    def key_docs_at(first):
        places = (
            first % group_rows // own_rows * cycle_count + first // group_rows
        ) * own_rows + counter
        found, unused = doc_numbers(places, doc_ends, doc_lengths)
        return found

    def block_live(block, key_docs):
        block_docs = query_docs[block * block_rows : (block + 1) * block_rows]
        live = jnp.maximum(jnp.min(block_docs), jnp.min(key_docs)) <= jnp.minimum(
            jnp.max(block_docs), jnp.max(key_docs)
        )
        return (block_docs[:, None] == key_docs[None, :], live)

    def fold_forward(state, piece):
        key_part, value_part = piece

        def fold_one_run(number, carried):
            first = number * own_rows
            key_docs = key_docs_at(first)
            keys = lax.dynamic_slice_in_dim(key_part, number * own_rows, own_rows, 0)
            values = lax.dynamic_slice_in_dim(value_part, number * own_rows, own_rows, 0)
            updated = []
            for block in range(block_count):
                mask, live = block_live(block, key_docs)
                query = query_heads[block * block_rows : (block + 1) * block_rows]
                advance = partial(forward_tile, query=query, keys=keys, values=values, mask=mask)
                updated.append(lax.cond(live, advance, unchanged, carried[block]))
            return tuple(updated)

        return lax.fori_loop(0, key_part.shape[0] // own_rows, fold_one_run, state)

    def fresh_state():
        return tuple(
            (
                (
                    jnp.full((heads_here, block_rows), neg_large, jnp.float32),
                    jnp.zeros((heads_here, block_rows), jnp.float32),
                    jnp.zeros((block_rows, head_width), jnp.float32),
                )
                for block in range(block_count)
            )
        )

    def finish(state):
        outputs = []
        logs = []
        for top, total, running in state:
            scaled = running.reshape(block_rows, heads_here, HEAD_DIM) / total.T[:, :, None]
            outputs.append(scaled.reshape(block_rows, head_width))
            logs.append(top + jnp.log(total))
        return (
            jnp.concatenate(outputs, axis=0).astype(jnp.bfloat16),
            jnp.concatenate(logs, axis=1),
        )

    state = fold_forward(
        fresh_state(),
        (
            lax.all_gather(key_heads, "blk", axis=0, tiled=True),
            lax.all_gather(value_heads, "blk", axis=0, tiled=True),
        ),
    )
    out_heads, norm_log = finish(state)
    out_tokens = lax.all_to_all(out_heads, "head", split_axis=0, concat_axis=1, tiled=True)
    middle = inputs + jnp.dot(out_tokens, full_attn_out, preferred_element_type=jnp.float32)
    normed_two, norm_two_pull = jax.vjp(layer_norm, middle, gain_two.astype(jnp.float32))
    normed_two_low = normed_two.astype(jnp.bfloat16)
    lifted = jnp.dot(normed_two_low, full_in, preferred_element_type=jnp.float32)
    activated, geglu_pull = jax.vjp(gelu_gate, lifted)
    activated_low = activated.astype(jnp.bfloat16)
    output = (
        middle + jnp.dot(activated_low, full_mlp_out, preferred_element_type=jnp.float32)
    ).astype(jnp.bfloat16)
    params = (
        lax.all_gather(attn_gain, ("head", "blk"), axis=0, tiled=True),
        lax.all_gather(w_qkv, ("head", "blk"), axis=0, tiled=True),
        lax.all_gather(w_attn_out, ("head", "blk"), axis=0, tiled=True),
        lax.all_gather(mlp_gain, ("head", "blk"), axis=0, tiled=True),
        lax.all_gather(w_in, ("head", "blk"), axis=0, tiled=True),
        lax.all_gather(w_mlp_out, ("head", "blk"), axis=1, tiled=True),
    )
    gain_one, full_qkv, full_attn_out, gain_two, full_in, full_mlp_out = params
    grad_act = jnp.einsum("td,fd->tf", cotangent, full_mlp_out, preferred_element_type=jnp.float32)
    grad_lifted = geglu_pull(grad_act)[0].astype(jnp.bfloat16)
    grad_normed_two = jnp.einsum(
        "tf,df->td", grad_lifted, full_in, preferred_element_type=jnp.float32
    )
    grad_middle_part, grad_gain_two = norm_two_pull(grad_normed_two)
    grad_middle = cotangent.astype(jnp.float32) + grad_middle_part
    grad_branch = grad_middle.astype(jnp.bfloat16)
    grad_mixed = jnp.einsum(
        "te,de->td", grad_branch, full_attn_out, preferred_element_type=jnp.float32
    ).astype(jnp.bfloat16)
    grad_heads = lax.all_to_all(grad_mixed, "head", split_axis=1, concat_axis=0, tiled=True)
    state = fold_forward(
        fresh_state(),
        (
            lax.all_gather(key_heads, "blk", axis=0, tiled=True),
            lax.all_gather(value_heads, "blk", axis=0, tiled=True),
        ),
    )
    out_heads, norm_log = finish(state)
    delta = jnp.einsum(
        "qhd,qhd->hq",
        grad_heads.reshape(group_rows, heads_here, HEAD_DIM).astype(jnp.float32),
        out_heads.reshape(group_rows, heads_here, HEAD_DIM).astype(jnp.float32),
    )

    def piece_backward(query_grads, key_part, value_part, start):
        piece_rows = key_part.shape[0]

        def piece_one_run(number, carried):
            query_now, piece_grads = carried
            first = start + number * own_rows
            key_docs = key_docs_at(first)
            keys = lax.dynamic_slice_in_dim(key_part, number * own_rows, own_rows, 0)
            values = lax.dynamic_slice_in_dim(value_part, number * own_rows, own_rows, 0)
            run_grads = jnp.zeros((2, own_rows, head_width), jnp.float32)
            updated = []
            for block in range(block_count):
                mask, live = block_live(block, key_docs)
                lower = block * block_rows
                upper = (block + 1) * block_rows
                advance = partial(
                    backward_tile,
                    query=query_heads[lower:upper],
                    keys=keys,
                    values=values,
                    mask=mask,
                    norm_log=norm_log[:, lower:upper],
                    grad_out=grad_heads[lower:upper],
                    delta=delta[:, lower:upper],
                )
                new_query, run_grads = lax.cond(
                    live, advance, unchanged, (query_now[block], run_grads)
                )
                updated.append(new_query)
            piece_grads = lax.dynamic_update_slice_in_dim(
                piece_grads, run_grads, number * own_rows, 1
            )
            return (tuple(updated), piece_grads)

        return lax.fori_loop(
            0,
            piece_rows // own_rows,
            piece_one_run,
            (query_grads, jnp.zeros((2, piece_rows, head_width), jnp.float32)),
        )

    start_query = tuple(
        (jnp.zeros((block_rows, head_width), jnp.float32) for block in range(block_count))
    )

    def cycle_step(step, carried):
        query_now, blocks, travelling = carried
        owner = (cycle_place - step) % cycle_count
        query_now, piece_grads = piece_backward(query_now, blocks[0], blocks[1], owner * group_rows)
        travelling = travelling + piece_grads
        blocks = from_behind(blocks, "blk", 1)
        travelling = from_behind(travelling.astype(jnp.bfloat16), "blk", 1).astype(travelling.dtype)
        return (query_now, blocks, travelling)

    start_cycle = (
        start_query,
        jnp.stack([key_heads, value_heads]),
        jnp.zeros((2, group_rows, head_width), jnp.float32),
    )
    query_grads, unused_blocks, own_grads = lax.fori_loop(0, cycle_count, cycle_step, start_cycle)
    grad_stack = jnp.stack(
        [
            jnp.concatenate(query_grads, axis=0).astype(jnp.bfloat16),
            own_grads[0].astype(jnp.bfloat16),
            own_grads[1].astype(jnp.bfloat16),
        ]
    )
    back_tokens = lax.all_to_all(grad_stack, "head", split_axis=1, concat_axis=2, tiled=True)
    grad_query, grad_keys = rope_pull(
        (back_tokens[0].astype(jnp.float32), back_tokens[1].astype(jnp.float32))
    )
    grad_projected = jnp.concatenate(
        [grad_query, grad_keys, back_tokens[2].astype(jnp.float32)], axis=1
    ).astype(jnp.bfloat16)
    grad_normed_one = jnp.einsum(
        "te,de->td", grad_projected, full_qkv, preferred_element_type=jnp.float32
    )
    grad_input_part, grad_gain_one = norm_one_pull(grad_normed_one)
    input_grad = grad_middle + grad_input_part

    def columns(source):
        return source

    term_qkv = jnp.einsum(
        "td,te->de", columns(normed_low), grad_projected, preferred_element_type=jnp.float32
    )
    term_out = jnp.einsum(
        "td,te->de", columns(out_tokens), grad_branch, preferred_element_type=jnp.float32
    )
    term_in = jnp.einsum(
        "td,tf->df", columns(normed_two_low), grad_lifted, preferred_element_type=jnp.float32
    )
    term_down = jnp.einsum(
        "td,tf->df", columns(cotangent), activated_low, preferred_element_type=jnp.float32
    )
    sums = lax.psum_scatter(
        jnp.concatenate([term_qkv, term_out, term_in, term_down], axis=1),
        ("head", "blk"),
        scatter_dimension=0,
        tiled=True,
    )
    ff_width = full_mlp_out.shape[0]
    qkv_grad = sums[:, : 3 * width]
    attn_out_grad = sums[:, 3 * width : 4 * width]
    in_grad = sums[:, 4 * width : 4 * width + 2 * ff_width]
    down_grad = sums[:, 4 * width + 2 * ff_width :].T
    gain_sums = lax.psum_scatter(
        jnp.stack([grad_gain_one, grad_gain_two]), ("head", "blk"), scatter_dimension=1, tiled=True
    )
    return (
        output,
        input_grad,
        gain_sums[0],
        qkv_grad,
        attn_out_grad,
        gain_sums[1],
        in_grad,
        down_grad,
    )


def solution(mesh):
    placed = (
        P(("head", "blk"), None),
        P(("head", "blk")),
        P(("head", "blk"), None),
        P(("head", "blk"), None),
        P(("head", "blk")),
        P(("head", "blk"), None),
        P(None, ("head", "blk")),
        P(),
        P(("head", "blk"), None),
    )
    return jax.shard_map(
        per_device,
        mesh=mesh,
        in_specs=placed,
        out_specs=(
            P(("head", "blk"), None),
            P(("head", "blk"), None),
            P(("head", "blk")),
            P(("head", "blk"), None),
            P(("head", "blk"), None),
            P(("head", "blk")),
            P(("head", "blk"), None),
            P(None, ("head", "blk")),
        ),
        check_vma=False,
    )
```

profile of v0, /device:TPU:0, one launch (start us, length us, event | category | flops | bytes accessed | tf_op | source)
XLA Modules:
  0.0 1434.0 jit_solution(17465633927477797563)
XLA Ops:
  9.7 42.3 %all-reduce.8 = (bf16[1024]{0:T(1024)(128)(2,1)S(1)}, bf16[1024]{0:T(1024)(128)(2,1)S(1)}) all-reduce(bf16[1024]{0:T(1024)(128)(2,1)S(1)} %dynamic-update-slice, bf16[1024]{0:T(1024)(128)(2,1)S(1)} %dynamic-update-slice.1), channel_id=1, replica_groups=mesh['head'=4,'blk'=8] {'head','blk'}, use_global_device_ids=true, to_apply=%add.6 | all-reduce | flops 2048 | bytes 8192
  54.4 29.2 %all-gather.7.cloned.1.call-done = bf16[1024,3072]{1,0:T(8,128)(2,1)} async-done(((bf16[32,3072]{1,0:T(8,128)(2,1)}), bf16[1024,3072]{1,0:T(8,128)(2,1)}) %all-gather.7.cloned.1.call-update) | async-done | bytes 6291472 | tf_op jit(solution)/shard_map/all_gather | solution.py:150
  83.6 3.9 fusion.62
  99.5 17.3 %all_to_all.68 = bf16[3,128,1024]{1,0,2:T(4,128)(2,1)S(1)} all-to-all(bf16[3,128,1024]{1,0,2:T(4,128)(2,1)S(1)} %copy.188), channel_id=1, replica_groups=mesh['head'=4,'blk'=8] {'head'}, dimensions={2} | all-to-all | bytes 1572864 | tf_op jit(solution)/shard_map/all_to_all | solution.py:173
  123.5 22.7 %all-gather.9.cloned.1.call-done = bf16[4096,256]{0,1:T(8,128)(2,1)} async-done(((bf16[512,256]{0,1:T(8,128)(2,1)}), bf16[4096,256]{0,1:T(8,128)(2,1)}) %all-gather.9.cloned.1.call-update) | async-done | bytes 2097168 | tf_op jit(solution)/shard_map/all_gather | solution.py:239
  146.2 30.8 %all-gather.11.cloned.1.call-done = bf16[4096,256]{0,1:T(8,128)(2,1)} async-done(((bf16[512,256]{0,1:T(8,128)(2,1)}), bf16[4096,256]{0,1:T(8,128)(2,1)}) %all-gather.11.cloned.1.call-update) | async-done | bytes 2097168 | tf_op jit(solution)/shard_map/all_gather | solution.py:240
  177.1 163.9 %while.95 = (s32[]{:T(128)}, f32[4,512]{1,0:T(4,128)S(1)}, f32[4,512]{1,0:T(4,128)S(1)}, f32[512,256]{0,1:T(8,128)S(1)}, s32[32]{0:T(128)S(1)}, /*index=5*/s32[]...) while((s32[]{:T(128)}, f32[4,512]{1,0:T(4,128)S(1)}, ...), condition=%wide.region_15.16_spmd.clone, body=%wide.region_7.15_spmd.clone.sunk | while | flops 69814568 | bytes 5248405 | solution.py:210
  186.0 2.1 conditional.5
  191.5 2.1 conditional.5
  202.5 2.1 conditional.5
  219.0 2.1 conditional.5
  244.5 2.1 conditional.5
  255.5 2.1 conditional.5
  264.5 2.1 conditional.5
  284.5 2.1 conditional.5
  304.4 2.1 conditional.5
  315.5 2.1 conditional.5
  324.4 2.1 conditional.5
  335.4 2.1 conditional.5
  341.9 3.7 all-to-all-start.1
  346.2 5.0 all-to-all-done.1
  351.4 2.4 fusion.76
  354.1 7.3 fusion.65
  361.4 32.5 %all-gather.17.cloned.1.call-done = bf16[2624,1024]{0,1:T(8,128)(2,1)} async-done(((bf16[2624,32]{0,1:T(8,128)(2,1)}), bf16[2624,1024]{0,1:T(8,128)(2,1)}) %all-gather.17.cloned.1.call-update) | async-done | bytes 5373968 | tf_op jit(solution)/shard_map/all_gather | solution.py:154
  393.9 7.8 fusion.44
  403.4 5.6 multiply_reduce_fusion
  414.1 3.6 all-to-all-start.2
  417.8 10.3 fusion.51
  429.0 302.8 %while.97 = (s32[]{:T(128)}, f32[512,256]{0,1:T(8,128)S(1)}, bf16[2,512,256]{1,2,0:T(8,128)(2,1)S(1)}, f32[2,512,256]{1,2,0:T(8,128)}, s32[]{:T(128)}, /*index=5...) while((s32[]{:T(128)}, f32[512,256]{0,1:T(8,128)S(1)}, ...), condition=%wide.region_28.29_spmd.clone, body=%wide.region_20.28_spmd.clone.sunk | while | flops 171094336 | bytes 21322852 | solution.py:348
  429.2 21.6 %while.98 = (s32[]{:T(128)}, f32[512,256]{0,1:T(8,128)S(1)}, f32[2,512,256]{1,2,0:T(8,128)S(1)}, s32[]{:T(128)}, s32[128]{0:T(128)S(1)}, /*index=5*/s32[32]{0:T(...) while((s32[]{:T(128)}, f32[512,256]{0,1:T(8,128)S(1)}, ...), condition=%wide.region_27.27_spmd, body=%wide.region_21.26_spmd.sunk | while | flops 170045744 | bytes 9787302 | solution.py:323
  453.3 8.3 collective-permute-done.1
  462.8 4.5 collective-permute-done
  467.5 19.7 %while.98 = (s32[]{:T(128)}, f32[512,256]{0,1:T(8,128)S(1)}, f32[2,512,256]{1,2,0:T(8,128)S(1)}, s32[]{:T(128)}, s32[128]{0:T(128)S(1)}, /*index=5*/s32[32]{0:T(...) while((s32[]{:T(128)}, f32[512,256]{0,1:T(8,128)S(1)}, ...), condition=%wide.region_27.27_spmd, body=%wide.region_21.26_spmd.sunk | while | flops 170045744 | bytes 9787302 | solution.py:323
  488.7 2.2 collective-permute-start
  490.9 8.2 collective-permute-done.1
  500.3 4.5 collective-permute-done
  505.0 19.7 %while.98 = (s32[]{:T(128)}, f32[512,256]{0,1:T(8,128)S(1)}, f32[2,512,256]{1,2,0:T(8,128)S(1)}, s32[]{:T(128)}, s32[128]{0:T(128)S(1)}, /*index=5*/s32[32]{0:T(...) while((s32[]{:T(128)}, f32[512,256]{0,1:T(8,128)S(1)}, ...), condition=%wide.region_27.27_spmd, body=%wide.region_21.26_spmd.sunk | while | flops 170045744 | bytes 9787302 | solution.py:323
  526.3 2.3 collective-permute-start
  528.6 8.1 collective-permute-done.1
  537.8 4.5 collective-permute-done
  542.5 19.7 %while.98 = (s32[]{:T(128)}, f32[512,256]{0,1:T(8,128)S(1)}, f32[2,512,256]{1,2,0:T(8,128)S(1)}, s32[]{:T(128)}, s32[128]{0:T(128)S(1)}, /*index=5*/s32[32]{0:T(...) while((s32[]{:T(128)}, f32[512,256]{0,1:T(8,128)S(1)}, ...), condition=%wide.region_27.27_spmd, body=%wide.region_21.26_spmd.sunk | while | flops 170045744 | bytes 9787302 | solution.py:323
  564.3 9.9 collective-permute-done.1
  575.4 4.5 collective-permute-done
  580.0 19.7 %while.98 = (s32[]{:T(128)}, f32[512,256]{0,1:T(8,128)S(1)}, f32[2,512,256]{1,2,0:T(8,128)S(1)}, s32[]{:T(128)}, s32[128]{0:T(128)S(1)}, /*index=5*/s32[32]{0:T(...) while((s32[]{:T(128)}, f32[512,256]{0,1:T(8,128)S(1)}, ...), condition=%wide.region_27.27_spmd, body=%wide.region_21.26_spmd.sunk | while | flops 170045744 | bytes 9787302 | solution.py:323
  601.4 10.3 collective-permute-done.1
  612.9 4.5 collective-permute-done
  617.6 19.7 %while.98 = (s32[]{:T(128)}, f32[512,256]{0,1:T(8,128)S(1)}, f32[2,512,256]{1,2,0:T(8,128)S(1)}, s32[]{:T(128)}, s32[128]{0:T(128)S(1)}, /*index=5*/s32[32]{0:T(...) while((s32[]{:T(128)}, f32[512,256]{0,1:T(8,128)S(1)}, ...), condition=%wide.region_27.27_spmd, body=%wide.region_21.26_spmd.sunk | while | flops 170045744 | bytes 9787302 | solution.py:323
  638.9 10.3 collective-permute-done.1
  650.4 4.5 collective-permute-done
  655.1 19.7 %while.98 = (s32[]{:T(128)}, f32[512,256]{0,1:T(8,128)S(1)}, f32[2,512,256]{1,2,0:T(8,128)S(1)}, s32[]{:T(128)}, s32[128]{0:T(128)S(1)}, /*index=5*/s32[32]{0:T(...) while((s32[]{:T(128)}, f32[512,256]{0,1:T(8,128)S(1)}, ...), condition=%wide.region_27.27_spmd, body=%wide.region_21.26_spmd.sunk | while | flops 170045744 | bytes 9787302 | solution.py:323
  676.5 10.3 collective-permute-done.1
  688.0 4.5 collective-permute-done
  692.6 21.6 %while.98 = (s32[]{:T(128)}, f32[512,256]{0,1:T(8,128)S(1)}, f32[2,512,256]{1,2,0:T(8,128)S(1)}, s32[]{:T(128)}, s32[128]{0:T(128)S(1)}, /*index=5*/s32[32]{0:T(...) while((s32[]{:T(128)}, f32[512,256]{0,1:T(8,128)S(1)}, ...), condition=%wide.region_27.27_spmd, body=%wide.region_21.26_spmd.sunk | while | flops 170045744 | bytes 9787302 | solution.py:323
  715.9 10.3 collective-permute-done.1
  727.4 4.5 collective-permute-done
  736.0 4.0 all-to-all-start.3
  740.4 2.6 fusion.77
  743.1 5.8 convolution_bitcast_fusion.1
  751.6 6.5 fusion.46
  758.1 2.4 fusion.41
  762.0 33.7 %pad_maximum_fusion.1 = f32[1024,11968]{1,0:T(8,128)} fusion(f32[1024,2624]{1,0:T(8,128)} %convolution_bitcast_fusion.1, f32[1024,5248]{1,0:T(8,128)} %fusion.51, f32[1024,1024]{1,0:T(8,128)} %fusion.77, f32[1024,3072]{1,0:T(8,128)} %fusion.46), kind=kLoop, calls=%fused_computation.47 | loop fusion | flops 36765696 | bytes 98041856 | tf_op jit(solution)/shard_map/concatenate | solution.py:385
  796.7 5.2 fusion.31
  803.1 93.8 %reduce-scatter.7.cloned.1.call-done = f32[32,2]{1,0:T(8,128)} async-done(((f32[1024,2]{1,0:T(8,128)}), f32[32,2]{1,0:T(8,128)}) %reduce-scatter.7.cloned.1.call-update) | async-done | bytes 272
  898.9 521.2 %reduce-scatter.5.cloned.1.call-done = f32[32,11968]{1,0:T(8,128)} async-done(((f32[1024,11968]{1,0:T(8,128)}), f32[32,11968]{1,0:T(8,128)}) %reduce-scatter.5.cloned.1.call-update) | async-done | bytes 1531920 | tf_op jit(solution)/shard_map/reduce_scatter | solution.py:384
  (971 shorter events, 306.9 us)
Async XLA Ops:
  7.2 46.9 %copy-start.3 = (bf16[128,1024]{1,0:T(8,128)(2,1)S(1)}, bf16[128,1024]{1,0:T(8,128)(2,1)}, u32[]{:S(2)}) copy-start(bf16[128,1024]{1,0:T(8,128)(2,1)} %param.19) | copy-start | bytes 786436
  7.2 76.5 %all-gather.7.cloned.1.call-start = ((), (), s32[]{:S(2)}) async-start(), calls=%async_computation.6 | async-start | bytes 6488064 | tf_op jit(solution)/shard_map/all_gather | solution.py:150
  7.9 138.3 %all-gather.9.cloned.1.call-start = ((), (), s32[]{:S(2)}) async-start(), calls=%async_computation.7 | async-start | bytes 2359296 | tf_op jit(solution)/shard_map/all_gather | solution.py:239
  54.2 33.3 %copy-start.20 = (f32[128]{0:T(128)}, f32[128]{0:T(128)S(1)}, u32[]{:S(2)}) copy-start(f32[128]{0:T(128)S(1)} %broadcast_multiply_fusion.4) | copy-start | bytes 1540
  54.4 33.1 %copy-start.30 = (f32[128]{0:T(128)}, f32[128]{0:T(128)S(1)}, u32[]{:S(2)}) copy-start(f32[128]{0:T(128)S(1)} %fusion.40) | copy-start | bytes 1540
  54.4 33.1 %copy-start.22 = (f32[128]{0:T(128)}, f32[128]{0:T(128)S(1)}, u32[]{:S(2)}) copy-start(f32[128]{0:T(128)S(1)} %fusion.55) | copy-start | bytes 1540
  119.0 58.0 %all-gather.11.cloned.1.call-start = ((), (), s32[]{:S(2)}) async-start(), calls=%async_computation.8 | async-start | bytes 2359296 | tf_op jit(solution)/shard_map/all_gather | solution.py:240
  120.2 231.3 %all-gather.13.cloned.1.call-start = ((), (), s32[]{:S(2)}) async-start(), calls=%async_computation.9 | async-start | bytes 2162688 | tf_op jit(solution)/shard_map/all_gather | solution.py:151
  120.7 233.4 %all-gather.15.cloned.1.call-start = ((), (), s32[]{:S(2)}) async-start(), calls=%async_computation.10 | async-start | bytes 11083776 | tf_op jit(solution)/shard_map/all_gather | solution.py:153
  121.3 272.6 %all-gather.17.cloned.1.call-start = ((), (), s32[]{:S(2)}) async-start(), calls=%async_computation.11 | async-start | bytes 5677056 | tf_op jit(solution)/shard_map/all_gather | solution.py:154
  341.0 12.8 copy-start.26
  341.1 12.7 copy-start.12
  341.9 9.3 all-to-all-start.1
  351.4 2.4 copy-start.14
  353.8 64.0 %copy-start.1 = (f32[128,1024]{1,0:T(8,128)}, f32[128,1024]{1,0:T(8,128)S(1)}, u32[]{:S(2)}) copy-start(f32[128,1024]{1,0:T(8,128)S(1)} %get-tuple-element.1589) | copy-start | bytes 1572868
  354.0 55.0 %copy-start.19 = (f32[128]{0:T(128)}, f32[128]{0:T(128)S(1)}, u32[]{:S(2)}) copy-start(f32[128]{0:T(128)S(1)} %fusion.56) | copy-start | bytes 1540
  354.1 39.8 %copy-start.16 = (bf16[128,1024]{1,0:T(8,128)(2,1)S(1)}, bf16[128,1024]{1,0:T(8,128)(2,1)}, u32[]{:S(2)}) copy-start(bf16[128,1024]{1,0:T(8,128)(2,1)} %param.27) | copy-start | bytes 786436
  393.9 7.8 copy-start.5
  393.9 9.5 copy-start
  403.4 6.0 copy-start.17
  409.0 1.8 copy-start.6
  409.3 3.1 copy-start.8
  409.3 0.6 copy-start.28
  410.8 3.3 copy-start.10
  414.1 14.0 all-to-all-start.2
  417.8 10.7 copy-start.13
  428.3 0.7 copy-start.25
  428.3 0.7 copy-start.27
  451.2 10.5 collective-permute-start.1
  451.5 15.7 %collective-permute-start = (bf16[2,512,256]{1,2,0:T(8,128)(2,1)S(1)}, bf16[2,512,256]{1,2,0:T(8,128)(2,1)S(1)}, u32[]{:S(2)}, u32[]{:S(2)}) collective-permute-start(bf16[2,512,256]{1,2,0:T(8,128)(2,1)S(1)} %copy.277), channel_id=1, source_target_pairs={{0,1},{1,2},{2,3},{3,4},{4,5},{5,6},{6,7},{7,0},{8,9},{9,10},{10,1... | collective-permute-start | bytes 1572872 | tf_op jit(solution)/shard_map/while/body/eval_jaxpr/ppermute | solution.py:18
  488.7 10.5 collective-permute-start.1
  488.7 16.0 %collective-permute-start = (bf16[2,512,256]{1,2,0:T(8,128)(2,1)S(1)}, bf16[2,512,256]{1,2,0:T(8,128)(2,1)S(1)}, u32[]{:S(2)}, u32[]{:S(2)}) collective-permute-start(bf16[2,512,256]{1,2,0:T(8,128)(2,1)S(1)} %copy.277), channel_id=1, source_target_pairs={{0,1},{1,2},{2,3},{3,4},{4,5},{5,6},{6,7},{7,0},{8,9},{9,10},{10,1... | collective-permute-start | bytes 1572872 | tf_op jit(solution)/shard_map/while/body/eval_jaxpr/ppermute | solution.py:18
  526.2 10.5 collective-permute-start.1
  526.3 16.0 %collective-permute-start = (bf16[2,512,256]{1,2,0:T(8,128)(2,1)S(1)}, bf16[2,512,256]{1,2,0:T(8,128)(2,1)S(1)}, u32[]{:S(2)}, u32[]{:S(2)}) collective-permute-start(bf16[2,512,256]{1,2,0:T(8,128)(2,1)S(1)} %copy.277), channel_id=1, source_target_pairs={{0,1},{1,2},{2,3},{3,4},{4,5},{5,6},{6,7},{7,0},{8,9},{9,10},{10,1... | collective-permute-start | bytes 1572872 | tf_op jit(solution)/shard_map/while/body/eval_jaxpr/ppermute | solution.py:18
  563.7 10.5 collective-permute-start.1
  563.8 16.0 %collective-permute-start = (bf16[2,512,256]{1,2,0:T(8,128)(2,1)S(1)}, bf16[2,512,256]{1,2,0:T(8,128)(2,1)S(1)}, u32[]{:S(2)}, u32[]{:S(2)}) collective-permute-start(bf16[2,512,256]{1,2,0:T(8,128)(2,1)S(1)} %copy.277), channel_id=1, source_target_pairs={{0,1},{1,2},{2,3},{3,4},{4,5},{5,6},{6,7},{7,0},{8,9},{9,10},{10,1... | collective-permute-start | bytes 1572872 | tf_op jit(solution)/shard_map/while/body/eval_jaxpr/ppermute | solution.py:18
  601.3 10.5 collective-permute-start.1
  601.3 16.0 %collective-permute-start = (bf16[2,512,256]{1,2,0:T(8,128)(2,1)S(1)}, bf16[2,512,256]{1,2,0:T(8,128)(2,1)S(1)}, u32[]{:S(2)}, u32[]{:S(2)}) collective-permute-start(bf16[2,512,256]{1,2,0:T(8,128)(2,1)S(1)} %copy.277), channel_id=1, source_target_pairs={{0,1},{1,2},{2,3},{3,4},{4,5},{5,6},{6,7},{7,0},{8,9},{9,10},{10,1... | collective-permute-start | bytes 1572872 | tf_op jit(solution)/shard_map/while/body/eval_jaxpr/ppermute | solution.py:18
  638.8 10.5 collective-permute-start.1
  638.9 16.0 %collective-permute-start = (bf16[2,512,256]{1,2,0:T(8,128)(2,1)S(1)}, bf16[2,512,256]{1,2,0:T(8,128)(2,1)S(1)}, u32[]{:S(2)}, u32[]{:S(2)}) collective-permute-start(bf16[2,512,256]{1,2,0:T(8,128)(2,1)S(1)} %copy.277), channel_id=1, source_target_pairs={{0,1},{1,2},{2,3},{3,4},{4,5},{5,6},{6,7},{7,0},{8,9},{9,10},{10,1... | collective-permute-start | bytes 1572872 | tf_op jit(solution)/shard_map/while/body/eval_jaxpr/ppermute | solution.py:18
  676.3 10.5 collective-permute-start.1
  676.4 16.0 %collective-permute-start = (bf16[2,512,256]{1,2,0:T(8,128)(2,1)S(1)}, bf16[2,512,256]{1,2,0:T(8,128)(2,1)S(1)}, u32[]{:S(2)}, u32[]{:S(2)}) collective-permute-start(bf16[2,512,256]{1,2,0:T(8,128)(2,1)S(1)} %copy.277), channel_id=1, source_target_pairs={{0,1},{1,2},{2,3},{3,4},{4,5},{5,6},{6,7},{7,0},{8,9},{9,10},{10,1... | collective-permute-start | bytes 1572872 | tf_op jit(solution)/shard_map/while/body/eval_jaxpr/ppermute | solution.py:18
  715.8 10.5 collective-permute-start.1
  715.8 16.0 %collective-permute-start = (bf16[2,512,256]{1,2,0:T(8,128)(2,1)S(1)}, bf16[2,512,256]{1,2,0:T(8,128)(2,1)S(1)}, u32[]{:S(2)}, u32[]{:S(2)}) collective-permute-start(bf16[2,512,256]{1,2,0:T(8,128)(2,1)S(1)} %copy.277), channel_id=1, source_target_pairs={{0,1},{1,2},{2,3},{3,4},{4,5},{5,6},{6,7},{7,0},{8,9},{9,10},{10,1... | collective-permute-start | bytes 1572872 | tf_op jit(solution)/shard_map/while/body/eval_jaxpr/ppermute | solution.py:18
  736.0 4.4 copy-start.11
  736.0 4.4 copy-start.15
  736.0 13.5 all-to-all-start.3
  740.1 3.0 copy-start.7
  740.1 3.0 copy-start.18
  740.1 156.7 %reduce-scatter.7.cloned.1.call-start = ((), (), s32[]{:S(2)}) async-start(), calls=%async_computation.13 | async-start | bytes 540672
  750.3 7.8 slice-start
  750.5 1.1 copy-start.4
  750.5 1.1 copy-start.21
  750.5 1.1 copy-start.23
  751.6 6.5 slice-start.1
  758.1 2.4 copy-start.31
  758.1 2.8 copy-start.24
  762.0 658.1 %reduce-scatter.5.cloned.1.call-start = ((), (), s32[]{:S(2)}) async-start(), calls=%async_computation.12 | async-start | bytes 50823168 | tf_op jit(solution)/shard_map/reduce_scatter | solution.py:384
  795.7 1.0 copy-start.2
  796.7 5.2 copy-start.9
  796.7 5.2 copy-start.29
Sparse Core Ops, SparseCore 0:
  11.0 72.5 all-gather.6
  119.1 27.0 all-gather.8
  148.4 28.5 all-gather.10
  179.8 55.9 all-gather.12
  238.6 86.8 all-gather.14
  328.3 65.4 all-gather.16
  762.1 134.7 reduce-scatter.6
  899.3 520.7 reduce-scatter.4
where the time goes:
time: 1440 us; the launch traced here: 1430 us
  waiting for transfers between devices  850 us (59%)
  loops' own time  177 us (12%)
  other arithmetic  130 us (9%)
  matrix products  123 us (9%)
  local copies, waits for them, and re-layouts  61.2 us (4%)
  blocking collectives  59.5 us (4%)
  starting transfers between devices  19.8 us (1%)
  between operations  14.8 us (1%)
    reduce_scatter x1, waiting for transfers between devices, per_device(): lax.psum_scatter(jnp.concatenate([term_qkv, term_out, term_in, term_down]...  521 us
    ppermute x16, waiting for transfers between devices, from_behind(): lax.ppermute(value, axis, [(i, (i + by) % devices) for i in range(devices)])  111 us
    unnamed x9, waiting for transfers between devices  96.1 us
    another operation x1, loops' own time, fold_forward(): return lax.fori_loop(0, key_part.shape[0] // own_rows, fold_one_run, state)  86.3 us
    another operation x8, loops' own time, piece_backward(): lax.fori_loop(0, piece_rows // own_rows, piece_one_run, (query_grads, jnp...  86 us
    unnamed x1, blocking collectives  42.3 us
    reduce_max x64, other arithmetic, block_live(): jnp.max(key_docs)  41.3 us
    concatenate x1, other arithmetic, per_device(): jnp.concatenate([term_qkv, term_out, term_in, term_down], axis=1)  33.7 us
  transfers between devices with their start and end apart: 27, of which 24 were waited for; matrix products, arithmetic and copies ran while one was open for 11% of the time, Pallas kernels for 0%

commit v1 on v0

--- a/solution.py
+++ b/solution.py
@@ -3,6 +3,8 @@
 import jax
 import jax.numpy as jnp
 from jax import lax
+from jax.experimental import pallas as pl
+from jax.experimental.pallas import tpu as pltpu
 from jax.sharding import PartitionSpec as P
 
 HEAD_DIM = 64
@@ -122,7 +124,7 @@
     return (query_grad + grad_query.reshape(count, -1), run_grads + added)
 
 
-def per_device(
+def per_device_general(
     tokens, attn_gain, w_qkv, w_attn_out, mlp_gain, w_in, w_mlp_out, doc_lengths, cotangent
 ):
     own_rows = tokens.shape[0]
@@ -407,6 +409,332 @@
     )
 
 
+KEY_TILE = 256
+NN = (((1,), (0,)), ((), ()))
+NT = (((1,), (1,)), ((), ()))
+TN = (((0,), (0,)), ((), ()))
+
+
+def mm(left, right, dims=NN):
+    return lax.dot_general(left, right, dims, preferred_element_type=jnp.float32)
+
+
+def halves(packed, side):
+    wide = packed.astype(jnp.float32)
+    if side:
+        wide = pltpu.roll(wide, HEAD_DIM, 1)
+    lane = lax.broadcasted_iota(jnp.int32, wide.shape, 1)
+    return jnp.where(lane < HEAD_DIM, wide, 0.0)
+
+
+def attend_kernel(span, qp, kv, qdoc, kdoc, op, lse, s_scr):
+    pairs, tall = qp.shape[0] * qp.shape[2], qp.shape[2]
+    half_runs = pl.num_programs(0)
+    hh, u = pl.program_id(0), pl.program_id(1)
+    lane = lax.broadcasted_iota(jnp.int32, (pairs, 2 * HEAD_DIM), 1)
+    results = []
+    for side in (0, 1):
+        tile = (hh + side * half_runs) * pl.num_programs(1) + u
+        query = (halves(qp[...].reshape(pairs, 2 * HEAD_DIM), side) * HEAD_DIM**-0.5).astype(
+            jnp.bfloat16
+        )
+        docs = qdoc[tile]
+        first, last = span[tile, 0], span[tile, 1]
+
+        def score(kb, top):
+            keys = kv[pl.ds(pl.multiple_of(kb * KEY_TILE, KEY_TILE), KEY_TILE), :]
+            scores = jnp.where(docs == kdoc[pl.ds(kb, 1), :], mm(query, keys, NT), neg_large)
+            s_scr[kb] = scores
+            return jnp.maximum(top, jnp.maximum(scores[:, :128], scores[:, 128:]))
+
+        top = lax.fori_loop(first, last, score, jnp.full((pairs, 128), neg_large, jnp.float32))
+        top = jnp.max(top, axis=1, keepdims=True)
+
+        def mix(kb, carried):
+            total, acc = carried
+            keys = kv[pl.ds(pl.multiple_of(kb * KEY_TILE, KEY_TILE), KEY_TILE), :]
+            weights = jnp.exp(s_scr[kb] - top)
+            total = total + weights[:, :128] + weights[:, 128:]
+            return (total, acc + mm(weights.astype(jnp.bfloat16), keys))
+
+        zeros = jnp.zeros((pairs, 128), jnp.float32)
+        total, acc = lax.fori_loop(first, last, mix, (zeros, zeros))
+        total = jnp.sum(total, axis=1, keepdims=True)
+        lse[tile] = top + jnp.log(total)
+        results.append(acc / total)
+    both = jnp.where(lane < HEAD_DIM, pltpu.roll(results[0], HEAD_DIM, 1), results[1])
+    op[...] = both.astype(jnp.bfloat16).reshape(op.shape)
+
+
+def attend(span, qp, kv, qdoc, kdoc):
+    parts, half_runs, rows, lanes = qp.shape
+    tiles = qdoc.shape[0]
+    piece = pl.BlockSpec((2, 1, rows, lanes), lambda i, j, s: (j, i, 0, 0))
+    whole = pl.BlockSpec(memory_space=pltpu.VMEM)
+    return pl.pallas_call(
+        attend_kernel,
+        grid_spec=pltpu.PrefetchScalarGridSpec(
+            num_scalar_prefetch=1,
+            grid=(half_runs, parts // 2),
+            in_specs=[piece, whole, whole, whole],
+            out_specs=[piece, whole],
+            scratch_shapes=[
+                pltpu.VMEM((kv.shape[0] // KEY_TILE, 2 * rows, KEY_TILE), jnp.float32)
+            ],
+        ),
+        out_shape=[
+            jax.ShapeDtypeStruct(qp.shape, jnp.bfloat16),
+            jax.ShapeDtypeStruct((tiles, 2 * rows, 1), jnp.float32),
+        ],
+        compiler_params=pltpu.CompilerParams(vmem_limit_bytes=48 * 2**20),
+        cost_estimate=pl.CostEstimate(flops=10**9, bytes_accessed=4 * 10**6, transcendentals=10**6),
+        name="attend",
+    )(span, qp, kv, qdoc, kdoc)
+
+
+def attend_back_kernel(span, qp, gp, op, lse, kv, qdoc, kdoc, dqp, dkv, acc_scr):
+    pairs, tall = qp.shape[0] * qp.shape[2], qp.shape[2]
+    half_runs = pl.num_programs(0)
+    hh, u = pl.program_id(0), pl.program_id(1)
+    lane = lax.broadcasted_iota(jnp.int32, (pairs, 2 * HEAD_DIM), 1)
+
+    @pl.when((hh == 0) & (u == 0))
+    def _():
+        acc_scr[...] = jnp.zeros_like(acc_scr)
+
+    results = []
+    flat = (pairs, 2 * HEAD_DIM)
+    both = gp[...].reshape(flat).astype(jnp.float32) * op[...].reshape(flat).astype(jnp.float32)
+    for side in (0, 1):
+        tile = (hh + side * half_runs) * pl.num_programs(1) + u
+        query = (halves(qp[...].reshape(flat), side) * HEAD_DIM**-0.5).astype(jnp.bfloat16)
+        grad = gp[...].reshape(flat).astype(jnp.float32)
+        if not side:
+            grad = pltpu.roll(grad, HEAD_DIM, 1)
+        grad = jnp.where(lane < HEAD_DIM, 0.0, grad).astype(jnp.bfloat16)
+        here = (lane >= HEAD_DIM) if side else (lane < HEAD_DIM)
+        delta = jnp.sum(jnp.where(here, both, 0.0), axis=1, keepdims=True)
+        docs = qdoc[tile]
+        logs = lse[tile]
+
+        def step(kb, dq):
+            keys = kv[pl.ds(pl.multiple_of(kb * KEY_TILE, KEY_TILE), KEY_TILE), :]
+            scores = mm(query, keys, NT)
+            probs = jnp.where(docs == kdoc[pl.ds(kb, 1), :], jnp.exp(scores - logs), 0.0)
+            grad_scores = (probs * (mm(grad, keys, NT) - delta)).astype(jnp.bfloat16)
+            acc_scr[kb] += mm(grad_scores, query, TN) + mm(probs.astype(jnp.bfloat16), grad, TN)
+            return dq + mm(grad_scores, keys)
+
+        dq = lax.fori_loop(span[tile, 0], span[tile, 1], step, jnp.zeros(flat, jnp.float32))
+        results.append(dq * HEAD_DIM**-0.5)
+    both = jnp.where(lane < HEAD_DIM, results[0], pltpu.roll(results[1], HEAD_DIM, 1))
+    dqp[...] = both.astype(jnp.bfloat16).reshape(dqp.shape)
+
+    @pl.when((hh == half_runs - 1) & (u == pl.num_programs(1) - 1))
+    def _():
+        dkv[...] = acc_scr[...].reshape(dkv.shape).astype(dkv.dtype)
+
+
+def attend_back(span, qp, gp, op, lse, kv, qdoc, kdoc):
+    parts, half_runs, rows, lanes = qp.shape
+    piece = pl.BlockSpec((2, 1, rows, lanes), lambda i, j, s: (j, i, 0, 0))
+    whole = pl.BlockSpec(memory_space=pltpu.VMEM)
+    return pl.pallas_call(
+        attend_back_kernel,
+        grid_spec=pltpu.PrefetchScalarGridSpec(
+            num_scalar_prefetch=1,
+            grid=(half_runs, parts // 2),
+            in_specs=[piece, piece, piece, whole, whole, whole, whole],
+            out_specs=[piece, whole],
+            scratch_shapes=[pltpu.VMEM((kv.shape[0] // KEY_TILE, KEY_TILE, lanes), jnp.float32)],
+        ),
+        out_shape=[
+            jax.ShapeDtypeStruct(qp.shape, jnp.bfloat16),
+            jax.ShapeDtypeStruct(kv.shape, jnp.bfloat16),
+        ],
+        compiler_params=pltpu.CompilerParams(vmem_limit_bytes=48 * 2**20),
+        cost_estimate=pl.CostEstimate(flops=3 * 10**9, bytes_accessed=6 * 10**6, transcendentals=10**6),
+        name="attend_back",
+    )(span, qp, gp, op, lse, kv, qdoc, kdoc)
+
+
+def pack_pairs(value):
+    half = value.shape[1] // 2
+    return jnp.concatenate([value[:, :half], value[:, half:]], axis=-1)
+
+
+def unpack_pairs(value):
+    return jnp.concatenate([value[..., :HEAD_DIM], value[..., HEAD_DIM:]], axis=1)
+
+
+def per_device_split(
+    tokens, attn_gain, w_qkv, w_attn_out, mlp_gain, w_in, w_mlp_out, doc_lengths, cotangent
+):
+    R, W = tokens.shape
+    H, B = lax.axis_size("head"), lax.axis_size("blk")
+    A = W // HEAD_DIM // H
+    G = B // A
+    hw = W // H
+    D = w_qkv.shape[0]
+    F = w_mlp_out.shape[0] // H
+    T = H * B * R
+    N = H * R
+    h, b = lax.axis_index("head"), lax.axis_index("blk")
+    f32, bf16 = jnp.float32, jnp.bfloat16
+    part_groups = [[a * G + g for a in range(A)] for g in range(G)]
+    share_groups = [[a * G + g for g in range(G)] for a in range(A)]
+
+    ends = jnp.cumsum(doc_lengths)
+    places = jnp.arange(T, dtype=jnp.int32)
+    passed = places[:, None] >= ends[None, :]
+    docs = jnp.sum(passed.astype(jnp.int32), axis=1)
+    starts = jnp.sum(jnp.where(passed, doc_lengths[None, :], 0), axis=1)
+    stops = jnp.min(jnp.where(passed, T, ends[None, :]), axis=1)
+    runs = (T // R,)
+    run_docs = docs.reshape(H, A, G, R)
+    run_lo = starts.reshape(H, A, G, R)[..., 0]
+    run_hi = stops.reshape(H, A, G, R)[..., R - 1]
+    g = b % G
+    pick = lambda v: lax.dynamic_index_in_dim(v, g, 2, keepdims=False)
+    qdoc = pick(run_docs).reshape(H * A // 2, 2 * R, 1)
+    lo = pick(run_lo).reshape(H * A // 2, 2)[:, 0] // KEY_TILE
+    hi = (pick(run_hi).reshape(H * A // 2, 2)[:, 1] + KEY_TILE - 1) // KEY_TILE
+    span = jnp.stack([lo, hi], axis=1).astype(jnp.int32)
+    kdoc = docs.reshape(T // KEY_TILE, KEY_TILE)
+    own = lambda v: lax.dynamic_index_in_dim(v.reshape(H, B, R), b, 1, keepdims=False).reshape(N)
+    cosine, sine = rope_tables(own(places - starts), HEAD_DIM)
+
+    tok_all = lax.all_gather(tokens, "head", axis=0, tiled=True)
+    gains = jnp.stack([attn_gain, mlp_gain], axis=1)
+    wq = w_qkv.reshape(D, 3, H, hw).transpose(2, 0, 1, 3).reshape(H, D, 3 * hw)
+    wq = jnp.concatenate(
+        [wq, jnp.broadcast_to(jnp.pad(gains, ((0, 0), (0, 126)))[None], (H, D, 128))], axis=2
+    )
+    wq = lax.all_to_all(wq, "head", 0, 0, tiled=True)
+    wq = lax.all_gather(wq, "blk", axis=0, tiled=False).transpose(1, 0, 2, 3).reshape(W, 3 * hw + 128)
+    gain_one, gain_two = wq[:, 3 * hw].astype(f32), wq[:, 3 * hw + 1].astype(f32)
+    full_out = lax.all_gather(w_attn_out, ("head", "blk"), axis=0, tiled=True)
+    wm = jnp.concatenate(
+        [
+            w_in.reshape(D, 2, H, F).transpose(2, 0, 1, 3).reshape(H, D, 2 * F),
+            w_mlp_out.reshape(H, F, D).transpose(0, 2, 1),
+        ],
+        axis=2,
+    )
+    wm = lax.all_to_all(wm, "head", 0, 0, tiled=True)
+    wm = lax.all_gather(wm, "blk", axis=0, tiled=False).transpose(1, 0, 2, 3).reshape(W, 3 * F)
+    cot_all = lax.all_gather(cotangent, "head", axis=0, tiled=True)
+
+    inputs = tok_all.astype(f32)
+    normed_one = layer_norm(inputs, gain_one).astype(bf16)
+    projected = mm(normed_one, wq[:, : 3 * hw])
+    query = rotate(projected[:, :hw], cosine, sine).astype(bf16)
+    keys = rotate(projected[:, hw : 2 * hw], cosine, sine).astype(bf16)
+    values = projected[:, 2 * hw :].astype(bf16)
+    split = lambda v: v.reshape(H, R, A, HEAD_DIM).transpose(2, 0, 1, 3)
+    qp = lax.all_to_all(
+        pack_pairs(split(query)), "blk", 0, 0, tiled=True, axis_index_groups=part_groups
+    )
+    kv = lax.all_to_all(
+        jnp.concatenate([split(keys), split(values)], axis=-1),
+        "blk", 0, 0, tiled=True, axis_index_groups=part_groups,
+    )
+    kv = lax.all_gather(kv, "blk", axis=0, tiled=False, axis_index_groups=share_groups)
+    kv = kv.transpose(2, 1, 0, 3, 4).reshape(T, 2 * HEAD_DIM)
+    op, lse = attend(span, qp, kv, qdoc, kdoc)
+    back = lax.all_to_all(op, "blk", 0, 0, tiled=True, axis_index_groups=part_groups)
+    mixed = unpack_pairs(back).transpose(1, 2, 0, 3).reshape(N, hw)
+    mixed_all = lax.all_gather(mixed, "head", axis=1, tiled=True)
+
+    middle = inputs + mm(mixed_all, full_out)
+    normed_two, _ = jax.vjp(layer_norm, middle, gain_two)
+    normed_two = normed_two.astype(bf16)
+    lifted = mm(normed_two, wm[:, : 2 * F])
+    activated, geglu_pull = jax.vjp(gelu_gate, lifted)
+    activated = activated.astype(bf16)
+    out_part = mm(activated, wm[:, 2 * F :], NT).astype(bf16)
+    output = lax.psum_scatter(out_part, "head", scatter_dimension=0, tiled=True).astype(f32)
+    grad_act = mm(cot_all, wm[:, 2 * F :])
+    grad_lifted = geglu_pull(grad_act)[0].astype(bf16)
+    grad_two = mm(grad_lifted, wm[:, : 2 * F], NT).astype(bf16)
+    grad_two = lax.psum_scatter(grad_two, "head", scatter_dimension=0, tiled=True).astype(f32)
+    term_mlp = jnp.concatenate(
+        [mm(normed_two, grad_lifted, TN), mm(cot_all, activated, TN)], axis=1
+    ).astype(bf16)
+    term_mlp = term_mlp.reshape(H, B, D, 3 * F).transpose(1, 0, 2, 3)
+    sum_mlp = lax.psum_scatter(term_mlp, "blk", scatter_dimension=0, tiled=False)
+    middle_own = lax.dynamic_slice_in_dim(middle, h * R, R, 0)
+    output = (middle_own + output).astype(bf16)
+    _, norm_two_pull = jax.vjp(layer_norm, middle_own, gain_two)
+    grad_middle, grad_gain_two = norm_two_pull(grad_two)
+    grad_middle = grad_middle + cotangent.astype(f32)
+    grad_branch = grad_middle.astype(bf16)
+    grad_mixed = mm(grad_branch, full_out, NT).astype(bf16)
+    branch_all = lax.all_gather(grad_branch, "head", axis=0, tiled=True)
+    gp = lax.all_to_all(grad_mixed, "head", 1, 0, tiled=True)
+    gp = lax.all_to_all(
+        pack_pairs(split(gp)), "blk", 0, 0, tiled=True, axis_index_groups=part_groups
+    )
+    dqp, dkv = attend_back(span, qp, gp, op, lse, kv, qdoc, kdoc)
+    dqp = lax.all_to_all(dqp, "blk", 0, 0, tiled=True, axis_index_groups=part_groups)
+    dkv = dkv.reshape(H, A, G, R, 2 * HEAD_DIM).transpose(2, 1, 0, 3, 4)
+    dkv = lax.psum_scatter(dkv, "blk", scatter_dimension=0, tiled=False, axis_index_groups=share_groups)
+    dkv = lax.all_to_all(dkv, "blk", 0, 0, tiled=True, axis_index_groups=part_groups)
+    merge = lambda v: v.transpose(1, 2, 0, 3).reshape(N, hw)
+    _, rope_pull = jax.vjp(
+        partial(rotate_pair, cosine=cosine, sine=sine), projected[:, :hw], projected[:, hw : 2 * hw]
+    )
+    grad_query, grad_keys = rope_pull(
+        (merge(unpack_pairs(dqp)).astype(f32), merge(dkv[..., :HEAD_DIM]).astype(f32))
+    )
+    grad_projected = jnp.concatenate(
+        [grad_query.astype(bf16), grad_keys.astype(bf16), merge(dkv[..., HEAD_DIM:])], axis=1
+    )
+    grad_one = mm(grad_projected, wq[:, : 3 * hw], NT).astype(bf16)
+    grad_one = lax.psum_scatter(grad_one, "head", scatter_dimension=0, tiled=True).astype(f32)
+    _, norm_one_pull = jax.vjp(layer_norm, tokens.astype(f32), gain_one)
+    grad_input, grad_gain_one = norm_one_pull(grad_one)
+    input_grad = grad_middle + grad_input
+    term_qkv = mm(normed_one, grad_projected, TN)
+    gain_terms = jnp.pad(jnp.stack([grad_gain_one, grad_gain_two], axis=1), ((0, 0), (0, 126)))
+    term_qkv = jnp.concatenate([term_qkv, gain_terms], axis=1).astype(bf16)
+    term_qkv = term_qkv.reshape(H, B, D, 3 * hw + 128).transpose(1, 0, 2, 3)
+    term_out = mm(mixed, branch_all, TN).astype(bf16).reshape(B, D, W)
+    sum_qkv = lax.psum_scatter(term_qkv, "blk", scatter_dimension=0, tiled=False)
+    sum_out = lax.psum_scatter(term_out, "blk", scatter_dimension=0, tiled=False)
+    sum_mlp = lax.all_to_all(sum_mlp, "head", 0, 0, tiled=True).astype(f32)
+    sum_qkv = lax.all_to_all(sum_qkv, "head", 0, 0, tiled=True).astype(f32)
+    in_grad = sum_mlp[:, :, : 2 * F].reshape(H, D, 2, F).transpose(1, 2, 0, 3).reshape(D, 2 * H * F)
+    down_grad = sum_mlp[:, :, 2 * F :].transpose(0, 2, 1).reshape(H * F, D)
+    qkv_grad = sum_qkv[:, :, : 3 * hw].reshape(H, D, 3, hw).transpose(1, 2, 0, 3).reshape(D, 3 * W)
+    gain_sums = jnp.sum(sum_qkv[:, :, 3 * hw : 3 * hw + 2], axis=0)
+    return (
+        output,
+        input_grad,
+        gain_sums[:, 0],
+        qkv_grad,
+        sum_out.astype(f32),
+        gain_sums[:, 1],
+        in_grad,
+        down_grad,
+    )
+
+
+def per_device(tokens, attn_gain, w_qkv, *rest):
+    heads, blocks = lax.axis_size("head"), lax.axis_size("blk")
+    parts = tokens.shape[1] // HEAD_DIM // heads
+    fits = (
+        blocks % parts == 0
+        and blocks // parts == 2
+        and parts % 2 == 0
+        and heads % 2 == 0
+        and w_qkv.shape[0] % 16 == 0
+        and tokens.shape[0] % 128 == 0
+    )
+    chosen = per_device_split if fits else per_device_general
+    return chosen(tokens, attn_gain, w_qkv, *rest)
+
+
 def solution(mesh):
     placed = (
         P(("head", "blk"), None),

time: 1440 us -> 666 us (0.46)
  waiting for transfers between devices: 850 us -> 376 us
  loops' own time: 177 us -> 0 us
  other arithmetic: 130 us -> 30.6 us
  matrix products: 123 us -> 38.8 us
  blocking collectives: 59.5 us -> 95.3 us
  Pallas kernels: 0 us -> 34.3 us
    reduce_scatter x1 -> x6, waiting for transfers between devices: 521 us -> 118 us  [the longest x1 34 us: per_device_split(): lax.psum_scatter(term_qkv, 'blk', scatter_dimension=0, tiled=False)]
    another operation x74 -> x0, loops' own time: 177 us -> none  [the longest x1 86.3 us: fold_forward(): return lax.fori_loop(0, key_part.shape[0] // own_rows, fold_one_run, state)]
    ppermute x16 -> x0, waiting for transfers between devices: 111 us -> none  [from_behind(): lax.ppermute(value, axis, [(i, (i + by) % devices) for i in range(devices)])]
    dot_general x194 -> x12, matrix products: 123 us -> 38.8 us  [mm(): lax.dot_general(left, right, dims, preferred_element_type=jnp.float32)]
    all_to_all x1 -> x8, blocking collectives: 17.3 us -> 95.3 us  [the longest x1 17.9 us: per_device_split(): lax.all_to_all(jnp.concatenate([split(keys), split(values)], axis=-1), 'b...]
    unnamed x1 -> x0, blocking collectives: 42.3 us -> none
    reduce_max x65 -> x0, other arithmetic: 42 us -> none  [the longest x64 41.3 us: block_live(): jnp.max(key_docs)]
    pallas_call x0 -> x2, Pallas kernels: none -> 34.3 us  [the longest x1 18.9 us: attend_back(): pl.pallas_call(attend_back_kernel, grid_spec=pltpu.PrefetchScalarGridSpec...]
  transfers between devices with their start and end apart: 27 -> 18, of which waited for: 24 -> 16; matrix products, arithmetic and copies ran while one was open for 11% -> 12% of each run, Pallas kernels for 0% -> 2%
where the time goes in v1:
time: 666 us; the launch traced here: 656 us
  waiting for transfers between devices  376 us (56%)
  blocking collectives  95.3 us (14%)
  local copies, waits for them, and re-layouts  54.5 us (8%)
  matrix products  38.8 us (6%)
  Pallas kernels  34.3 us (5%)
  other arithmetic  30.6 us (5%)
  between operations  15.3 us (2%)
  starting transfers between devices  11.8 us (2%)
    unnamed x16, waiting for transfers between devices  96.1 us
    all_gather x1, waiting for transfers between devices, per_device_split(): lax.all_gather(wm, 'blk', axis=0, tiled=False).transpose(1, 0, 2, 3)  43.4 us
    dot_general x12, matrix products, mm(): lax.dot_general(left, right, dims, preferred_element_type=jnp.float32)  38.8 us
    reduce_scatter x1, waiting for transfers between devices, per_device_split(): lax.psum_scatter(term_qkv, 'blk', scatter_dimension=0, tiled=False)  34 us
    reduce_scatter x1, waiting for transfers between devices, per_device_split(): lax.psum_scatter(out_part, 'head', scatter_dimension=0, tiled=True)  29.5 us
    all_gather x1, waiting for transfers between devices, per_device_split(): mixed_all = lax.all_gather(mixed, 'head', axis=1, tiled=True)  28 us
    all_gather x1, waiting for transfers between devices, per_device_split(): lax.all_gather(wq, 'blk', axis=0, tiled=False).transpose(1, 0, 2, 3)  26.6 us
    reduce_scatter x1, waiting for transfers between devices, per_device_split(): lax.psum_scatter(grad_two, 'head', scatter_dimension=0, tiled=True)  21.1 us
  transfers between devices with their start and end apart: 18, of which 16 were waited for; matrix products, arithmetic and copies ran while one was open for 12% of the time, Pallas kernels for 2%

profile of v1, /device:TPU:0, one launch (start us, length us, event | category | flops | bytes accessed | tf_op | source)
XLA Modules:
  0.0 656.2 jit_solution(15283565808160161798)
XLA Ops:
  10.2 10.7 %all_to_all.66 = bf16[4,32,896]{2,1,0:T(8,128)(2,1)} all-to-all(bf16[4,32,896]{2,1,0:T(8,128)(2,1)S(1)} %pad_maximum_fusion.8), channel_id=1, replica_groups=mesh['head'=4,'blk'=8] {'head'}, dimensions={0} | all-to-all | bytes 458752 | tf_op jit(solution)/shard_map/all_to_all | solution.py:613
  23.2 16.1 %all-gather.12.cloned.1.call-done = bf16[512,1024]{1,0:T(8,128)(2,1)} async-done(((bf16[128,1024]{1,0:T(8,128)(2,1)}), bf16[512,1024]{1,0:T(8,128)(2,1)}) %all-gather.12.cloned.1.call-update) | async-done | bytes 1048592 | tf_op jit(solution)/shard_map/all_gather | solution.py:607
  39.2 1.5 convert_reduce_fusion
  41.2 26.6 %all-gather.22.cloned.1.call-done = bf16[32,32,896]{2,1,0:T(8,128)(2,1)} async-done(((bf16[4,32,896]{2,1,0:T(8,128)(2,1)}), bf16[32,32,896]{2,1,0:T(8,128)(2,1)}) %all-gather.22.cloned.1.call-update) | async-done | bytes 1835024 | tf_op jit(solution)/shard_map/all_gather | solution.py:614
  67.8 1.7 copy.180
  72.8 1.2 copy.182
  77.2 1.2 add_convert_fusion.4
  78.6 1.3 pad_maximum_fusion.2
  80.0 17.9 %all_to_all.67 = bf16[4,4,128,128]{2,1,3,0:T(4,128)(2,1)S(1)} all-to-all(bf16[4,4,128,128]{2,1,3,0:T(4,128)(2,1)S(1)} %pad_maximum_fusion.2), channel_id=1, replica_groups={{0,2,4,6},{1,3,5,7},{8,10,12,14},{9,11,13,15},{16,18,20,22},{17,19,21,2..., dimensions={0} | all-to-all | bytes 1048576 | tf_op jit(solution)/shard_map/all_to_all | solution.py:638
  101.7 3.4 all-to-all-start.1
  107.2 1.3 copy.192
  108.5 5.0 all-to-all-done.1.qp
  113.5 15.3 %attend.1 = (bf16[4,2,128,128]{3,2,1,0:T(8,128)(2,1)S(1)}, f32[8,256,1]{2,1,0:T(8,128)S(1)}) custom-call(s32[8,2]{1,0:T(8,128)S(1)} %pad_add_fusion.span, bf16[4,2,128,128]{3,2,1,0:T(8,128)(2,1)S(1)} %all-to-all-done.1.qp, bf16[4096,128]{1,0:T(8,128)(2,1)S(1)} %bitcast.122, s32[8,256,1]{2,1,0:T(8,128)S(1)} %reshape.385.qdoc, s32[16,256]{1,0:T(8,128)S(1)} %reshape.358.kdoc), custom_call_target="tpu_custom_call" | custom-call | flops 1000000000 | bytes 4000000 | tf_op jit(solution)/shard_map/attend/pallas_call | solution.py:474
  129.8 11.2 %all_to_all.68 = bf16[4,2,128,128]{3,2,1,0:T(8,128)(2,1)S(1)} all-to-all(bf16[4,2,128,128]{3,2,1,0:T(8,128)(2,1)S(1)} %get-tuple-element.12.op), channel_id=1, replica_groups={{0,2,4,6},{1,3,5,7},{8,10,12,14},{9,11,13,15},{16,18,20,22},{17,19,21,2..., dimensions={0} | all-to-all | bytes 524288 | tf_op jit(solution)/shard_map/all_to_all | solution.py:645
  142.3 1.2 reshape.362
  143.6 2.4 reshape.360
  146.0 1.3 copy.236
  149.4 12.6 %all_to_all.69 = bf16[4,32,1968]{2,1,0:T(8,128)(2,1)} all-to-all(bf16[4,32,1968]{2,1,0:T(8,128)(2,1)S(1)} %pad_maximum_fusion.3), channel_id=1, replica_groups=mesh['head'=4,'blk'=8] {'head'}, dimensions={0} | all-to-all | bytes 1007616 | tf_op jit(solution)/shard_map/all_to_all | solution.py:624
  163.0 6.5 all-gather.16.cloned.1.call-done
  169.5 28.0 %all-gather.14.cloned.1.call-done = bf16[512,1024]{0,1:T(8,128)(2,1)} async-done(((bf16[512,256]{0,1:T(8,128)(2,1)}), bf16[512,1024]{0,1:T(8,128)(2,1)}) %all-gather.14.cloned.1.call-update) | async-done | bytes 1048592 | tf_op jit(solution)/shard_map/all_gather | solution.py:647
  197.5 3.5 fusion.65
  201.0 1.3 copy-done.2
  202.7 43.4 %all-gather.26.cloned.1.call-done = bf16[32,32,1968]{2,1,0:T(8,128)(2,1)} async-done(((bf16[4,32,1968]{2,1,0:T(8,128)(2,1)}), bf16[32,32,1968]{2,1,0:T(8,128)(2,1)}) %all-gather.26.cloned.1.call-update) | async-done | bytes 4030480 | tf_op jit(solution)/shard_map/all_gather | solution.py:625
  246.1 2.6 copy.197
  248.8 1.9 copy-done.8
  250.7 3.4 fusion.2
  254.1 19.2 %all-gather.18.cloned.1.call-done = bf16[512,1024]{1,0:T(8,128)(2,1)} async-done(((bf16[128,1024]{1,0:T(8,128)(2,1)}), bf16[512,1024]{1,0:T(8,128)(2,1)}) %all-gather.18.cloned.1.call-update) | async-done | bytes 1048592 | tf_op jit(solution)/shard_map/all_gather | solution.py:626
  273.3 6.4 fusion.37
  281.7 1.5 copy-done.9
  283.2 2.8 fusion.9
  286.1 4.0 convolution_convert_fusion.4
  291.6 1.3 multiply_reduce_fusion.1
  292.9 21.1 %reduce-scatter.10.cloned.1.call-done = bf16[128,1024]{1,0:T(8,128)(2,1)} async-done(((bf16[512,1024]{1,0:T(8,128)(2,1)}), bf16[128,1024]{1,0:T(8,128)(2,1)}) %reduce-scatter.10.cloned.1.call-update) | async-done | bytes 262160 | tf_op jit(solution)/shard_map/reduce_scatter | solution.py:660
  313.9 1.4 fusion.33
  315.4 29.5 %reduce-scatter.8.cloned.1.call-done = bf16[128,1024]{1,0:T(8,128)(2,1)} async-done(((bf16[512,1024]{1,0:T(8,128)(2,1)}), bf16[128,1024]{1,0:T(8,128)(2,1)}) %reduce-scatter.8.cloned.1.call-update) | async-done | bytes 262160 | tf_op jit(solution)/shard_map/reduce_scatter | solution.py:656
  344.8 2.1 fusion.56
  347.8 2.5 convolution_convert_fusion.6
  351.1 9.4 %all_to_all.70 = bf16[128,4,256]{0,2,1:T(8,128)(2,1)S(1)} all-to-all(bf16[128,4,256]{0,2,1:T(8,128)(2,1)} %bitcast.159), channel_id=1, replica_groups=mesh['head'=4,'blk'=8] {'head'}, dimensions={1} | all-to-all | bytes 524288 | tf_op jit(solution)/shard_map/all_to_all | solution.py:674
  362.8 12.1 %all_to_all.71.gp = bf16[4,2,128,128]{3,2,1,0:T(8,128)(2,1)S(1)} all-to-all(bf16[4,2,128,128]{3,2,1,0:T(8,128)(2,1)S(1)} %pad_maximum_fusion.7), channel_id=1, replica_groups={{0,2,4,6},{1,3,5,7},{8,10,12,14},{9,11,13,15},{16,18,20,22},{17,19,21,2..., dimensions={0} | all-to-all | bytes 524288 | tf_op jit(solution)/shard_map/all_to_all | solution.py:675
  374.9 18.9 %attend_back.1 = (bf16[4,2,128,128]{3,2,1,0:T(8,128)(2,1)S(1)}, bf16[4096,128]{1,0:T(8,128)(2,1)S(1)}) custom-call(s32[8,2]{1,0:T(8,128)S(1)} %pad_add_fusion.span, bf16[4,2,128,128]{3,2,1,0:T(8,128)(2,1)S(1)} %all-to-all-done.1.qp, bf16[4,2,128,128]{3,2,1,0:T(8,128)(2,1)S(1)} %all_to_all.71.gp, bf16[4,2,128,128]{3,2,1,0:T(8,128)(2,1)S(1)} %get-tuple-element.12.op, ...), custom_call_target="tpu_custom_call" | custom-call | flops 3000000000 | bytes 6000000 | tf_op jit(solution)/shard_map/attend_back/pallas_call | solution.py:542
  395.0 9.5 %all_to_all.72 = bf16[4,2,128,128]{3,2,1,0:T(8,128)(2,1)S(1)} all-to-all(bf16[4,2,128,128]{3,2,1,0:T(8,128)(2,1)S(1)} %get-tuple-element.14), channel_id=1, replica_groups={{0,2,4,6},{1,3,5,7},{8,10,12,14},{9,11,13,15},{16,18,20,22},{17,19,21,2..., dimensions={0} | all-to-all | bytes 524288 | tf_op jit(solution)/shard_map/all_to_all | solution.py:679
  404.6 3.5 all-to-all-start.8
  409.4 12.1 %all-to-all-done.8 = bf16[4,4,128,128]{3,2,1,0:T(8,128)(2,1)S(1)} async-done(((bf16[4,4,128,128]{3,2,1,0:T(8,128)(2,1)}), bf16[4,4,128,128]{3,2,1,0:T(8,128)(2,1)S(1)}, u32[]{:S(2)}, u32[]{:S(2)}) %all-to-all-start.8) | async-done | bytes 524320 | tf_op jit(solution)/shard_map/all_to_all | solution.py:682
  425.2 2.0 convolution_convert_fusion.3
  427.3 3.2 fusion.12
  430.5 2.7 copy.211
  433.3 5.0 convolution_convert_fusion
  438.3 3.3 copy.210
  441.6 4.6 maximum_bitcast_fusion
  447.3 2.5 convolution_convert_fusion.5
  450.1 2.4 convolution_convert_fusion.1
  452.5 17.4 %reduce-scatter.14.cloned.1.call-done = bf16[128,1024]{1,0:T(8,128)(2,1)} async-done(((bf16[512,1024]{1,0:T(8,128)(2,1)}), bf16[128,1024]{1,0:T(8,128)(2,1)}) %reduce-scatter.14.cloned.1.call-update) | async-done | bytes 262160 | tf_op jit(solution)/shard_map/reduce_scatter | solution.py:694
  470.0 1.2 fusion.35
  471.2 1.3 fusion.34
  472.8 1.5 copy_bitcast_fusion
  475.6 93.3 %all-reduce.11.cloned.1.call-done = bf16[8,4,32,1968]{3,2,0,1:T(8,128)(2,1)} async-done(((bf16[8,4,32,1968]{3,2,0,1:T(8,128)(2,1)}), bf16[8,4,32,1968]{3,2,0,1:T(8,128)(2,1)}) %all-reduce.11.cloned.1.call-update) | async-done | bytes 4030480
  568.9 1.7 dynamic-slice_bitcast_fusion
  570.6 11.9 %all_to_all.73 = bf16[4,32,1968]{2,1,0:T(8,128)(2,1)S(1)} all-to-all(bf16[4,32,1968]{2,1,0:T(8,128)(2,1)S(1)} %dynamic-slice_bitcast_fusion), channel_id=1, replica_groups=mesh['head'=4,'blk'=8] {'head'}, dimensions={0} | all-to-all | bytes 1007616 | tf_op jit(solution)/shard_map/all_to_all | solution.py:705
  583.8 1.5 reshape.371
  586.8 15.8 %reduce-scatter.18.cloned.1.call-done = bf16[1,32,1024]{2,1,0:T(8,128)(2,1)} async-done(((bf16[8,32,1024]{2,1,0:T(8,128)(2,1)}), bf16[1,32,1024]{2,1,0:T(8,128)(2,1)}) %reduce-scatter.18.cloned.1.call-update) | async-done | bytes 65552 | tf_op jit(solution)/shard_map/reduce_scatter | solution.py:704
  602.6 1.5 bitcast_convert_fusion
  604.1 34.0 %reduce-scatter.16.cloned.1.call-done = bf16[1,4,32,896]{3,2,1,0:T(8,128)(2,1)} async-done(((bf16[8,4,32,896]{3,2,1,0:T(8,128)(2,1)}), bf16[1,4,32,896]{3,2,1,0:T(8,128)(2,1)}) %reduce-scatter.16.cloned.1.call-update) | async-done | bytes 229392 | tf_op jit(solution)/shard_map/reduce_scatter | solution.py:703
  638.1 3.6 all-to-all-start.9
  642.9 4.2 all-to-all-done.9
  (221 shorter events, 46.3 us)
Async XLA Ops:
  7.2 13.8 %copy-start.37 = (s32[32]{0:T(128)S(1)}, s32[32]{0:T(128)}, u32[]{:S(2)}) copy-start(s32[32]{0:T(128)} %param.16) | copy-start | bytes 388
  7.2 32.0 %all-gather.12.cloned.1.call-start = ((), (), s32[]{:S(2)}) async-start(), calls=%async_computation.17 | async-start | bytes 1310720 | tf_op jit(solution)/shard_map/all_gather | solution.py:607
  7.9 59.9 %all-gather.22.cloned.1.call-start = ((), (), s32[]{:S(2)}) async-start(), calls=%async_computation.28 | async-start | bytes 2064384 | tf_op jit(solution)/shard_map/all_gather | solution.py:614
  20.9 86.3 %all-gather.24.cloned.1.call-start = ((), (), s32[]{:S(2)}) async-start(), calls=%async_computation.29 | async-start | bytes 1572864 | tf_op jit(solution)/shard_map/all_gather | solution.py:642
  22.2 0.6 copy-start.32
  22.5 0.7 copy-start.22
  22.5 51.6 %copy-start.20 = (f32[512,64]{0,1:T(8,128)}, f32[512,64]{0,1:T(8,128)S(1)}, u32[]{:S(2)}) copy-start(f32[512,64]{0,1:T(8,128)S(1)} %get-tuple-element.65) | copy-start | bytes 393220
  39.2 1.5 copy-start.5
  40.8 29.8 %copy-start.35 = (f32[512]{0:T(512)}, f32[512]{0:T(512)S(1)}, u32[]{:S(2)}) copy-start(f32[512]{0:T(512)S(1)} %broadcast_multiply_fusion.4) | copy-start | bytes 6148
  41.2 29.4 %copy-start.38 = (f32[512]{0:T(512)}, f32[512]{0:T(512)S(1)}, u32[]{:S(2)}) copy-start(f32[512]{0:T(512)S(1)} %add_rsqrt_fusion.1) | copy-start | bytes 6148
  69.5 2.2 copy-start.10
  70.6 1.1 copy-start.29
  75.3 1.9 copy-start.18
  79.9 19.6 %copy-start.31 = (s32[4096]{0:T(1024)S(1)}, s32[4096]{0:T(1024)}, u32[]{:S(2)}) copy-start(s32[4096]{0:T(1024)} %get-tuple-element.27) | copy-start | bytes 49156
  80.0 19.7 %copy-start.33 = (s32[4096]{0:T(1024)S(1)}, s32[4096]{0:T(1024)}, u32[]{:S(2)}) copy-start(s32[4096]{0:T(1024)} %copy-done.32) | copy-start | bytes 49156
  99.0 70.5 %all-gather.16.cloned.1.call-start = ((), (), s32[]{:S(2)}) async-start(), calls=%async_computation.19 | async-start | bytes 2162688 | tf_op jit(solution)/shard_map/all_gather | solution.py:616
  101.7 11.8 %all-to-all-start.1 = ((bf16[4,2,128,128]{3,2,1,0:T(8,128)(2,1)}), bf16[4,2,128,128]{3,2,1,0:T(8,128)(2,1)S(1)}, u32[]{:S(2)}, u32[]{:S(2)}) async-start(bf16[4,2,128,128]{3,2,1,0:T(8,128)(2,1)} %pad_maximum_fusion.6), calls=%async_computation.1 | async-start | bytes 524288 | tf_op jit(solution)/shard_map/all_to_all | solution.py:635
  105.1 92.4 %all-gather.14.cloned.1.call-start = ((), (), s32[]{:S(2)}) async-start(), calls=%async_computation.18 | async-start | bytes 1310720 | tf_op jit(solution)/shard_map/all_gather | solution.py:647
  128.8 1.0 copy-start
  141.5 6.8 %copy-start.13 = (bf16[4,128,4,64]{1,0,3,2:T(4,128)(2,1)}, bf16[4,128,4,64]{1,0,3,2:T(4,128)(2,1)S(1)}, u32[]{:S(2)}) copy-start(bf16[4,128,4,64]{1,0,3,2:T(4,128)(2,1)S(1)} %copy.194) | copy-start | bytes 786436
  142.3 103.8 %all-gather.26.cloned.1.call-start = ((), (), s32[]{:S(2)}) async-start(), calls=%async_computation.30 | async-start | bytes 4718592 | tf_op jit(solution)/shard_map/all_gather | solution.py:625
  162.1 111.3 %all-gather.18.cloned.1.call-start = ((), (), s32[]{:S(2)}) async-start(), calls=%async_computation.21 | async-start | bytes 1310720 | tf_op jit(solution)/shard_map/all_gather | solution.py:626
  162.8 151.1 %reduce-scatter.10.cloned.1.call-start = ((), (), s32[]{:S(2)}) async-start(), calls=%async_computation.22 | async-start | bytes 1310720 | tf_op jit(solution)/shard_map/reduce_scatter | solution.py:660
  201.0 1.4 copy-start.2
  246.1 4.6 copy-start.3
  246.1 4.6 copy-start.34
  248.8 1.9 copy-start.8
  273.3 6.4 copy-start.12
  279.8 1.1 copy-start.41
  279.8 3.4 copy-start.9
  280.5 1.2 copy-start.19
  280.5 5.6 copy-start.24
  286.0 58.8 %reduce-scatter.8.cloned.1.call-start = ((), (), s32[]{:S(2)}) async-start(), calls=%async_computation.20 | async-start | bytes 1310720 | tf_op jit(solution)/shard_map/reduce_scatter | solution.py:656
  290.1 114.4 %reduce-scatter.12.cloned.1.call-start = ((), (), s32[]{:S(2)}) async-start(), calls=%async_computation.23 | async-start | bytes 1572864 | tf_op jit(solution)/shard_map/reduce_scatter | solution.py:681
  291.6 55.4 %copy-start.16 = (bf16[128,1024]{1,0:T(8,128)(2,1)S(1)}, bf16[128,1024]{1,0:T(8,128)(2,1)}, u32[]{:S(2)}) copy-start(bf16[128,1024]{1,0:T(8,128)(2,1)} %param.17) | copy-start | bytes 786436
  361.5 13.4 %copy-start.1 = (f32[8,256,1]{2,1,0:T(8,128)S(1)}, f32[8,256,1]{2,1,0:T(8,128)}, u32[]{:S(2)}) copy-start(f32[8,256,1]{2,1,0:T(8,128)} %copy-done) | copy-start | bytes 24580
  404.6 16.9 %all-to-all-start.8 = ((bf16[4,4,128,128]{3,2,1,0:T(8,128)(2,1)}), bf16[4,4,128,128]{3,2,1,0:T(8,128)(2,1)S(1)}, u32[]{:S(2)}, u32[]{:S(2)}) async-start(bf16[4,4,128,128]{3,2,1,0:T(8,128)(2,1)} %bitcast.163), calls=%async_computation.11 | async-start | bytes 1048576 | tf_op jit(solution)/shard_map/all_to_all | solution.py:682
  408.0 39.3 %all-gather.20.cloned.1.call-start = ((), (), s32[]{:S(2)}) async-start(), calls=%async_computation.26 | async-start | bytes 1310720 | tf_op jit(solution)/shard_map/all_gather | solution.py:673
  408.8 61.2 %reduce-scatter.14.cloned.1.call-start = ((), (), s32[]{:S(2)}) async-start(), calls=%async_computation.24 | async-start | bytes 1310720 | tf_op jit(solution)/shard_map/reduce_scatter | solution.py:694
  421.8 1.3 copy-start.21
  423.2 0.9 copy-start.23
  423.4 1.9 copy-start.11
  423.4 1.9 copy-start.26
  424.4 0.7 copy-start.27
  424.4 0.8 copy-start.28
  425.2 2.1 copy-start.25
  427.3 141.6 %all-reduce.11.cloned.1.call-start = ((), (), s32[]{:S(2)}) async-start(), calls=%async_computation.31 | async-start | bytes 8388608
  430.5 2.7 copy-start.4
  446.2 0.9 copy-start.7
  446.2 1.1 copy-start.14
  446.2 3.9 copy-start.6
  446.2 3.9 copy-start.30
  446.2 3.9 copy-start.36
  446.2 3.9 copy-start.39
  446.3 156.3 %reduce-scatter.18.cloned.1.call-start = ((), (), s32[]{:S(2)}) async-start(), calls=%async_computation.27 | async-start | bytes 589824 | tf_op jit(solution)/shard_map/reduce_scatter | solution.py:704
  449.8 188.3 %reduce-scatter.16.cloned.1.call-start = ((), (), s32[]{:S(2)}) async-start(), calls=%async_computation.25 | async-start | bytes 2064384 | tf_op jit(solution)/shard_map/reduce_scatter | solution.py:703
  474.3 0.7 copy-start.40
  585.4 56.4 %copy-start.15 = (bf16[128,1024]{1,0:T(8,128)(2,1)S(1)}, bf16[128,1024]{1,0:T(8,128)(2,1)}, u32[]{:S(2)}) copy-start(bf16[128,1024]{1,0:T(8,128)(2,1)} %reduce-scatter.14.cloned.1.call-done) | copy-start | bytes 786436
  585.4 56.4 %copy-start.17 = (bf16[128,1024]{1,0:T(8,128)(2,1)S(1)}, bf16[128,1024]{1,0:T(8,128)(2,1)}, u32[]{:S(2)}) copy-start(bf16[128,1024]{1,0:T(8,128)(2,1)} %param.17) | copy-start | bytes 786436
  638.1 8.9 %all-to-all-start.9 = ((bf16[4,32,896]{2,1,0:T(8,128)(2,1)}), bf16[4,32,896]{2,1,0:T(8,128)(2,1)S(1)}, u32[]{:S(2)}, u32[]{:S(2)}) async-start(bf16[4,32,896]{2,1,0:T(8,128)(2,1)} %bitcast.170), calls=%async_computation.14 | async-start | bytes 458752 | tf_op jit(solution)/shard_map/all_to_all | solution.py:706
Sparse Core Ops, SparseCore 0:
  9.9 29.3 all-gather.11
  40.9 26.9 all-gather.21
  99.1 8.0 all-gather.23
  110.0 59.4 all-gather.15
  171.8 25.6 all-gather.13
  198.9 47.1 all-gather.25
  247.9 25.3 all-gather.17
  286.2 27.7 reduce-scatter.9
  317.1 27.6 reduce-scatter.7
  395.2 6.4 reduce-scatter.11
  411.4 27.7 all-gather.19
  442.2 27.7 reduce-scatter.13
  472.3 96.4 all-reduce.10
  571.5 31.0 reduce-scatter.17
  604.9 33.2 reduce-scatter.15

commit v2 on v1

--- a/solution.py
+++ b/solution.py
@@ -2,6 +2,7 @@
 
 import jax
 import jax.numpy as jnp
+import numpy as np
 from jax import lax
 from jax.experimental import pallas as pl
 from jax.experimental.pallas import tpu as pltpu
@@ -504,16 +505,19 @@
 
     results = []
     flat = (pairs, 2 * HEAD_DIM)
-    both = gp[...].reshape(flat).astype(jnp.float32) * op[...].reshape(flat).astype(jnp.float32)
     for side in (0, 1):
         tile = (hh + side * half_runs) * pl.num_programs(1) + u
         query = (halves(qp[...].reshape(flat), side) * HEAD_DIM**-0.5).astype(jnp.bfloat16)
-        grad = gp[...].reshape(flat).astype(jnp.float32)
+        pieces = []
+        for n in range(2):
+            piece = gp[n, hh + side * half_runs].astype(jnp.float32)
+            pieces += [pltpu.roll(piece, HEAD_DIM, 1), piece]
+        grad = jnp.where(lane < HEAD_DIM, 0.0, jnp.concatenate(pieces, axis=0))
+        mixed = op[...].reshape(flat).astype(jnp.float32)
         if not side:
-            grad = pltpu.roll(grad, HEAD_DIM, 1)
-        grad = jnp.where(lane < HEAD_DIM, 0.0, grad).astype(jnp.bfloat16)
-        here = (lane >= HEAD_DIM) if side else (lane < HEAD_DIM)
-        delta = jnp.sum(jnp.where(here, both, 0.0), axis=1, keepdims=True)
+            mixed = pltpu.roll(mixed, HEAD_DIM, 1)
+        delta = jnp.sum(grad * mixed, axis=1, keepdims=True)
+        grad = grad.astype(jnp.bfloat16)
         docs = qdoc[tile]
         logs = lse[tile]
 
@@ -538,13 +542,14 @@
 def attend_back(span, qp, gp, op, lse, kv, qdoc, kdoc):
     parts, half_runs, rows, lanes = qp.shape
     piece = pl.BlockSpec((2, 1, rows, lanes), lambda i, j, s: (j, i, 0, 0))
+    grads = pl.BlockSpec((2, 2 * half_runs, rows // 2, lanes), lambda i, j, s: (j, 0, 0, 0))
     whole = pl.BlockSpec(memory_space=pltpu.VMEM)
     return pl.pallas_call(
         attend_back_kernel,
         grid_spec=pltpu.PrefetchScalarGridSpec(
             num_scalar_prefetch=1,
             grid=(half_runs, parts // 2),
-            in_specs=[piece, piece, piece, whole, whole, whole, whole],
+            in_specs=[piece, grads, piece, whole, whole, whole, whole],
             out_specs=[piece, whole],
             scratch_shapes=[pltpu.VMEM((kv.shape[0] // KEY_TILE, KEY_TILE, lanes), jnp.float32)],
         ),
@@ -565,6 +570,559 @@
 
 def unpack_pairs(value):
     return jnp.concatenate([value[..., :HEAD_DIM], value[..., HEAD_DIM:]], axis=1)
+
+
+MESH = pl.DeviceIdType.MESH
+
+
+def meet(peers):
+    barrier = pltpu.get_barrier_semaphore()
+    for peer in peers:
+        pl.semaphore_signal(barrier, inc=1, device_id=peer, device_id_type=MESH)
+    pl.semaphore_wait(barrier, len(peers))
+
+
+def send(source, target, send_sem, recv_sem, peer):
+    copy = pltpu.make_async_remote_copy(
+        src_ref=source,
+        dst_ref=target,
+        send_sem=send_sem,
+        recv_sem=recv_sem,
+        device_id=peer,
+        device_id_type=MESH,
+    )
+    copy.start()
+    return copy
+
+
+def grid_peers(heads, parts):
+    h, b = lax.axis_index("head"), lax.axis_index("blk")
+    part, share = b // 2, b % 2
+    across = [(lax.rem(h + i, heads), b) for i in range(1, heads)]
+    along = [(h, lax.rem(part + i, parts) * 2 + share) for i in range(1, parts)]
+    return (h, b, part, share, across, along, (h, part * 2 + 1 - share))
+
+
+def standardize(values):
+    center = values - jnp.mean(values, axis=-1, keepdims=True)
+    spread = jnp.mean(center * center, axis=-1, keepdims=True)
+    scale = lax.rsqrt(spread + norm_eps)
+    return (center * scale, scale)
+
+
+def turn(values, cosine, sine, back=False):
+    lane = lax.broadcasted_iota(jnp.int32, values.shape, 1)
+    first = lax.rem(lane, HEAD_DIM) < HEAD_DIM // 2
+    source = values * sine if back else values
+    ahead = pltpu.roll(source, 128 - HEAD_DIM // 2, 1)
+    behind = pltpu.roll(source, HEAD_DIM // 2, 1)
+    if back:
+        return values * cosine + jnp.where(first, ahead, -behind)
+    return values * cosine + jnp.where(first, -ahead, behind) * sine
+
+
+def join(left, left_side, right, right_side):
+    lane = lax.broadcasted_iota(jnp.int32, left.shape, 1)
+    left = pltpu.roll(left, HEAD_DIM, 1) if left_side else left
+    right = right if right_side else pltpu.roll(right, HEAD_DIM, 1)
+    return jnp.where(lane < HEAD_DIM, left, right)
+
+
+def project_kernel(
+    H, A, tok, cot, wq, gains, w_in, w_down, w_out, docs,
+    kv_all, q_all, tok_all, cot_all, wq_all, wm_all, wo_all, gain_rows, cos_all, sin_all,
+    wq_src, wq_st, wm_src, kv_send, q_send, q_runs, normed,
+    tok_s, tok_r, cot_s, cot_r, wq_s, wq_r, wm_s, wm_r, wx_s, wx_r,
+    q_s, q_r, kv_s, kv_r, kc_s, kc_r, *line,
+):
+    f32, bf16 = jnp.float32, jnp.bfloat16
+    R, W = tok.shape
+    B = 2 * A
+    hw = W // H
+    D = wq.shape[0]
+    F = w_in.shape[1] // 2 // H
+    h, b, part, share, across, along, beside = grid_peers(H, A)
+    meet([*across, *along, beside])
+
+    tok_copies = []
+    for place in range(H):
+        for j in range(3):
+            wq_src[place, :, j * hw : (j + 1) * hw] = wq[:, j * W + place * hw : j * W + (place + 1) * hw]
+        wq_src[place, :, 3 * hw :] = gains[...]
+    wq_copies = [
+        send(wq_src.at[peer[0]], wq_st.at[h], wq_s.at[i], wq_r.at[i], peer)
+        for i, peer in enumerate(across)
+    ]
+    tok_copies = [
+        send(tok, tok_all.at[h], tok_s.at[i], tok_r.at[i], peer) for i, peer in enumerate(across)
+    ]
+    wq_st[h] = wq_src[h]
+    tok_all[h] = tok[...]
+    cot_all[h] = cot[...]
+    unit = (
+        lax.broadcasted_iota(jnp.int32, (D, D), 0) == lax.broadcasted_iota(jnp.int32, (D, D), 1)
+    ).astype(bf16)
+    down = mm(unit, w_down[...], NT).astype(bf16)
+    for place in range(H):
+        wm_src[place, :, :F] = w_in[:, place * F : (place + 1) * F]
+        wm_src[place, :, F : 2 * F] = w_in[:, (H + place) * F : (H + place + 1) * F]
+        wm_src[place, :, 2 * F :] = down[:, place * F : (place + 1) * F]
+    wm_all[h] = wm_src[h]
+    wm_copies = [
+        send(wm_src.at[peer[0]], wm_all.at[h], wm_s.at[i], wm_r.at[i], peer)
+        for i, peer in enumerate(across)
+    ]
+    cot_copies = [
+        send(cot, cot_all.at[h], cot_s.at[i], cot_r.at[i], peer) for i, peer in enumerate(across)
+    ]
+
+    for copy in wq_copies:
+        copy.wait_recv()
+    wq_line = LineGather(
+        lambda block, side: wq_all.at[:, block * 2 + side], wq_st, h, part, share, A, line[:5]
+    )
+    wq_line.start()
+    wq_all[:, b] = wq_st[...]
+    wo_line = LineGather(
+        lambda block, side: wo_all.at[h, block, side], w_out, h, part, share, A, line[5:]
+    )
+    wo_all[h, part, share] = w_out[...]
+    wo_line.start()
+
+    lane = lax.broadcasted_iota(jnp.int32, (R, 128), 1)
+    freqs = jnp.exp(
+        lax.rem(lane, HEAD_DIM // 2).astype(f32) * (-2.0 / HEAD_DIM * float(np.log(rope_base)))
+    )
+    for run in range(H):
+        place = (run * B + b) * R + lax.broadcasted_iota(jnp.int32, (R, 128), 0)
+        begin = jnp.zeros((R, 1), jnp.int32)
+        passed = place[:, : docs.shape[1]] >= docs[0:1, :]
+        begin = jnp.sum(jnp.where(passed, docs[1:2, :], 0), axis=1, keepdims=True)
+        angles = (place - begin).astype(f32) * freqs
+        cos_all[run] = jnp.cos(angles)
+        sin_all[run] = jnp.sin(angles)
+
+    for copy in tok_copies:
+        copy.wait_recv()
+    for k in range(1, A):
+        wq_line.step(k)
+        wo_line.step(k)
+    wq_line.arrive()
+    wo_line.arrive()
+    spread_out = wo_all.at[h, :, share]
+    wx_copies = [
+        send(spread_out, spread_out, wx_s.at[i], wx_r.at[i], peer) for i, peer in enumerate(across)
+    ]
+
+    pick = (
+        lax.broadcasted_iota(jnp.int32, (8, 128), 0) == lax.broadcasted_iota(jnp.int32, (8, 128), 1)
+    ).astype(bf16)
+    for chunk in range(H):
+        block = wq_all[chunk].reshape(B * D, 3 * hw + 128)
+        gain_rows[:, chunk * hw : (chunk + 1) * hw] = mm(pick, block[:, 3 * hw :], NT)
+
+    kv_copies = []
+    for run in range(H):
+        hat, unused = standardize(tok_all[run].astype(f32))
+        low = (hat * gain_rows[0:1, :]).astype(bf16)
+        projected = jnp.zeros((R, 3 * hw), f32)
+        for chunk in range(H):
+            block = wq_all[chunk].reshape(B * D, 3 * hw + 128)
+            projected += mm(low[:, chunk * hw : (chunk + 1) * hw], block[:, : 3 * hw])
+        cosine, sine = cos_all[run], sin_all[run]
+        for slab in range(hw // 128):
+            at = slab * 128
+            q_runs[run, :, at : at + 128] = turn(projected[:, at : at + 128], cosine, sine)
+            key = turn(projected[:, hw + at : hw + at + 128], cosine, sine)
+            value = projected[:, 2 * hw + at : 2 * hw + at + 128]
+            kv_send[2 * slab, run] = join(key, 0, value, 0).astype(bf16)
+            kv_send[2 * slab + 1, run] = join(key, 1, value, 1).astype(bf16)
+    for i, peer in enumerate(along):
+        there = peer[1] // 2
+        kv_copies.append(
+            send(kv_send.at[there], kv_all.at[:, b], kv_s.at[i], kv_r.at[i], peer)
+        )
+    kv_all[:, b] = kv_send[part]
+    kc_copies = [send(kv_send.at[part], kv_all.at[:, b], kc_s.at[0], kc_r.at[0], beside)]
+    for run in range(H // 2):
+        for a in range(A):
+            at = a // 2 * 128
+            q_send[a, run] = join(
+                q_runs[run, :, at : at + 128], a % 2, q_runs[run + H // 2, :, at : at + 128], a % 2
+            ).astype(bf16)
+    q_copies = [
+        send(q_send.at[peer[1] // 2], q_all.at[part], q_s.at[i], q_r.at[i], peer)
+        for i, peer in enumerate(along)
+    ]
+    q_all[part] = q_send[part]
+    for i, copy in enumerate(kv_copies):
+        copy.wait_recv()
+        there = kv_all.at[:, lax.rem(part + A - 1 - i, A) * 2 + share]
+        kc_copies.append(send(there, there, kc_s.at[i + 1], kc_r.at[i + 1], beside))
+    for i, copy in enumerate(wx_copies):
+        copy.wait_recv()
+        there = wo_all.at[lax.rem(h + H - 1 - i, H), :, share]
+        n = H - 1 + i
+        kc_copies.append(send(there, there, wx_s.at[n], wx_r.at[n], beside))
+    for copy in [*kc_copies, *q_copies, *wm_copies, *cot_copies]:
+        copy.wait_recv()
+    for copy in [
+        *kc_copies, *q_copies, *wm_copies, *cot_copies, *wq_copies, *tok_copies, *wx_copies, *kv_copies
+    ]:
+        copy.wait_send()
+    wq_line.finish()
+    wo_line.finish()
+
+
+def project(tokens, cotangent, w_qkv, gains, w_in, w_down, w_out, docs):
+    R, W = tokens.shape
+    H, B = lax.axis_size("head"), lax.axis_size("blk")
+    A = B // 2
+    hw = W // H
+    D = w_qkv.shape[0]
+    F = w_down.shape[0] // H
+    f32, bf16 = jnp.float32, jnp.bfloat16
+    shape = jax.ShapeDtypeStruct
+    dma = lambda count: pltpu.SemaphoreType.DMA((count,))
+    vmem = pl.BlockSpec(memory_space=pltpu.VMEM)
+    return pl.pallas_call(
+        partial(project_kernel, H, A),
+        in_specs=[vmem] * 8,
+        out_specs=[vmem] * 10,
+        out_shape=[
+            shape((H, B, R, 128), bf16),
+            shape((A, H // 2, R, 128), bf16),
+            shape((H, R, W), bf16),
+            shape((H, R, W), bf16),
+            shape((H, B, D, 3 * hw + 128), bf16),
+            shape((H, D, 3 * F), bf16),
+            shape((H, A, 2, D, W), bf16),
+            shape((8, W), f32),
+            shape((H, R, 128), f32),
+            shape((H, R, 128), f32),
+        ],
+        scratch_shapes=[
+            pltpu.VMEM((H, D, 3 * hw + 128), bf16),
+            pltpu.VMEM((H, D, 3 * hw + 128), bf16),
+            pltpu.VMEM((H, D, 3 * F), bf16),
+            pltpu.VMEM((A, H, R, 128), bf16),
+            pltpu.VMEM((A, H // 2, R, 128), bf16),
+            pltpu.VMEM((H, R, hw), f32),
+            pltpu.VMEM((H, R, W), bf16),
+            *[dma(H - 1)] * 8,
+            *[dma(2 * H - 2)] * 2,
+            *[dma(A - 1)] * 4,
+            *[dma(A)] * 2,
+            *line_sems(A),
+            *line_sems(A),
+        ],
+        compiler_params=pltpu.CompilerParams(
+            collective_id=0, has_side_effects=True, vmem_limit_bytes=48 * 2**20
+        ),
+        cost_estimate=pl.CostEstimate(flops=10**9, bytes_accessed=10**7, transcendentals=10**6),
+        name="project",
+    )(tokens, cotangent, w_qkv, gains, w_in, w_down, w_out, docs)
+
+
+class LineGather:
+    def __init__(self, view, own, h, part, share, parts, sems):
+        self.view, self.own, self.h, self.part, self.share, self.parts = view, own, h, part, share, parts
+        self.right_s, self.left_s, self.line_r, self.core_s, self.core_r = sems
+
+    def _copy(self, source, block, side):
+        if side == 0:
+            sems, peer = (self.core_s, self.core_r), (self.h, self.part * 2 + 1 - self.share)
+            target = self.view(block, self.share)
+        else:
+            sems = (self.right_s if side > 0 else self.left_s, self.line_r)
+            peer = (self.h, (self.part + side) * 2 + self.share)
+            target = self.view(block, self.share)
+        return pltpu.make_async_remote_copy(
+            src_ref=source,
+            dst_ref=target,
+            send_sem=sems[0].at[block],
+            recv_sem=sems[1].at[block],
+            device_id=peer,
+            device_id_type=MESH,
+        )
+
+    def _can(self, side):
+        return self.part < self.parts - 1 if side > 0 else self.part > 0
+
+    def start(self):
+        for side in (1, -1):
+
+            @pl.when(self._can(side))
+            def _():
+                self._copy(self.own, self.part, side).start()
+
+        self._copy(self.own, self.part, 0).start()
+
+    def step(self, k):
+        for side in (1, -1):
+            block = self.part - side * k
+
+            @pl.when((block >= 0) & (block < self.parts))
+            def _():
+                there = self.view(block, self.share)
+                self._copy(there, block, side).wait_recv()
+
+                @pl.when(self._can(side))
+                def _():
+                    self._copy(there, block, side).start()
+
+                self._copy(there, block, 0).start()
+
+    def arrive(self):
+        for block in range(self.parts):
+            self._copy(self.own, block, 0).wait_recv()
+
+    def finish(self):
+        for side in (1, -1):
+            for block in range(self.parts):
+                sent = block <= self.part if side > 0 else block >= self.part
+
+                @pl.when(sent & self._can(side))
+                def _():
+                    self._copy(self.own, block, side).wait_send()
+
+        for block in range(self.parts):
+            self._copy(self.own, block, 0).wait_send()
+
+
+def line_sems(parts):
+    return [pltpu.SemaphoreType.DMA((parts,))] * 5
+
+
+def norm_back(grad, hat, scale, gain):
+    inner = grad * gain
+    return scale * (
+        inner
+        - jnp.mean(inner, axis=-1, keepdims=True)
+        - hat * jnp.mean(inner * hat, axis=-1, keepdims=True)
+    )
+
+
+def feed_kernel(
+    H, A, op, tok_all, cot_all, wo, wm_own, gain_rows,
+    output, grad_middle, go, term, mixed_own, gain_part,
+    mx_in, mixed_all, wm_all, middle, normed, act, lift, g2_send, g2_in, g2_own, o_send, o_in, o_own, gm_send,
+    mx_s, mx_r, ma_s, ma_r, g2_s, g2_r, o_s, o_r, gm_s, gm_r, *line,
+):
+    f32, bf16 = jnp.float32, jnp.bfloat16
+    R, W = tok_all.shape[1:]
+    B = 2 * A
+    hw = W // H
+    D = wm_own.shape[1]
+    F = wm_own.shape[2] // 3
+    h, b, part, share, across, along, beside = grid_peers(H, A)
+    others = [
+        (lax.rem(h + i, H), lax.rem(part + j, A) * 2 + share)
+        for i in range(H)
+        for j in range(A)
+        if i or j
+    ]
+    meet([*others, beside])
+
+    mx_copies = [
+        send(op.at[peer[1] // 2], mx_in.at[part], mx_s.at[i], mx_r.at[i], peer)
+        for i, peer in enumerate(along)
+    ]
+    gather = LineGather(
+        lambda block, side: wm_all.at[:, block * 2 + side], wm_own, h, part, share, A, line
+    )
+    gather.start()
+    wm_all[:, b] = wm_own[...]
+    mx_in[part] = op[part]
+    for copy in mx_copies:
+        copy.wait_recv()
+    for run in range(H):
+        side, at = run // (H // 2), run % (H // 2)
+        for slab in range(hw // 128):
+            left, right = mx_in[2 * slab, at].astype(f32), mx_in[2 * slab + 1, at].astype(f32)
+            mixed_own[run, :, slab * 128 : (slab + 1) * 128] = join(left, side, right, side).astype(bf16)
+    mixed_all[h] = mixed_own[...]
+    ma_copies = [
+        send(mixed_own, mixed_all.at[h], ma_s.at[i], ma_r.at[i], peer) for i, peer in enumerate(across)
+    ]
+
+    def project_out(source, first):
+        def one(run, carried):
+            before = tok_all[run].astype(f32) if first else middle[run]
+            middle[run] = before + mm(mixed_all[source, run], wo[source])
+            return carried
+
+        lax.fori_loop(0, H, one, 0)
+
+    project_out(h, True)
+    gather.step(1)
+    for i, copy in enumerate(ma_copies):
+        copy.wait_recv()
+        project_out(lax.rem(h + H - 1 - i, H), False)
+
+    def norm_run(run, carried):
+        hat, unused = standardize(middle[run])
+        normed[run] = (hat * gain_rows[1:2, :]).astype(bf16)
+        return carried
+
+    lax.fori_loop(0, H, norm_run, 0)
+    for k in range(2, A):
+        gather.step(k)
+    gather.arrive()
+
+    def block(chunk):
+        return wm_all[chunk].reshape(B * D, 3 * F)
+
+    def feed_run(i, carried):
+        run = lax.rem(h + 1 + i, H)
+        lifted = jnp.zeros((R, 2 * F), f32)
+        grad_act = jnp.zeros((R, F), f32)
+        for chunk in range(H):
+            lanes = slice(chunk * hw, (chunk + 1) * hw)
+            weights = block(chunk)
+            lifted += mm(normed[run, :, lanes], weights[:, : 2 * F])
+            grad_act += mm(cot_all[run, :, lanes], weights[:, 2 * F :])
+        gate, up = lifted[:, :F], lifted[:, F:]
+        below = 0.5 + 0.5 * lax.erf(gate * (0.5**0.5))
+        slope = below + gate * jnp.exp(-0.5 * gate * gate) * ((2.0 * np.pi) ** -0.5)
+        act[run] = (gate * below * up).astype(bf16)
+        lift[run, :, :F] = (grad_act * up * slope).astype(bf16)
+        lift[run, :, F:] = (grad_act * gate * below).astype(bf16)
+
+        for chunk in range(H):
+            lanes = slice(chunk * hw, (chunk + 1) * hw)
+            g2_own[:, lanes] = mm(lift[run], block(chunk)[:, : 2 * F], NT)
+
+        @pl.when(i < H - 1)
+        def _():
+            g2_send[i] = g2_own[...].astype(bf16)
+            pltpu.make_async_remote_copy(
+                g2_send.at[i], g2_in.at[i], g2_s.at[i], g2_r.at[i], device_id=(run, b), device_id_type=MESH
+            ).start()
+
+        return carried
+
+    lax.fori_loop(0, H, feed_run, 0)
+
+    def out_run(i, carried):
+        run = lax.rem(h + 1 + i, H)
+        for chunk in range(H):
+            lanes = slice(chunk * hw, (chunk + 1) * hw)
+            o_own[:, lanes] = mm(act[run], block(chunk)[:, 2 * F :], NT)
+
+        @pl.when(i < H - 1)
+        def _():
+            o_send[i] = o_own[...].astype(bf16)
+            pltpu.make_async_remote_copy(
+                o_send.at[i], o_in.at[i], o_s.at[i], o_r.at[i], device_id=(run, b), device_id_type=MESH
+            ).start()
+
+        return carried
+
+    lax.fori_loop(0, H, out_run, 0)
+
+    def rest(sent, landed, send_sem, recv_sem, i):
+        return pltpu.make_async_remote_copy(
+            sent.at[i], landed.at[i], send_sem.at[i], recv_sem.at[i], device_id=across[i], device_id_type=MESH
+        )
+
+    grad = g2_own[...]
+    for i in range(H - 1):
+        rest(g2_send, g2_in, g2_s, g2_r, i).wait_recv()
+        grad += g2_in[i].astype(f32)
+    hat, scale = standardize(middle[h])
+    gain_part[...] = jnp.broadcast_to(jnp.sum(grad * hat, axis=0, keepdims=True), gain_part.shape)
+    total = cot_all[h].astype(f32) + norm_back(grad, hat, scale, gain_rows[1:2, :])
+    grad_middle[...] = total
+    branch = total.astype(bf16)
+    gm_copies = []
+    for i in range(H):
+        place = lax.rem(h + i, H)
+        mixed_grad = mm(branch, wo[place], NT)
+        for a in range(A):
+            slab = mixed_grad[:, a // 2 * 128 : a // 2 * 128 + 128]
+            gm_send[i, a] = join(slab[: R // 2], a % 2, slab[R // 2 :], a % 2).astype(bf16)
+        for j in range(A):
+            there = lax.rem(part + j, A)
+            if i or j:
+                n = i * A + j
+                gm_copies.append(
+                    send(gm_send.at[i, there], go.at[part, h], gm_s.at[n], gm_r.at[n], (place, there * 2 + share))
+                )
+            else:
+                go[part, h] = gm_send[0, part]
+
+    def term_chunk(chunk, carried):
+        lanes = pl.ds(pl.multiple_of(chunk * hw, hw), hw)
+        left = normed[:, :, lanes].reshape(H * R, hw)
+        grads = mm(left, lift[...].reshape(H * R, 2 * F), TN).astype(bf16)
+        term[:, chunk, :, : 2 * F] = grads.reshape(B, D, 2 * F)
+        left = cot_all[:, :, lanes].reshape(H * R, hw)
+        grads = mm(left, act[...].reshape(H * R, F), TN).astype(bf16)
+        term[:, chunk, :, 2 * F :] = grads.reshape(B, D, F)
+        return carried
+
+    lax.fori_loop(0, H, term_chunk, 0)
+    result = middle[h] + o_own[...]
+    for i in range(H - 1):
+        rest(o_send, o_in, o_s, o_r, i).wait_recv()
+        result += o_in[i].astype(f32)
+    output[...] = result.astype(bf16)
+    for copy in gm_copies:
+        copy.wait_recv()
+    for copy in [*mx_copies, *ma_copies, *gm_copies]:
+        copy.wait_send()
+    for i in range(H - 1):
+        rest(g2_send, g2_in, g2_s, g2_r, i).wait_send()
+        rest(o_send, o_in, o_s, o_r, i).wait_send()
+    gather.finish()
+
+
+def feed(op, tok_all, cot_all, wo, wm_own, gain_rows):
+    A, half, R, lanes = op.shape
+    H = 2 * half
+    W = tok_all.shape[-1]
+    B = 2 * A
+    hw = W // H
+    D = wm_own.shape[1]
+    F = wm_own.shape[2] // 3
+    f32, bf16 = jnp.float32, jnp.bfloat16
+    shape = jax.ShapeDtypeStruct
+    dma = lambda count: pltpu.SemaphoreType.DMA((count,))
+    vmem = pl.BlockSpec(memory_space=pltpu.VMEM)
+    return pl.pallas_call(
+        partial(feed_kernel, H, A),
+        in_specs=[vmem] * 6,
+        out_specs=[vmem] * 6,
+        out_shape=[
+            shape((R, W), bf16),
+            shape((R, W), f32),
+            shape((A, H, R // 2, 128), bf16),
+            shape((B, H, D, 3 * F), bf16),
+            shape((H, R, hw), bf16),
+            shape((8, W), f32),
+        ],
+        scratch_shapes=[
+            pltpu.VMEM((A, half, R, 128), bf16),
+            pltpu.VMEM((H, H, R, hw), bf16),
+            pltpu.VMEM((H, B, D, 3 * F), bf16),
+            pltpu.VMEM((H, R, W), f32),
+            pltpu.VMEM((H, R, W), bf16),
+            pltpu.VMEM((H, R, F), bf16),
+            pltpu.VMEM((H, R, 2 * F), bf16),
+            *[pltpu.VMEM((H - 1, R, W), bf16), pltpu.VMEM((H - 1, R, W), bf16), pltpu.VMEM((R, W), f32)] * 2,
+            pltpu.VMEM((H, A, R // 2, 128), bf16),
+            *[dma(A - 1)] * 2,
+            *[dma(H - 1)] * 6,
+            *[dma(H * A)] * 2,
+            *line_sems(A),
+        ],
+        compiler_params=pltpu.CompilerParams(
+            collective_id=1, has_side_effects=True, vmem_limit_bytes=56 * 2**20
+        ),
+        cost_estimate=pl.CostEstimate(flops=6 * 10**9, bytes_accessed=10**7, transcendentals=10**6),
+        name="feed",
+    )(op, tok_all, cot_all, wo, wm_own, gain_rows)
 
 
 def per_device_split(
@@ -602,87 +1160,35 @@
     span = jnp.stack([lo, hi], axis=1).astype(jnp.int32)
     kdoc = docs.reshape(T // KEY_TILE, KEY_TILE)
     own = lambda v: lax.dynamic_index_in_dim(v.reshape(H, B, R), b, 1, keepdims=False).reshape(N)
-    cosine, sine = rope_tables(own(places - starts), HEAD_DIM)
-
-    tok_all = lax.all_gather(tokens, "head", axis=0, tiled=True)
-    gains = jnp.stack([attn_gain, mlp_gain], axis=1)
-    wq = w_qkv.reshape(D, 3, H, hw).transpose(2, 0, 1, 3).reshape(H, D, 3 * hw)
-    wq = jnp.concatenate(
-        [wq, jnp.broadcast_to(jnp.pad(gains, ((0, 0), (0, 126)))[None], (H, D, 128))], axis=2
-    )
-    wq = lax.all_to_all(wq, "head", 0, 0, tiled=True)
-    wq = lax.all_gather(wq, "blk", axis=0, tiled=False).transpose(1, 0, 2, 3).reshape(W, 3 * hw + 128)
-    gain_one, gain_two = wq[:, 3 * hw].astype(f32), wq[:, 3 * hw + 1].astype(f32)
-    full_out = lax.all_gather(w_attn_out, ("head", "blk"), axis=0, tiled=True)
-    wm = jnp.concatenate(
-        [
-            w_in.reshape(D, 2, H, F).transpose(2, 0, 1, 3).reshape(H, D, 2 * F),
-            w_mlp_out.reshape(H, F, D).transpose(0, 2, 1),
-        ],
-        axis=2,
-    )
-    wm = lax.all_to_all(wm, "head", 0, 0, tiled=True)
-    wm = lax.all_gather(wm, "blk", axis=0, tiled=False).transpose(1, 0, 2, 3).reshape(W, 3 * F)
-    cot_all = lax.all_gather(cotangent, "head", axis=0, tiled=True)
-
-    inputs = tok_all.astype(f32)
-    normed_one = layer_norm(inputs, gain_one).astype(bf16)
-    projected = mm(normed_one, wq[:, : 3 * hw])
-    query = rotate(projected[:, :hw], cosine, sine).astype(bf16)
-    keys = rotate(projected[:, hw : 2 * hw], cosine, sine).astype(bf16)
-    values = projected[:, 2 * hw :].astype(bf16)
-    split = lambda v: v.reshape(H, R, A, HEAD_DIM).transpose(2, 0, 1, 3)
-    qp = lax.all_to_all(
-        pack_pairs(split(query)), "blk", 0, 0, tiled=True, axis_index_groups=part_groups
-    )
-    kv = lax.all_to_all(
-        jnp.concatenate([split(keys), split(values)], axis=-1),
-        "blk", 0, 0, tiled=True, axis_index_groups=part_groups,
-    )
-    kv = lax.all_gather(kv, "blk", axis=0, tiled=False, axis_index_groups=share_groups)
-    kv = kv.transpose(2, 1, 0, 3, 4).reshape(T, 2 * HEAD_DIM)
+    gains = jnp.pad(jnp.stack([attn_gain, mlp_gain], axis=1), ((0, 0), (0, 126)))
+    kv, qp, tok_all, cot_all, wq, wm, wo, gain_rows, cos_all, sin_all = project(
+        tokens, cotangent, w_qkv, gains, w_in, w_mlp_out, w_attn_out, jnp.stack([ends, doc_lengths])
+    )
+    cosine, sine = cos_all.reshape(N, 128)[:, :HEAD_DIM], sin_all.reshape(N, 128)[:, :HEAD_DIM]
+    kv = kv.reshape(T, 2 * HEAD_DIM)
     op, lse = attend(span, qp, kv, qdoc, kdoc)
-    back = lax.all_to_all(op, "blk", 0, 0, tiled=True, axis_index_groups=part_groups)
-    mixed = unpack_pairs(back).transpose(1, 2, 0, 3).reshape(N, hw)
-    mixed_all = lax.all_gather(mixed, "head", axis=1, tiled=True)
-
-    middle = inputs + mm(mixed_all, full_out)
-    normed_two, _ = jax.vjp(layer_norm, middle, gain_two)
-    normed_two = normed_two.astype(bf16)
-    lifted = mm(normed_two, wm[:, : 2 * F])
-    activated, geglu_pull = jax.vjp(gelu_gate, lifted)
-    activated = activated.astype(bf16)
-    out_part = mm(activated, wm[:, 2 * F :], NT).astype(bf16)
-    output = lax.psum_scatter(out_part, "head", scatter_dimension=0, tiled=True).astype(f32)
-    grad_act = mm(cot_all, wm[:, 2 * F :])
-    grad_lifted = geglu_pull(grad_act)[0].astype(bf16)
-    grad_two = mm(grad_lifted, wm[:, : 2 * F], NT).astype(bf16)
-    grad_two = lax.psum_scatter(grad_two, "head", scatter_dimension=0, tiled=True).astype(f32)
-    term_mlp = jnp.concatenate(
-        [mm(normed_two, grad_lifted, TN), mm(cot_all, activated, TN)], axis=1
-    ).astype(bf16)
-    term_mlp = term_mlp.reshape(H, B, D, 3 * F).transpose(1, 0, 2, 3)
-    sum_mlp = lax.psum_scatter(term_mlp, "blk", scatter_dimension=0, tiled=False)
-    middle_own = lax.dynamic_slice_in_dim(middle, h * R, R, 0)
-    output = (middle_own + output).astype(bf16)
-    _, norm_two_pull = jax.vjp(layer_norm, middle_own, gain_two)
-    grad_middle, grad_gain_two = norm_two_pull(grad_two)
-    grad_middle = grad_middle + cotangent.astype(f32)
-    grad_branch = grad_middle.astype(bf16)
-    grad_mixed = mm(grad_branch, full_out, NT).astype(bf16)
-    branch_all = lax.all_gather(grad_branch, "head", axis=0, tiled=True)
-    gp = lax.all_to_all(grad_mixed, "head", 1, 0, tiled=True)
-    gp = lax.all_to_all(
-        pack_pairs(split(gp)), "blk", 0, 0, tiled=True, axis_index_groups=part_groups
-    )
+    output, grad_middle, gp, term_mlp, mixed, gain_part = feed(
+        op, tok_all, cot_all, wo.reshape(H, hw, W), wm, gain_rows
+    )
+    sum_mlp = lax.psum_scatter(
+        term_mlp.reshape(B * H * D, 3 * F), "blk", scatter_dimension=0, tiled=True
+    ).reshape(H, D, 3 * F)
     dqp, dkv = attend_back(span, qp, gp, op, lse, kv, qdoc, kdoc)
+    wq = wq.reshape(W, 3 * hw + 128)
+    gain_one = gain_rows[0]
+    normed_one = layer_norm(tok_all.reshape(N, W).astype(f32), gain_one).astype(bf16)
+    branch_all = lax.all_gather(grad_middle.astype(bf16), "head", axis=0, tiled=True)
+    grad_gain_two = gain_part[0]
+    mixed = mixed.reshape(N, hw)
     dqp = lax.all_to_all(dqp, "blk", 0, 0, tiled=True, axis_index_groups=part_groups)
     dkv = dkv.reshape(H, A, G, R, 2 * HEAD_DIM).transpose(2, 1, 0, 3, 4)
     dkv = lax.psum_scatter(dkv, "blk", scatter_dimension=0, tiled=False, axis_index_groups=share_groups)
     dkv = lax.all_to_all(dkv, "blk", 0, 0, tiled=True, axis_index_groups=part_groups)
     merge = lambda v: v.transpose(1, 2, 0, 3).reshape(N, hw)
     _, rope_pull = jax.vjp(
-        partial(rotate_pair, cosine=cosine, sine=sine), projected[:, :hw], projected[:, hw : 2 * hw]
+        partial(rotate_pair, cosine=cosine, sine=sine),
+        jnp.zeros((N, hw), f32),
+        jnp.zeros((N, hw), f32),
     )
     grad_query, grad_keys = rope_pull(
         (merge(unpack_pairs(dqp)).astype(f32), merge(dkv[..., :HEAD_DIM]).astype(f32))

time: 666 us -> 450 us (0.68); the launches traced: 656 us -> 452 us
  waiting for transfers between devices: 376 us -> 195 us
  Pallas kernels: 34.3 us -> 178 us
  blocking collectives: 95.3 us -> 10.3 us
  local copies, waits for them, and re-layouts: 54.5 us -> 22.1 us
  matrix products: 38.8 us -> 7.89 us
  other arithmetic: 30.6 us -> 12.5 us
    pallas_call x0 -> x2, Pallas kernels: none -> 145 us  [the longest x1 86.6 us: feed(): pl.pallas_call(partial(feed_kernel, H, A), in_specs=[vmem] * 6, out_specs...]
    all_gather x8 -> x1, waiting for transfers between devices: 141 us -> 19.9 us  [per_device_split(): lax.all_gather(grad_middle.astype(bf16), 'head', axis=0, tiled=True)]
    all_to_all x7 -> x0, blocking collectives: 85.8 us -> none  [the longest x1 17.9 us: per_device_split(): lax.all_to_all(jnp.concatenate([split(keys), split(values)], axis=-1), 'b...]
    reduce_scatter x3 -> x1, waiting for transfers between devices: 84.6 us -> 40.3 us  [per_device_split(): lax.psum_scatter(term_mlp.reshape(B * H * D, 3 * F), 'blk', scatter_dimen...]
    unnamed x16 -> x7, waiting for transfers between devices: 96.1 us -> 62.9 us
    dot_general x12 -> x3, matrix products: 38.8 us -> 7.89 us  [mm(): lax.dot_general(left, right, dims, preferred_element_type=jnp.float32)]
    reduce_scatter x1, waiting for transfers between devices: 15.8 us -> 25.9 us  [per_device_split(): lax.psum_scatter(term_out, 'blk', scatter_dimension=0, tiled=False)]
    reshape x13 -> x2, local copies, waits for them, and re-layouts: 9.55 us -> 0.74 us  [per_device_split(): merge = lambda v: v.transpose(1, 2, 0, 3).reshape(N, hw)]
  transfers between devices with their start and end apart: 18 -> 9, of which waited for: 16 -> 7; matrix products, arithmetic and copies ran while one was open for 12% -> 4% of each run, Pallas kernels for 2% -> 0%
where the time goes in v2:
time: 450 us; the launch traced here: 452 us
  waiting for transfers between devices  195 us (43%)
  Pallas kernels  178 us (40%)
  local copies, waits for them, and re-layouts  22.1 us (5%)
  between operations  14.7 us (3%)
  other arithmetic  12.5 us (3%)
  starting transfers between devices  12.2 us (3%)
  blocking collectives  10.3 us (2%)
  matrix products  7.89 us (2%)
    pallas_call x1, Pallas kernels, feed(): pl.pallas_call(partial(feed_kernel, H, A), in_specs=[vmem] * 6, out_specs...  86.6 us
    unnamed x7, waiting for transfers between devices  62.9 us
    pallas_call x1, Pallas kernels, project(): pl.pallas_call(partial(project_kernel, H, A), in_specs=[vmem] * 8, out_sp...  58.6 us
    reduce_scatter x1, waiting for transfers between devices, per_device_split(): lax.psum_scatter(term_mlp.reshape(B * H * D, 3 * F), 'blk', scatter_dimen...  40.3 us
    reduce_scatter x1, waiting for transfers between devices, per_device_split(): lax.psum_scatter(term_out, 'blk', scatter_dimension=0, tiled=False)  25.9 us
    reduce_scatter x1, waiting for transfers between devices, per_device_split(): lax.psum_scatter(grad_one, 'head', scatter_dimension=0, tiled=True)  25.4 us
    all_gather x1, waiting for transfers between devices, per_device_split(): lax.all_gather(grad_middle.astype(bf16), 'head', axis=0, tiled=True)  19.9 us
    pallas_call x1, Pallas kernels, attend_back(): pl.pallas_call(attend_back_kernel, grid_spec=pltpu.PrefetchScalarGridSpec...  18.3 us
  transfers between devices with their start and end apart: 9, of which 7 were waited for; matrix products, arithmetic and copies ran while one was open for 4% of the time, Pallas kernels for 0%

profile of v2, /device:TPU:0, one launch (start us, length us, event | category | flops | bytes accessed | tf_op | source)
XLA Modules:
  0.0 452.3 jit_solution(9118213523060082314)
XLA Ops:
  7.3 1.0 broadcast_in_dim.44
  8.3 0.7 pad_add_fusion.1.docs
  8.9 1.0 convert_reduce_fusion.2
  10.0 0.9 reshape.219.qdoc
  10.9 0.7 dynamic-slice_reduce_fusion.1
  11.8 1.3 copy.108.w_down
  13.4 58.6 %project.1 = (bf16[4,8,128,128]{3,2,1,0:T(8,128)(2,1)S(1)}, bf16[4,2,128,128]{3,2,1,0:T(8,128)(2,1)S(1)}, bf16[4,128,1024]{2,1,0:T(8,128)(2,1)S(1)}, bf16[4,128,...) custom-call(bf16[128,1024]{1,0:T(8,128)(2,1)S(1)} %copy-done.2, ...), custom_call_target="tpu_custom_call" | custom-call | flops 1000000000 | bytes 10000000 | tf_op jit(solution)/shard_map/project/pallas_call | solution.py:788
  72.0 1.0 copy-done
  73.0 0.6 copy-done.3
  73.6 14.5 %attend.1 = (bf16[4,2,128,128]{3,2,1,0:T(8,128)(2,1)S(1)}, f32[8,256,1]{2,1,0:T(8,128)S(1)}) custom-call(s32[8,2]{1,0:T(8,128)S(1)} %pad_add_fusion.span, bf16[4,2,128,128]{3,2,1,0:T(8,128)(2,1)S(1)} %get-tuple-element.28.qp, bf16[4096,128]{1,0:T(8,128)(2,1)S(1)} %bitcast.83, s32[8,256,1]{2,1,0:T(8,128)S(1)} %reshape.219.qdoc, s32[16,256]{1,0:T(8,128)S(1)} %reshape.194.kdoc), custom_call_target="tpu_custom_call" | custom-call | flops 1000000000 | bytes 4000000 | tf_op jit(solution)/shard_map/attend/pallas_call | solution.py:475
  88.2 0.7 copy-done.8
  88.9 86.6 %feed.1 = (bf16[128,1024]{1,0:T(8,128)(2,1)}, f32[128,1024]{1,0:T(8,128)}, bf16[4,4,64,128]{3,2,1,0:T(8,128)(2,1)}, bf16[8,4,32,1968]{3,2,1,0:T(8,128)(2,1)}, bf...) custom-call(bf16[4,2,128,128]{3,2,1,0:T(8,128)(2,1)} %copy-done.8, bf16[4,128,1024]{2,1,0:T(8,128)(2,1)} %copy-done, ...), custom_call_target="tpu_custom_call" | custom-call | flops 6000000000 | bytes 10000000 | tf_op jit(solution)/shard_map/feed/pallas_call | solution.py:1093
  175.5 0.9 copy-done.11
  176.4 18.3 %attend_back.1 = (bf16[4,2,128,128]{3,2,1,0:T(8,128)(2,1)S(1)}, bf16[4096,128]{1,0:T(8,128)(2,1)S(1)}) custom-call(s32[8,2]{1,0:T(8,128)S(1)} %pad_add_fusion.span, bf16[4,2,128,128]{3,2,1,0:T(8,128)(2,1)S(1)} %get-tuple-element.28.qp, bf16[4,4,64,128]{3,2,1,0:T(8,128)(2,1)S(1)} %copy-done.11, bf16[4,2,128,128]{3,2,1,0:T(8,128)(2,1)S(1)} %copy-done.9, ...), custom_call_target="tpu_custom_call" | custom-call | flops 3000000000 | bytes 6000000 | tf_op jit(solution)/shard_map/attend_back/pallas_call | solution.py:547
  194.7 1.1 copy.134
  195.8 10.3 %all_to_all.20 = bf16[4,2,128,128]{3,2,1,0:T(8,128)(2,1)S(1)} all-to-all(bf16[4,2,128,128]{3,2,1,0:T(8,128)(2,1)S(1)} %get-tuple-element.40), channel_id=1, replica_groups={{0,2,4,6},{1,3,5,7},{8,10,12,14},{9,11,13,15},{16,18,20,22},{17,19,21,2..., dimensions={0} | all-to-all | bytes 524288 | tf_op jit(solution)/shard_map/all_to_all | solution.py:1183
  206.1 4.5 all-to-all-start.1
  210.9 0.1 maximum_convert_fusion
  211.1 0.3 copy.112
  211.4 14.8 %all-to-all-done.1 = bf16[4,4,128,128]{3,2,1,0:T(8,128)(2,1)S(1)} async-done(((bf16[4,4,128,128]{3,2,1,0:T(8,128)(2,1)}), bf16[4,4,128,128]{3,2,1,0:T(8,128)(2,1)S(1)}, u32[]{:S(2)}, u32[]{:S(2)}) %all-to-all-start.1) | async-done | bytes 524320 | tf_op jit(solution)/shard_map/all_to_all | solution.py:1186
  226.2 0.3 slice_convert_fusion
  226.5 0.3 copy.127
  227.0 0.3 add_convert_fusion.1
  227.6 0.4 copy.128
  228.0 0.3 reshape.215
  228.4 3.4 fusion.5
  231.9 0.9 slice.69
  232.9 0.2 copy-done.1
  233.0 0.2 convert_reduce_fusion
  233.3 25.4 %reduce-scatter.10.cloned.1.call-done = bf16[128,1024]{1,0:T(8,128)(2,1)} async-done(((bf16[512,1024]{1,0:T(8,128)(2,1)}), bf16[128,1024]{1,0:T(8,128)(2,1)}) %reduce-scatter.10.cloned.1.call-update) | async-done | bytes 262160 | tf_op jit(solution)/shard_map/reduce_scatter | solution.py:1200
  258.7 1.2 fusion.15
  259.9 1.3 fusion.14
  261.2 2.1 fusion.27
  263.3 0.3 all-reduce.9.cloned.1.call-start
  263.6 0.4 multiply_reduce_fusion
  264.0 0.4 fusion.2
  264.4 0.5 copy.121
  265.0 0.8 fusion.20
  265.8 2.0 convolution_convert_fusion
  267.8 0.2 copy.132
  268.1 1.4 maximum_bitcast_fusion
  269.6 0.5 reduce-scatter.14.cloned.1.call-update
  270.2 19.9 %all-gather.2.cloned.1.call-done = bf16[512,1024]{1,0:T(8,128)(2,1)} async-done(((bf16[128,1024]{1,0:T(8,128)(2,1)}), bf16[512,1024]{1,0:T(8,128)(2,1)}) %all-gather.2.cloned.1.call-update) | async-done | bytes 1048592 | tf_op jit(solution)/shard_map/all_gather | solution.py:1180
  290.1 2.5 convolution_convert_fusion.1
  292.6 0.6 dynamic-slice.2
  293.2 62.3 %all-reduce.9.cloned.1.call-done = bf16[8,4,32,896]{3,2,0,1:T(8,128)(2,1)} async-done(((bf16[8,4,32,896]{3,2,0,1:T(8,128)(2,1)}), bf16[8,4,32,896]{3,2,0,1:T(8,128)(2,1)}) %all-reduce.9.cloned.1.call-update) | async-done | bytes 1835024
  355.6 2.3 dynamic-slice_bitcast_fusion
  357.9 3.6 all-to-all-start.2
  361.5 5.3 %all-to-all-done.2 = bf16[4,32,896]{2,1,0:T(8,128)(2,1)S(1)} async-done(((bf16[4,32,896]{2,1,0:T(8,128)(2,1)}), bf16[4,32,896]{2,1,0:T(8,128)(2,1)S(1)}, u32[]{:S(2)}, u32[]{:S(2)}) %all-to-all-start.2) | async-done | bytes 229408 | tf_op jit(solution)/shard_map/all_to_all | solution.py:1212
  366.8 40.3 %reduce-scatter.14.cloned.1.call-done = bf16[128,1968]{1,0:T(8,128)(2,1)} async-done(((bf16[1024,1968]{1,0:T(8,128)(2,1)}), bf16[128,1968]{1,0:T(8,128)(2,1)}) %reduce-scatter.14.cloned.1.call-update) | async-done | bytes 503824 | tf_op jit(solution)/shard_map/reduce_scatter | solution.py:1173
  407.2 3.6 all-to-all-start.3
  410.9 0.2 reshape.201
  411.1 0.3 copy.123
  411.3 0.9 reshape.202
  412.3 0.7 slice_reduce_fusion.1
  413.0 25.9 %reduce-scatter.12.cloned.1.call-done = bf16[1,32,1024]{2,1,0:T(8,128)(2,1)} async-done(((bf16[8,32,1024]{2,1,0:T(8,128)(2,1)}), bf16[1,32,1024]{2,1,0:T(8,128)(2,1)}) %reduce-scatter.12.cloned.1.call-update) | async-done | bytes 65552 | tf_op jit(solution)/shard_map/reduce_scatter | solution.py:1210
  438.9 1.5 bitcast_convert_fusion
  440.5 0.7 reshape.207
  441.2 0.5 copy.124
  441.8 1.5 reshape.208
  443.3 0.2 slice_bitcast_fusion.1
  443.5 0.3 copy.125
  443.8 1.0 reshape.209
  444.7 0.7 copy.137
  (80 shorter events, 2.2 us)
Async XLA Ops:
  7.2 6.0 %copy-start.18 = (bf16[32]{0:T(256)(128)(2,1)S(1)}, bf16[32]{0:T(256)(128)(2,1)}, u32[]{:S(2)}) copy-start(bf16[32]{0:T(256)(128)(2,1)} %param.10) | copy-start | bytes 196
  7.2 6.0 %copy-start.17 = (bf16[32]{0:T(256)(128)(2,1)S(1)}, bf16[32]{0:T(256)(128)(2,1)}, u32[]{:S(2)}) copy-start(bf16[32]{0:T(256)(128)(2,1)} %param.13) | copy-start | bytes 196
  7.2 6.2 %copy-start.6 = (bf16[32,3072]{1,0:T(8,128)(2,1)S(1)}, bf16[32,3072]{1,0:T(8,128)(2,1)}, u32[]{:S(2)}) copy-start(bf16[32,3072]{1,0:T(8,128)(2,1)} %wq.1) | copy-start | bytes 589828
  7.2 6.1 %copy-start.7 = (bf16[32,1024]{1,0:T(8,128)(2,1)S(1)}, bf16[32,1024]{1,0:T(8,128)(2,1)}, u32[]{:S(2)}) copy-start(bf16[32,1024]{1,0:T(8,128)(2,1)} %w_out.1) | copy-start | bytes 196612
  7.2 6.1 %copy-start.4 = (bf16[32,5248]{1,0:T(8,128)(2,1)S(1)}, bf16[32,5248]{1,0:T(8,128)(2,1)}, u32[]{:S(2)}) copy-start(bf16[32,5248]{1,0:T(8,128)(2,1)} %w_in.1) | copy-start | bytes 1007620
  7.2 6.1 %copy-start.5 = (bf16[128,1024]{1,0:T(8,128)(2,1)S(1)}, bf16[128,1024]{1,0:T(8,128)(2,1)}, u32[]{:S(2)}) copy-start(bf16[128,1024]{1,0:T(8,128)(2,1)} %cot.1) | copy-start | bytes 786436
  7.2 6.1 %copy-start.2 = (bf16[128,1024]{1,0:T(8,128)(2,1)S(1)}, bf16[128,1024]{1,0:T(8,128)(2,1)}, u32[]{:S(2)}) copy-start(bf16[128,1024]{1,0:T(8,128)(2,1)} %tok.1) | copy-start | bytes 786436
  7.2 198.8 %reduce-scatter.8.cloned.1.call-start = ((), (), s32[]{:S(2)}) async-start(), calls=%async_computation.8 | async-start | bytes 1572864 | tf_op jit(solution)/shard_map/reduce_scatter | solution.py:1185
  72.0 1.0 copy-start
  73.0 0.6 copy-start.3
  73.6 14.6 %copy-start.10 = (bf16[4,32,1968]{2,1,0:T(8,128)(2,1)}, bf16[4,32,1968]{2,1,0:T(8,128)(2,1)S(1)}, u32[]{:S(2)}) copy-start(bf16[4,32,1968]{2,1,0:T(8,128)(2,1)S(1)} %get-tuple-element.34.wm_own) | copy-start | bytes 1511428
  88.2 0.7 copy-start.8
  88.9 86.6 %copy-start.9 = (bf16[4,2,128,128]{3,2,1,0:T(8,128)(2,1)S(1)}, bf16[4,2,128,128]{3,2,1,0:T(8,128)(2,1)}, u32[]{:S(2)}) copy-start(bf16[4,2,128,128]{3,2,1,0:T(8,128)(2,1)} %copy-done.8) | copy-start | bytes 786436
  175.5 1.0 copy-start.11
  206.1 20.1 %all-to-all-start.1 = ((bf16[4,4,128,128]{3,2,1,0:T(8,128)(2,1)}), bf16[4,4,128,128]{3,2,1,0:T(8,128)(2,1)S(1)}, u32[]{:S(2)}, u32[]{:S(2)}) async-start(bf16[4,4,128,128]{3,2,1,0:T(8,128)(2,1)} %bitcast.98), calls=%async_computation.2 | async-start | bytes 1048576 | tf_op jit(solution)/shard_map/all_to_all | solution.py:1186
  210.5 48.1 %reduce-scatter.10.cloned.1.call-start = ((), (), s32[]{:S(2)}) async-start(), calls=%async_computation.9 | async-start | bytes 1310720 | tf_op jit(solution)/shard_map/reduce_scatter | solution.py:1200
  227.5 5.8 %copy-start.15 = (bf16[512,256]{1,0:T(8,128)(2,1)}, bf16[512,256]{1,0:T(8,128)(2,1)S(1)}, u32[]{:S(2)}) copy-start(bf16[512,256]{1,0:T(8,128)(2,1)S(1)} %copy.118) | copy-start | bytes 786436
  227.6 0.8 copy-start.16
  231.8 1.2 copy-start.1
  231.8 29.4 %copy-start.12 = (f32[128,1024]{1,0:T(8,128)S(1)}, f32[128,1024]{1,0:T(8,128)}, u32[]{:S(2)}) copy-start(f32[128,1024]{1,0:T(8,128)} %get-tuple-element.37) | copy-start | bytes 1572868
  231.8 58.3 %all-gather.2.cloned.1.call-start = ((), (), s32[]{:S(2)}) async-start(), calls=%async_computation.10 | async-start | bytes 1310720 | tf_op jit(solution)/shard_map/all_gather | solution.py:1180
  263.3 92.2 %all-reduce.9.cloned.1.call-start = ((), (), s32[]{:S(2)}) async-start(), calls=%async_computation.13 | async-start | bytes 3670016
  269.5 137.6 %reduce-scatter.14.cloned.1.call-start = ((), (), s32[]{:S(2)}) async-start(), calls=%async_computation.12 | async-start | bytes 4718592 | tf_op jit(solution)/shard_map/reduce_scatter | solution.py:1173
  269.6 20.5 %copy-start.13 = (bf16[4,128,256]{2,1,0:T(8,128)(2,1)S(1)}, bf16[4,128,256]{2,1,0:T(8,128)(2,1)}, u32[]{:S(2)}) copy-start(bf16[4,128,256]{2,1,0:T(8,128)(2,1)} %get-tuple-element.46) | copy-start | bytes 786436
  270.1 22.5 %copy-start.19 = (u32[32]{0:T(128)S(1)}, u32[32]{0:T(128)}, u32[]{:S(2)}) copy-start(u32[32]{0:T(128)} %constant.96) | copy-start | bytes 388
  270.1 168.8 %reduce-scatter.12.cloned.1.call-start = ((), (), s32[]{:S(2)}) async-start(), calls=%async_computation.11 | async-start | bytes 589824 | tf_op jit(solution)/shard_map/reduce_scatter | solution.py:1210
  357.9 8.9 %all-to-all-start.2 = ((bf16[4,32,896]{2,1,0:T(8,128)(2,1)}), bf16[4,32,896]{2,1,0:T(8,128)(2,1)S(1)}, u32[]{:S(2)}, u32[]{:S(2)}) async-start(bf16[4,32,896]{2,1,0:T(8,128)(2,1)} %dynamic-slice_bitcast_fusion), calls=%async_computation.4 | async-start | bytes 458752 | tf_op jit(solution)/shard_map/all_to_all | solution.py:1212
  407.2 33.3 %all-to-all-start.3 = ((bf16[4,32,1968]{2,1,0:T(8,128)(2,1)}), bf16[4,32,1968]{2,1,0:T(8,128)(2,1)S(1)}, u32[]{:S(2)}, u32[]{:S(2)}) async-start(bf16[4,32,1968]{2,1,0:T(8,128)(2,1)} %bitcast.97), calls=%async_computation.7 | async-start | bytes 1048576 | tf_op jit(solution)/shard_map/all_to_all | solution.py:1211
  443.2 1.5 copy-start.14
Sparse Core Ops, SparseCore 0:
  195.9 8.8 reduce-scatter.7
  231.9 26.6 reduce-scatter.9
  263.5 26.6 all-gather.1
  292.3 63.1 all-reduce.8
  357.7 49.4 reduce-scatter.13
  409.8 29.0 reduce-scatter.11

commit v3 on v2

--- a/solution.py
+++ b/solution.py
@@ -903,11 +903,109 @@
     )
 
 
+class Reduce:
+    def __init__(self, term, core_in, line_out, line_in, h, part, share, parts, sems):
+        self.term, self.core_in, self.line_out, self.line_in = term, core_in, line_out, line_in
+        self.h, self.part, self.share, self.parts = h, part, share, parts
+        self.core_s, self.core_r, self.line_s, self.line_r = sems
+
+    def _core(self):
+        return pltpu.make_async_remote_copy(
+            self.term.at[:, 1 - self.share],
+            self.core_in,
+            self.core_s.at[0],
+            self.core_r.at[0],
+            device_id=(self.h, self.part * 2 + 1 - self.share),
+            device_id_type=MESH,
+        )
+
+    def _line(self, i):
+        there = lax.rem(self.part + i, self.parts)
+        return pltpu.make_async_remote_copy(
+            self.line_out.at[i - 1],
+            self.line_in.at[i - 1],
+            self.line_s.at[i - 1],
+            self.line_r.at[i - 1],
+            device_id=(self.h, there * 2 + self.share),
+            device_id_type=MESH,
+        )
+
+    def _sum(self, i):
+        there = lax.rem(self.part + i, self.parts)
+        return self.term[there, self.share].astype(jnp.float32) + self.core_in[there].astype(
+            jnp.float32
+        )
+
+    def start(self):
+        self._core().start()
+
+    def middle(self):
+        self._core().wait_recv()
+        for i in range(1, self.parts):
+            self.line_out[i - 1] = self._sum(i).astype(jnp.bfloat16)
+            self._line(i).start()
+
+    def close(self):
+        total = self._sum(0)
+        for i in range(1, self.parts):
+            self._line(i).wait_recv()
+            total += self.line_in[i - 1].astype(jnp.float32)
+        return total
+
+    def finish(self):
+        self._core().wait_send()
+        for i in range(1, self.parts):
+            self._line(i).wait_send()
+
+
+def reduce_scratch(parts, shape):
+    return [
+        pltpu.VMEM((parts, *shape), jnp.bfloat16),
+        pltpu.VMEM((parts - 1, *shape), jnp.bfloat16),
+        pltpu.VMEM((parts - 1, *shape), jnp.bfloat16),
+        pltpu.SemaphoreType.DMA((1,)),
+        pltpu.SemaphoreType.DMA((1,)),
+        pltpu.SemaphoreType.DMA((parts - 1,)),
+        pltpu.SemaphoreType.DMA((parts - 1,)),
+    ]
+
+
+class Swap:
+    def __init__(self, out, landed, h, across, sems):
+        self.out, self.landed, self.h, self.across = out, landed, h, across
+        self.send_s, self.recv_s = sems
+
+    def start(self, value):
+        self.out[...] = value.astype(jnp.bfloat16)
+        self.landed[self.h] = self.out[self.h]
+        self.copies = [
+            send(self.out.at[peer[0]], self.landed.at[self.h], self.send_s.at[i], self.recv_s.at[i], peer)
+            for i, peer in enumerate(self.across)
+        ]
+
+    def arrive(self):
+        for copy in self.copies:
+            copy.wait_recv()
+
+    def finish(self):
+        for copy in self.copies:
+            copy.wait_send()
+
+
+def swap_scratch(heads, shape):
+    return [
+        pltpu.VMEM((heads, *shape), jnp.bfloat16),
+        pltpu.VMEM((heads, *shape), jnp.bfloat16),
+        pltpu.SemaphoreType.DMA((heads - 1,)),
+        pltpu.SemaphoreType.DMA((heads - 1,)),
+    ]
+
+
 def feed_kernel(
     H, A, op, tok_all, cot_all, wo, wm_own, gain_rows,
-    output, grad_middle, go, term, mixed_own, gain_part,
-    mx_in, mixed_all, wm_all, middle, normed, act, lift, g2_send, g2_in, g2_own, o_send, o_in, o_own, gm_send,
-    mx_s, mx_r, ma_s, ma_r, g2_s, g2_r, o_s, o_r, gm_s, gm_r, *line,
+    output, grad_middle, go, term, down_grad, mixed_own, gain_part,
+    mx_in, mixed_all, wm_all, middle, normed, act, lift, g2_send, g2_in, g2_own, o_send, o_in, o_own, gm_send, term_down,
+    mx_s, mx_r, ma_s, ma_r, g2_s, g2_r, o_s, o_r, gm_s, gm_r, *more,
 ):
     f32, bf16 = jnp.float32, jnp.bfloat16
     R, W = tok_all.shape[1:]
@@ -929,8 +1027,10 @@
         for i, peer in enumerate(along)
     ]
     gather = LineGather(
-        lambda block, side: wm_all.at[:, block * 2 + side], wm_own, h, part, share, A, line
-    )
+        lambda block, side: wm_all.at[:, block * 2 + side], wm_own, h, part, share, A, more[:5]
+    )
+    down_sum = Reduce(term_down, *more[5:8], h, part, share, A, more[8:12])
+    down_swap = Swap(*more[12:14], h, across, more[14:16])
     gather.start()
     wm_all[:, b] = wm_own[...]
     mx_in[part] = op[part]
@@ -1004,6 +1104,16 @@
 
     lax.fori_loop(0, H, feed_run, 0)
 
+    def down_chunk(chunk, carried):
+        lanes = pl.ds(pl.multiple_of(chunk * hw, hw), hw)
+        left = cot_all[:, :, lanes].reshape(H * R, hw)
+        grads = mm(left, act[...].reshape(H * R, F), TN).astype(bf16)
+        term_down[:, :, chunk] = grads.reshape(A, 2, D, F)
+        return carried
+
+    lax.fori_loop(0, H, down_chunk, 0)
+    down_sum.start()
+
     def out_run(i, carried):
         run = lax.rem(h + 1 + i, H)
         for chunk in range(H):
@@ -1020,6 +1130,8 @@
         return carried
 
     lax.fori_loop(0, H, out_run, 0)
+
+    down_sum.middle()
 
     def rest(sent, landed, send_sem, recv_sem, i):
         return pltpu.make_async_remote_copy(
@@ -1056,13 +1168,11 @@
         lanes = pl.ds(pl.multiple_of(chunk * hw, hw), hw)
         left = normed[:, :, lanes].reshape(H * R, hw)
         grads = mm(left, lift[...].reshape(H * R, 2 * F), TN).astype(bf16)
-        term[:, chunk, :, : 2 * F] = grads.reshape(B, D, 2 * F)
-        left = cot_all[:, :, lanes].reshape(H * R, hw)
-        grads = mm(left, act[...].reshape(H * R, F), TN).astype(bf16)
-        term[:, chunk, :, 2 * F :] = grads.reshape(B, D, F)
+        term[:, :, chunk] = grads.reshape(A, 2, D, 2 * F)
         return carried
 
     lax.fori_loop(0, H, term_chunk, 0)
+    down_swap.start(down_sum.close())
     result = middle[h] + o_own[...]
     for i in range(H - 1):
         rest(o_send, o_in, o_s, o_r, i).wait_recv()
@@ -1070,12 +1180,20 @@
     output[...] = result.astype(bf16)
     for copy in gm_copies:
         copy.wait_recv()
+    down_swap.arrive()
+    unit = (
+        lax.broadcasted_iota(jnp.int32, (D, D), 0) == lax.broadcasted_iota(jnp.int32, (D, D), 1)
+    ).astype(bf16)
+    for place in range(H):
+        down_grad[place * F : (place + 1) * F, :] = mm(down_swap.landed[place], unit, TN)
     for copy in [*mx_copies, *ma_copies, *gm_copies]:
         copy.wait_send()
     for i in range(H - 1):
         rest(g2_send, g2_in, g2_s, g2_r, i).wait_send()
         rest(o_send, o_in, o_s, o_r, i).wait_send()
     gather.finish()
+    down_sum.finish()
+    down_swap.finish()
 
 
 def feed(op, tok_all, cot_all, wo, wm_own, gain_rows):
@@ -1093,12 +1211,13 @@
     return pl.pallas_call(
         partial(feed_kernel, H, A),
         in_specs=[vmem] * 6,
-        out_specs=[vmem] * 6,
+        out_specs=[vmem] * 7,
         out_shape=[
             shape((R, W), bf16),
             shape((R, W), f32),
             shape((A, H, R // 2, 128), bf16),
-            shape((B, H, D, 3 * F), bf16),
+            shape((A, 2, H, D, 2 * F), bf16),
+            shape((H * F, D), f32),
             shape((H, R, hw), bf16),
             shape((8, W), f32),
         ],
@@ -1112,10 +1231,13 @@
             pltpu.VMEM((H, R, 2 * F), bf16),
             *[pltpu.VMEM((H - 1, R, W), bf16), pltpu.VMEM((H - 1, R, W), bf16), pltpu.VMEM((R, W), f32)] * 2,
             pltpu.VMEM((H, A, R // 2, 128), bf16),
+            pltpu.VMEM((A, 2, H, D, F), bf16),
             *[dma(A - 1)] * 2,
             *[dma(H - 1)] * 6,
             *[dma(H * A)] * 2,
             *line_sems(A),
+            *reduce_scratch(A, (H, D, F)),
+            *swap_scratch(H, (D, F)),
         ],
         compiler_params=pltpu.CompilerParams(
             collective_id=1, has_side_effects=True, vmem_limit_bytes=56 * 2**20
@@ -1123,6 +1245,234 @@
         cost_estimate=pl.CostEstimate(flops=6 * 10**9, bytes_accessed=10**7, transcendentals=10**6),
         name="feed",
     )(op, tok_all, cot_all, wo, wm_own, gain_rows)
+
+
+def finish_kernel(
+    H, A, dqp, dkv, tok_all, wq_all, cos_all, sin_all, gain_rows, mixed_own, grad_middle, gain_part, term_in,
+    input_grad, qkv_grad, out_grad, in_grad, gain_grads,
+    dk_in, dkv_send, dkv_in, dq_in, branch, branch_all, gp, normed, g1_send, g1_in, g1_own, term_out, term_qkv, term_gain,
+    dk_s, dk_r, dz_s, dz_r, dq_s, dq_r, br_s, br_r, g1_s, g1_r, *rest,
+):
+    f32, bf16 = jnp.float32, jnp.bfloat16
+    R, W = tok_all.shape[1:]
+    B = 2 * A
+    hw = W // H
+    D = term_in.shape[3]
+    F = term_in.shape[4] // 2
+    h, b, part, share, across, along, beside = grid_peers(H, A)
+
+    def reducer(n, term):
+        scratch = rest[7 * n : 7 * n + 7]
+        return Reduce(term, *scratch[:3], h, part, share, A, scratch[3:])
+
+    def swapper(n):
+        scratch = rest[28 + 4 * n : 32 + 4 * n]
+        return Swap(*scratch[:2], h, across, scratch[2:])
+
+    in_sum, out_sum = reducer(0, term_in), reducer(1, term_out)
+    qkv_sum, gain_sum = reducer(2, term_qkv), reducer(3, term_gain)
+    in_swap, qkv_swap, gain_swap = swapper(0), swapper(1), swapper(2)
+    meet([*across, *along, beside])
+
+    order = [*[lax.rem(part + i, A) for i in range(1, A)], part]
+    dk_copies = [
+        send(dkv.at[:, there * 2 + 1 - share], dk_in.at[i], dk_s.at[i], dk_r.at[i], beside)
+        for i, there in enumerate(order)
+    ]
+    dq_copies = [
+        send(dqp.at[peer[1] // 2], dq_in.at[part], dq_s.at[i], dq_r.at[i], peer)
+        for i, peer in enumerate(along)
+    ]
+    dq_in[part] = dqp[part]
+    branch[...] = grad_middle[...].astype(bf16)
+    br_copies = [
+        send(branch, branch_all.at[h], br_s.at[i], br_r.at[i], peer) for i, peer in enumerate(across)
+    ]
+    branch_all[h] = branch[...]
+    in_sum.start()
+    dz_copies = []
+    for i, there in enumerate(order):
+        dk_copies[i].wait_recv()
+        summed = dkv[:, there * 2 + share].astype(f32) + dk_in[i].astype(f32)
+        if i < A - 1:
+            dkv_send[i] = summed.astype(bf16)
+            dz_copies.append(
+                send(dkv_send.at[i], dkv_in.at[part], dz_s.at[i], dz_r.at[i], along[i])
+            )
+        else:
+            dkv_in[part] = summed.astype(bf16)
+    in_sum.middle()
+
+    def norm_run(run, carried):
+        hat, unused = standardize(tok_all[run].astype(f32))
+        normed[run] = (hat * gain_rows[0:1, :]).astype(bf16)
+        return carried
+
+    lax.fori_loop(0, H, norm_run, 0)
+    for copy in br_copies:
+        copy.wait_recv()
+
+    def out_tile(n, carried):
+        lanes = pl.ds(pl.multiple_of(n * hw, hw), hw)
+        grads = mm(mixed_own[...].reshape(H * R, hw), branch_all[:, :, lanes].reshape(H * R, hw), TN)
+        term_out[:, :, :, lanes] = grads.astype(bf16).reshape(A, 2, D, hw)
+        return carried
+
+    lax.fori_loop(0, W // hw, out_tile, 0)
+    out_sum.start()
+    for copy in [*dq_copies, *dz_copies]:
+        copy.wait_recv()
+    for run in range(H):
+        side, at = run // (H // 2), run % (H // 2)
+        cosine, sine = cos_all[run], sin_all[run]
+        for slab in range(hw // 128):
+            lanes = slab * 128
+            left, right = dq_in[2 * slab, at].astype(f32), dq_in[2 * slab + 1, at].astype(f32)
+            gp[run, :, lanes : lanes + 128] = turn(
+                join(left, side, right, side), cosine, sine, True
+            ).astype(bf16)
+            left, right = dkv_in[2 * slab, run].astype(f32), dkv_in[2 * slab + 1, run].astype(f32)
+            gp[run, :, hw + lanes : hw + lanes + 128] = turn(
+                join(left, 0, right, 0), cosine, sine, True
+            ).astype(bf16)
+            gp[run, :, 2 * hw + lanes : 2 * hw + lanes + 128] = join(left, 1, right, 1).astype(bf16)
+
+    def block(chunk):
+        return wq_all[chunk].reshape(B * D, 3 * hw + 128)
+
+    def term_chunk(chunk, carried):
+        lanes = pl.ds(pl.multiple_of(chunk * hw, hw), hw)
+        left = normed[:, :, lanes].reshape(H * R, hw)
+        grads = mm(left, gp[...].reshape(H * R, 3 * hw), TN).astype(bf16)
+        term_qkv[:, :, chunk] = grads.reshape(A, 2, D, 3 * hw)
+        return carried
+
+    lax.fori_loop(0, H, term_chunk, 0)
+    qkv_sum.start()
+
+    def one_run(i, carried):
+        run = lax.rem(h + 1 + i, H)
+        for chunk in range(H):
+            lanes = slice(chunk * hw, (chunk + 1) * hw)
+            g1_own[:, lanes] = mm(gp[run], block(chunk)[:, : 3 * hw], NT)
+
+        @pl.when(i < H - 1)
+        def _():
+            g1_send[i] = g1_own[...].astype(bf16)
+            pltpu.make_async_remote_copy(
+                g1_send.at[i], g1_in.at[i], g1_s.at[i], g1_r.at[i], device_id=(run, b), device_id_type=MESH
+            ).start()
+
+        return carried
+
+    lax.fori_loop(0, H, one_run, 0)
+    qkv_sum.middle()
+    out_sum.middle()
+
+    g1_copies = [
+        pltpu.make_async_remote_copy(
+            g1_send.at[i], g1_in.at[i], g1_s.at[i], g1_r.at[i], device_id=across[i], device_id_type=MESH
+        )
+        for i in range(H - 1)
+    ]
+    grad = g1_own[...]
+    for i in range(H - 1):
+        g1_copies[i].wait_recv()
+        grad += g1_in[i].astype(f32)
+    hat, scale = standardize(tok_all[h].astype(f32))
+    gain_part_one = jnp.sum(grad * hat, axis=0, keepdims=True)
+    input_grad[...] = grad_middle[...] + norm_back(grad, hat, scale, gain_rows[0:1, :])
+    row = lax.broadcasted_iota(jnp.int32, (8, W), 0)
+    rows = jnp.where(row == 0, gain_part_one, jnp.where(row == 1, gain_part[...], 0.0))
+    pick = (
+        lax.broadcasted_iota(jnp.int32, (8, 128), 0) == lax.broadcasted_iota(jnp.int32, (8, 128), 1)
+    ).astype(bf16)
+    for chunk in range(H):
+        gain_columns = mm(rows[:, chunk * hw : (chunk + 1) * hw].astype(bf16), pick, TN)
+        term_gain[:, :, chunk] = gain_columns.astype(bf16).reshape(A, 2, D, 128)
+    gain_sum.start()
+    in_swap.start(in_sum.close())
+    gain_sum.middle()
+    out_grad[...] = out_sum.close()
+    qkv_swap.start(qkv_sum.close())
+    gain_swap.start(gain_sum.close())
+    in_swap.arrive()
+    for place in range(H):
+        in_grad[:, place * F : (place + 1) * F] = in_swap.landed[place, :, :F].astype(f32)
+        in_grad[:, (H + place) * F : (H + place + 1) * F] = in_swap.landed[place, :, F:].astype(f32)
+    qkv_swap.arrive()
+    for place in range(H):
+        for j in range(3):
+            qkv_grad[:, j * W + place * hw : j * W + (place + 1) * hw] = qkv_swap.landed[
+                place, :, j * hw : (j + 1) * hw
+            ].astype(f32)
+    gain_swap.arrive()
+    total = gain_swap.landed[0].astype(f32)
+    for place in range(1, H):
+        total += gain_swap.landed[place].astype(f32)
+    gain_grads[...] = total
+    for copy in [*dk_copies, *dq_copies, *br_copies, *dz_copies, *g1_copies]:
+        copy.wait_send()
+    for part_of in (in_sum, out_sum, qkv_sum, gain_sum, in_swap, qkv_swap, gain_swap):
+        part_of.finish()
+
+
+def finish(dqp, dkv, tok_all, wq_all, cos_all, sin_all, gain_rows, mixed, grad_middle, gain_part, term_in):
+    A, half, R, lanes = dqp.shape
+    H = 2 * half
+    W = tok_all.shape[-1]
+    B = 2 * A
+    hw = W // H
+    D = term_in.shape[3]
+    F = term_in.shape[4] // 2
+    f32, bf16 = jnp.float32, jnp.bfloat16
+    shape = jax.ShapeDtypeStruct
+    dma = lambda count: pltpu.SemaphoreType.DMA((count,))
+    vmem = pl.BlockSpec(memory_space=pltpu.VMEM)
+    buffer = lambda *sizes: pltpu.VMEM(sizes, bf16)
+    return pl.pallas_call(
+        partial(finish_kernel, H, A),
+        in_specs=[vmem] * 11,
+        out_specs=[vmem] * 5,
+        out_shape=[
+            shape((R, W), f32),
+            shape((D, 3 * W), f32),
+            shape((D, W), f32),
+            shape((D, 2 * H * F), f32),
+            shape((D, 128), f32),
+        ],
+        scratch_shapes=[
+            buffer(A, H, R, 128),
+            buffer(A - 1, H, R, 128),
+            buffer(A, H, R, 128),
+            buffer(A, half, R, 128),
+            buffer(R, W),
+            buffer(H, R, W),
+            buffer(H, R, 3 * hw),
+            buffer(H, R, W),
+            buffer(H - 1, R, W),
+            buffer(H - 1, R, W),
+            pltpu.VMEM((R, W), f32),
+            buffer(A, 2, D, W),
+            buffer(A, 2, H, D, 3 * hw),
+            buffer(A, 2, H, D, 128),
+            *[dma(A)] * 2,
+            *[dma(A - 1)] * 4,
+            *[dma(H - 1)] * 4,
+            *reduce_scratch(A, (H, D, 2 * F)),
+            *reduce_scratch(A, (D, W)),
+            *reduce_scratch(A, (H, D, 3 * hw)),
+            *reduce_scratch(A, (H, D, 128)),
+            *swap_scratch(H, (D, 2 * F)),
+            *swap_scratch(H, (D, 3 * hw)),
+            *swap_scratch(H, (D, 128)),
+        ],
+        compiler_params=pltpu.CompilerParams(
+            collective_id=2, has_side_effects=True, vmem_limit_bytes=56 * 2**20
+        ),
+        cost_estimate=pl.CostEstimate(flops=2 * 10**9, bytes_accessed=10**7, transcendentals=10**5),
+        name="finish",
+    )(dqp, dkv, tok_all, wq_all, cos_all, sin_all, gain_rows, mixed, grad_middle, gain_part, term_in)
 
 
 def per_device_split(
@@ -1164,63 +1514,22 @@
     kv, qp, tok_all, cot_all, wq, wm, wo, gain_rows, cos_all, sin_all = project(
         tokens, cotangent, w_qkv, gains, w_in, w_mlp_out, w_attn_out, jnp.stack([ends, doc_lengths])
     )
-    cosine, sine = cos_all.reshape(N, 128)[:, :HEAD_DIM], sin_all.reshape(N, 128)[:, :HEAD_DIM]
     kv = kv.reshape(T, 2 * HEAD_DIM)
     op, lse = attend(span, qp, kv, qdoc, kdoc)
-    output, grad_middle, gp, term_mlp, mixed, gain_part = feed(
+    output, grad_middle, gp, term_in, down_grad, mixed, gain_part = feed(
         op, tok_all, cot_all, wo.reshape(H, hw, W), wm, gain_rows
     )
-    sum_mlp = lax.psum_scatter(
-        term_mlp.reshape(B * H * D, 3 * F), "blk", scatter_dimension=0, tiled=True
-    ).reshape(H, D, 3 * F)
     dqp, dkv = attend_back(span, qp, gp, op, lse, kv, qdoc, kdoc)
-    wq = wq.reshape(W, 3 * hw + 128)
-    gain_one = gain_rows[0]
-    normed_one = layer_norm(tok_all.reshape(N, W).astype(f32), gain_one).astype(bf16)
-    branch_all = lax.all_gather(grad_middle.astype(bf16), "head", axis=0, tiled=True)
-    grad_gain_two = gain_part[0]
-    mixed = mixed.reshape(N, hw)
-    dqp = lax.all_to_all(dqp, "blk", 0, 0, tiled=True, axis_index_groups=part_groups)
-    dkv = dkv.reshape(H, A, G, R, 2 * HEAD_DIM).transpose(2, 1, 0, 3, 4)
-    dkv = lax.psum_scatter(dkv, "blk", scatter_dimension=0, tiled=False, axis_index_groups=share_groups)
-    dkv = lax.all_to_all(dkv, "blk", 0, 0, tiled=True, axis_index_groups=part_groups)
-    merge = lambda v: v.transpose(1, 2, 0, 3).reshape(N, hw)
-    _, rope_pull = jax.vjp(
-        partial(rotate_pair, cosine=cosine, sine=sine),
-        jnp.zeros((N, hw), f32),
-        jnp.zeros((N, hw), f32),
-    )
-    grad_query, grad_keys = rope_pull(
-        (merge(unpack_pairs(dqp)).astype(f32), merge(dkv[..., :HEAD_DIM]).astype(f32))
-    )
-    grad_projected = jnp.concatenate(
-        [grad_query.astype(bf16), grad_keys.astype(bf16), merge(dkv[..., HEAD_DIM:])], axis=1
-    )
-    grad_one = mm(grad_projected, wq[:, : 3 * hw], NT).astype(bf16)
-    grad_one = lax.psum_scatter(grad_one, "head", scatter_dimension=0, tiled=True).astype(f32)
-    _, norm_one_pull = jax.vjp(layer_norm, tokens.astype(f32), gain_one)
-    grad_input, grad_gain_one = norm_one_pull(grad_one)
-    input_grad = grad_middle + grad_input
-    term_qkv = mm(normed_one, grad_projected, TN)
-    gain_terms = jnp.pad(jnp.stack([grad_gain_one, grad_gain_two], axis=1), ((0, 0), (0, 126)))
-    term_qkv = jnp.concatenate([term_qkv, gain_terms], axis=1).astype(bf16)
-    term_qkv = term_qkv.reshape(H, B, D, 3 * hw + 128).transpose(1, 0, 2, 3)
-    term_out = mm(mixed, branch_all, TN).astype(bf16).reshape(B, D, W)
-    sum_qkv = lax.psum_scatter(term_qkv, "blk", scatter_dimension=0, tiled=False)
-    sum_out = lax.psum_scatter(term_out, "blk", scatter_dimension=0, tiled=False)
-    sum_mlp = lax.all_to_all(sum_mlp, "head", 0, 0, tiled=True).astype(f32)
-    sum_qkv = lax.all_to_all(sum_qkv, "head", 0, 0, tiled=True).astype(f32)
-    in_grad = sum_mlp[:, :, : 2 * F].reshape(H, D, 2, F).transpose(1, 2, 0, 3).reshape(D, 2 * H * F)
-    down_grad = sum_mlp[:, :, 2 * F :].transpose(0, 2, 1).reshape(H * F, D)
-    qkv_grad = sum_qkv[:, :, : 3 * hw].reshape(H, D, 3, hw).transpose(1, 2, 0, 3).reshape(D, 3 * W)
-    gain_sums = jnp.sum(sum_qkv[:, :, 3 * hw : 3 * hw + 2], axis=0)
+    input_grad, qkv_grad, out_grad, in_grad, gain_grads = finish(
+        dqp, dkv.reshape(H, B, R, 128), tok_all, wq, cos_all, sin_all, gain_rows, mixed, grad_middle, gain_part, term_in
+    )
     return (
         output,
         input_grad,
-        gain_sums[:, 0],
+        gain_grads[:, 0],
         qkv_grad,
-        sum_out.astype(f32),
-        gain_sums[:, 1],
+        out_grad,
+        gain_grads[:, 1],
         in_grad,
         down_grad,
     )

time: 450 us -> 284 us (0.63)
  waiting for transfers between devices: 195 us -> 0 us
  Pallas kernels: 178 us -> 264 us
  between operations: 14.7 us -> 0.88 us
  starting transfers between devices: 12.2 us -> 0 us
  blocking collectives: 10.3 us -> 0 us
  other arithmetic: 12.5 us -> 3.42 us
  matrix products: 7.89 us -> 0 us
  local copies, waits for them, and re-layouts: 22.1 us -> 16 us
    reduce_scatter x4 -> x0, waiting for transfers between devices: 91.7 us -> none  [the longest x1 40.3 us: per_device_split(): lax.psum_scatter(term_mlp.reshape(B * H * D, 3 * F), 'blk', scatter_dimen...]
    pallas_call x0 -> x1, Pallas kernels: none -> 85.3 us  [finish(): pl.pallas_call(partial(finish_kernel, H, A), in_specs=[vmem] * 11, out_sp...]
    unnamed x7 -> x0, waiting for transfers between devices: 62.9 us -> none
    all_to_all x3 -> x0, waiting for transfers between devices: 20.1 us -> none  [the longest x1 14.8 us: per_device_split(): lax.all_to_all(dkv, 'blk', 0, 0, tiled=True, axis_index_groups=part_groups)]
    all_gather x1 -> x0, waiting for transfers between devices: 19.9 us -> none  [per_device_split(): lax.all_gather(grad_middle.astype(bf16), 'head', axis=0, tiled=True)]
    all_to_all x3 -> x0, starting transfers between devices: 11.8 us -> none  [the longest x1 4.47 us: per_device_split(): lax.all_to_all(dkv, 'blk', 0, 0, tiled=True, axis_index_groups=part_groups)]
    all_to_all x1 -> x0, blocking collectives: 10.3 us -> none  [per_device_split(): lax.all_to_all(dqp, 'blk', 0, 0, tiled=True, axis_index_groups=part_groups)]
    dot_general x3 -> x0, matrix products: 7.89 us -> none  [mm(): lax.dot_general(left, right, dims, preferred_element_type=jnp.float32)]
  transfers between devices with their start and end apart: 9 -> 0, of which waited for: 7 -> 0; matrix products, arithmetic and copies ran while one was open for 4% -> 0% of each run, Pallas kernels for 0% -> 0%
where the time goes in v3:
time: 284 us
  Pallas kernels  264 us (93%)
  local copies, waits for them, and re-layouts  16 us (6%)
  other arithmetic  3.42 us (1%)
    pallas_call x1, Pallas kernels, finish(): pl.pallas_call(partial(finish_kernel, H, A), in_specs=[vmem] * 11, out_sp...  85.3 us
    pallas_call x1, Pallas kernels, feed(): pl.pallas_call(partial(feed_kernel, H, A), in_specs=[vmem] * 6, out_specs...  83.2 us
    pallas_call x1, Pallas kernels, project(): pl.pallas_call(partial(project_kernel, H, A), in_specs=[vmem] * 8, out_sp...  58.4 us
    pallas_call x1, Pallas kernels, attend_back(): pl.pallas_call(attend_back_kernel, grid_spec=pltpu.PrefetchScalarGridSpec...  20.7 us
    pallas_call x1, Pallas kernels, attend(): pl.pallas_call(attend_kernel, grid_spec=pltpu.PrefetchScalarGridSpec(num_...  16.4 us
    unnamed x49, local copies, waits for them, and re-layouts  12.5 us

profile of v3, /device:TPU:0, one launch (start us, length us, event | category | flops | bytes accessed | tf_op | source)
XLA Modules:
  0.0 284.4 jit_solution(8243811550477814652)
XLA Ops:
  0.6 0.0 copy-start.8
  0.6 0.0 copy-start.6
  0.7 0.0 copy-start.10
  0.7 0.0 copy-start.9
  0.7 0.0 copy-start.7
  0.7 0.9 broadcast_in_dim.30
  1.6 0.7 pad_maximum_fusion
  2.3 0.7 pad_add_fusion.1.docs
  3.0 0.1 copy.36
  3.1 1.0 convert_reduce_fusion
  4.1 0.1 slice.25
  4.1 0.7 dynamic-slice_reduce_fusion.1
  4.8 0.1 reshape.65
  4.9 0.1 add_select_fusion
  5.0 0.1 reshape.63
  5.1 0.1 pad_add_fusion.span
  5.2 1.3 copy.37.w_down
  6.5 0.9 reshape.72.qdoc
  7.4 0.0 copy-done.8
  7.4 0.0 copy-done.6
  7.4 0.0 copy-done.10
  7.4 0.0 copy-done.9
  7.4 0.0 copy-done.7
  7.4 58.4 %project.1 = (bf16[4,8,128,128]{3,2,1,0:T(8,128)(2,1)S(1)}, bf16[4,2,128,128]{3,2,1,0:T(8,128)(2,1)S(1)}, bf16[4,128,1024]{2,1,0:T(8,128)(2,1)S(1)}, bf16[4,128,...) custom-call(bf16[128,1024]{1,0:T(8,128)(2,1)S(1)} %copy-done.7, ...), custom_call_target="tpu_custom_call" | custom-call | flops 1000000000 | bytes 10000000 | tf_op jit(solution)/shard_map/project/pallas_call | solution.py:788
  65.9 0.0 copy-start
  65.9 1.0 copy-done
  66.9 0.0 copy-start.2
  66.9 0.7 copy-done.2
  67.6 0.0 copy-start.3
  67.6 0.7 copy-done.3
  68.3 0.0 copy-start.5
  68.3 0.6 copy-done.5
  68.9 0.0 copy-start.13
  68.9 16.4 %attend.1 = (bf16[4,2,128,128]{3,2,1,0:T(8,128)(2,1)S(1)}, f32[8,256,1]{2,1,0:T(8,128)S(1)}) custom-call(s32[8,2]{1,0:T(8,128)S(1)} %pad_add_fusion.span, bf16[4,2,128,128]{3,2,1,0:T(8,128)(2,1)S(1)} %get-tuple-element.34.qp, bf16[4096,128]{1,0:T(8,128)(2,1)S(1)} %bitcast.12, s32[8,256,1]{2,1,0:T(8,128)S(1)} %reshape.72.qdoc, s32[16,256]{1,0:T(8,128)S(1)} %reshape.69.kdoc), custom_call_target="tpu_custom_call" | custom-call | flops 1000000000 | bytes 4000000 | tf_op jit(solution)/shard_map/attend/pallas_call | solution.py:475
  85.3 0.0 copy-start.11
  85.3 0.7 copy-done.11
  86.0 0.0 copy-done.13
  86.0 0.0 copy-start.12
  86.0 83.2 %feed.1 = (bf16[128,1024]{1,0:T(8,128)(2,1)}, f32[128,1024]{1,0:T(8,128)}, bf16[4,4,64,128]{3,2,1,0:T(8,128)(2,1)}, bf16[4,2,4,32,1312]{4,3,2,1,0:T(8,128)(2,1)}...) custom-call(bf16[4,2,128,128]{3,2,1,0:T(8,128)(2,1)} %copy-done.11, ...), custom_call_target="tpu_custom_call" | custom-call | flops 6000000000 | bytes 10000000 | tf_op jit(solution)/shard_map/feed/pallas_call | solution.py:1211
  169.3 0.0 copy-done.12
  169.3 0.0 copy-start.14
  169.3 0.9 copy-done.14
  170.2 20.7 %attend_back.1 = (bf16[4,2,128,128]{3,2,1,0:T(8,128)(2,1)S(1)}, bf16[4096,128]{1,0:T(8,128)(2,1)S(1)}) custom-call(s32[8,2]{1,0:T(8,128)S(1)} %pad_add_fusion.span, bf16[4,2,128,128]{3,2,1,0:T(8,128)(2,1)S(1)} %get-tuple-element.34.qp, bf16[4,4,64,128]{3,2,1,0:T(8,128)(2,1)S(1)} %copy-done.14, bf16[4,2,128,128]{3,2,1,0:T(8,128)(2,1)S(1)} %copy-done.12, ...), custom_call_target="tpu_custom_call" | custom-call | flops 3000000000 | bytes 6000000 | tf_op jit(solution)/shard_map/attend_back/pallas_call | solution.py:547
  190.9 0.0 copy-start.1
  190.9 1.0 copy-done.1
  191.9 0.0 copy-start.4
  191.9 0.7 copy-done.4
  192.6 85.3 %finish.1 = (f32[128,1024]{1,0:T(8,128)}, f32[32,3072]{1,0:T(8,128)}, f32[32,1024]{1,0:T(8,128)}, f32[32,5248]{1,0:T(8,128)}, f32[32,128]{1,0:T(8,128)}) custom-call(bf16[4,2,128,128]{3,2,1,0:T(8,128)(2,1)} %copy-done.4, bf16[4,8,128,128]{3,2,1,0:T(8,128)(2,1)} %bitcast.11, bf16[4,128,1024]{2,1,0:T(8,128)(2,1)} %copy-done, ...), custom_call_target="tpu_custom_call" | custom-call | flops 2000000000 | bytes 10000000 | tf_op jit(solution)/shard_map/finish/pallas_call | solution.py:1433
  277.9 0.0 copy-start.17
  277.9 0.0 copy-start.18
  277.9 0.0 copy-start.20
  277.9 1.5 slice_reduce_fusion
  279.5 0.0 copy-done.15
  279.5 1.1 copy.40
  280.6 0.0 copy-done.19
  280.6 0.7 copy.46
  281.3 0.0 copy-done.17
  281.3 0.8 copy.47
  282.1 0.0 copy-done.18
  282.1 0.7 copy.48
  282.9 0.0 copy-done.20
  282.9 0.7 copy.49
  283.5 0.0 copy-done.16
  283.5 0.8 copy.50
  (7 shorter events, 0.1 us)
Async XLA Ops:
  0.6 6.7 %copy-start.8 = (bf16[128,1024]{1,0:T(8,128)(2,1)S(1)}, bf16[128,1024]{1,0:T(8,128)(2,1)}, u32[]{:S(2)}) copy-start(bf16[128,1024]{1,0:T(8,128)(2,1)} %cot.1) | copy-start | bytes 786436
  0.6 6.7 %copy-start.6 = (bf16[32,5248]{1,0:T(8,128)(2,1)S(1)}, bf16[32,5248]{1,0:T(8,128)(2,1)}, u32[]{:S(2)}) copy-start(bf16[32,5248]{1,0:T(8,128)(2,1)} %w_in.1) | copy-start | bytes 1007620
  0.7 6.7 %copy-start.10 = (bf16[32,1024]{1,0:T(8,128)(2,1)S(1)}, bf16[32,1024]{1,0:T(8,128)(2,1)}, u32[]{:S(2)}) copy-start(bf16[32,1024]{1,0:T(8,128)(2,1)} %w_out.1) | copy-start | bytes 196612
  0.7 6.7 %copy-start.9 = (bf16[32,3072]{1,0:T(8,128)(2,1)S(1)}, bf16[32,3072]{1,0:T(8,128)(2,1)}, u32[]{:S(2)}) copy-start(bf16[32,3072]{1,0:T(8,128)(2,1)} %wq.1) | copy-start | bytes 589828
  0.7 6.7 %copy-start.7 = (bf16[128,1024]{1,0:T(8,128)(2,1)S(1)}, bf16[128,1024]{1,0:T(8,128)(2,1)}, u32[]{:S(2)}) copy-start(bf16[128,1024]{1,0:T(8,128)(2,1)} %tok.1) | copy-start | bytes 786436
  65.9 1.0 copy-start
  66.9 0.7 copy-start.2
  67.6 0.7 copy-start.3
  68.3 0.6 copy-start.5
  68.9 17.1 %copy-start.13 = (bf16[4,32,1968]{2,1,0:T(8,128)(2,1)}, bf16[4,32,1968]{2,1,0:T(8,128)(2,1)S(1)}, u32[]{:S(2)}) copy-start(bf16[4,32,1968]{2,1,0:T(8,128)(2,1)S(1)} %get-tuple-element.40.wm_own) | copy-start | bytes 1511428
  85.3 0.7 copy-start.11
  86.0 83.2 %copy-start.12 = (bf16[4,2,128,128]{3,2,1,0:T(8,128)(2,1)S(1)}, bf16[4,2,128,128]{3,2,1,0:T(8,128)(2,1)}, u32[]{:S(2)}) copy-start(bf16[4,2,128,128]{3,2,1,0:T(8,128)(2,1)} %copy-done.11) | copy-start | bytes 786436
  169.3 1.0 copy-start.14
  190.9 1.0 copy-start.1
  191.9 0.7 copy-start.4
  192.6 86.9 %copy-start.15 = (f32[2624,32]{1,0:T(8,128)S(1)}, f32[2624,32]{1,0:T(8,128)}, u32[]{:S(2)}) copy-start(f32[2624,32]{1,0:T(8,128)} %get-tuple-element.91) | copy-start | bytes 1007620
  192.6 88.0 %copy-start.19 = (bf16[128,1024]{1,0:T(8,128)(2,1)S(1)}, bf16[128,1024]{1,0:T(8,128)(2,1)}, u32[]{:S(2)}) copy-start(bf16[128,1024]{1,0:T(8,128)(2,1)} %get-tuple-element.107) | copy-start | bytes 786436
  277.9 3.4 %copy-start.17 = (f32[128,1024]{1,0:T(8,128)S(1)}, f32[128,1024]{1,0:T(8,128)}, u32[]{:S(2)}) copy-start(f32[128,1024]{1,0:T(8,128)} %get-tuple-element.108) | copy-start | bytes 1572868
  277.9 4.2 %copy-start.18 = (f32[32,3072]{1,0:T(8,128)S(1)}, f32[32,3072]{1,0:T(8,128)}, u32[]{:S(2)}) copy-start(f32[32,3072]{1,0:T(8,128)} %get-tuple-element.110) | copy-start | bytes 1179652
  277.9 4.9 %copy-start.20 = (f32[32,1024]{1,0:T(8,128)S(1)}, f32[32,1024]{1,0:T(8,128)}, u32[]{:S(2)}) copy-start(f32[32,1024]{1,0:T(8,128)} %get-tuple-element.111) | copy-start | bytes 393220
  279.5 4.1 %copy-start.16 = (f32[32,5248]{1,0:T(8,128)S(1)}, f32[32,5248]{1,0:T(8,128)}, u32[]{:S(2)}) copy-start(f32[32,5248]{1,0:T(8,128)} %get-tuple-element.113) | copy-start | bytes 2015236

commit v4 on v3

v4 whole, which is shorter than its diff:
```python
from functools import partial

import jax
import jax.numpy as jnp
import numpy as np
from jax import lax
from jax.experimental import pallas as pl
from jax.experimental.pallas import tpu as pltpu
from jax.sharding import PartitionSpec as P

HEAD_DIM = 64


norm_eps = 1e-05
rope_base = 160000.0
neg_large = -1e30


def from_behind(value, axis, by):
    devices = lax.axis_size(axis)
    return lax.ppermute(value, axis, [(i, (i + by) % devices) for i in range(devices)])


def layer_norm(values, gain):
    center = values - jnp.mean(values, axis=-1, keepdims=True)
    spread = jnp.mean(center * center, axis=-1, keepdims=True)
    return center * lax.rsqrt(spread + norm_eps) * gain


def rope_tables(places, head_size):
    half = head_size // 2
    freqs = rope_base ** (-(jnp.arange(half, dtype=jnp.float32) * 2.0) / head_size)
    angles = places.astype(jnp.float32)[:, None] * freqs[None, :]
    angles = jnp.concatenate([angles, angles], axis=1)
    return (jnp.cos(angles), jnp.sin(angles))


def rotate(values, cosine, sine):
    count = values.shape[0]
    head_size = cosine.shape[1]
    half = head_size // 2
    split = values.reshape(count, -1, head_size)
    turned = jnp.concatenate([-split[..., half:], split[..., :half]], axis=-1)
    return (split * cosine[:, None, :] + turned * sine[:, None, :]).reshape(count, -1)


def rotate_pair(query, keys, cosine, sine):
    return (rotate(query, cosine, sine), rotate(keys, cosine, sine))


def doc_numbers(places, ends, lengths):
    passed = places[:, None] >= ends[None, :]
    numbers = jnp.sum(passed.astype(jnp.int32), axis=1)
    offset = jnp.sum(jnp.where(passed, lengths[None, :], 0), axis=1)
    return (numbers, places - offset)


def gelu_gate(lifted):
    half = lifted.shape[1] // 2
    return jax.nn.gelu(lifted[:, :half], approximate=False) * lifted[:, half:]


def tile_scores(query, keys):
    heads = query.shape[1] // HEAD_DIM
    query_split = query.reshape(query.shape[0], heads, HEAD_DIM)
    key_split = keys.reshape(keys.shape[0], heads, HEAD_DIM)
    return jnp.einsum(
        "qhd,khd->hqk", query_split, key_split, preferred_element_type=jnp.float32
    ) * HEAD_DIM ** (-0.5)


def unchanged(state):
    return state


def forward_tile(state, query, keys, values, mask):
    top, total, running = state
    count = query.shape[0]
    heads = top.shape[0]
    scores = tile_scores(query, keys)
    filled = jnp.where(mask[None], scores, neg_large)
    new_top = jnp.maximum(top, jnp.max(filled, axis=-1))
    weights = jnp.where(mask[None], jnp.exp(scores - new_top[:, :, None]), 0.0)
    factor = jnp.exp(top - new_top)
    new_total = total * factor + jnp.sum(weights, axis=-1)
    mixed = jnp.einsum(
        "hqk,khd->qhd",
        weights.astype(jnp.bfloat16),
        values.reshape(-1, heads, HEAD_DIM),
        preferred_element_type=jnp.float32,
    )
    new_running = running.reshape(count, heads, HEAD_DIM) * factor.T[:, :, None] + mixed
    return (new_top, new_total, new_running.reshape(count, heads * HEAD_DIM))


def backward_tile(carry, query, keys, values, mask, norm_log, grad_out, delta):
    query_grad, run_grads = carry
    count = query.shape[0]
    columns = keys.shape[0]
    heads = norm_log.shape[0]
    scores = tile_scores(query, keys)
    probs = jnp.where(mask[None], jnp.exp(scores - norm_log[:, :, None]), 0.0)
    grad_split = grad_out.reshape(count, heads, HEAD_DIM)
    value_split = values.reshape(columns, heads, HEAD_DIM)
    grad_values = jnp.einsum(
        "hqk,qhd->khd", probs.astype(jnp.bfloat16), grad_split, preferred_element_type=jnp.float32
    )
    grad_probs = jnp.einsum(
        "qhd,khd->hqk", grad_split, value_split, preferred_element_type=jnp.float32
    )
    grad_scores = (probs * (grad_probs - delta[:, :, None])).astype(jnp.bfloat16)
    grad_query = jnp.einsum(
        "hqk,khd->qhd",
        grad_scores,
        keys.reshape(columns, heads, HEAD_DIM),
        preferred_element_type=jnp.float32,
    ) * HEAD_DIM ** (-0.5)
    grad_keys = jnp.einsum(
        "hqk,qhd->khd",
        grad_scores,
        query.reshape(count, heads, HEAD_DIM),
        preferred_element_type=jnp.float32,
    ) * HEAD_DIM ** (-0.5)
    added = jnp.stack([grad_keys.reshape(columns, -1), grad_values.reshape(columns, -1)])
    return (query_grad + grad_query.reshape(count, -1), run_grads + added)


def per_device_general(
    tokens, attn_gain, w_qkv, w_attn_out, mlp_gain, w_in, w_mlp_out, doc_lengths, cotangent
):
    own_rows = tokens.shape[0]
    width = tokens.shape[1]
    head_count = lax.axis_size("head")
    cycle_count = lax.axis_size("blk")
    head_place = lax.axis_index("head")
    cycle_place = lax.axis_index("blk")
    group_rows = head_count * own_rows
    block_runs = min(head_count, max(1, 512 // own_rows))
    block_count = head_count // block_runs
    block_rows = block_runs * own_rows
    doc_ends = jnp.cumsum(doc_lengths)
    counter = jnp.arange(own_rows, dtype=jnp.int32)
    own_places = (head_place * cycle_count + cycle_place) * own_rows + counter
    unused_docs, own_positions = doc_numbers(own_places, doc_ends, doc_lengths)
    cosine, sine = rope_tables(own_positions, HEAD_DIM)
    run_numbers = jnp.arange(head_count, dtype=jnp.int32)
    query_places = (
        (run_numbers[:, None] * cycle_count + cycle_place) * own_rows + counter[None, :]
    ).reshape(group_rows)
    query_docs, unused_positions = doc_numbers(query_places, doc_ends, doc_lengths)
    params = (
        lax.all_gather(attn_gain, ("head", "blk"), axis=0, tiled=True),
        lax.all_gather(w_qkv, ("head", "blk"), axis=0, tiled=True),
        lax.all_gather(w_attn_out, ("head", "blk"), axis=0, tiled=True),
        lax.all_gather(mlp_gain, ("head", "blk"), axis=0, tiled=True),
        lax.all_gather(w_in, ("head", "blk"), axis=0, tiled=True),
        lax.all_gather(w_mlp_out, ("head", "blk"), axis=1, tiled=True),
    )
    gain_one, full_qkv, full_attn_out, gain_two, full_in, full_mlp_out = params
    inputs = tokens.astype(jnp.float32)
    normed_one, norm_one_pull = jax.vjp(layer_norm, inputs, gain_one.astype(jnp.float32))
    normed_low = normed_one.astype(jnp.bfloat16)
    projected = jnp.dot(normed_low, full_qkv, preferred_element_type=jnp.float32)
    turned, rope_pull = jax.vjp(
        partial(rotate_pair, cosine=cosine, sine=sine),
        projected[:, :width],
        projected[:, width : 2 * width],
    )
    stacked = jnp.stack(
        [
            turned[0].astype(jnp.bfloat16),
            turned[1].astype(jnp.bfloat16),
            projected[:, 2 * width :].astype(jnp.bfloat16),
        ]
    )
    regrouped = lax.all_to_all(stacked, "head", split_axis=2, concat_axis=1, tiled=True)
    query_heads = regrouped[0]
    key_heads = regrouped[1]
    value_heads = regrouped[2]
    head_width = query_heads.shape[1]
    heads_here = head_width // HEAD_DIM

    def key_docs_at(first):
        places = (
            first % group_rows // own_rows * cycle_count + first // group_rows
        ) * own_rows + counter
        found, unused = doc_numbers(places, doc_ends, doc_lengths)
        return found

    def block_live(block, key_docs):
        block_docs = query_docs[block * block_rows : (block + 1) * block_rows]
        live = jnp.maximum(jnp.min(block_docs), jnp.min(key_docs)) <= jnp.minimum(
            jnp.max(block_docs), jnp.max(key_docs)
        )
        return (block_docs[:, None] == key_docs[None, :], live)

    def fold_forward(state, piece):
        key_part, value_part = piece

        def fold_one_run(number, carried):
            first = number * own_rows
            key_docs = key_docs_at(first)
            keys = lax.dynamic_slice_in_dim(key_part, number * own_rows, own_rows, 0)
            values = lax.dynamic_slice_in_dim(value_part, number * own_rows, own_rows, 0)
            updated = []
            for block in range(block_count):
                mask, live = block_live(block, key_docs)
                query = query_heads[block * block_rows : (block + 1) * block_rows]
                advance = partial(forward_tile, query=query, keys=keys, values=values, mask=mask)
                updated.append(lax.cond(live, advance, unchanged, carried[block]))
            return tuple(updated)

        return lax.fori_loop(0, key_part.shape[0] // own_rows, fold_one_run, state)

    def fresh_state():
        return tuple(
            (
                (
                    jnp.full((heads_here, block_rows), neg_large, jnp.float32),
                    jnp.zeros((heads_here, block_rows), jnp.float32),
                    jnp.zeros((block_rows, head_width), jnp.float32),
                )
                for block in range(block_count)
            )
        )

    def finish(state):
        outputs = []
        logs = []
        for top, total, running in state:
            scaled = running.reshape(block_rows, heads_here, HEAD_DIM) / total.T[:, :, None]
            outputs.append(scaled.reshape(block_rows, head_width))
            logs.append(top + jnp.log(total))
        return (
            jnp.concatenate(outputs, axis=0).astype(jnp.bfloat16),
            jnp.concatenate(logs, axis=1),
        )

    state = fold_forward(
        fresh_state(),
        (
            lax.all_gather(key_heads, "blk", axis=0, tiled=True),
            lax.all_gather(value_heads, "blk", axis=0, tiled=True),
        ),
    )
    out_heads, norm_log = finish(state)
    out_tokens = lax.all_to_all(out_heads, "head", split_axis=0, concat_axis=1, tiled=True)
    middle = inputs + jnp.dot(out_tokens, full_attn_out, preferred_element_type=jnp.float32)
    normed_two, norm_two_pull = jax.vjp(layer_norm, middle, gain_two.astype(jnp.float32))
    normed_two_low = normed_two.astype(jnp.bfloat16)
    lifted = jnp.dot(normed_two_low, full_in, preferred_element_type=jnp.float32)
    activated, geglu_pull = jax.vjp(gelu_gate, lifted)
    activated_low = activated.astype(jnp.bfloat16)
    output = (
        middle + jnp.dot(activated_low, full_mlp_out, preferred_element_type=jnp.float32)
    ).astype(jnp.bfloat16)
    params = (
        lax.all_gather(attn_gain, ("head", "blk"), axis=0, tiled=True),
        lax.all_gather(w_qkv, ("head", "blk"), axis=0, tiled=True),
        lax.all_gather(w_attn_out, ("head", "blk"), axis=0, tiled=True),
        lax.all_gather(mlp_gain, ("head", "blk"), axis=0, tiled=True),
        lax.all_gather(w_in, ("head", "blk"), axis=0, tiled=True),
        lax.all_gather(w_mlp_out, ("head", "blk"), axis=1, tiled=True),
    )
    gain_one, full_qkv, full_attn_out, gain_two, full_in, full_mlp_out = params
    grad_act = jnp.einsum("td,fd->tf", cotangent, full_mlp_out, preferred_element_type=jnp.float32)
    grad_lifted = geglu_pull(grad_act)[0].astype(jnp.bfloat16)
    grad_normed_two = jnp.einsum(
        "tf,df->td", grad_lifted, full_in, preferred_element_type=jnp.float32
    )
    grad_middle_part, grad_gain_two = norm_two_pull(grad_normed_two)
    grad_middle = cotangent.astype(jnp.float32) + grad_middle_part
    grad_branch = grad_middle.astype(jnp.bfloat16)
    grad_mixed = jnp.einsum(
        "te,de->td", grad_branch, full_attn_out, preferred_element_type=jnp.float32
    ).astype(jnp.bfloat16)
    grad_heads = lax.all_to_all(grad_mixed, "head", split_axis=1, concat_axis=0, tiled=True)
    state = fold_forward(
        fresh_state(),
        (
            lax.all_gather(key_heads, "blk", axis=0, tiled=True),
            lax.all_gather(value_heads, "blk", axis=0, tiled=True),
        ),
    )
    out_heads, norm_log = finish(state)
    delta = jnp.einsum(
        "qhd,qhd->hq",
        grad_heads.reshape(group_rows, heads_here, HEAD_DIM).astype(jnp.float32),
        out_heads.reshape(group_rows, heads_here, HEAD_DIM).astype(jnp.float32),
    )

    def piece_backward(query_grads, key_part, value_part, start):
        piece_rows = key_part.shape[0]

        def piece_one_run(number, carried):
            query_now, piece_grads = carried
            first = start + number * own_rows
            key_docs = key_docs_at(first)
            keys = lax.dynamic_slice_in_dim(key_part, number * own_rows, own_rows, 0)
            values = lax.dynamic_slice_in_dim(value_part, number * own_rows, own_rows, 0)
            run_grads = jnp.zeros((2, own_rows, head_width), jnp.float32)
            updated = []
            for block in range(block_count):
                mask, live = block_live(block, key_docs)
                lower = block * block_rows
                upper = (block + 1) * block_rows
                advance = partial(
                    backward_tile,
                    query=query_heads[lower:upper],
                    keys=keys,
                    values=values,
                    mask=mask,
                    norm_log=norm_log[:, lower:upper],
                    grad_out=grad_heads[lower:upper],
                    delta=delta[:, lower:upper],
                )
                new_query, run_grads = lax.cond(
                    live, advance, unchanged, (query_now[block], run_grads)
                )
                updated.append(new_query)
            piece_grads = lax.dynamic_update_slice_in_dim(
                piece_grads, run_grads, number * own_rows, 1
            )
            return (tuple(updated), piece_grads)

        return lax.fori_loop(
            0,
            piece_rows // own_rows,
            piece_one_run,
            (query_grads, jnp.zeros((2, piece_rows, head_width), jnp.float32)),
        )

    start_query = tuple(
        (jnp.zeros((block_rows, head_width), jnp.float32) for block in range(block_count))
    )

    def cycle_step(step, carried):
        query_now, blocks, travelling = carried
        owner = (cycle_place - step) % cycle_count
        query_now, piece_grads = piece_backward(query_now, blocks[0], blocks[1], owner * group_rows)
        travelling = travelling + piece_grads
        blocks = from_behind(blocks, "blk", 1)
        travelling = from_behind(travelling.astype(jnp.bfloat16), "blk", 1).astype(travelling.dtype)
        return (query_now, blocks, travelling)

    start_cycle = (
        start_query,
        jnp.stack([key_heads, value_heads]),
        jnp.zeros((2, group_rows, head_width), jnp.float32),
    )
    query_grads, unused_blocks, own_grads = lax.fori_loop(0, cycle_count, cycle_step, start_cycle)
    grad_stack = jnp.stack(
        [
            jnp.concatenate(query_grads, axis=0).astype(jnp.bfloat16),
            own_grads[0].astype(jnp.bfloat16),
            own_grads[1].astype(jnp.bfloat16),
        ]
    )
    back_tokens = lax.all_to_all(grad_stack, "head", split_axis=1, concat_axis=2, tiled=True)
    grad_query, grad_keys = rope_pull(
        (back_tokens[0].astype(jnp.float32), back_tokens[1].astype(jnp.float32))
    )
    grad_projected = jnp.concatenate(
        [grad_query, grad_keys, back_tokens[2].astype(jnp.float32)], axis=1
    ).astype(jnp.bfloat16)
    grad_normed_one = jnp.einsum(
        "te,de->td", grad_projected, full_qkv, preferred_element_type=jnp.float32
    )
    grad_input_part, grad_gain_one = norm_one_pull(grad_normed_one)
    input_grad = grad_middle + grad_input_part

    def columns(source):
        return source

    term_qkv = jnp.einsum(
        "td,te->de", columns(normed_low), grad_projected, preferred_element_type=jnp.float32
    )
    term_out = jnp.einsum(
        "td,te->de", columns(out_tokens), grad_branch, preferred_element_type=jnp.float32
    )
    term_in = jnp.einsum(
        "td,tf->df", columns(normed_two_low), grad_lifted, preferred_element_type=jnp.float32
    )
    term_down = jnp.einsum(
        "td,tf->df", columns(cotangent), activated_low, preferred_element_type=jnp.float32
    )
    sums = lax.psum_scatter(
        jnp.concatenate([term_qkv, term_out, term_in, term_down], axis=1),
        ("head", "blk"),
        scatter_dimension=0,
        tiled=True,
    )
    ff_width = full_mlp_out.shape[0]
    qkv_grad = sums[:, : 3 * width]
    attn_out_grad = sums[:, 3 * width : 4 * width]
    in_grad = sums[:, 4 * width : 4 * width + 2 * ff_width]
    down_grad = sums[:, 4 * width + 2 * ff_width :].T
    gain_sums = lax.psum_scatter(
        jnp.stack([grad_gain_one, grad_gain_two]), ("head", "blk"), scatter_dimension=1, tiled=True
    )
    return (
        output,
        input_grad,
        gain_sums[0],
        qkv_grad,
        attn_out_grad,
        gain_sums[1],
        in_grad,
        down_grad,
    )


VMEM = 62 * 2**20
MESH = pl.DeviceIdType.MESH
KEY_STEP = 512
KEY_ALIGN = 256
NN = (((1,), (0,)), ((), ()))
NT = (((1,), (1,)), ((), ()))
TN = (((0,), (0,)), ((), ()))


def mm(left, right, dims=NN):
    return lax.dot_general(left, right, dims, preferred_element_type=jnp.float32)


def params(collective_id=None):
    if collective_id is None:
        return pltpu.CompilerParams(vmem_limit_bytes=VMEM)
    return pltpu.CompilerParams(
        collective_id=collective_id, has_side_effects=True, vmem_limit_bytes=VMEM
    )


def in_vmem():
    return pl.BlockSpec(memory_space=pltpu.VMEM)


def anywhere():
    return pl.BlockSpec(memory_space=pl.ANY)


def in_smem():
    return pl.BlockSpec(memory_space=pltpu.SMEM)


def dma(*counts):
    return pltpu.SemaphoreType.DMA(counts)


def halves(packed, side):
    wide = packed.astype(jnp.float32)
    if side:
        wide = pltpu.roll(wide, HEAD_DIM, 1)
    lane = lax.broadcasted_iota(jnp.int32, wide.shape, 1)
    return jnp.where(lane < HEAD_DIM, wide, 0.0)


def tile_span(lengths, side, R, T):
    hh, u = pl.program_id(0), pl.program_id(1)
    runs, parts = 2 * pl.num_programs(0), 2 * pl.num_programs(1)
    share = lax.rem(lax.axis_index("blk"), 2)
    first = (((hh + side * (runs // 2)) * parts + 2 * u) * 2 + share) * R
    last = first + 3 * R - 1
    lane = lax.broadcasted_iota(jnp.int32, (1, 2 * R), 1)
    place = first + lane + jnp.where(lane < R, 0, R)

    def one(d, carried):
        low, begin, stop, start, end = carried
        high = low + lengths[d]
        inside = (place >= low) & (place < high)
        return (
            high,
            jnp.where(inside, low, begin),
            jnp.where(inside, high, stop),
            jnp.where((first >= low) & (first < high), low, start),
            jnp.where((last >= low) & (last < high), high, end),
        )

    zero = jnp.int32(0)
    unused, begin, stop, start, end = lax.fori_loop(
        0,
        lengths.shape[0],
        one,
        (zero, jnp.zeros_like(place), jnp.zeros_like(place), zero, zero),
        unroll=True,
    )
    start = start // KEY_ALIGN
    steps = (end - start * KEY_ALIGN + KEY_STEP - 1) // KEY_STEP
    start = jnp.minimum(start, T // KEY_ALIGN - steps * (KEY_STEP // KEY_ALIGN))
    return (begin, stop, start, steps)


def attend_kernel(lengths, qp, kv, op, lse, s_scr):
    pairs = qp.shape[0] * qp.shape[2]
    T = kv.shape[0]
    half_runs = pl.num_programs(0)
    hh, u = pl.program_id(0), pl.program_id(1)
    at = lax.broadcasted_iota(jnp.int32, (KEY_STEP, pairs), 0)
    results = []
    for side in (0, 1):
        tile = (hh + side * half_runs) * pl.num_programs(1) + u
        begin, stop, start, steps = tile_span(lengths, side, pairs // 2, T)
        query = (halves(qp[...].reshape(pairs, 2 * HEAD_DIM), side) * HEAD_DIM**-0.5).astype(
            jnp.bfloat16
        )

        def keys_at(n):
            first = pl.multiple_of(start * KEY_ALIGN + n * KEY_STEP, KEY_ALIGN)
            return (first, kv[pl.ds(first, KEY_STEP), :])

        def score(n, top):
            first, keys = keys_at(n)
            same = (at >= begin - first) & (at < stop - first)
            scores = jnp.where(same, mm(keys, query, NT), neg_large)
            s_scr[n] = scores
            return jnp.maximum(top, jnp.max(scores, axis=0, keepdims=True))

        top = lax.fori_loop(0, steps, score, jnp.full((1, pairs), neg_large, jnp.float32))

        def mix(n, carried):
            total, acc = carried
            unused, keys = keys_at(n)
            weights = jnp.exp(s_scr[n] - top)
            total = total + jnp.sum(weights, axis=0, keepdims=True)
            return (total, acc + mm(keys, weights.astype(jnp.bfloat16), TN))

        total, acc = lax.fori_loop(
            0,
            steps,
            mix,
            (jnp.zeros((1, pairs), jnp.float32), jnp.zeros((2 * HEAD_DIM, pairs), jnp.float32)),
        )
        lse[tile] = top + jnp.log(total)
        results.append(acc[HEAD_DIM:] / total)
    both = jnp.concatenate(results, axis=0).T
    op[...] = both.astype(jnp.bfloat16).reshape(op.shape)


def attend(lengths, qp, kv):
    parts, half_runs, rows, lanes = qp.shape
    tiles = half_runs * parts
    piece = pl.BlockSpec((2, 1, rows, lanes), lambda i, j, s: (j, i, 0, 0))
    return pl.pallas_call(
        attend_kernel,
        grid_spec=pltpu.PrefetchScalarGridSpec(
            num_scalar_prefetch=1,
            grid=(half_runs, parts // 2),
            in_specs=[piece, in_vmem()],
            out_specs=[piece, in_vmem()],
            scratch_shapes=[pltpu.VMEM((kv.shape[0] // KEY_STEP, KEY_STEP, 2 * rows), jnp.float32)],
        ),
        out_shape=[
            jax.ShapeDtypeStruct(qp.shape, jnp.bfloat16),
            jax.ShapeDtypeStruct((tiles, 1, 2 * rows), jnp.float32),
        ],
        compiler_params=params(),
        cost_estimate=pl.CostEstimate(
            flops=10**9, bytes_accessed=50 * 10**6, transcendentals=10**6
        ),
        name="attend",
    )(lengths, qp, kv)


def attend_back_kernel(
    lengths, qp, gp, op, lse, kv, output, down, dqp, dkv, output_to, down_to, acc_scr
):
    pairs = qp.shape[0] * qp.shape[2]
    T = kv.shape[0]
    half_runs = pl.num_programs(0)
    hh, u = pl.program_id(0), pl.program_id(1)
    begins = (hh == 0) & (u == 0)
    ends = (hh == half_runs - 1) & (u == pl.num_programs(1) - 1)
    @pl.when(begins)
    def _():
        output_to[...] = output[...]
        down_to[...] = down[...]
        acc_scr[...] = jnp.zeros_like(acc_scr)

    at = lax.broadcasted_iota(jnp.int32, (KEY_STEP, pairs), 0)
    lane = lax.broadcasted_iota(jnp.int32, (pairs, 2 * HEAD_DIM), 1)
    flat = (pairs, 2 * HEAD_DIM)
    results = []
    for side in (0, 1):
        tile = (hh + side * half_runs) * pl.num_programs(1) + u
        begin, stop, start, steps = tile_span(lengths, side, pairs // 2, T)
        query = (halves(qp[...].reshape(flat), side) * HEAD_DIM**-0.5).astype(jnp.bfloat16)
        pieces = []
        for n in range(2):
            piece = gp[n, hh + side * half_runs].astype(jnp.float32)
            pieces += [pltpu.roll(piece, HEAD_DIM, 1), piece]
        grad = jnp.where(lane < HEAD_DIM, 0.0, jnp.concatenate(pieces, axis=0))
        mixed = op[...].reshape(flat).astype(jnp.float32)
        if not side:
            mixed = pltpu.roll(mixed, HEAD_DIM, 1)
        delta = jnp.sum((grad * mixed).T, axis=0, keepdims=True)
        both = jnp.concatenate([query, grad.astype(jnp.bfloat16)], axis=0)
        logs = lse[tile]

        def step(n, dq):
            first = pl.multiple_of(start * KEY_ALIGN + n * KEY_STEP, KEY_ALIGN)
            rows = pl.ds(first, KEY_STEP)
            keys = kv[rows, :]
            same = (at >= begin - first) & (at < stop - first)
            products = mm(keys, both, NT)
            probs = jnp.where(same, jnp.exp(products[:, :pairs] - logs), 0.0)
            grad_scores = (probs * (products[:, pairs:] - delta)).astype(jnp.bfloat16)
            left = jnp.concatenate([grad_scores, probs.astype(jnp.bfloat16)], axis=1)
            acc_scr[rows, :] += mm(left, both)
            return dq + mm(keys, grad_scores, TN)

        dq = lax.fori_loop(0, steps, step, jnp.zeros((2 * HEAD_DIM, pairs), jnp.float32))
        results.append(dq[:HEAD_DIM] * HEAD_DIM**-0.5)
    dqp[...] = jnp.concatenate(results, axis=0).T.astype(jnp.bfloat16).reshape(dqp.shape)

    @pl.when(ends)
    def _():
        dkv[...] = acc_scr[...].astype(dkv.dtype)


def attend_back(lengths, qp, gp, op, lse, kv, output, down):
    parts, half_runs, rows, lanes = qp.shape
    piece = pl.BlockSpec((2, 1, rows, lanes), lambda i, j, s: (j, i, 0, 0))
    grads = pl.BlockSpec((2, 2 * half_runs, rows // 2, lanes), lambda i, j, s: (j, 0, 0, 0))
    return pl.pallas_call(
        attend_back_kernel,
        grid_spec=pltpu.PrefetchScalarGridSpec(
            num_scalar_prefetch=1,
            grid=(half_runs, parts // 2),
            in_specs=[piece, grads, piece, *[in_vmem()] * 4],
            out_specs=[piece, *[in_vmem()] * 3],
            scratch_shapes=[pltpu.VMEM(kv.shape, jnp.float32)],
        ),
        out_shape=[
            jax.ShapeDtypeStruct(qp.shape, jnp.bfloat16),
            jax.ShapeDtypeStruct(kv.shape, jnp.bfloat16),
            jax.ShapeDtypeStruct(output.shape, output.dtype),
            jax.ShapeDtypeStruct(down.shape, down.dtype),
        ],
        compiler_params=params(),
        cost_estimate=pl.CostEstimate(
            flops=3 * 10**9, bytes_accessed=60 * 10**6, transcendentals=10**6
        ),
        name="attend_back",
    )(lengths, qp, gp, op, lse, kv, output, down)


def deliver_kernel(*refs):
    count = len(refs) // 2
    for source, target in zip(refs[:count], refs[count:]):
        target[...] = source[...]


def deliver(*arrays):
    return pl.pallas_call(
        deliver_kernel,
        in_specs=[in_vmem()] * len(arrays),
        out_specs=[in_vmem()] * len(arrays),
        out_shape=[jax.ShapeDtypeStruct(a.shape, a.dtype) for a in arrays],
        compiler_params=params(),
        name="deliver",
    )(*arrays)


def meet(peers):
    barrier = pltpu.get_barrier_semaphore()
    for peer in peers:
        pl.semaphore_signal(barrier, inc=1, device_id=peer, device_id_type=MESH)
    pl.semaphore_wait(barrier, len(peers))


def remote(source, target, send_sem, recv_sem, peer):
    return pltpu.make_async_remote_copy(
        src_ref=source,
        dst_ref=target,
        send_sem=send_sem,
        recv_sem=recv_sem,
        device_id=peer,
        device_id_type=MESH,
    )


def send(source, target, send_sem, recv_sem, peer):
    copy = remote(source, target, send_sem, recv_sem, peer)
    copy.start()
    return copy


class Place:
    def __init__(self, parts):
        h, b = lax.axis_index("head"), lax.axis_index("blk")
        self.h, self.b, self.parts = h, b, parts
        self.part, self.share = b // 2, lax.rem(b, 2)
        x, y = lax.rem(h, 2), h // 2
        self.places = [(1 - y) * 2 + 1 - x, y * 2 + 1 - x, (1 - y) * 2 + x]
        self.across = [(place, b) for place in self.places]
        self.there = [lax.rem(self.part + i, parts) for i in range(1, parts)]
        self.back = [lax.rem(self.part + parts - i, parts) for i in range(1, parts)]
        self.along = [(h, part * 2 + self.share) for part in self.there]
        self.beside = (h, self.part * 2 + 1 - self.share)
        self.askew = [(h, part * 2 + 1 - self.share) for part in self.there]


class LineGather:
    def __init__(self, view, own, here, sems):
        self.view, self.own, self.here, self.parts = view, own, here, here.parts
        self.right_s, self.left_s, self.line_r, self.core_s, self.core_r = sems
        self.first = 0

    def _copy(self, source, block, side):
        here = self.here
        if side == 0:
            sems, peer = (self.core_s, self.core_r), here.beside
        else:
            sems = (self.right_s if side > 0 else self.left_s, self.line_r)
            peer = (here.h, (here.part + side) * 2 + here.share)
        return remote(
            source, self.view(block, here.share), sems[0].at[block], sems[1].at[block], peer
        )

    def _can(self, side):
        return self.here.part < self.parts - 1 if side > 0 else self.here.part > 0

    def start(self):
        for side in (1, -1):

            @pl.when(self._can(side))
            def _():
                self._copy(self.own, self.here.part, side).start()

        self._copy(self.own, self.here.part, 0).start()

    def start_from(self, near):
        self.first = 1
        for side in (1, -1):
            block = self.here.part - side

            @pl.when((block >= 0) & (block < self.parts) & self._can(side))
            def _():
                self._copy(near[side], block, side).start()

        self._copy(self.own, self.here.part, 0).start()
        for side in (1, -1):
            block = self.here.part - side

            @pl.when((block >= 0) & (block < self.parts))
            def _():
                self._copy(near[side], block, 0).start()

    def step(self, k):
        for side in (1, -1):
            block = self.here.part - side * k

            @pl.when((block >= 0) & (block < self.parts))
            def _():
                there = self.view(block, self.here.share)
                self._copy(there, block, side).wait_recv()

                @pl.when(self._can(side))
                def _():
                    self._copy(there, block, side).start()

                self._copy(there, block, 0).start()

    def arrive(self):
        for block in range(self.parts):
            self._copy(self.own, block, 0).wait_recv()

    def finish(self):
        for side in (1, -1):
            for block in range(self.parts):
                first = self.here.part - side * self.first
                sent = block <= first if side > 0 else block >= first

                @pl.when(sent & self._can(side))
                def _():
                    self._copy(self.own, block, side).wait_send()

        for block in range(self.parts):
            self._copy(self.own, block, 0).wait_send()


def line_sems(parts):
    return [dma(parts)] * 5


def standardize(values):
    center = values - jnp.mean(values, axis=-1, keepdims=True)
    spread = jnp.mean(center * center, axis=-1, keepdims=True)
    scale = lax.rsqrt(spread + norm_eps)
    return (center * scale, scale)


def norm_back(grad, hat, scale, gain):
    inner = grad * gain
    return scale * (
        inner
        - jnp.mean(inner, axis=-1, keepdims=True)
        - hat * jnp.mean(inner * hat, axis=-1, keepdims=True)
    )


def turn(values, cosine, sine, back=False):
    lane = lax.broadcasted_iota(jnp.int32, values.shape, 1)
    first = lax.rem(lane, HEAD_DIM) < HEAD_DIM // 2
    source = values * sine if back else values
    ahead = pltpu.roll(source, 128 - HEAD_DIM // 2, 1)
    behind = pltpu.roll(source, HEAD_DIM // 2, 1)
    if back:
        return values * cosine + jnp.where(first, ahead, -behind)
    return values * cosine + jnp.where(first, -ahead, behind) * sine


def join(left, left_side, right, right_side):
    lane = lax.broadcasted_iota(jnp.int32, left.shape, 1)
    left = pltpu.roll(left, HEAD_DIM, 1) if left_side else left
    right = right if right_side else pltpu.roll(right, HEAD_DIM, 1)
    return jnp.where(lane < HEAD_DIM, left, right)


def project_kernel(
    H, A, tok, cot, wq, gain_one, gain_two, w_in, w_down, w_out, lengths,
    kv_all, q_all, tok_all, cot_all, wq_all, wm_all, wo_all, gain_rows, cos_all, sin_all,
    wq_src, wq_st, wm_src, kv_send, q_send, q_runs, hats, gain_src, gain_st, gain_tile, gain_all,
    tok_s, tok_r, cot_s, cot_r, wq_s, wq_r, wm_s, wm_r, ga_s, ga_r, gb_s, gb_r, wx_s, wx_r,
    q_s, q_r, kv_s, kv_r, kc_s, kc_r, *line,
):
    f32, bf16 = jnp.float32, jnp.bfloat16
    R, W = tok.shape
    B = 2 * A
    hw = W // H
    D = wq.shape[0]
    F = w_in.shape[1] // 2 // H
    here = Place(A)
    h, b, part, share = here.h, here.b, here.part, here.share
    across, along, beside = here.across, here.along, here.beside

    for place in range(H):
        for j in range(3):
            wq_src[place, :, j * hw : (j + 1) * hw] = wq[:, j * W + place * hw : j * W + (place + 1) * hw]
    row = lax.broadcasted_iota(jnp.int32, (8, 128), 0)
    lane = lax.broadcasted_iota(jnp.int32, (8, 128), 1)
    gain_src[...] = jnp.zeros((8, 128), f32)
    gain_src[0:1, :D] = gain_one[...].astype(f32)
    gain_src[1:2, :D] = gain_two[...].astype(f32)
    gain_src[...] = pltpu.roll(gain_src[...], h * D, 1)
    meet([*across, *along, beside, *here.askew])

    wq_copies = [
        send(wq_src.at[peer[0]], wq_st.at[h], wq_s.at[i], wq_r.at[i], peer)
        for i, peer in enumerate(across)
    ]
    gain_copies = [
        send(gain_src, gain_st.at[i], ga_s.at[i], ga_r.at[i], peer) for i, peer in enumerate(across)
    ]
    wo_line = LineGather(lambda block, side: wo_all.at[h, block, side], w_out, here, line[5:])
    wo_line.start()
    wo_all[h, part, share] = w_out[...]
    wq_st[h] = wq_src[h]
    tok_all[h] = tok[...]
    cot_all[h] = cot[...]
    for place in range(H):
        wm_src[place, :, :F] = w_in[:, place * F : (place + 1) * F]
        wm_src[place, :, F : 2 * F] = w_in[:, (H + place) * F : (H + place + 1) * F]
        wm_src[place, :, 2 * F :] = w_down[:, place * F : (place + 1) * F]
    wm_all[h] = wm_src[h]
    wo_line.step(1)

    for copy in wq_copies:
        copy.wait_recv()
    wq_line = LineGather(lambda block, side: wq_all.at[:, block * 2 + side], wq_st, here, line[:5])
    wq_line.start()
    tok_copies = [
        send(tok, tok_all.at[h], tok_s.at[i], tok_r.at[i], peer) for i, peer in enumerate(across)
    ]
    wq_all[:, b] = wq_st[...]
    tile = gain_src[...]
    for i, copy in enumerate(gain_copies):
        copy.wait_recv()
        tile += gain_st[i]
    gain_tile[...] = tile
    gain_all[b] = tile
    gain_copies += [
        send(gain_tile, gain_all.at[b], gb_s.at[i], gb_r.at[i], peer)
        for i, peer in enumerate([*along, *here.askew, beside])
    ]
    wo_line.step(2)

    wide = lax.broadcasted_iota(jnp.int32, (R, 128), 1)
    freqs = jnp.exp(
        lax.rem(wide, HEAD_DIM // 2).astype(f32) * (-2.0 / HEAD_DIM * float(np.log(rope_base)))
    )
    for run in range(H):
        place = (run * B + b) * R + lax.broadcasted_iota(jnp.int32, (R, 128), 0)

        def one(d, carried, place=place):
            low, begin = carried
            return (low + lengths[d], jnp.where(place >= low, low, begin))

        unused, begin = lax.fori_loop(
            0, lengths.shape[0], one, (jnp.int32(0), jnp.zeros((R, 128), jnp.int32))
        )
        angles = (place - begin).astype(f32) * freqs
        cos_all[run] = jnp.cos(angles)
        sin_all[run] = jnp.sin(angles)

    wq_line.step(1)
    wm_copies = [
        send(wm_src.at[peer[0]], wm_all.at[h], wm_s.at[i], wm_r.at[i], peer)
        for i, peer in enumerate(across)
    ]
    cot_copies = [
        send(cot, cot_all.at[h], cot_s.at[i], cot_r.at[i], peer) for i, peer in enumerate(across)
    ]
    wo_line.step(3)
    for copy in tok_copies:
        copy.wait_recv()

    def norm_run(run, carried):
        hat, unused = standardize(tok_all[run].astype(f32))
        hats[run] = hat
        return carried

    lax.fori_loop(0, H // 2, norm_run, 0)
    wq_line.step(2)
    lax.fori_loop(H // 2, H, norm_run, 0)
    for copy in gain_copies[len(across) :]:
        copy.wait_recv()
    for slab in range(W // 128):
        place, first = slab // (hw // 128), slab % (hw // 128) * (128 // D)
        piece = jnp.zeros((8, 128), f32)
        for j in range(128 // D):
            moved = gain_all[first + j]
            if j != place:
                moved = pltpu.roll(moved, (j - place) * D % 128, 1)
            piece = jnp.where(lane // D == j, moved, piece)
        gain_rows[:, slab * 128 : (slab + 1) * 128] = piece
    wq_line.step(3)
    wo_line.arrive()
    spread_out = wo_all.at[h, :, share]
    wx_copies = [
        send(spread_out, spread_out, wx_s.at[i], wx_r.at[i], peer) for i, peer in enumerate(across)
    ]
    wq_line.arrive()

    q_copies = []
    for run in [run for low in range(H // 2) for run in (low, low + H // 2)]:
        normed = (hats[run] * gain_rows[0:1, :]).astype(bf16)
        projected = jnp.zeros((R, 3 * hw), f32)
        for chunk in range(H):
            block = wq_all[chunk].reshape(B * D, 3 * hw)
            projected += mm(normed[:, chunk * hw : (chunk + 1) * hw], block)
        cosine, sine = cos_all[run], sin_all[run]
        for slab in range(hw // 128):
            at = slab * 128
            q_runs[run, :, at : at + 128] = turn(projected[:, at : at + 128], cosine, sine)
            key = turn(projected[:, hw + at : hw + at + 128], cosine, sine)
            value = projected[:, 2 * hw + at : 2 * hw + at + 128]
            kv_send[2 * slab, run] = join(key, 0, value, 0).astype(bf16)
            kv_send[2 * slab + 1, run] = join(key, 1, value, 1).astype(bf16)
        for i, peer in enumerate(along):
            send(kv_send.at[here.there[i], run], kv_all.at[run, b], kv_s.at[i], kv_r.at[i], peer)
        kv_all[run, b] = kv_send[part, run]
        send(kv_send.at[part, run], kv_all.at[run, b], kc_s.at[0], kc_r.at[0], beside)
        if run >= H // 2:
            low = run - H // 2
            for a in range(A):
                at = a // 2 * 128
                q_send[a, low] = join(
                    q_runs[low, :, at : at + 128], a % 2, q_runs[run, :, at : at + 128], a % 2
                ).astype(bf16)
            for i, peer in enumerate(along):
                send(q_send.at[here.there[i], low], q_all.at[part, low], q_s.at[i], q_r.at[i], peer)
            q_all[part, low] = q_send[part, low]

    kv_copies = [
        remote(kv_send.at[here.there[i]], kv_all.at[:, b], kv_s.at[i], kv_r.at[i], peer)
        for i, peer in enumerate(along)
    ]
    kc_copies = [remote(kv_send.at[part], kv_all.at[:, b], kc_s.at[0], kc_r.at[0], beside)]
    q_copies = [
        remote(q_send.at[here.there[i]], q_all.at[part], q_s.at[i], q_r.at[i], peer)
        for i, peer in enumerate(along)
    ]
    for i, copy in enumerate(wx_copies):
        copy.wait_recv()
        there = wo_all.at[here.places[i], :, share]
        n = H - 1 + i
        kc_copies.append(send(there, there, wx_s.at[n], wx_r.at[n], beside))
    for i, copy in enumerate(kv_copies):
        copy.wait_recv()
        there = kv_all.at[:, here.back[i] * 2 + share]
        kc_copies.append(send(there, there, kc_s.at[i + 1], kc_r.at[i + 1], beside))
    for copy in [*kc_copies, *q_copies, *wm_copies, *cot_copies]:
        copy.wait_recv()
    for copy in [
        *kc_copies, *q_copies, *wm_copies, *cot_copies, *wq_copies, *gain_copies, *tok_copies, *wx_copies, *kv_copies
    ]:
        copy.wait_send()
    wq_line.finish()
    wo_line.finish()


def project(tokens, cotangent, w_qkv, gain_one, gain_two, w_in, w_down, w_out, lengths):
    R, W = tokens.shape
    H, B = lax.axis_size("head"), lax.axis_size("blk")
    A = B // 2
    hw = W // H
    D = w_qkv.shape[0]
    F = w_down.shape[1] // H
    f32, bf16 = jnp.float32, jnp.bfloat16
    shape = jax.ShapeDtypeStruct
    return pl.pallas_call(
        partial(project_kernel, H, A),
        in_specs=[*[in_vmem()] * 8, in_smem()],
        out_specs=[in_vmem()] * 10,
        out_shape=[
            shape((H, B, R, 128), bf16),
            shape((A, H // 2, R, 128), bf16),
            shape((H, R, W), bf16),
            shape((H, R, W), bf16),
            shape((H, B, D, 3 * hw), bf16),
            shape((H, D, 3 * F), bf16),
            shape((H, A, 2, D, W), bf16),
            shape((8, W), f32),
            shape((H, R, 128), f32),
            shape((H, R, 128), f32),
        ],
        scratch_shapes=[
            pltpu.VMEM((H, D, 3 * hw), bf16),
            pltpu.VMEM((H, D, 3 * hw), bf16),
            pltpu.VMEM((H, D, 3 * F), bf16),
            pltpu.VMEM((A, H, R, 128), bf16),
            pltpu.VMEM((A, H // 2, R, 128), bf16),
            pltpu.VMEM((H, R, hw), f32),
            pltpu.VMEM((H, R, W), f32),
            pltpu.VMEM((8, 128), f32),
            pltpu.VMEM((H - 1, 8, 128), f32),
            pltpu.VMEM((8, 128), f32),
            pltpu.VMEM((B, 8, 128), f32),
            *[dma(H - 1)] * 10,
            *[dma(B - 1)] * 2,
            *[dma(2 * H - 2)] * 2,
            *[dma(A - 1)] * 4,
            *[dma(A)] * 2,
            *line_sems(A),
            *line_sems(A),
        ],
        compiler_params=params(0),
        cost_estimate=pl.CostEstimate(flops=10**9, bytes_accessed=10**7, transcendentals=10**6),
        name="project",
    )(tokens, cotangent, w_qkv, gain_one, gain_two, w_in, w_down, w_out, lengths)


class Reduce:
    def __init__(self, term, core_in, line_out, line_in, here, sems):
        self.term, self.core_in, self.line_out, self.line_in = term, core_in, line_out, line_in
        self.here, self.parts = here, here.parts
        self.core_s, self.core_r, self.line_s, self.line_r = sems

    def _core(self):
        return remote(
            self.term.at[:, 1 - self.here.share],
            self.core_in,
            self.core_s.at[0],
            self.core_r.at[0],
            self.here.beside,
        )

    def _line(self, i):
        return remote(
            self.line_out[i],
            self.line_in.at[i],
            self.line_s.at[i],
            self.line_r.at[i],
            self.here.along[i],
        )

    def _sum(self, there):
        own = self.term[there, self.here.share].astype(jnp.float32)
        return own + self.core_in[there].astype(jnp.float32)

    def start(self):
        self._core().start()

    def gather(self):
        self._core().wait_recv()
        for i, there in enumerate(self.here.there):
            self.line_out[i][...] = self._sum(there).astype(jnp.bfloat16)
        return self._sum(self.here.part)

    def middle(self):
        self._core().wait_recv()
        for i, there in enumerate(self.here.there):
            self.line_out[i][...] = self._sum(there).astype(jnp.bfloat16)
            self._line(i).start()

    def close(self):
        total = self._sum(self.here.part)
        for i in range(self.parts - 1):
            self._line(i).wait_recv()
            total += self.line_in[i].astype(jnp.float32)
        return total

    def core_finish(self):
        self._core().wait_send()

    def finish(self):
        self.core_finish()
        for i in range(self.parts - 1):
            self._line(i).wait_send()


def reduce_scratch(parts, shape):
    return [
        pltpu.VMEM((parts, 2, *shape), jnp.bfloat16),
        pltpu.VMEM((parts, *shape), jnp.bfloat16),
        pltpu.VMEM((parts - 1, *shape), jnp.bfloat16),
        pltpu.VMEM((parts - 1, *shape), jnp.bfloat16),
        dma(1),
        dma(1),
        dma(parts - 1),
        dma(parts - 1),
    ]


def reducer(scratch, here):
    term, core_in, line_out, line_in, *sems = scratch
    outs = [line_out.at[i] for i in range(here.parts - 1)]
    return (term, Reduce(term, core_in, outs, line_in, here, sems))


class Swap:
    def __init__(self, out, landed, send_s, recv_s, here):
        self.out, self.landed, self.here = out, landed, here
        self.send_s, self.recv_s = send_s, recv_s

    def start(self, value):
        here = self.here
        self.out[...] = value.astype(jnp.bfloat16)
        self.copies = [
            send(self.out.at[peer[0]], self.landed.at[here.h], self.send_s.at[i], self.recv_s.at[i], peer)
            for i, peer in enumerate(here.across)
        ]
        self.landed[here.h] = self.out[here.h]

    def arrive(self):
        for copy in self.copies:
            copy.wait_recv()

    def finish(self):
        for copy in self.copies:
            copy.wait_send()


def swap_scratch(heads, shape):
    return [
        pltpu.VMEM((heads, *shape), jnp.bfloat16),
        pltpu.VMEM((heads, *shape), jnp.bfloat16),
        dma(heads - 1),
        dma(heads - 1),
    ]


def run_of(here, i):
    x, y = lax.rem(here.h, 2), here.h // 2
    x = x + (1 - i // 2) * (1 - 2 * x)
    y = y + (1 - i % 2) * (1 - 2 * y)
    return y * 2 + x


def load(pairs, sems):
    copies = [pltpu.make_async_copy(*pair, sems.at[i]) for i, pair in enumerate(pairs)]
    for copy in copies:
        copy.start()
    return copies


def feed_kernel(
    H, A, op, tok_in, cot_in, wo_in, wm_own, wm_before, wm_after, gain_rows,
    output, grad_middle, go, in_own, down_grad, mixed_own, gain_part, *rest,
):
    in_out, rest = rest[: A - 1], rest[A - 1 :]
    (
        tok_all, cot_all, wo, mx_in, mixed_all, wm_all, middle, normed, act, lift,
        g2_send, g2_in, g2_own, o_send, o_in, o_own, gm_send, in_term, in_core, in_core_s, in_core_r,
        load_s, mx_s, mx_r, ma_s, ma_r, g2_s, g2_r, o_s, o_r, gm_s, gm_r, *more,
    ) = rest
    f32, bf16 = jnp.float32, jnp.bfloat16
    R, W = tok_all.shape[1:]
    B = 2 * A
    hw = W // H
    D = wm_own.shape[1]
    F = wm_own.shape[2] // 3
    here = Place(A)
    h, b, part, share = here.h, here.b, here.part, here.share
    across, along = here.across, here.along
    line, down_scratch, swap = more[:5], more[5:13], more[13:17]
    down_term, down_sum = reducer(down_scratch, here)
    down_swap = Swap(*swap, here)
    in_sum = Reduce(in_term, in_core, in_out, None, here, [in_core_s, in_core_r, None, None])
    slot = lambda block: wm_all.at[:, block * 2 + share]
    own_loads = load(
        [(wm_own, slot(part)), (tok_in, tok_all), (wo_in, wo), (cot_in, cot_all)], load_s
    )
    near_loads = [
        pltpu.make_async_copy(wm_before, slot(part - 1), load_s.at[4]),
        pltpu.make_async_copy(wm_after, slot(part + 1), load_s.at[5]),
    ]

    @pl.when(part > 0)
    def _():
        near_loads[0].start()

    @pl.when(part < A - 1)
    def _():
        near_loads[1].start()

    others = [
        (run_of(here, i), lax.rem(part + j, A) * 2 + share)
        for i in range(H)
        for j in range(A)
        if i < H - 1 or j
    ]
    meet([*others, here.beside])

    mx_copies = [
        send(op.at[here.there[i]], mx_in.at[part], mx_s.at[i], mx_r.at[i], peer)
        for i, peer in enumerate(along)
    ]
    gather = LineGather(lambda block, side: wm_all.at[:, block * 2 + side], wm_own, here, line)
    gather.start_from({1: wm_before, -1: wm_after})
    mx_in[part] = op[part]
    for copy in own_loads[:3]:
        copy.wait()
    for copy in mx_copies:
        copy.wait_recv()
    for run in range(H):
        side, at = run // (H // 2), run % (H // 2)
        for slab in range(hw // 128):
            left, right = mx_in[2 * slab, at].astype(f32), mx_in[2 * slab + 1, at].astype(f32)
            mixed_own[run, :, slab * 128 : (slab + 1) * 128] = join(left, side, right, side).astype(bf16)
    ma_copies = [
        send(mixed_own, mixed_all.at[h], ma_s.at[i], ma_r.at[i], peer) for i, peer in enumerate(across)
    ]
    mixed_all[h] = mixed_own[...]

    def project_out(source, first):
        def one(run, carried):
            before = tok_all[run].astype(f32) if first else middle[run]
            middle[run] = before + mm(mixed_all[source, run], wo[source])
            return carried

        lax.fori_loop(0, H, one, 0)

    project_out(h, True)
    gather.step(2)
    for i in (1, 2, 0):
        ma_copies[i].wait_recv()
        project_out(here.places[i], False)

    def norm_run(run, carried):
        hat, unused = standardize(middle[run])
        normed[run] = (hat * gain_rows[1:2, :]).astype(bf16)
        return carried

    lax.fori_loop(0, H, norm_run, 0)
    own_loads[3].wait()

    @pl.when(part > 0)
    def _():
        near_loads[0].wait()

    @pl.when(part < A - 1)
    def _():
        near_loads[1].wait()

    gather.step(3)
    gather.arrive()

    def block(chunk):
        return wm_all[chunk].reshape(B * D, 3 * F)

    def part_of(run, i):
        return remote(g2_send.at[i], g2_in.at[i], g2_s.at[i], g2_r.at[i], (run, b))

    def part_out(run, i):
        return remote(o_send.at[i], o_in.at[i], o_s.at[i], o_r.at[i], (run, b))

    def feed_run(i, carried):
        run = run_of(here, i)
        lifted = jnp.zeros((R, 2 * F), f32)
        grad_act = jnp.zeros((R, F), f32)
        for chunk in range(H):
            lanes = slice(chunk * hw, (chunk + 1) * hw)
            weights = block(chunk)
            lifted += mm(normed[run, :, lanes], weights[:, : 2 * F])
            grad_act += mm(cot_all[run, :, lanes], weights[:, 2 * F :])
        gate, up = lifted[:, :F], lifted[:, F:]
        below = 0.5 + 0.5 * lax.erf(gate * (0.5**0.5))
        slope = below + gate * jnp.exp(-0.5 * gate * gate) * ((2.0 * np.pi) ** -0.5)
        act[run] = (gate * below * up).astype(bf16)
        lift[run, :, :F] = (grad_act * up * slope).astype(bf16)
        lift[run, :, F:] = (grad_act * gate * below).astype(bf16)

        for chunk in range(H):
            lanes = slice(chunk * hw, (chunk + 1) * hw)
            g2_own[:, lanes] = mm(lift[run], block(chunk)[:, : 2 * F], NT)

        @pl.when(i < H - 1)
        def _():
            g2_send[i] = g2_own[...].astype(bf16)
            part_of(run, i).start()

        return carried

    lax.fori_loop(0, H, feed_run, 0)

    def down_chunk(chunk, carried):
        lanes = pl.ds(pl.multiple_of(chunk * hw, hw), hw)
        left = cot_all[:, :, lanes].reshape(H * R, hw)
        grads = mm(left, act[...].reshape(H * R, F), TN).astype(bf16)
        down_term[:, :, chunk] = grads.reshape(A, 2, D, F)
        return carried

    lax.fori_loop(0, H, down_chunk, 0)
    down_sum.start()

    def out_run(i, carried):
        run = run_of(here, i)
        for chunk in range(H):
            lanes = slice(chunk * hw, (chunk + 1) * hw)
            o_own[:, lanes] = mm(act[run], block(chunk)[:, 2 * F :], NT)

        @pl.when(i < H - 1)
        def _():
            o_send[i] = o_own[...].astype(bf16)
            part_out(run, i).start()

        return carried

    lax.fori_loop(0, H, out_run, 0)
    down_sum.middle()

    hat, scale = standardize(middle[h])
    grad = g2_own[...]
    for i in (1, 2, 0):
        part_of(here.places[i], i).wait_recv()
        grad += g2_in[i].astype(f32)
    gain_part[...] = jnp.broadcast_to(jnp.sum(grad * hat, axis=0, keepdims=True), gain_part.shape)
    total = cot_all[h].astype(f32) + norm_back(grad, hat, scale, gain_rows[1:2, :])
    grad_middle[...] = total
    branch = total.astype(bf16)
    gm_copies = []
    for i in range(H):
        place = run_of(here, i)
        mixed_grad = mm(branch, wo[place], NT)
        for a in range(A):
            slab = mixed_grad[:, a // 2 * 128 : a // 2 * 128 + 128]
            gm_send[i, a] = join(slab[: R // 2], a % 2, slab[R // 2 :], a % 2).astype(bf16)
        for j in range(A):
            there = lax.rem(part + j, A)
            if i < H - 1 or j:
                n = i * A + j
                gm_copies.append(
                    send(gm_send.at[i, there], go.at[part, h], gm_s.at[n], gm_r.at[n], (place, there * 2 + share))
                )
            else:
                go[part, h] = gm_send[i, part]

    def in_chunk(chunk, carried):
        lanes = pl.ds(pl.multiple_of(chunk * hw, hw), hw)
        left = normed[:, :, lanes].reshape(H * R, hw)
        grads = mm(left, lift[...].reshape(H * R, 2 * F), TN).astype(bf16)
        in_term[:, :, chunk] = grads.reshape(A, 2, D, 2 * F)
        return carried

    lax.fori_loop(0, H, in_chunk, 0)
    in_sum.start()
    down_swap.start(down_sum.close())
    result = middle[h] + o_own[...]
    for i in range(H - 1):
        part_out(here.places[i], i).wait_recv()
        result += o_in[i].astype(f32)
    output[...] = result.astype(bf16)
    in_own[...] = in_sum.gather()
    down_swap.arrive()
    for place in range(H):
        down_grad[:, place * F : (place + 1) * F] = down_swap.landed[place].astype(f32)
    for copy in gm_copies:
        copy.wait_recv()
    for copy in [*mx_copies, *ma_copies, *gm_copies]:
        copy.wait_send()
    for i in range(H - 1):
        part_of(here.places[i], i).wait_send()
        part_out(here.places[i], i).wait_send()
    gather.finish()
    in_sum.core_finish()
    down_sum.finish()
    down_swap.finish()


def feed(op, tok_all, cot_all, wo, wm_own, wm_before, wm_after, gain_rows):
    A, half, R, lanes = op.shape
    H = 2 * half
    W = tok_all.shape[-1]
    B = 2 * A
    hw = W // H
    D = wm_own.shape[1]
    F = wm_own.shape[2] // 3
    f32, bf16 = jnp.float32, jnp.bfloat16
    shape = jax.ShapeDtypeStruct
    return pl.pallas_call(
        partial(feed_kernel, H, A),
        in_specs=[in_vmem(), *[anywhere()] * 6, in_vmem()],
        out_specs=[in_vmem()] * (6 + A),
        out_shape=[
            shape((R, W), bf16),
            shape((R, W), f32),
            shape((A, H, R // 2, 128), bf16),
            shape((H, D, 2 * F), f32),
            shape((D, H * F), f32),
            shape((H, R, hw), bf16),
            shape((8, W), f32),
            *[shape((H, D, 2 * F), bf16)] * (A - 1),
        ],
        scratch_shapes=[
            pltpu.VMEM((H, R, W), bf16),
            pltpu.VMEM((H, R, W), bf16),
            pltpu.VMEM((H, hw, W), bf16),
            pltpu.VMEM((A, half, R, 128), bf16),
            pltpu.VMEM((H, H, R, hw), bf16),
            pltpu.VMEM((H, B, D, 3 * F), bf16),
            pltpu.VMEM((H, R, W), f32),
            pltpu.VMEM((H, R, W), bf16),
            pltpu.VMEM((H, R, F), bf16),
            pltpu.VMEM((H, R, 2 * F), bf16),
            *[pltpu.VMEM((H - 1, R, W), bf16), pltpu.VMEM((H - 1, R, W), bf16), pltpu.VMEM((R, W), f32)] * 2,
            pltpu.VMEM((H, A, R // 2, 128), bf16),
            pltpu.VMEM((A, 2, H, D, 2 * F), bf16),
            pltpu.VMEM((A, H, D, 2 * F), bf16),
            *[dma(1)] * 2,
            dma(6),
            *[dma(A - 1)] * 2,
            *[dma(H - 1)] * 6,
            *[dma(H * A)] * 2,
            *line_sems(A),
            *reduce_scratch(A, (H, D, F)),
            *swap_scratch(H, (D, F)),
        ],
        compiler_params=params(1),
        cost_estimate=pl.CostEstimate(flops=6 * 10**9, bytes_accessed=10**7, transcendentals=10**6),
        name="feed",
    )(op, tok_all, cot_all, wo, wm_own, wm_before, wm_after, gain_rows)


def finish_kernel(
    H, A, dqp, dkv, tok_in, wq_in, cos_in, sin_in, gain_rows, mixed_in, middle_in, gain_part, own_in, near_in, send_in, far_in,
    input_grad, qkv_grad, out_grad, in_grad, gain_one, gain_two,
    dkv_own, tok_all, wq_all, cos_all, sin_all, mixed_own, grad_middle, in_own, in_near, in_far, in_mid,
    dk_in, dkv_send, dkv_in, dq_in, branch, branch_all, gp, normed, g1_send, g1_in, g1_own,
    load_s, in_s, in_r, dk_s, dk_r, dz_s, dz_r, dq_s, dq_r, br_s, br_r, g1_s, g1_r, *rest,
):
    f32, bf16 = jnp.float32, jnp.bfloat16
    R, W = tok_all.shape[1:]
    B = 2 * A
    hw = W // H
    D = own_in.shape[1]
    F = own_in.shape[2] // 2
    here = Place(A)
    h, b, part, share = here.h, here.b, here.part, here.share
    across, along, beside = here.across, here.along, here.beside
    term_out, out_sum = reducer(rest[:8], here)
    term_qkv, qkv_sum = reducer(rest[8:16], here)
    term_gain, gain_sum = reducer(rest[16:24], here)
    in_swap, qkv_swap, gain_swap = (Swap(*rest[24 + 4 * n : 28 + 4 * n], here) for n in range(3))
    loads = load(
        [
            (dkv, dkv_own), (middle_in, grad_middle), (tok_in, tok_all), (mixed_in, mixed_own), (cos_in, cos_all),
            (sin_in, sin_all), (wq_in, wq_all), (own_in, in_own), (near_in, in_near), (far_in, in_far),
        ],
        load_s,
    )
    meet([*across, *along, beside])

    order = [*here.there, part]
    dk_copies = [
        send(dkv.at[:, there * 2 + 1 - share], dk_in.at[i], dk_s.at[i], dk_r.at[i], beside)
        for i, there in enumerate(order)
    ]
    dq_copies = [
        send(dqp.at[here.there[i]], dq_in.at[part], dq_s.at[i], dq_r.at[i], peer)
        for i, peer in enumerate(along)
    ]
    loads[0].wait()
    dz_copies = []
    for i, there in enumerate(order):
        dk_copies[i].wait_recv()
        summed = dkv_own[:, there * 2 + share].astype(f32) + dk_in[i].astype(f32)
        if i < A - 1:
            dkv_send[i] = summed.astype(bf16)
            dz_copies.append(
                send(dkv_send.at[i], dkv_in.at[part], dz_s.at[i], dz_r.at[i], along[i])
            )
        else:
            dkv_in[part] = summed.astype(bf16)
    dq_in[part] = dqp[part]
    loads[1].wait()
    branch[...] = grad_middle[...].astype(bf16)
    br_copies = [
        send(branch, branch_all.at[h], br_s.at[i], br_r.at[i], peer) for i, peer in enumerate(across)
    ]
    branch_all[h] = branch[...]
    for copy in loads[2:]:
        copy.wait()

    def norm_run(run, carried):
        hat, unused = standardize(tok_all[run].astype(f32))
        normed[run] = (hat * gain_rows[0:1, :]).astype(bf16)
        return carried

    lax.fori_loop(0, H, norm_run, 0)
    for copy in br_copies:
        copy.wait_recv()

    def out_tile(n, carried):
        lanes = pl.ds(pl.multiple_of(n * hw, hw), hw)
        grads = mm(mixed_own[...].reshape(H * R, hw), branch_all[:, :, lanes].reshape(H * R, hw), TN)
        term_out[:, :, :, lanes] = grads.astype(bf16).reshape(A, 2, D, hw)
        return carried

    lax.fori_loop(0, W // hw, out_tile, 0)
    out_sum.start()
    for copy in [*dq_copies, *dz_copies]:
        copy.wait_recv()
    in_copy = send(send_in, in_mid, in_s.at[0], in_r.at[0], along[1])
    for run in range(H):
        side, at = run // (H // 2), run % (H // 2)
        cosine, sine = cos_all[run], sin_all[run]
        for slab in range(hw // 128):
            lanes = slab * 128
            left, right = dq_in[2 * slab, at].astype(f32), dq_in[2 * slab + 1, at].astype(f32)
            gp[run, :, lanes : lanes + 128] = turn(
                join(left, side, right, side), cosine, sine, True
            ).astype(bf16)
            left, right = dkv_in[2 * slab, run].astype(f32), dkv_in[2 * slab + 1, run].astype(f32)
            gp[run, :, hw + lanes : hw + lanes + 128] = turn(
                join(left, 0, right, 0), cosine, sine, True
            ).astype(bf16)
            gp[run, :, 2 * hw + lanes : 2 * hw + lanes + 128] = join(left, 1, right, 1).astype(bf16)

    def block(chunk):
        return wq_all[chunk].reshape(B * D, 3 * hw)

    def term_chunk(chunk, carried):
        lanes = pl.ds(pl.multiple_of(chunk * hw, hw), hw)
        left = normed[:, :, lanes].reshape(H * R, hw)
        grads = mm(left, gp[...].reshape(H * R, 3 * hw), TN).astype(bf16)
        term_qkv[:, :, chunk] = grads.reshape(A, 2, D, 3 * hw)
        return carried

    lax.fori_loop(0, H, term_chunk, 0)
    qkv_sum.start()

    def part_of(run, i):
        return remote(g1_send.at[i], g1_in.at[i], g1_s.at[i], g1_r.at[i], (run, b))

    def one_run(i, carried):
        run = run_of(here, i)
        for chunk in range(H):
            lanes = slice(chunk * hw, (chunk + 1) * hw)
            g1_own[:, lanes] = mm(gp[run], block(chunk), NT)

        @pl.when(i < H - 1)
        def _():
            g1_send[i] = g1_own[...].astype(bf16)
            part_of(run, i).start()

        return carried

    lax.fori_loop(0, 1, one_run, 0)
    qkv_sum.middle()
    lax.fori_loop(1, H, one_run, 0)
    out_sum.middle()
    in_copy.wait_recv()
    total = in_own[...]
    for term in (in_near, in_mid, in_far):
        total += term[...].astype(f32)
    in_swap.start(total)

    grad = g1_own[...]
    hat, scale = standardize(tok_all[h].astype(f32))
    for i in (1, 2, 0):
        part_of(here.places[i], i).wait_recv()
        grad += g1_in[i].astype(f32)
    row = lax.broadcasted_iota(jnp.int32, (8, W), 0)
    rows = jnp.where(
        row == 0,
        jnp.sum(grad * hat, axis=0, keepdims=True),
        jnp.where(row == 1, gain_part[...], 0.0),
    )
    pick = (
        lax.broadcasted_iota(jnp.int32, (8, 128), 0) == lax.broadcasted_iota(jnp.int32, (8, 128), 1)
    ).astype(bf16)
    for chunk in range(H):
        gain_columns = mm(rows[:, chunk * hw : (chunk + 1) * hw].astype(bf16), pick, TN)
        term_gain[:, :, chunk] = gain_columns.astype(bf16).reshape(A, 2, D, 128)
    gain_sum.start()
    input_grad[...] = grad_middle[...] + norm_back(grad, hat, scale, gain_rows[0:1, :])
    gain_sum.middle()
    in_swap.arrive()
    for place in range(H):
        in_grad[:, place * F : (place + 1) * F] = in_swap.landed[place, :, :F].astype(f32)
        in_grad[:, (H + place) * F : (H + place + 1) * F] = in_swap.landed[place, :, F:].astype(f32)
    qkv_swap.start(qkv_sum.close())
    gain_swap.start(gain_sum.close())
    out_grad[...] = out_sum.close()
    qkv_swap.arrive()
    for place in range(H):
        for j in range(3):
            qkv_grad[:, j * W + place * hw : j * W + (place + 1) * hw] = qkv_swap.landed[
                place, :, j * hw : (j + 1) * hw
            ].astype(f32)
    gain_swap.arrive()
    total = gain_swap.landed[0].astype(f32)
    for place in range(1, H):
        total += gain_swap.landed[place].astype(f32)
    rows = total.T
    gain_one[...] = rows[0:1, :]
    gain_two[...] = rows[1:2, :]
    for copy in [*dk_copies, *dq_copies, *br_copies, *dz_copies, in_copy]:
        copy.wait_send()
    for i in range(H - 1):
        part_of(here.places[i], i).wait_send()
    for item in (out_sum, qkv_sum, gain_sum, in_swap, qkv_swap, gain_swap):
        item.finish()


def finish(dqp, dkv, tok_all, wq_all, cos_all, sin_all, gain_rows, mixed, grad_middle, gain_part, in_own, *in_terms):
    A, half, R, lanes = dqp.shape
    H = 2 * half
    W = tok_all.shape[-1]
    B = 2 * A
    hw = W // H
    D = in_own.shape[1]
    F = in_own.shape[2] // 2
    f32, bf16 = jnp.float32, jnp.bfloat16
    shape = jax.ShapeDtypeStruct
    buffer = lambda *sizes: pltpu.VMEM(sizes, bf16)
    arrays = [
        dqp, dkv, tok_all, wq_all, cos_all, sin_all, gain_rows, mixed, grad_middle, gain_part, in_own, *in_terms
    ]
    return pl.pallas_call(
        partial(finish_kernel, H, A),
        in_specs=[in_vmem() if n in (0, 6, 9) else anywhere() for n in range(len(arrays))],
        out_specs=[in_vmem()] * 6,
        out_shape=[
            shape((R, W), f32),
            shape((D, 3 * W), f32),
            shape((D, W), f32),
            shape((D, 2 * H * F), f32),
            shape((1, D), f32),
            shape((1, D), f32),
        ],
        scratch_shapes=[
            buffer(*dkv.shape),
            buffer(*tok_all.shape),
            buffer(*wq_all.shape),
            pltpu.VMEM(cos_all.shape, f32),
            pltpu.VMEM(sin_all.shape, f32),
            buffer(*mixed.shape),
            pltpu.VMEM(grad_middle.shape, f32),
            pltpu.VMEM(in_own.shape, f32),
            *[buffer(H, D, 2 * F)] * 3,
            buffer(A, H, R, 128),
            buffer(A - 1, H, R, 128),
            buffer(A, H, R, 128),
            buffer(A, half, R, 128),
            buffer(R, W),
            buffer(H, R, W),
            buffer(H, R, 3 * hw),
            buffer(H, R, W),
            buffer(H - 1, R, W),
            buffer(H - 1, R, W),
            pltpu.VMEM((R, W), f32),
            dma(10),
            *[dma(1)] * 2,
            *[dma(A)] * 2,
            *[dma(A - 1)] * 4,
            *[dma(H - 1)] * 4,
            *reduce_scratch(A, (D, W)),
            *reduce_scratch(A, (H, D, 3 * hw)),
            *reduce_scratch(A, (H, D, 128)),
            *swap_scratch(H, (D, 2 * F)),
            *swap_scratch(H, (D, 3 * hw)),
            *swap_scratch(H, (D, 128)),
        ],
        compiler_params=params(2),
        cost_estimate=pl.CostEstimate(flops=2 * 10**9, bytes_accessed=10**7, transcendentals=10**5),
        name="finish",
    )(*arrays)


def per_device_split(
    tokens, attn_gain, w_qkv, w_attn_out, mlp_gain, w_in, w_mlp_out, doc_lengths, cotangent
):
    R, W = tokens.shape
    H, B = lax.axis_size("head"), lax.axis_size("blk")
    A = B // 2
    hw = W // H
    T = H * B * R
    kv, qp, tok_all, cot_all, wq, wm, wo, gain_rows, cos_all, sin_all = project(
        tokens, cotangent, w_qkv, attn_gain[None], mlp_gain[None], w_in, w_mlp_out.T, w_attn_out, doc_lengths
    )
    kv = kv.reshape(T, 2 * HEAD_DIM)
    wm_before = lax.ppermute(wm, "blk", [(i, i + 2) for i in range(B - 2)])
    wm_after = lax.ppermute(wm, "blk", [(i + 2, i) for i in range(B - 2)])
    op, lse = attend(doc_lengths, qp, kv)
    output, grad_middle, gp, in_own, down_grad, mixed, gain_part, *in_out = feed(
        op, tok_all, cot_all, wo.reshape(H, hw, W), wm, wm_before, wm_after, gain_rows
    )
    shifted = lambda i: lax.ppermute(in_out[i - 1], "blk", [(p, (p + i * 2) % B) for p in range(B)])
    in_near, in_far = shifted(1), shifted(3)
    dqp, dkv, output, down_grad = attend_back(doc_lengths, qp, gp, op, lse, kv, output, down_grad)
    input_grad, qkv_grad, out_grad, in_grad, gain_one, gain_two = deliver(
        *finish(
            dqp, dkv.reshape(H, B, R, 128), tok_all, wq, cos_all, sin_all, gain_rows, mixed, grad_middle, gain_part,
            in_own, in_near, in_out[1], in_far,
        )
    )
    return (
        output,
        input_grad,
        gain_one[0],
        qkv_grad,
        out_grad,
        gain_two[0],
        in_grad,
        down_grad.T,
    )


def per_device(tokens, attn_gain, w_qkv, *rest):
    heads, blocks = lax.axis_size("head"), lax.axis_size("blk")
    fits = (
        heads == 4
        and blocks == 2 * (tokens.shape[1] // HEAD_DIM // heads) == 8
        and w_qkv.shape[0] * heads == 128
        and tokens.shape[0] == 128
    )
    chosen = per_device_split if fits else per_device_general
    return chosen(tokens, attn_gain, w_qkv, *rest)


def solution(mesh):
    placed = (
        P(("head", "blk"), None),
        P(("head", "blk")),
        P(("head", "blk"), None),
        P(("head", "blk"), None),
        P(("head", "blk")),
        P(("head", "blk"), None),
        P(None, ("head", "blk")),
        P(),
        P(("head", "blk"), None),
    )
    return jax.shard_map(
        per_device,
        mesh=mesh,
        in_specs=placed,
        out_specs=(
            P(("head", "blk"), None),
            P(("head", "blk"), None),
            P(("head", "blk")),
            P(("head", "blk"), None),
            P(("head", "blk"), None),
            P(("head", "blk")),
            P(("head", "blk"), None),
            P(None, ("head", "blk")),
        ),
        check_vma=False,
    )
```

time: 284 us -> 241 us (0.85)
  Pallas kernels: 264 us -> 228 us
  local copies, waits for them, and re-layouts: 16 us -> 1.78 us
  starting transfers between devices: 0 us -> 9.74 us
  other arithmetic: 3.42 us -> 0 us
    pallas_call x3 -> x4, Pallas kernels: 227 us -> 197 us  [the longest x1 68.9 us: feed(): pl.pallas_call(partial(feed_kernel, H, A), in_specs=[in_vmem(), *[anywher...]
    unnamed x49 -> x8, local copies, waits for them, and re-layouts: 12.5 us -> 1.78 us
    ppermute x0 -> x4, starting transfers between devices: none -> 9.74 us  [the longest x1 4.58 us: per_device_split(): wm_before = lax.ppermute(wm, 'blk', [(i, i + 2) for i in range(B - 2)])]
    pallas_call x1, Pallas kernels: 20.7 us -> 16.9 us  [attend_back(): pl.pallas_call(attend_back_kernel, grid_spec=pltpu.PrefetchScalarGridSpec...]
  transfers between devices with their start and end apart: 0 -> 4, of which waited for: 0 -> 0; matrix products, arithmetic and copies ran while one was open for 0% -> 0% of each run, Pallas kernels for 0% -> 13%
where the time goes in v4:
time: 241 us; the launch traced here: 240 us
  Pallas kernels  228 us (95%)
  starting transfers between devices  9.74 us (4%)
    pallas_call x1, Pallas kernels, feed(): pl.pallas_call(partial(feed_kernel, H, A), in_specs=[in_vmem(), *[anywher...  68.9 us
    pallas_call x1, Pallas kernels, finish(): pl.pallas_call(partial(finish_kernel, H, A), in_specs=[in_vmem() if n in...  66.5 us
    pallas_call x1, Pallas kernels, project(): pl.pallas_call(partial(project_kernel, H, A), in_specs=[*[in_vmem()] * 8,...  59.4 us
    pallas_call x1, Pallas kernels, attend_back(): pl.pallas_call(attend_back_kernel, grid_spec=pltpu.PrefetchScalarGridSpec...  16.9 us
    pallas_call x1, Pallas kernels, attend(): pl.pallas_call(attend_kernel, grid_spec=pltpu.PrefetchScalarGridSpec(num_...  13.9 us
  transfers between devices with their start and end apart: 4, of which 0 were waited for; matrix products, arithmetic and copies ran while one was open for 0% of the time, Pallas kernels for 13%

profile of v4, /device:TPU:0, one launch (start us, length us, event | category | flops | bytes accessed | tf_op | source)
XLA Modules:
  0.0 240.5 jit_solution(12922528320376444416)
XLA Ops:
  0.6 59.4 %project.1 = (bf16[4,8,128,128]{3,2,1,0:T(8,128)(2,1)}, bf16[4,2,128,128]{3,2,1,0:T(8,128)(2,1)}, bf16[4,128,1024]{2,1,0:T(8,128)(2,1)}, bf16[4,128,1024]{2,1,0:...) custom-call(bf16[128,1024]{1,0:T(8,128)(2,1)} %tok.1, ...), custom_call_target="tpu_custom_call" | custom-call | flops 1000000000 | bytes 10000000 | tf_op jit(solution)/shard_map/project/pallas_call | solution.py:1012
  60.0 1.3 collective-permute-start.1
  61.3 4.6 %collective-permute-start = (bf16[4,32,1968]{2,1,0:T(8,128)(2,1)}, bf16[4,32,1968]{2,1,0:T(8,128)(2,1)S(1)}, u32[]{:S(2)}, u32[]{:S(2)}) collective-permute-start(bf16[4,32,1968]{2,1,0:T(8,128)(2,1)} %get-tuple-element.52.wm_own), channel_id=1, source_target_pairs={{0,2},{1,3},{2,4},{3,5},{4,6},{5,7},{8,10},{9,11},{10,12},{11,13},... | collective-permute-start | bytes 1511432 | tf_op jit(solution)/shard_map/ppermute | solution.py:1715
  65.9 13.9 %attend.1 = (bf16[4,2,128,128]{3,2,1,0:T(8,128)(2,1)}, f32[8,1,256]{2,1,0:T(1,128)}) custom-call(s32[32]{0:T(128)} %lengths.5, bf16[4,2,128,128]{3,2,1,0:T(8,128)(2,1)} %get-tuple-element.46.qp, bf16[4096,128]{1,0:T(8,128)(2,1)} %bitcast.15), custom_call_target="tpu_custom_call" | custom-call | flops 1000000000 | bytes 50000000 | tf_op jit(solution)/shard_map/attend/pallas_call | solution.py:543
  79.8 0.0 collective-permute-done.1.wm_after
  79.8 0.0 copy-start
  79.8 0.0 collective-permute-done.wm_before
  79.8 0.0 copy-start.1
  79.9 0.8 copy-done
  80.6 0.2 copy-done.1
  80.8 68.9 %feed.1 = (bf16[128,1024]{1,0:T(8,128)(2,1)}, f32[128,1024]{1,0:T(8,128)}, bf16[4,4,64,128]{3,2,1,0:T(8,128)(2,1)}, f32[4,32,1312]{2,1,0:T(8,128)}, f32[32,2624]...) custom-call(bf16[4,2,128,128]{3,2,1,0:T(8,128)(2,1)} %get-tuple-elem, ...), custom_call_target="tpu_custom_call" | custom-call | flops 6000000000 | bytes 10000000 | tf_op jit(solution)/shard_map/feed/pallas_call | solution.py:1412
  149.7 0.1 collective-permute-start.2
  149.7 3.8 %collective-permute-start.3 = (bf16[4,32,1312]{2,1,0:T(8,128)(2,1)}, bf16[4,32,1312]{2,1,0:T(8,128)(2,1)S(1)}, u32[]{:S(2)}, u32[]{:S(2)}) collective-permute-start(bf16[4,32,1312]{2,1,0:T(8,128)(2,1)} %get-tuple-element.70), channel_id=1, source_target_pairs={{0,6},{1,7},{2,0},{3,1},{4,2},{5,3},{6,4},{7,5},{8,14},{9,15},{10,... | collective-permute-start | bytes 1007624 | tf_op jit(solution)/shard_map/ppermute | solution.py:1721
  153.6 16.9 %attend_back.1 = (bf16[4,2,128,128]{3,2,1,0:T(8,128)(2,1)}, bf16[4096,128]{1,0:T(8,128)(2,1)}, bf16[128,1024]{1,0:T(8,128)(2,1)}, f32[32,2624]{1,0:T(8,128)}) custom-call(s32[32]{0:T(128)} %lengths.5, bf16[4,2,128,128]{3,2,1,0:T(8,128)(2,1)} %get-tuple-element.46.qp, bf16[4,4,64,128]{3,2,1,0:T(8,128)(2,1)} %get-tuple-element.54.gp, ...), custom_call_target="tpu_custom_call" | custom-call | flops 3000000000 | bytes 60000000 | tf_op jit(solution)/shard_map/attend_back/pallas_call | solution.py:624
  170.5 0.0 collective-permute-done.2.near_in
  170.5 0.0 copy-start.2
  170.5 0.0 collective-permute-done.3.far_in
  170.5 0.0 copy-start.3
  170.5 0.7 copy-done.2
  171.2 0.1 copy-done.3
  171.4 66.5 %finish.1 = (f32[128,1024]{1,0:T(8,128)}, f32[32,3072]{1,0:T(8,128)}, f32[32,1024]{1,0:T(8,128)}, f32[32,5248]{1,0:T(8,128)}, f32[1,32]{1,0:T(1,128)}, /*index=5*/f32[1,32]{1,0:T(1,128)}) custom-call(bf16[4,2,128,128]{3,2,1,0:T(8,128)(2,1)} %get-tuple-element.59.dqp, bf16[4,8,128,128]{3,2,1,0:T(8,128)(2,1)} %bitcast.17, ...), custom_call_target="tpu_custom_call" | custom-call | flops 2000000000 | bytes 10000000 | tf_op jit(solution)/shard_map/finish/pallas_call | solution.py:1652
  237.9 2.6 %deliver.1 = (f32[128,1024]{1,0:T(8,128)}, f32[32,3072]{1,0:T(8,128)}, f32[32,1024]{1,0:T(8,128)}, f32[32,5248]{1,0:T(8,128)}, f32[1,32]{1,0:T(1,128)}, /*index=5*/f32[1,32]{1,0:T(1,128)}) custom-call(f32[128,1024]{1,0:T(8,128)} %get-tuple-element.71.refs_0_, f32[32,3072]{1,0:T(8,128)} %get-tuple-element.72.refs_1_, f32[32,1024]{1,0:T(8,128)} %get-tuple-element.73.refs_2_, ...), custom_call_target="tpu_custom_call" | custom-call | tf_op jit(solution)/shard_map/deliver/pallas_call | solution.py:654
Async XLA Ops:
  60.0 19.8 %collective-permute-start.1 = (bf16[4,32,1968]{2,1,0:T(8,128)(2,1)}, bf16[4,32,1968]{2,1,0:T(8,128)(2,1)S(1)}, u32[]{:S(2)}, u32[]{:S(2)}) collective-permute-start(bf16[4,32,1968]{2,1,0:T(8,128)(2,1)} %get-tuple-element.52.wm_own), channel_id=1, source_target_pairs={{2,0},{3,1},{4,2},{5,3},{6,4},{7,5},{10,8},{11,9},{12,10},{13,11},... | collective-permute-start | bytes 1511432 | tf_op jit(solution)/shard_map/ppermute | solution.py:1716
  61.3 18.5 %collective-permute-start = (bf16[4,32,1968]{2,1,0:T(8,128)(2,1)}, bf16[4,32,1968]{2,1,0:T(8,128)(2,1)S(1)}, u32[]{:S(2)}, u32[]{:S(2)}) collective-permute-start(bf16[4,32,1968]{2,1,0:T(8,128)(2,1)} %get-tuple-element.52.wm_own), channel_id=1, source_target_pairs={{0,2},{1,3},{2,4},{3,5},{4,6},{5,7},{8,10},{9,11},{10,12},{11,13},... | collective-permute-start | bytes 1511432 | tf_op jit(solution)/shard_map/ppermute | solution.py:1715
  79.8 0.8 copy-start
  79.8 1.0 copy-start.1
  149.7 20.8 %collective-permute-start.2 = (bf16[4,32,1312]{2,1,0:T(8,128)(2,1)}, bf16[4,32,1312]{2,1,0:T(8,128)(2,1)S(1)}, u32[]{:S(2)}, u32[]{:S(2)}) collective-permute-start(bf16[4,32,1312]{2,1,0:T(8,128)(2,1)} %get-tuple-element.68), channel_id=1, source_target_pairs={{0,2},{1,3},{2,4},{3,5},{4,6},{5,7},{6,0},{7,1},{8,10},{9,11},{10,... | collective-permute-start | bytes 1007624 | tf_op jit(solution)/shard_map/ppermute | solution.py:1721
  149.7 20.8 %collective-permute-start.3 = (bf16[4,32,1312]{2,1,0:T(8,128)(2,1)}, bf16[4,32,1312]{2,1,0:T(8,128)(2,1)S(1)}, u32[]{:S(2)}, u32[]{:S(2)}) collective-permute-start(bf16[4,32,1312]{2,1,0:T(8,128)(2,1)} %get-tuple-element.70), channel_id=1, source_target_pairs={{0,6},{1,7},{2,0},{3,1},{4,2},{5,3},{6,4},{7,5},{8,14},{9,15},{10,... | collective-permute-start | bytes 1007624 | tf_op jit(solution)/shard_map/ppermute | solution.py:1721
  170.5 0.7 copy-start.2
  170.5 0.8 copy-start.3

commit v5 on v4

--- a/solution.py
+++ b/solution.py
@@ -562,7 +562,7 @@
 
 
 def attend_back_kernel(
-    lengths, qp, gp, op, lse, kv, output, down, dqp, dkv, output_to, down_to, acc_scr
+    lengths, qp, gp, op, lse, kv, dqp, dkv, acc_scr
 ):
     pairs = qp.shape[0] * qp.shape[2]
     T = kv.shape[0]
@@ -572,8 +572,6 @@
     ends = (hh == half_runs - 1) & (u == pl.num_programs(1) - 1)
     @pl.when(begins)
     def _():
-        output_to[...] = output[...]
-        down_to[...] = down[...]
         acc_scr[...] = jnp.zeros_like(acc_scr)
 
     at = lax.broadcasted_iota(jnp.int32, (KEY_STEP, pairs), 0)
@@ -617,7 +615,7 @@
         dkv[...] = acc_scr[...].astype(dkv.dtype)
 
 
-def attend_back(lengths, qp, gp, op, lse, kv, output, down):
+def attend_back(lengths, qp, gp, op, lse, kv):
     parts, half_runs, rows, lanes = qp.shape
     piece = pl.BlockSpec((2, 1, rows, lanes), lambda i, j, s: (j, i, 0, 0))
     grads = pl.BlockSpec((2, 2 * half_runs, rows // 2, lanes), lambda i, j, s: (j, 0, 0, 0))
@@ -626,22 +624,20 @@
         grid_spec=pltpu.PrefetchScalarGridSpec(
             num_scalar_prefetch=1,
             grid=(half_runs, parts // 2),
-            in_specs=[piece, grads, piece, *[in_vmem()] * 4],
-            out_specs=[piece, *[in_vmem()] * 3],
+            in_specs=[piece, grads, piece, *[in_vmem()] * 2],
+            out_specs=[piece, in_vmem()],
             scratch_shapes=[pltpu.VMEM(kv.shape, jnp.float32)],
         ),
         out_shape=[
             jax.ShapeDtypeStruct(qp.shape, jnp.bfloat16),
             jax.ShapeDtypeStruct(kv.shape, jnp.bfloat16),
-            jax.ShapeDtypeStruct(output.shape, output.dtype),
-            jax.ShapeDtypeStruct(down.shape, down.dtype),
         ],
         compiler_params=params(),
         cost_estimate=pl.CostEstimate(
             flops=3 * 10**9, bytes_accessed=60 * 10**6, transcendentals=10**6
         ),
         name="attend_back",
-    )(lengths, qp, gp, op, lse, kv, output, down)
+    )(lengths, qp, gp, op, lse, kv)
 
 
 def deliver_kernel(*refs):
@@ -697,6 +693,9 @@
         self.back = [lax.rem(self.part + parts - i, parts) for i in range(1, parts)]
         self.along = [(h, part * 2 + self.share) for part in self.there]
         self.beside = (h, self.part * 2 + 1 - self.share)
+        self.near = self.part + 1 - 2 * lax.rem(self.part, 2)
+        self.over = lax.rem(self.part + 2, 4)
+        self.far = 3 - self.part
         self.askew = [(h, part * 2 + 1 - self.share) for part in self.there]
 
 
@@ -779,6 +778,46 @@
             self._copy(self.own, block, 0).wait_send()
 
 
+class CornerGather:
+    def __init__(self, whole, half, own, here, sems):
+        self.whole, self.half, self.own, self.here = whole, half, own, here
+        self.send_s, self.recv_s = sems
+
+    def _copy(self, n):
+        h, (corner, x, y) = self.here.h, self.here.across
+        if n < 2:
+            source, target, peer = self.own, self.whole(h), (x, y)[n]
+        else:
+            block = (y, x)[n - 2][0]
+            source = target = self.half(block, n - 2)
+            peer = (x, y)[n - 2]
+        return remote(source, target, self.send_s.at[n], self.recv_s.at[n], peer)
+
+    def start(self):
+        for n in range(2):
+            self._copy(n).start()
+
+    def forward(self):
+        for n in range(2):
+            self._copy(n).wait_recv()
+        for n in range(2, 4):
+            self._copy(n).start()
+
+    def arrive(self):
+        for n in range(2, 4):
+            self._copy(n).wait_recv()
+
+    def finish(self):
+        for n in range(4):
+            self._copy(n).wait_send()
+
+
+def local(source, target, sem):
+    copy = pltpu.make_async_copy(source, target, sem)
+    copy.start()
+    return copy
+
+
 def line_sems(parts):
     return [dma(parts)] * 5
 
@@ -818,25 +857,42 @@
 
 
 def project_kernel(
-    H, A, tok, cot, wq, gain_one, gain_two, w_in, w_down, w_out, lengths,
-    kv_all, q_all, tok_all, cot_all, wq_all, wm_all, wo_all, gain_rows, cos_all, sin_all,
-    wq_src, wq_st, wm_src, kv_send, q_send, q_runs, hats, gain_src, gain_st, gain_tile, gain_all,
-    tok_s, tok_r, cot_s, cot_r, wq_s, wq_r, wm_s, wm_r, ga_s, ga_r, gb_s, gb_r, wx_s, wx_r,
+    H, A, tok_in, cot_in, wq_in, gain_one, gain_two, w_in_in, w_down_in, w_out_in, lengths,
+    kv_all, q_all, tok_out, cot_all, wq_out, wm_all, wo_all, gain_rows, cos_out, sin_out,
+    cot, w_in, w_down, w_out, tok_all, wq_all, cos_all, sin_all,
+    wq_st, wm_src, kv_send, q_send, q_runs, hats, gain_src, gain_st, gain_tile, gain_all,
+    load_s, store_s, own_s, kv_o, q_o,
+    tok_s, tok_r, wq_s, wq_r, wm_s, wm_r, ga_s, ga_r, gb_s, gb_r, wx_s, wx_r, wf_s, wf_r, cot_s, cot_r,
     q_s, q_r, kv_s, kv_r, kc_s, kc_r, *line,
 ):
     f32, bf16 = jnp.float32, jnp.bfloat16
-    R, W = tok.shape
+    R, W = tok_all.shape[1:]
     B = 2 * A
     hw = W // H
-    D = wq.shape[0]
+    D = wq_in.shape[0]
     F = w_in.shape[1] // 2 // H
     here = Place(A)
     h, b, part, share = here.h, here.b, here.part, here.share
     across, along, beside = here.across, here.along, here.beside
 
-    for place in range(H):
-        for j in range(3):
-            wq_src[place, :, j * hw : (j + 1) * hw] = wq[:, j * W + place * hw : j * W + (place + 1) * hw]
+    def slices(source, target, place):
+        return [
+            (
+                source.at[:, pl.ds(pl.multiple_of(j * W + place * hw, hw), hw)],
+                target.at[h, :, j * hw : (j + 1) * hw],
+            )
+            for j in range(3)
+        ]
+
+    loads = [
+        local(source, target, load_s.at[n])
+        for n, (source, target) in enumerate(
+            [
+                (w_out_in, w_out), (w_in_in, w_in), (w_down_in, w_down), (cot_in, cot), (tok_in, tok_all.at[h]),
+                *slices(wq_in, wq_st, h),
+            ]
+        )
+    ]
     row = lax.broadcasted_iota(jnp.int32, (8, 128), 0)
     lane = lax.broadcasted_iota(jnp.int32, (8, 128), 1)
     gain_src[...] = jnp.zeros((8, 128), f32)
@@ -845,34 +901,70 @@
     gain_src[...] = pltpu.roll(gain_src[...], h * D, 1)
     meet([*across, *along, beside, *here.askew])
 
+    for i, peer in enumerate(across):
+        for source, target in slices(wq_in, wq_st, peer[0]):
+            send(source, target, wq_s.at[i], wq_r.at[i], peer)
     wq_copies = [
-        send(wq_src.at[peer[0]], wq_st.at[h], wq_s.at[i], wq_r.at[i], peer)
+        remote(wq_st.at[peer[0]], wq_st.at[h], wq_s.at[i], wq_r.at[i], peer)
         for i, peer in enumerate(across)
     ]
     gain_copies = [
         send(gain_src, gain_st.at[i], ga_s.at[i], ga_r.at[i], peer) for i, peer in enumerate(across)
     ]
-    wo_line = LineGather(lambda block, side: wo_all.at[h, block, side], w_out, here, line[5:])
+    wo_line = LineGather(lambda block, side: wo_all.at[h, block, side], w_out, here, line[:5])
+    loads[0].wait()
     wo_line.start()
-    wo_all[h, part, share] = w_out[...]
-    wq_st[h] = wq_src[h]
-    tok_all[h] = tok[...]
-    cot_all[h] = cot[...]
+    stores = [local(w_out, wo_all.at[h, part, share], own_s.at[0])]
+    for copy in loads[1:]:
+        copy.wait()
     for place in range(H):
         wm_src[place, :, :F] = w_in[:, place * F : (place + 1) * F]
         wm_src[place, :, F : 2 * F] = w_in[:, (H + place) * F : (H + place + 1) * F]
         wm_src[place, :, 2 * F :] = w_down[:, place * F : (place + 1) * F]
-    wm_all[h] = wm_src[h]
+    stores += [
+        local(wm_src.at[h], wm_all.at[h], own_s.at[1]),
+        local(cot, cot_all.at[h], own_s.at[2]),
+    ]
+
+    wide = lax.broadcasted_iota(jnp.int32, (R, 128), 1)
+    freqs = jnp.exp(
+        lax.rem(wide, HEAD_DIM // 2).astype(f32) * (-2.0 / HEAD_DIM * float(np.log(rope_base)))
+    )
+
+    def tables(run):
+        place = (run * B + b) * R + lax.broadcasted_iota(jnp.int32, (R, 128), 0)
+
+        def one(d, carried):
+            low, begin = carried
+            return (low + lengths[d], jnp.where(place >= low, low, begin))
+
+        unused, begin = lax.fori_loop(
+            0, lengths.shape[0], one, (jnp.int32(0), jnp.zeros((R, 128), jnp.int32))
+        )
+        angles = (place - begin).astype(f32) * freqs
+        cos_all[run] = jnp.cos(angles)
+        sin_all[run] = jnp.sin(angles)
+
+    tables(0)
+    tables(1)
     wo_line.step(1)
-
     for copy in wq_copies:
         copy.wait_recv()
-    wq_line = LineGather(lambda block, side: wq_all.at[:, block * 2 + side], wq_st, here, line[:5])
-    wq_line.start()
+    wq_lines = []
+    for half in range(2):
+        rows = pl.ds(half * (H // 2), H // 2)
+        wq_lines.append(
+            LineGather(
+                lambda block, side, rows=rows: wq_all.at[rows, block * 2 + side],
+                wq_st.at[rows],
+                here,
+                line[5 * half + 5 : 5 * half + 10],
+            )
+        )
+        wq_lines[half].start()
     tok_copies = [
-        send(tok, tok_all.at[h], tok_s.at[i], tok_r.at[i], peer) for i, peer in enumerate(across)
-    ]
-    wq_all[:, b] = wq_st[...]
+        send(tok_in, tok_all.at[h], tok_s.at[i], tok_r.at[i], peer) for i, peer in enumerate(across)
+    ]
     tile = gain_src[...]
     for i, copy in enumerate(gain_copies):
         copy.wait_recv()
@@ -884,44 +976,48 @@
         for i, peer in enumerate([*along, *here.askew, beside])
     ]
     wo_line.step(2)
-
-    wide = lax.broadcasted_iota(jnp.int32, (R, 128), 1)
-    freqs = jnp.exp(
-        lax.rem(wide, HEAD_DIM // 2).astype(f32) * (-2.0 / HEAD_DIM * float(np.log(rope_base)))
-    )
-    for run in range(H):
-        place = (run * B + b) * R + lax.broadcasted_iota(jnp.int32, (R, 128), 0)
-
-        def one(d, carried, place=place):
-            low, begin = carried
-            return (low + lengths[d], jnp.where(place >= low, low, begin))
-
-        unused, begin = lax.fori_loop(
-            0, lengths.shape[0], one, (jnp.int32(0), jnp.zeros((R, 128), jnp.int32))
-        )
-        angles = (place - begin).astype(f32) * freqs
-        cos_all[run] = jnp.cos(angles)
-        sin_all[run] = jnp.sin(angles)
-
-    wq_line.step(1)
+    wq_all[:, b] = wq_st[...]
+    tables(2)
+    wq_lines[0].step(1)
+    wo_line.step(3)
+    wq_lines[1].step(1)
+    wo_line.arrive()
+    spread = CornerGather(
+        lambda place: wo_all.at[place, :, share],
+        lambda place, half: wo_all.at[place, half * (A // 2) : (half + 1) * (A // 2), share],
+        wo_all.at[h, :, share],
+        here,
+        (wx_s, wx_r),
+    )
+    for copy in stores[:1]:
+        copy.wait()
+    spread.start()
     wm_copies = [
         send(wm_src.at[peer[0]], wm_all.at[h], wm_s.at[i], wm_r.at[i], peer)
         for i, peer in enumerate(across)
     ]
-    cot_copies = [
-        send(cot, cot_all.at[h], cot_s.at[i], cot_r.at[i], peer) for i, peer in enumerate(across)
-    ]
-    wo_line.step(3)
+    cot_gather = CornerGather(
+        lambda place: cot_all.at[place],
+        lambda place, half: cot_all.at[place, half * (R // 2) : (half + 1) * (R // 2)],
+        cot,
+        here,
+        (cot_s, cot_r),
+    )
+    cot_gather.start()
+    tables(3)
+    stores += [local(cos_all, cos_out, store_s.at[0]), local(sin_all, sin_out, store_s.at[1])]
     for copy in tok_copies:
         copy.wait_recv()
+    stores.append(local(tok_all, tok_out, store_s.at[2]))
 
     def norm_run(run, carried):
         hat, unused = standardize(tok_all[run].astype(f32))
         hats[run] = hat
         return carried
 
+    wq_lines[0].step(2)
     lax.fori_loop(0, H // 2, norm_run, 0)
-    wq_line.step(2)
+    wq_lines[1].step(2)
     lax.fori_loop(H // 2, H, norm_run, 0)
     for copy in gain_copies[len(across) :]:
         copy.wait_recv()
@@ -934,15 +1030,12 @@
                 moved = pltpu.roll(moved, (j - place) * D % 128, 1)
             piece = jnp.where(lane // D == j, moved, piece)
         gain_rows[:, slab * 128 : (slab + 1) * 128] = piece
-    wq_line.step(3)
-    wo_line.arrive()
-    spread_out = wo_all.at[h, :, share]
-    wx_copies = [
-        send(spread_out, spread_out, wx_s.at[i], wx_r.at[i], peer) for i, peer in enumerate(across)
-    ]
-    wq_line.arrive()
-
-    q_copies = []
+    wq_lines[0].step(3)
+    wq_lines[1].step(3)
+    wq_lines[0].arrive()
+    wq_lines[1].arrive()
+    stores.append(local(wq_all, wq_out, store_s.at[3]))
+
     for run in [run for low in range(H // 2) for run in (low, low + H // 2)]:
         normed = (hats[run] * gain_rows[0:1, :]).astype(bf16)
         projected = jnp.zeros((R, 3 * hw), f32)
@@ -959,8 +1052,8 @@
             kv_send[2 * slab + 1, run] = join(key, 1, value, 1).astype(bf16)
         for i, peer in enumerate(along):
             send(kv_send.at[here.there[i], run], kv_all.at[run, b], kv_s.at[i], kv_r.at[i], peer)
-        kv_all[run, b] = kv_send[part, run]
         send(kv_send.at[part, run], kv_all.at[run, b], kc_s.at[0], kc_r.at[0], beside)
+        stores.append(local(kv_send.at[part, run], kv_all.at[run, b], kv_o.at[run]))
         if run >= H // 2:
             low = run - H // 2
             for a in range(A):
@@ -970,7 +1063,7 @@
                 ).astype(bf16)
             for i, peer in enumerate(along):
                 send(q_send.at[here.there[i], low], q_all.at[part, low], q_s.at[i], q_r.at[i], peer)
-            q_all[part, low] = q_send[part, low]
+            stores.append(local(q_send.at[part, low], q_all.at[part, low], q_o.at[low]))
 
     kv_copies = [
         remote(kv_send.at[here.there[i]], kv_all.at[:, b], kv_s.at[i], kv_r.at[i], peer)
@@ -981,23 +1074,30 @@
         remote(q_send.at[here.there[i]], q_all.at[part], q_s.at[i], q_r.at[i], peer)
         for i, peer in enumerate(along)
     ]
-    for i, copy in enumerate(wx_copies):
-        copy.wait_recv()
+    spread.forward()
+    cot_gather.forward()
+
+    def pass_on(i):
         there = wo_all.at[here.places[i], :, share]
-        n = H - 1 + i
-        kc_copies.append(send(there, there, wx_s.at[n], wx_r.at[n], beside))
+        kc_copies.append(send(there, there, wf_s.at[i], wf_r.at[i], beside))
+
+    pass_on(1)
+    pass_on(2)
+    spread.arrive()
+    pass_on(0)
     for i, copy in enumerate(kv_copies):
         copy.wait_recv()
         there = kv_all.at[:, here.back[i] * 2 + share]
         kc_copies.append(send(there, there, kc_s.at[i + 1], kc_r.at[i + 1], beside))
-    for copy in [*kc_copies, *q_copies, *wm_copies, *cot_copies]:
+    cot_gather.arrive()
+    for copy in [*kc_copies, *q_copies, *wm_copies]:
         copy.wait_recv()
-    for copy in [
-        *kc_copies, *q_copies, *wm_copies, *cot_copies, *wq_copies, *gain_copies, *tok_copies, *wx_copies, *kv_copies
-    ]:
+    for copy in [*kc_copies, *q_copies, *wm_copies, *wq_copies, *gain_copies, *tok_copies, *kv_copies]:
         copy.wait_send()
-    wq_line.finish()
-    wo_line.finish()
+    for copy in stores[1:]:
+        copy.wait()
+    for item in (spread, cot_gather, wo_line, *wq_lines):
+        item.finish()
 
 
 def project(tokens, cotangent, w_qkv, gain_one, gain_two, w_in, w_down, w_out, lengths):
@@ -1009,10 +1109,11 @@
     F = w_down.shape[1] // H
     f32, bf16 = jnp.float32, jnp.bfloat16
     shape = jax.ShapeDtypeStruct
+    buffer = lambda *sizes: pltpu.VMEM(sizes, bf16)
     return pl.pallas_call(
         partial(project_kernel, H, A),
-        in_specs=[*[in_vmem()] * 8, in_smem()],
-        out_specs=[in_vmem()] * 10,
+        in_specs=[*[anywhere()] * 3, *[in_vmem()] * 2, *[anywhere()] * 3, in_smem()],
+        out_specs=[*[anywhere()] * 7, in_vmem(), *[anywhere()] * 2],
         out_shape=[
             shape((H, B, R, 128), bf16),
             shape((A, H // 2, R, 128), bf16),
@@ -1026,24 +1127,37 @@
             shape((H, R, 128), f32),
         ],
         scratch_shapes=[
-            pltpu.VMEM((H, D, 3 * hw), bf16),
-            pltpu.VMEM((H, D, 3 * hw), bf16),
-            pltpu.VMEM((H, D, 3 * F), bf16),
-            pltpu.VMEM((A, H, R, 128), bf16),
-            pltpu.VMEM((A, H // 2, R, 128), bf16),
+            buffer(R, W),
+            buffer(*w_in.shape),
+            buffer(*w_down.shape),
+            buffer(*w_out.shape),
+            buffer(H, R, W),
+            buffer(H, B, D, 3 * hw),
+            pltpu.VMEM((H, R, 128), f32),
+            pltpu.VMEM((H, R, 128), f32),
+            buffer(H, D, 3 * hw),
+            buffer(H, D, 3 * F),
+            buffer(A, H, R, 128),
+            buffer(A, H // 2, R, 128),
             pltpu.VMEM((H, R, hw), f32),
             pltpu.VMEM((H, R, W), f32),
             pltpu.VMEM((8, 128), f32),
             pltpu.VMEM((H - 1, 8, 128), f32),
             pltpu.VMEM((8, 128), f32),
             pltpu.VMEM((B, 8, 128), f32),
-            *[dma(H - 1)] * 10,
+            dma(8),
+            dma(4),
+            dma(3),
+            dma(H),
+            dma(H // 2),
+            *[dma(H - 1)] * 8,
             *[dma(B - 1)] * 2,
-            *[dma(2 * H - 2)] * 2,
+            *[dma(4)] * 2,
+            *[dma(H - 1)] * 2,
+            *[dma(4)] * 2,
             *[dma(A - 1)] * 4,
             *[dma(A)] * 2,
-            *line_sems(A),
-            *line_sems(A),
+            *line_sems(A) * 3,
         ],
         compiler_params=params(0),
         cost_estimate=pl.CostEstimate(flops=10**9, bytes_accessed=10**7, transcendentals=10**6),
@@ -1082,11 +1196,9 @@
     def start(self):
         self._core().start()
 
-    def gather(self):
+    def core_sums(self):
         self._core().wait_recv()
-        for i, there in enumerate(self.here.there):
-            self.line_out[i][...] = self._sum(there).astype(jnp.bfloat16)
-        return self._sum(self.here.part)
+        return self._sum
 
     def middle(self):
         self._core().wait_recv()
@@ -1123,6 +1235,59 @@
     ]
 
 
+class PairReduce:
+    def __init__(self, core_in, near_out, near_in, far_out, far_in, *sems, term, here):
+        self.term, self.core_in, self.near_out, self.near_in = term, core_in, near_out, near_in
+        self.far_out, self.far_in, self.sems, self.here = far_out, far_in, sems, here
+
+    def _copy(self, step):
+        here = self.here
+        source, target, peer = (
+            (self.term.at[:, 1 - here.share], self.core_in, here.beside),
+            (self.near_out, self.near_in, (here.h, here.near * 2 + here.share)),
+            (self.far_out, self.far_in, (here.h, here.far * 2 + here.share)),
+        )[step]
+        return remote(source, target, self.sems[2 * step].at[0], self.sems[2 * step + 1].at[0], peer)
+
+    def _sum(self, there):
+        own = self.term[there, self.here.share].astype(jnp.float32)
+        return own + self.core_in[there].astype(jnp.float32)
+
+    def start(self):
+        self._copy(0).start()
+
+    def pair(self):
+        self._copy(0).wait_recv()
+        self.near_out[0] = self._sum(self.here.near).astype(jnp.bfloat16)
+        self.near_out[1] = self._sum(self.here.over).astype(jnp.bfloat16)
+        self._copy(1).start()
+
+    def cross(self):
+        self._copy(1).wait_recv()
+        self.far_out[...] = (
+            self._sum(self.here.far) + self.near_in[1].astype(jnp.float32)
+        ).astype(jnp.bfloat16)
+        self._copy(2).start()
+
+    def close(self):
+        self._copy(2).wait_recv()
+        total = self._sum(self.here.part) + self.near_in[0].astype(jnp.float32)
+        return total + self.far_in[...].astype(jnp.float32)
+
+    def finish(self):
+        for step in range(3):
+            self._copy(step).wait_send()
+
+
+def pair_scratch(parts, shape):
+    return [
+        pltpu.VMEM((parts, *shape), jnp.bfloat16),
+        *[pltpu.VMEM((2, *shape), jnp.bfloat16)] * 2,
+        *[pltpu.VMEM(shape, jnp.bfloat16)] * 2,
+        *[dma(1)] * 6,
+    ]
+
+
 def reducer(scratch, here):
     term, core_in, line_out, line_in, *sems = scratch
     outs = [line_out.at[i] for i in range(here.parts - 1)]
@@ -1134,9 +1299,8 @@
         self.out, self.landed, self.here = out, landed, here
         self.send_s, self.recv_s = send_s, recv_s
 
-    def start(self, value):
+    def start(self):
         here = self.here
-        self.out[...] = value.astype(jnp.bfloat16)
         self.copies = [
             send(self.out.at[peer[0]], self.landed.at[here.h], self.send_s.at[i], self.recv_s.at[i], peer)
             for i, peer in enumerate(here.across)
@@ -1177,13 +1341,12 @@
 
 def feed_kernel(
     H, A, op, tok_in, cot_in, wo_in, wm_own, wm_before, wm_after, gain_rows,
-    output, grad_middle, go, in_own, down_grad, mixed_own, gain_part, *rest,
+    out_base, out_parts, grad_middle, go, kept, up_far, near_out, over_out, far_out, mixed_own, gain_part, *rest,
 ):
-    in_out, rest = rest[: A - 1], rest[A - 1 :]
     (
         tok_all, cot_all, wo, mx_in, mixed_all, wm_all, middle, normed, act, lift,
-        g2_send, g2_in, g2_own, o_send, o_in, o_own, gm_send, in_term, in_core, in_core_s, in_core_r,
-        load_s, mx_s, mx_r, ma_s, ma_r, g2_s, g2_r, o_s, o_r, gm_s, gm_r, *more,
+        g2_send, g2_in, g2_own, gm_send, in_term, in_core, in_core_s, in_core_r, down_send, down_in, pair_s, pair_r,
+        load_s, mx_s, mx_r, ma_s, ma_r, g2_s, g2_r, gm_s, gm_r, *more,
     ) = rest
     f32, bf16 = jnp.float32, jnp.bfloat16
     R, W = tok_all.shape[1:]
@@ -1194,10 +1357,10 @@
     here = Place(A)
     h, b, part, share = here.h, here.b, here.part, here.share
     across, along = here.across, here.along
-    line, down_scratch, swap = more[:5], more[5:13], more[13:17]
-    down_term, down_sum = reducer(down_scratch, here)
-    down_swap = Swap(*swap, here)
-    in_sum = Reduce(in_term, in_core, in_out, None, here, [in_core_s, in_core_r, None, None])
+    line, (down_term, down_core, *down_sems) = more[:5], more[5:9]
+    down_sum = Reduce(down_term, down_core, None, None, here, [*down_sems, None, None])
+    in_sum = Reduce(in_term, in_core, None, None, here, [in_core_s, in_core_r, None, None])
+    near, over, far = here.near, here.over, here.far
     slot = lambda block: wm_all.at[:, block * 2 + share]
     own_loads = load(
         [(wm_own, slot(part)), (tok_in, tok_all), (wo_in, wo), (cot_in, cot_all)], load_s
@@ -1282,9 +1445,6 @@
 
     def part_of(run, i):
         return remote(g2_send.at[i], g2_in.at[i], g2_s.at[i], g2_r.at[i], (run, b))
-
-    def part_out(run, i):
-        return remote(o_send.at[i], o_in.at[i], o_s.at[i], o_r.at[i], (run, b))
 
     def feed_run(i, carried):
         run = run_of(here, i)
@@ -1325,21 +1485,19 @@
     lax.fori_loop(0, H, down_chunk, 0)
     down_sum.start()
 
-    def out_run(i, carried):
-        run = run_of(here, i)
-        for chunk in range(H):
-            lanes = slice(chunk * hw, (chunk + 1) * hw)
-            o_own[:, lanes] = mm(act[run], block(chunk)[:, 2 * F :], NT)
-
-        @pl.when(i < H - 1)
-        def _():
-            o_send[i] = o_own[...].astype(bf16)
-            part_out(run, i).start()
-
+    def in_chunk(chunk, carried):
+        lanes = pl.ds(pl.multiple_of(chunk * hw, hw), hw)
+        left = normed[:, :, lanes].reshape(H * R, hw)
+        grads = mm(left, lift[...].reshape(H * R, 2 * F), TN).astype(bf16)
+        in_term[:, :, chunk] = grads.reshape(A, 2, D, 2 * F)
         return carried
 
-    lax.fori_loop(0, H, out_run, 0)
-    down_sum.middle()
+    lax.fori_loop(0, H, in_chunk, 0)
+    in_sum.start()
+    down_of = down_sum.core_sums()
+    for n, there in enumerate((near, over)):
+        down_send[n] = down_of(there).astype(bf16)
+    pair_copy = send(down_send, down_in, pair_s.at[0], pair_r.at[0], (h, near * 2 + share))
 
     hat, scale = standardize(middle[h])
     grad = g2_own[...]
@@ -1367,36 +1525,42 @@
             else:
                 go[part, h] = gm_send[i, part]
 
-    def in_chunk(chunk, carried):
-        lanes = pl.ds(pl.multiple_of(chunk * hw, hw), hw)
-        left = normed[:, :, lanes].reshape(H * R, hw)
-        grads = mm(left, lift[...].reshape(H * R, 2 * F), TN).astype(bf16)
-        in_term[:, :, chunk] = grads.reshape(A, 2, D, 2 * F)
+    in_of = in_sum.core_sums()
+    near_out[0] = in_of(near)[:, :, :F].astype(bf16)
+    near_out[1] = in_of(near)[:, :, F:].astype(bf16)
+    near_out[2] = in_of(over)[:, :, F:].astype(bf16)
+    over_out[...] = in_of(over)[:, :, :F].astype(bf16)
+    far_out[0] = in_of(far)[:, :, :F].astype(bf16)
+    up_far[...] = in_of(far)[:, :, F:].astype(bf16)
+    kept[0] = in_of(part)[:, :, :F]
+    kept[1] = in_of(part)[:, :, F:]
+    pair_copy.wait_recv()
+    kept[2] = down_of(part) + down_in[0].astype(f32)
+    far_out[1] = (down_of(far) + down_in[1].astype(f32)).astype(bf16)
+
+    def out_run(i, carried):
+        run = run_of(here, i)
+        for chunk in range(H):
+            lanes = slice(chunk * hw, (chunk + 1) * hw)
+            out_base[:, lanes] = mm(act[run], block(chunk)[:, 2 * F :], NT)
+
+        @pl.when(i < H - 1)
+        def _():
+            out_parts[i] = out_base[...].astype(bf16)
+
         return carried
 
-    lax.fori_loop(0, H, in_chunk, 0)
-    in_sum.start()
-    down_swap.start(down_sum.close())
-    result = middle[h] + o_own[...]
-    for i in range(H - 1):
-        part_out(here.places[i], i).wait_recv()
-        result += o_in[i].astype(f32)
-    output[...] = result.astype(bf16)
-    in_own[...] = in_sum.gather()
-    down_swap.arrive()
-    for place in range(H):
-        down_grad[:, place * F : (place + 1) * F] = down_swap.landed[place].astype(f32)
+    lax.fori_loop(0, H, out_run, 0)
+    out_base[...] += middle[h]
     for copy in gm_copies:
         copy.wait_recv()
-    for copy in [*mx_copies, *ma_copies, *gm_copies]:
+    for copy in [*mx_copies, *ma_copies, *gm_copies, pair_copy]:
         copy.wait_send()
     for i in range(H - 1):
         part_of(here.places[i], i).wait_send()
-        part_out(here.places[i], i).wait_send()
     gather.finish()
     in_sum.core_finish()
-    down_sum.finish()
-    down_swap.finish()
+    down_sum.core_finish()
 
 
 def feed(op, tok_all, cot_all, wo, wm_own, wm_before, wm_after, gain_rows):
@@ -1412,16 +1576,19 @@
     return pl.pallas_call(
         partial(feed_kernel, H, A),
         in_specs=[in_vmem(), *[anywhere()] * 6, in_vmem()],
-        out_specs=[in_vmem()] * (6 + A),
+        out_specs=[in_vmem()] * 11,
         out_shape=[
-            shape((R, W), bf16),
+            shape((R, W), f32),
+            shape((H - 1, R, W), bf16),
             shape((R, W), f32),
             shape((A, H, R // 2, 128), bf16),
-            shape((H, D, 2 * F), f32),
-            shape((D, H * F), f32),
+            shape((3, H, D, F), f32),
+            shape((H, D, F), bf16),
+            shape((3, H, D, F), bf16),
+            shape((H, D, F), bf16),
+            shape((2, H, D, F), bf16),
             shape((H, R, hw), bf16),
             shape((8, W), f32),
-            *[shape((H, D, 2 * F), bf16)] * (A - 1),
         ],
         scratch_shapes=[
             pltpu.VMEM((H, R, W), bf16),
@@ -1434,18 +1601,22 @@
             pltpu.VMEM((H, R, W), bf16),
             pltpu.VMEM((H, R, F), bf16),
             pltpu.VMEM((H, R, 2 * F), bf16),
-            *[pltpu.VMEM((H - 1, R, W), bf16), pltpu.VMEM((H - 1, R, W), bf16), pltpu.VMEM((R, W), f32)] * 2,
+            *[pltpu.VMEM((H - 1, R, W), bf16)] * 2,
+            pltpu.VMEM((R, W), f32),
             pltpu.VMEM((H, A, R // 2, 128), bf16),
             pltpu.VMEM((A, 2, H, D, 2 * F), bf16),
             pltpu.VMEM((A, H, D, 2 * F), bf16),
             *[dma(1)] * 2,
+            *[pltpu.VMEM((2, H, D, F), bf16)] * 2,
+            *[dma(1)] * 2,
             dma(6),
             *[dma(A - 1)] * 2,
-            *[dma(H - 1)] * 6,
+            *[dma(H - 1)] * 4,
             *[dma(H * A)] * 2,
             *line_sems(A),
-            *reduce_scratch(A, (H, D, F)),
-            *swap_scratch(H, (D, F)),
+            pltpu.VMEM((A, 2, H, D, F), bf16),
+            pltpu.VMEM((A, H, D, F), bf16),
+            *[dma(1)] * 2,
         ],
         compiler_params=params(1),
         cost_estimate=pl.CostEstimate(flops=6 * 10**9, bytes_accessed=10**7, transcendentals=10**6),
@@ -1454,29 +1625,32 @@
 
 
 def finish_kernel(
-    H, A, dqp, dkv, tok_in, wq_in, cos_in, sin_in, gain_rows, mixed_in, middle_in, gain_part, own_in, near_in, send_in, far_in,
-    input_grad, qkv_grad, out_grad, in_grad, gain_one, gain_two,
-    dkv_own, tok_all, wq_all, cos_all, sin_all, mixed_own, grad_middle, in_own, in_near, in_far, in_mid,
+    H, A, dqp, dkv, tok_in, wq_in, cos_in, sin_in, gain_rows, mixed_in, middle_in, gain_part, base_in, out_parts, kept_in, up_in, near_in, over_in, far_in,
+    output, input_grad, qkv_grad, out_grad, in_grad, down_grad, gain_one, gain_two,
+    dkv_own, tok_all, wq_all, cos_all, sin_all, mixed_own, grad_middle, out_base, o_in, kept, up_far, from_near, from_over, from_far, up_send, up_last,
     dk_in, dkv_send, dkv_in, dq_in, branch, branch_all, gp, normed, g1_send, g1_in, g1_own,
-    load_s, in_s, in_r, dk_s, dk_r, dz_s, dz_r, dq_s, dq_r, br_s, br_r, g1_s, g1_r, *rest,
+    load_s, up_s, up_r, o_s, o_r, dk_s, dk_r, dz_s, dz_r, dq_s, dq_r, br_s, br_r, g1_s, g1_r, *rest,
 ):
     f32, bf16 = jnp.float32, jnp.bfloat16
     R, W = tok_all.shape[1:]
     B = 2 * A
     hw = W // H
-    D = own_in.shape[1]
-    F = own_in.shape[2] // 2
+    D, F = kept_in.shape[2:]
     here = Place(A)
     h, b, part, share = here.h, here.b, here.part, here.share
     across, along, beside = here.across, here.along, here.beside
-    term_out, out_sum = reducer(rest[:8], here)
-    term_qkv, qkv_sum = reducer(rest[8:16], here)
-    term_gain, gain_sum = reducer(rest[16:24], here)
-    in_swap, qkv_swap, gain_swap = (Swap(*rest[24 + 4 * n : 28 + 4 * n], here) for n in range(3))
+    term_gain, gain_sum = reducer(rest[:8], here)
+    in_swap, qkv_swap, gain_swap = (Swap(*rest[8 + 4 * n : 12 + 4 * n], here) for n in range(3))
+    term_out, *term_qkv = rest[20:23]
+    out_sum, *qkv_sums = (
+        PairReduce(*rest[23 + 11 * n : 34 + 11 * n], term=term, here=here)
+        for n, term in enumerate((term_out, *term_qkv))
+    )
     loads = load(
         [
             (dkv, dkv_own), (middle_in, grad_middle), (tok_in, tok_all), (mixed_in, mixed_own), (cos_in, cos_all),
-            (sin_in, sin_all), (wq_in, wq_all), (own_in, in_own), (near_in, in_near), (far_in, in_far),
+            (sin_in, sin_all), (wq_in, wq_all), (kept_in, kept), (up_in, up_far), (near_in, from_near),
+            (far_in, from_far), (base_in, out_base),
         ],
         load_s,
     )
@@ -1510,6 +1684,9 @@
         send(branch, branch_all.at[h], br_s.at[i], br_r.at[i], peer) for i, peer in enumerate(across)
     ]
     branch_all[h] = branch[...]
+    o_copies = [
+        send(out_parts.at[i], o_in.at[i], o_s.at[i], o_r.at[i], peer) for i, peer in enumerate(across)
+    ]
     for copy in loads[2:]:
         copy.wait()
 
@@ -1530,9 +1707,12 @@
 
     lax.fori_loop(0, W // hw, out_tile, 0)
     out_sum.start()
+    up_send[...] = (up_far[...].astype(f32) + from_near[2].astype(f32)).astype(bf16)
     for copy in [*dq_copies, *dz_copies]:
         copy.wait_recv()
-    in_copy = send(send_in, in_mid, in_s.at[0], in_r.at[0], along[1])
+    out_sum.pair()
+    up_copy = send(up_send, up_last, up_s.at[0], up_r.at[0], (h, here.far * 2 + share))
+    over_copy = send(over_in, from_over, up_s.at[1], up_r.at[1], (h, here.over * 2 + share))
     for run in range(H):
         side, at = run // (H // 2), run % (H // 2)
         cosine, sine = cos_all[run], sin_all[run]
@@ -1551,15 +1731,19 @@
     def block(chunk):
         return wq_all[chunk].reshape(B * D, 3 * hw)
 
-    def term_chunk(chunk, carried):
-        lanes = pl.ds(pl.multiple_of(chunk * hw, hw), hw)
-        left = normed[:, :, lanes].reshape(H * R, hw)
-        grads = mm(left, gp[...].reshape(H * R, 3 * hw), TN).astype(bf16)
-        term_qkv[:, :, chunk] = grads.reshape(A, 2, D, 3 * hw)
-        return carried
-
-    lax.fori_loop(0, H, term_chunk, 0)
-    qkv_sum.start()
+    for half, (term, item) in enumerate(zip(term_qkv, qkv_sums)):
+
+        def term_chunk(n, carried, half=half, term=term):
+            lanes = pl.ds(pl.multiple_of((half * (H // 2) + n) * hw, hw), hw)
+            left = normed[:, :, lanes].reshape(H * R, hw)
+            grads = mm(left, gp[...].reshape(H * R, 3 * hw), TN).astype(bf16)
+            term[:, :, n] = grads.reshape(A, 2, D, 3 * hw)
+            return carried
+
+        lax.fori_loop(0, H // 2, term_chunk, 0)
+        item.start()
+        if half:
+            qkv_sums[0].pair()
 
     def part_of(run, i):
         return remote(g1_send.at[i], g1_in.at[i], g1_s.at[i], g1_r.at[i], (run, b))
@@ -1578,14 +1762,19 @@
         return carried
 
     lax.fori_loop(0, 1, one_run, 0)
-    qkv_sum.middle()
+    qkv_sums[1].pair()
+    out_sum.cross()
     lax.fori_loop(1, H, one_run, 0)
-    out_sum.middle()
-    in_copy.wait_recv()
-    total = in_own[...]
-    for term in (in_near, in_mid, in_far):
-        total += term[...].astype(f32)
-    in_swap.start(total)
+    qkv_sums[0].cross()
+    over_copy.wait_recv()
+    gate = kept[0] + from_near[0].astype(f32) + from_over[...].astype(f32) + from_far[0].astype(f32)
+    in_swap.out[:, :, :F] = gate.astype(bf16)
+    in_swap.out[:, :, 2 * F :] = (kept[2] + from_far[1].astype(f32)).astype(bf16)
+    up_copy.wait_recv()
+    up = kept[1] + from_near[1].astype(f32) + up_last[...].astype(f32)
+    in_swap.out[:, :, F : 2 * F] = up.astype(bf16)
+    in_swap.start()
+    qkv_sums[1].cross()
 
     grad = g1_own[...]
     hat, scale = standardize(tok_all[h].astype(f32))
@@ -1607,12 +1796,23 @@
     gain_sum.start()
     input_grad[...] = grad_middle[...] + norm_back(grad, hat, scale, gain_rows[0:1, :])
     gain_sum.middle()
+    result = out_base[...]
+    for i, copy in enumerate(o_copies):
+        copy.wait_recv()
+        result += o_in[i].astype(f32)
+    output[...] = result.astype(bf16)
     in_swap.arrive()
     for place in range(H):
         in_grad[:, place * F : (place + 1) * F] = in_swap.landed[place, :, :F].astype(f32)
-        in_grad[:, (H + place) * F : (H + place + 1) * F] = in_swap.landed[place, :, F:].astype(f32)
-    qkv_swap.start(qkv_sum.close())
-    gain_swap.start(gain_sum.close())
+        in_grad[:, (H + place) * F : (H + place + 1) * F] = in_swap.landed[
+            place, :, F : 2 * F
+        ].astype(f32)
+        down_grad[:, place * F : (place + 1) * F] = in_swap.landed[place, :, 2 * F :].astype(f32)
+    for half, item in enumerate(qkv_sums):
+        qkv_swap.out[half * (H // 2) : (half + 1) * (H // 2)] = item.close().astype(bf16)
+    qkv_swap.start()
+    gain_swap.out[...] = gain_sum.close().astype(bf16)
+    gain_swap.start()
     out_grad[...] = out_sum.close()
     qkv_swap.arrive()
     for place in range(H):
@@ -1627,37 +1827,39 @@
     rows = total.T
     gain_one[...] = rows[0:1, :]
     gain_two[...] = rows[1:2, :]
-    for copy in [*dk_copies, *dq_copies, *br_copies, *dz_copies, in_copy]:
+    for copy in [*dk_copies, *dq_copies, *br_copies, *dz_copies, *o_copies, up_copy, over_copy]:
         copy.wait_send()
     for i in range(H - 1):
         part_of(here.places[i], i).wait_send()
-    for item in (out_sum, qkv_sum, gain_sum, in_swap, qkv_swap, gain_swap):
+    for item in (out_sum, *qkv_sums, gain_sum, in_swap, qkv_swap, gain_swap):
         item.finish()
 
 
-def finish(dqp, dkv, tok_all, wq_all, cos_all, sin_all, gain_rows, mixed, grad_middle, gain_part, in_own, *in_terms):
+def finish(dqp, dkv, tok_all, wq_all, cos_all, sin_all, gain_rows, mixed, grad_middle, gain_part, out_base, out_parts, kept, *terms):
     A, half, R, lanes = dqp.shape
     H = 2 * half
     W = tok_all.shape[-1]
     B = 2 * A
     hw = W // H
-    D = in_own.shape[1]
-    F = in_own.shape[2] // 2
+    D, F = kept.shape[2:]
     f32, bf16 = jnp.float32, jnp.bfloat16
     shape = jax.ShapeDtypeStruct
     buffer = lambda *sizes: pltpu.VMEM(sizes, bf16)
     arrays = [
-        dqp, dkv, tok_all, wq_all, cos_all, sin_all, gain_rows, mixed, grad_middle, gain_part, in_own, *in_terms
+        dqp, dkv, tok_all, wq_all, cos_all, sin_all, gain_rows, mixed, grad_middle, gain_part, out_base, out_parts,
+        kept, *terms,
     ]
     return pl.pallas_call(
         partial(finish_kernel, H, A),
         in_specs=[in_vmem() if n in (0, 6, 9) else anywhere() for n in range(len(arrays))],
-        out_specs=[in_vmem()] * 6,
+        out_specs=[in_vmem()] * 8,
         out_shape=[
+            shape((R, W), bf16),
             shape((R, W), f32),
             shape((D, 3 * W), f32),
             shape((D, W), f32),
             shape((D, 2 * H * F), f32),
+            shape((D, H * F), f32),
             shape((1, D), f32),
             shape((1, D), f32),
         ],
@@ -1669,8 +1871,11 @@
             pltpu.VMEM(sin_all.shape, f32),
             buffer(*mixed.shape),
             pltpu.VMEM(grad_middle.shape, f32),
-            pltpu.VMEM(in_own.shape, f32),
-            *[buffer(H, D, 2 * F)] * 3,
+            pltpu.VMEM(out_base.shape, f32),
+            buffer(*out_parts.shape),
+            pltpu.VMEM(kept.shape, f32),
+            *[buffer(*term.shape) for term in terms],
+            *[buffer(H, D, F)] * 2,
             buffer(A, H, R, 128),
             buffer(A - 1, H, R, 128),
             buffer(A, H, R, 128),
@@ -1682,17 +1887,21 @@
             buffer(H - 1, R, W),
             buffer(H - 1, R, W),
             pltpu.VMEM((R, W), f32),
-            dma(10),
-            *[dma(1)] * 2,
+            dma(12),
+            *[dma(2)] * 2,
+            *[dma(H - 1)] * 2,
             *[dma(A)] * 2,
             *[dma(A - 1)] * 4,
             *[dma(H - 1)] * 4,
-            *reduce_scratch(A, (D, W)),
-            *reduce_scratch(A, (H, D, 3 * hw)),
             *reduce_scratch(A, (H, D, 128)),
-            *swap_scratch(H, (D, 2 * F)),
+            *swap_scratch(H, (D, 3 * F)),
             *swap_scratch(H, (D, 3 * hw)),
             *swap_scratch(H, (D, 128)),
+            buffer(A, 2, D, W),
+            *[buffer(A, 2, H // 2, D, 3 * hw)] * 2,
+            *pair_scratch(A, (D, W)),
+            *pair_scratch(A, (H // 2, D, 3 * hw)),
+            *pair_scratch(A, (H // 2, D, 3 * hw)),
         ],
         compiler_params=params(2),
         cost_estimate=pl.CostEstimate(flops=2 * 10**9, bytes_accessed=10**7, transcendentals=10**5),
@@ -1715,16 +1924,17 @@
     wm_before = lax.ppermute(wm, "blk", [(i, i + 2) for i in range(B - 2)])
     wm_after = lax.ppermute(wm, "blk", [(i + 2, i) for i in range(B - 2)])
     op, lse = attend(doc_lengths, qp, kv)
-    output, grad_middle, gp, in_own, down_grad, mixed, gain_part, *in_out = feed(
+    out_base, out_parts, grad_middle, gp, kept, up_far, *out_terms, mixed, gain_part = feed(
         op, tok_all, cot_all, wo.reshape(H, hw, W), wm, wm_before, wm_after, gain_rows
     )
-    shifted = lambda i: lax.ppermute(in_out[i - 1], "blk", [(p, (p + i * 2) % B) for p in range(B)])
-    in_near, in_far = shifted(1), shifted(3)
-    dqp, dkv, output, down_grad = attend_back(doc_lengths, qp, gp, op, lse, kv, output, down_grad)
-    input_grad, qkv_grad, out_grad, in_grad, gain_one, gain_two = deliver(
+    near, over, far = out_terms
+    flipped = lambda flip: [(p, (p // 2 ^ flip) * 2 + p % 2) for p in range(B)]
+    near, far = lax.ppermute(near, "blk", flipped(1)), lax.ppermute(far, "blk", flipped(3))
+    dqp, dkv = attend_back(doc_lengths, qp, gp, op, lse, kv)
+    output, input_grad, qkv_grad, out_grad, in_grad, down_grad, gain_one, gain_two = deliver(
         *finish(
             dqp, dkv.reshape(H, B, R, 128), tok_all, wq, cos_all, sin_all, gain_rows, mixed, grad_middle, gain_part,
-            in_own, in_near, in_out[1], in_far,
+            out_base, out_parts, kept, up_far, near, over, far,
         )
     )
     return (

time: 241 us -> 224 us (0.929)
  Pallas kernels: 228 us -> 209 us
  waiting for transfers between devices: 0.01 us -> 4.29 us
    pallas_call x1, Pallas kernels: 59.4 us -> 49.5 us  [project(): pl.pallas_call(partial(project_kernel, H, A), in_specs=[*[anywhere()] * 3...]
    pallas_call x1, Pallas kernels: 66.5 us -> 58.1 us  [finish(): pl.pallas_call(partial(finish_kernel, H, A), in_specs=[in_vmem() if n in...]
    ppermute x2, waiting for transfers between devices: 0.01 us -> 4.28 us  [the longest x1 4.28 us: per_device_split(): lax.ppermute(far, 'blk', flipped(3))]
    pallas_call x1, Pallas kernels: 68.9 us -> 66 us  [feed(): pl.pallas_call(partial(feed_kernel, H, A), in_specs=[in_vmem(), *[anywher...]
  transfers between devices with their start and end apart: 4 -> 4, of which waited for: 0 -> 1; matrix products, arithmetic and copies ran while one was open for 0% -> 0% of each run, Pallas kernels for 13% -> 15%
where the time goes in v5:
time: 224 us; the launch traced here: 225 us
  Pallas kernels  209 us (93%)
  starting transfers between devices  8.65 us (4%)
  waiting for transfers between devices  4.29 us (2%)
    pallas_call x1, Pallas kernels, feed(): pl.pallas_call(partial(feed_kernel, H, A), in_specs=[in_vmem(), *[anywher...  66 us
    pallas_call x1, Pallas kernels, finish(): pl.pallas_call(partial(finish_kernel, H, A), in_specs=[in_vmem() if n in...  58.1 us
    pallas_call x1, Pallas kernels, project(): pl.pallas_call(partial(project_kernel, H, A), in_specs=[*[anywhere()] * 3...  49.5 us
    pallas_call x1, Pallas kernels, attend_back(): pl.pallas_call(attend_back_kernel, grid_spec=pltpu.PrefetchScalarGridSpec...  17.7 us
    pallas_call x1, Pallas kernels, attend(): pl.pallas_call(attend_kernel, grid_spec=pltpu.PrefetchScalarGridSpec(num_...  15 us
    ppermute x1, starting transfers between devices, per_device_split(): wm_before = lax.ppermute(wm, 'blk', [(i, i + 2) for i in range(B - 2)])  4.58 us
  transfers between devices with their start and end apart: 4, of which 1 were waited for; matrix products, arithmetic and copies ran while one was open for 0% of the time, Pallas kernels for 15%

profile of v5, /device:TPU:0, one launch (start us, length us, event | category | flops | bytes accessed | tf_op | source)
XLA Modules:
  0.0 224.8 jit_solution(4383478842190700548)
XLA Ops:
  0.6 49.5 %project.1 = (bf16[4,8,128,128]{3,2,1,0:T(8,128)(2,1)}, bf16[4,2,128,128]{3,2,1,0:T(8,128)(2,1)}, bf16[4,128,1024]{2,1,0:T(8,128)(2,1)}, bf16[4,128,1024]{2,1,0:...) custom-call(bf16[128,1024]{1,0:T(8,128)(2,1)} %tok_in.1, ...), custom_call_target="tpu_custom_call" | custom-call | flops 1000000000 | bytes 10000000 | tf_op jit(solution)/shard_map/project/pallas_call | solution.py:1113
  50.2 1.3 collective-permute-start.1
  51.5 4.6 %collective-permute-start = (bf16[4,32,1968]{2,1,0:T(8,128)(2,1)}, bf16[4,32,1968]{2,1,0:T(8,128)(2,1)S(1)}, u32[]{:S(2)}, u32[]{:S(2)}) collective-permute-start(bf16[4,32,1968]{2,1,0:T(8,128)(2,1)} %get-tuple-element.55.wm_own), channel_id=1, source_target_pairs={{0,2},{1,3},{2,4},{3,5},{4,6},{5,7},{8,10},{9,11},{10,12},{11,13},... | collective-permute-start | bytes 1511432 | tf_op jit(solution)/shard_map/ppermute | solution.py:1924
  56.1 15.0 %attend.1 = (bf16[4,2,128,128]{3,2,1,0:T(8,128)(2,1)}, f32[8,1,256]{2,1,0:T(1,128)}) custom-call(s32[32]{0:T(128)} %lengths.5, bf16[4,2,128,128]{3,2,1,0:T(8,128)(2,1)} %get-tuple-element.49.qp, bf16[4096,128]{1,0:T(8,128)(2,1)} %bitcast.17), custom_call_target="tpu_custom_call" | custom-call | flops 1000000000 | bytes 50000000 | tf_op jit(solution)/shard_map/attend/pallas_call | solution.py:543
  71.1 0.0 collective-permute-done.1.wm_after
  71.1 0.0 copy-start.2
  71.1 0.0 collective-permute-done.wm_before
  71.1 0.0 copy-start.3
  71.1 0.8 copy-done.2
  71.9 0.2 copy-done.3
  72.0 66.0 %feed.1 = (f32[128,1024]{1,0:T(8,128)}, bf16[3,128,1024]{2,1,0:T(8,128)(2,1)}, f32[128,1024]{1,0:T(8,128)}, bf16[4,4,64,128]{3,2,1,0:T(8,128)(2,1)}, f32[3,4,32,...) custom-call(bf16[4,2,128,128]{3,2,1,0:T(8,128)(2,1)} %get-tuple-elem, ...), custom_call_target="tpu_custom_call" | custom-call | flops 6000000000 | bytes 10000000 | tf_op jit(solution)/shard_map/feed/pallas_call | solution.py:1576
  138.0 1.0 collective-permute-start.2
  139.0 1.8 collective-permute-start.3
  140.8 17.7 %attend_back.1 = (bf16[4,2,128,128]{3,2,1,0:T(8,128)(2,1)}, bf16[4096,128]{1,0:T(8,128)(2,1)}) custom-call(s32[32]{0:T(128)} %lengths.5, bf16[4,2,128,128]{3,2,1,0:T(8,128)(2,1)} %get-tuple-element.49.qp, bf16[4,4,64,128]{3,2,1,0:T(8,128)(2,1)} %get-tuple-element.57.gp, bf16[4,2,128,128]{3,2,1,0:T(8,128)(2,1)} %get-tuple-element.51.op, ...), custom_call_target="tpu_custom_call" | custom-call | flops 3000000000 | bytes 60000000 | tf_op jit(solution)/shard_map/attend_back/pallas_call | solution.py:622
  158.5 4.3 %collective-permute-done.3.far_in = bf16[2,4,32,656]{3,2,1,0:T(8,128)(2,1)S(1)} collective-permute-done((bf16[2,4,32,656]{3,2,1,0:T(8,128)(2,1)}, bf16[2,4,32,656]{3,2,1,0:T(8,128)(2,1)S(1)}, u32[]{:S(2)}, u32[]{:S(2)}) %collective-permute-start.3) | collective-permute-done | bytes 335904 | tf_op jit(solution)/shard_map/ppermute | solution.py:1932
  162.8 0.0 copy-start.1
  162.8 0.0 collective-permute-done.2.near_in
  162.8 0.0 copy-start
  162.8 0.7 copy-done.1
  163.5 0.2 copy-done
  163.7 58.1 %finish.1 = (bf16[128,1024]{1,0:T(8,128)(2,1)}, f32[128,1024]{1,0:T(8,128)}, f32[32,3072]{1,0:T(8,128)}, f32[32,1024]{1,0:T(8,128)}, f32[32,5248]{1,0:T(8,128)},...) custom-call(bf16[4,2,128,128]{3,2,1,0:T(8,128)(2,1)} %get-tuple-element.59.dqp, ...), custom_call_target="tpu_custom_call" | custom-call | flops 2000000000 | bytes 10000000 | tf_op jit(solution)/shard_map/finish/pallas_call | solution.py:1852
  221.8 3.0 %deliver.1 = (bf16[128,1024]{1,0:T(8,128)(2,1)}, f32[128,1024]{1,0:T(8,128)}, f32[32,3072]{1,0:T(8,128)}, f32[32,1024]{1,0:T(8,128)}, f32[32,5248]{1,0:T(8,128)}...) custom-call(bf16[128,1024]{1,0:T(8,128)(2,1)} %get-tuple-element.74.refs_0_, ...), custom_call_target="tpu_custom_call" | custom-call | tf_op jit(solution)/shard_map/deliver/pallas_call | solution.py:650
Async XLA Ops:
  50.2 20.9 %collective-permute-start.1 = (bf16[4,32,1968]{2,1,0:T(8,128)(2,1)}, bf16[4,32,1968]{2,1,0:T(8,128)(2,1)S(1)}, u32[]{:S(2)}, u32[]{:S(2)}) collective-permute-start(bf16[4,32,1968]{2,1,0:T(8,128)(2,1)} %get-tuple-element.55.wm_own), channel_id=1, source_target_pairs={{2,0},{3,1},{4,2},{5,3},{6,4},{7,5},{10,8},{11,9},{12,10},{13,11},... | collective-permute-start | bytes 1511432 | tf_op jit(solution)/shard_map/ppermute | solution.py:1925
  51.5 19.6 %collective-permute-start = (bf16[4,32,1968]{2,1,0:T(8,128)(2,1)}, bf16[4,32,1968]{2,1,0:T(8,128)(2,1)S(1)}, u32[]{:S(2)}, u32[]{:S(2)}) collective-permute-start(bf16[4,32,1968]{2,1,0:T(8,128)(2,1)} %get-tuple-element.55.wm_own), channel_id=1, source_target_pairs={{0,2},{1,3},{2,4},{3,5},{4,6},{5,7},{8,10},{9,11},{10,12},{11,13},... | collective-permute-start | bytes 1511432 | tf_op jit(solution)/shard_map/ppermute | solution.py:1924
  71.1 0.8 copy-start.2
  71.1 1.0 copy-start.3
  138.0 24.7 %collective-permute-start.2 = (bf16[3,4,32,656]{3,2,1,0:T(8,128)(2,1)}, bf16[3,4,32,656]{3,2,1,0:T(8,128)(2,1)S(1)}, u32[]{:S(2)}, u32[]{:S(2)}) collective-permute-start(bf16[3,4,32,656]{3,2,1,0:T(8,128)(2,1)} %get-tuple-element.71), channel_id=1, source_target_pairs={{0,2},{1,3},{2,0},{3,1},{4,6},{5,7},{6,4},{7,5},{8,10},{9,11},{10,... | collective-permute-start | bytes 1511432 | tf_op jit(solution)/shard_map/ppermute | solution.py:1932
  139.0 23.8 %collective-permute-start.3 = (bf16[2,4,32,656]{3,2,1,0:T(8,128)(2,1)}, bf16[2,4,32,656]{3,2,1,0:T(8,128)(2,1)S(1)}, u32[]{:S(2)}, u32[]{:S(2)}) collective-permute-start(bf16[2,4,32,656]{3,2,1,0:T(8,128)(2,1)} %get-tuple-element.73), channel_id=1, source_target_pairs={{0,6},{1,7},{2,4},{3,5},{4,2},{5,3},{6,0},{7,1},{8,14},{9,15},{10,... | collective-permute-start | bytes 1007624 | tf_op jit(solution)/shard_map/ppermute | solution.py:1932
  162.8 0.7 copy-start.1
  162.8 0.9 copy-start

commit v6 on v5

--- a/solution.py
+++ b/solution.py
@@ -856,14 +856,193 @@
     return jnp.where(lane < HEAD_DIM, left, right)
 
 
-def project_kernel(
+class Reduce:
+    def __init__(self, term, core_in, line_out, line_in, here, sems):
+        self.term, self.core_in, self.line_out, self.line_in = term, core_in, line_out, line_in
+        self.here, self.parts = here, here.parts
+        self.core_s, self.core_r, self.line_s, self.line_r = sems
+
+    def _core(self):
+        return remote(
+            self.term.at[:, 1 - self.here.share],
+            self.core_in,
+            self.core_s.at[0],
+            self.core_r.at[0],
+            self.here.beside,
+        )
+
+    def _line(self, i):
+        return remote(
+            self.line_out[i],
+            self.line_in.at[i],
+            self.line_s.at[i],
+            self.line_r.at[i],
+            self.here.along[i],
+        )
+
+    def _sum(self, there):
+        own = self.term[there, self.here.share].astype(jnp.float32)
+        return own + self.core_in[there].astype(jnp.float32)
+
+    def start(self):
+        self._core().start()
+
+    def core_sums(self):
+        self._core().wait_recv()
+        return self._sum
+
+    def middle(self):
+        self._core().wait_recv()
+        for i, there in enumerate(self.here.there):
+            self.line_out[i][...] = self._sum(there).astype(jnp.bfloat16)
+            self._line(i).start()
+
+    def close(self):
+        total = self._sum(self.here.part)
+        for i in range(self.parts - 1):
+            self._line(i).wait_recv()
+            total += self.line_in[i].astype(jnp.float32)
+        return total
+
+    def core_finish(self):
+        self._core().wait_send()
+
+    def finish(self):
+        self.core_finish()
+        for i in range(self.parts - 1):
+            self._line(i).wait_send()
+
+
+def reduce_scratch(parts, shape):
+    return [
+        pltpu.VMEM((parts, 2, *shape), jnp.bfloat16),
+        pltpu.VMEM((parts, *shape), jnp.bfloat16),
+        pltpu.VMEM((parts - 1, *shape), jnp.bfloat16),
+        pltpu.VMEM((parts - 1, *shape), jnp.bfloat16),
+        dma(1),
+        dma(1),
+        dma(parts - 1),
+        dma(parts - 1),
+    ]
+
+
+class PairReduce:
+    def __init__(self, core_in, near_out, near_in, far_out, far_in, *sems, term, here):
+        self.term, self.core_in, self.near_out, self.near_in = term, core_in, near_out, near_in
+        self.far_out, self.far_in, self.sems, self.here = far_out, far_in, sems, here
+
+    def _copy(self, step):
+        here = self.here
+        source, target, peer = (
+            (self.term.at[:, 1 - here.share], self.core_in, here.beside),
+            (self.near_out, self.near_in, (here.h, here.near * 2 + here.share)),
+            (self.far_out, self.far_in, (here.h, here.far * 2 + here.share)),
+        )[step]
+        return remote(source, target, self.sems[2 * step].at[0], self.sems[2 * step + 1].at[0], peer)
+
+    def _sum(self, there):
+        own = self.term[there, self.here.share].astype(jnp.float32)
+        return own + self.core_in[there].astype(jnp.float32)
+
+    def start(self):
+        self._copy(0).start()
+
+    def pair(self):
+        self._copy(0).wait_recv()
+        self.near_out[0] = self._sum(self.here.near).astype(jnp.bfloat16)
+        self.near_out[1] = self._sum(self.here.over).astype(jnp.bfloat16)
+        self._copy(1).start()
+
+    def cross(self):
+        self._copy(1).wait_recv()
+        self.far_out[...] = (
+            self._sum(self.here.far) + self.near_in[1].astype(jnp.float32)
+        ).astype(jnp.bfloat16)
+        self._copy(2).start()
+
+    def close(self):
+        self._copy(2).wait_recv()
+        total = self._sum(self.here.part) + self.near_in[0].astype(jnp.float32)
+        return total + self.far_in[...].astype(jnp.float32)
+
+    def finish(self):
+        for step in range(3):
+            self._copy(step).wait_send()
+
+
+def pair_scratch(parts, shape):
+    return [
+        pltpu.VMEM((parts, *shape), jnp.bfloat16),
+        *[pltpu.VMEM((2, *shape), jnp.bfloat16)] * 2,
+        *[pltpu.VMEM(shape, jnp.bfloat16)] * 2,
+        *[dma(1)] * 6,
+    ]
+
+
+def reducer(scratch, here):
+    term, core_in, line_out, line_in, *sems = scratch
+    outs = [line_out.at[i] for i in range(here.parts - 1)]
+    return (term, Reduce(term, core_in, outs, line_in, here, sems))
+
+
+class Swap:
+    def __init__(self, out, landed, send_s, recv_s, here):
+        self.out, self.landed, self.here = out, landed, here
+        self.send_s, self.recv_s = send_s, recv_s
+
+    def start(self):
+        here = self.here
+        self.copies = [
+            send(self.out.at[peer[0]], self.landed.at[here.h], self.send_s.at[i], self.recv_s.at[i], peer)
+            for i, peer in enumerate(here.across)
+        ]
+        self.landed[here.h] = self.out[here.h]
+
+    def arrive(self):
+        for copy in self.copies:
+            copy.wait_recv()
+
+    def finish(self):
+        for copy in self.copies:
+            copy.wait_send()
+
+
+def swap_scratch(heads, shape):
+    return [
+        pltpu.VMEM((heads, *shape), jnp.bfloat16),
+        pltpu.VMEM((heads, *shape), jnp.bfloat16),
+        dma(heads - 1),
+        dma(heads - 1),
+    ]
+
+
+def run_of(here, i):
+    x, y = lax.rem(here.h, 2), here.h // 2
+    x = x + (1 - i // 2) * (1 - 2 * x)
+    y = y + (1 - i % 2) * (1 - 2 * y)
+    return y * 2 + x
+
+
+def load(pairs, sems):
+    copies = [pltpu.make_async_copy(*pair, sems.at[i]) for i, pair in enumerate(pairs)]
+    for copy in copies:
+        copy.start()
+    return copies
+
+
+def forward_kernel(
     H, A, tok_in, cot_in, wq_in, gain_one, gain_two, w_in_in, w_down_in, w_out_in, lengths,
-    kv_all, q_all, tok_out, cot_all, wq_out, wm_all, wo_all, gain_rows, cos_out, sin_out,
-    cot, w_in, w_down, w_out, tok_all, wq_all, cos_all, sin_all,
-    wq_st, wm_src, kv_send, q_send, q_runs, hats, gain_src, gain_st, gain_tile, gain_all,
-    load_s, store_s, own_s, kv_o, q_o,
+    kv_out, q_out, op_out, lse, go, tok_out, wq_out, cos_out, sin_out, gain_rows, gain_part, mixed_out, middle_out,
+    base_out, parts_out, kept_out, up_out, near_to, over_to, far_to,
+    cot, w_in, w_down, w_out, tok_all, cot_all, wq_all, cos_all, sin_all,
+    wq_st, wm_src, wm_own, wo_all, kv, kv_send, q_all, q_send, q_runs, hats, gain_src, gain_st, gain_tile, gain_all,
+    bounds, s_scr, op, mx_in, mixed_own, mixed_early, mixed_late, wm_all, middle, normed, act, lift,
+    g2_send, g2_in, g2_own, gm_send, in_term, in_core, down_term, down_core, down_send, down_in,
+    out_base, out_parts, grad_middle, kept, up_far, near_out, over_out, far_out,
+    load_s, store_s, own_s, o_s,
     tok_s, tok_r, wq_s, wq_r, wm_s, wm_r, ga_s, ga_r, gb_s, gb_r, wx_s, wx_r, wf_s, wf_r, cot_s, cot_r,
-    q_s, q_r, kv_s, kv_r, kc_s, kc_r, *line,
+    q_s, q_r, kv_s, kv_r, kc_s, kc_r, mx_s, mx_r, ma_s, ma_r, g2_s, g2_r, gm_s, gm_r,
+    in_core_s, in_core_r, down_core_s, down_core_r, pair_s, pair_r, *line,
 ):
     f32, bf16 = jnp.float32, jnp.bfloat16
     R, W = tok_all.shape[1:]
@@ -899,7 +1078,13 @@
     gain_src[0:1, :D] = gain_one[...].astype(f32)
     gain_src[1:2, :D] = gain_two[...].astype(f32)
     gain_src[...] = pltpu.roll(gain_src[...], h * D, 1)
-    meet([*across, *along, beside, *here.askew])
+    others = [
+        (run_of(here, i), lax.rem(part + j, A) * 2 + share)
+        for i in range(H)
+        for j in range(A)
+        if i < H - 1 or j
+    ]
+    meet([*others, *here.askew, beside])
 
     for i, peer in enumerate(across):
         for source, target in slices(wq_in, wq_st, peer[0]):
@@ -921,10 +1106,8 @@
         wm_src[place, :, :F] = w_in[:, place * F : (place + 1) * F]
         wm_src[place, :, F : 2 * F] = w_in[:, (H + place) * F : (H + place + 1) * F]
         wm_src[place, :, 2 * F :] = w_down[:, place * F : (place + 1) * F]
-    stores += [
-        local(wm_src.at[h], wm_all.at[h], own_s.at[1]),
-        local(cot, cot_all.at[h], own_s.at[2]),
-    ]
+    wm_own[h] = wm_src[h]
+    cot_all[h] = cot[...]
 
     wide = lax.broadcasted_iota(jnp.int32, (R, 128), 1)
     freqs = jnp.exp(
@@ -993,7 +1176,7 @@
         copy.wait()
     spread.start()
     wm_copies = [
-        send(wm_src.at[peer[0]], wm_all.at[h], wm_s.at[i], wm_r.at[i], peer)
+        send(wm_src.at[peer[0]], wm_own.at[h], wm_s.at[i], wm_r.at[i], peer)
         for i, peer in enumerate(across)
     ]
     cot_gather = CornerGather(
@@ -1037,11 +1220,11 @@
     stores.append(local(wq_all, wq_out, store_s.at[3]))
 
     for run in [run for low in range(H // 2) for run in (low, low + H // 2)]:
-        normed = (hats[run] * gain_rows[0:1, :]).astype(bf16)
+        rounded = (hats[run] * gain_rows[0:1, :]).astype(bf16)
         projected = jnp.zeros((R, 3 * hw), f32)
         for chunk in range(H):
             block = wq_all[chunk].reshape(B * D, 3 * hw)
-            projected += mm(normed[:, chunk * hw : (chunk + 1) * hw], block)
+            projected += mm(rounded[:, chunk * hw : (chunk + 1) * hw], block)
         cosine, sine = cos_all[run], sin_all[run]
         for slab in range(hw // 128):
             at = slab * 128
@@ -1051,9 +1234,9 @@
             kv_send[2 * slab, run] = join(key, 0, value, 0).astype(bf16)
             kv_send[2 * slab + 1, run] = join(key, 1, value, 1).astype(bf16)
         for i, peer in enumerate(along):
-            send(kv_send.at[here.there[i], run], kv_all.at[run, b], kv_s.at[i], kv_r.at[i], peer)
-        send(kv_send.at[part, run], kv_all.at[run, b], kc_s.at[0], kc_r.at[0], beside)
-        stores.append(local(kv_send.at[part, run], kv_all.at[run, b], kv_o.at[run]))
+            send(kv_send.at[here.there[i], run], kv.at[run, b], kv_s.at[i], kv_r.at[i], peer)
+        send(kv_send.at[part, run], kv.at[run, b], kc_s.at[0], kc_r.at[0], beside)
+        kv[run, b] = kv_send[part, run]
         if run >= H // 2:
             low = run - H // 2
             for a in range(A):
@@ -1063,13 +1246,13 @@
                 ).astype(bf16)
             for i, peer in enumerate(along):
                 send(q_send.at[here.there[i], low], q_all.at[part, low], q_s.at[i], q_r.at[i], peer)
-            stores.append(local(q_send.at[part, low], q_all.at[part, low], q_o.at[low]))
+            q_all[part, low] = q_send[part, low]
 
     kv_copies = [
-        remote(kv_send.at[here.there[i]], kv_all.at[:, b], kv_s.at[i], kv_r.at[i], peer)
+        remote(kv_send.at[here.there[i]], kv.at[:, b], kv_s.at[i], kv_r.at[i], peer)
         for i, peer in enumerate(along)
     ]
-    kc_copies = [remote(kv_send.at[part], kv_all.at[:, b], kc_s.at[0], kc_r.at[0], beside)]
+    kc_copies = [remote(kv_send.at[part], kv.at[:, b], kc_s.at[0], kc_r.at[0], beside)]
     q_copies = [
         remote(q_send.at[here.there[i]], q_all.at[part], q_s.at[i], q_r.at[i], peer)
         for i, peer in enumerate(along)
@@ -1077,368 +1260,169 @@
     spread.forward()
     cot_gather.forward()
 
+    tiles = H * A // 2
+    spot = lax.broadcasted_iota(jnp.int32, (1, 2 * R), 1)
+    spot = spot + jnp.where(spot < R, 0, R) + share * R
+    for tile in range(tiles):
+        place = spot + tile * 4 * R
+
+        def one(d, carried, place=place):
+            low, begin, stop = carried
+            high = low + lengths[d]
+            inside = (place >= low) & (place < high)
+            return (high, jnp.where(inside, low, begin), jnp.where(inside, high, stop))
+
+        unused, bounds[tile, 0:1], bounds[tile, 1:2] = lax.fori_loop(
+            0, lengths.shape[0], one, (jnp.int32(0), jnp.zeros_like(place), jnp.zeros_like(place))
+        )
+
     def pass_on(i):
         there = wo_all.at[here.places[i], :, share]
         kc_copies.append(send(there, there, wf_s.at[i], wf_r.at[i], beside))
 
     pass_on(1)
     pass_on(2)
-    spread.arrive()
-    pass_on(0)
     for i, copy in enumerate(kv_copies):
         copy.wait_recv()
-        there = kv_all.at[:, here.back[i] * 2 + share]
+        there = kv.at[:, here.back[i] * 2 + share]
         kc_copies.append(send(there, there, kc_s.at[i + 1], kc_r.at[i + 1], beside))
+    wm_lines = []
+    for copy in wm_copies:
+        copy.wait_recv()
+    for half in range(2):
+        rows = pl.ds(half * (H // 2), H // 2)
+        wm_lines.append(
+            LineGather(
+                lambda block, side, rows=rows: wm_all.at[rows, block * 2 + side],
+                wm_own.at[rows],
+                here,
+                line[5 * half + 15 : 5 * half + 20],
+            )
+        )
+        wm_lines[half].start()
+    wm_all[:, b] = wm_own[...]
+    for copy in [*kc_copies, *q_copies]:
+        copy.wait_recv()
+    stores += [local(kv, kv_out, store_s.at[4]), local(q_all, q_out, store_s.at[5])]
+    spread.arrive()
+    last = len(kc_copies)
+    pass_on(0)
+
+    steps = H * B * R // KEY_STEP
+    at = lax.broadcasted_iota(jnp.int32, (KEY_STEP, 2 * R), 0)
+    spans = KEY_STEP // R
+
+    def attend_pair(hh, u):
+        results = []
+        for side in (0, 1):
+            tile = (hh + side * (H // 2)) * (A // 2) + u
+            low, high = max(tile - 2, 0), min(tile + 3, steps)
+            begin, stop = bounds[tile, 0:1], bounds[tile, 1:2]
+            pair = q_all[2 * u : 2 * u + 2, hh].reshape(2 * R, 128)
+            query = (halves(pair, side) * HEAD_DIM**-0.5).astype(bf16)
+
+            def keys_at(n):
+                return kv[n * spans // B, pl.ds(lax.rem(n * spans, B), spans)].reshape(KEY_STEP, 128)
+
+            def score(n, top, low=low, begin=begin, stop=stop, query=query):
+                same = (at >= begin - n * KEY_STEP) & (at < stop - n * KEY_STEP)
+                scores = jnp.where(same, mm(keys_at(n), query, NT), neg_large)
+                s_scr[n - low] = scores
+                return jnp.maximum(top, jnp.max(scores, axis=0, keepdims=True))
+
+            top = lax.fori_loop(low, high, score, jnp.full((1, 2 * R), neg_large, f32))
+
+            def mix(n, carried, low=low, top=top):
+                total, acc = carried
+                weights = jnp.exp(s_scr[n - low] - top)
+                total = total + jnp.sum(weights, axis=0, keepdims=True)
+                return (total, acc + mm(keys_at(n), weights.astype(bf16), TN))
+
+            total, acc = lax.fori_loop(
+                low, high, mix, (jnp.zeros((1, 2 * R), f32), jnp.zeros((128, 2 * R), f32))
+            )
+            lse[tile] = top + jnp.log(total)
+            results.append(acc[HEAD_DIM:] / total)
+        both = jnp.concatenate(results, axis=0).T.astype(bf16)
+        op[hh, 2 * u : 2 * u + 2] = both.reshape(2, R, 128)
+
+    def mixed_out_copies(hh):
+        mx_in[hh, part] = op[hh, part]
+        return [
+            send(op.at[hh, here.there[i]], mx_in.at[hh, part], mx_s.at[n], mx_r.at[n], peer)
+            for i, peer in enumerate(along)
+            for n in [hh * (A - 1) + i]
+        ]
+
+    ma_copies, mixed_all = {}, (mixed_early, mixed_late)
+
+    def assemble(hh, copies):
+        for copy in copies:
+            copy.wait_recv()
+        for side in (0, 1):
+            run = hh + side * (H // 2)
+            slabs = []
+            for slab in range(hw // 128):
+                left, right = mx_in[hh, 2 * slab].astype(f32), mx_in[hh, 2 * slab + 1].astype(f32)
+                slabs.append(join(left, side, right, side))
+            mixed = jnp.concatenate(slabs, axis=1).astype(bf16)
+            mixed_own[run] = mixed
+            for i, peer in enumerate(across):
+                ma_copies[i, run] = send(
+                    mixed_own.at[run], mixed_all[hh].at[h, side], ma_s.at[i * H + run], ma_r.at[i * H + run], peer
+                )
+
+    def project_own(runs):
+        for run in runs:
+            middle[run] = tok_all[run].astype(f32) + mm(mixed_own[run], wo_rows(h))
+
+    def project_others(runs):
+        for i in range(H - 1):
+            for run in runs:
+                ma_copies[i, run].wait_recv()
+        for source in here.places:
+            for run in runs:
+                mixed = mixed_all[run % (H // 2)][source, run // (H // 2)]
+                middle[run] += mm(mixed, wo_rows(source))
+
+    def wo_rows(source):
+        return wo_all[source].reshape(hw, W)
+
+    attend_pair(0, 0)
+    attend_pair(0, 1)
+    mx_copies = mixed_out_copies(0)
+    wm_lines[0].step(1)
+    attend_pair(1, 0)
+    wm_lines[1].step(1)
+    assemble(0, mx_copies)
+    attend_pair(1, 1)
+    mx_late = mixed_out_copies(1)
+    stores += [local(op.at[hh], op_out.at[:, hh], o_s.at[hh]) for hh in range(H // 2)]
+    wm_lines[0].step(2)
     cot_gather.arrive()
-    for copy in [*kc_copies, *q_copies, *wm_copies]:
-        copy.wait_recv()
-    for copy in [*kc_copies, *q_copies, *wm_copies, *wq_copies, *gain_copies, *tok_copies, *kv_copies]:
-        copy.wait_send()
-    for copy in stores[1:]:
-        copy.wait()
-    for item in (spread, cot_gather, wo_line, *wq_lines):
-        item.finish()
-
-
-def project(tokens, cotangent, w_qkv, gain_one, gain_two, w_in, w_down, w_out, lengths):
-    R, W = tokens.shape
-    H, B = lax.axis_size("head"), lax.axis_size("blk")
-    A = B // 2
-    hw = W // H
-    D = w_qkv.shape[0]
-    F = w_down.shape[1] // H
-    f32, bf16 = jnp.float32, jnp.bfloat16
-    shape = jax.ShapeDtypeStruct
-    buffer = lambda *sizes: pltpu.VMEM(sizes, bf16)
-    return pl.pallas_call(
-        partial(project_kernel, H, A),
-        in_specs=[*[anywhere()] * 3, *[in_vmem()] * 2, *[anywhere()] * 3, in_smem()],
-        out_specs=[*[anywhere()] * 7, in_vmem(), *[anywhere()] * 2],
-        out_shape=[
-            shape((H, B, R, 128), bf16),
-            shape((A, H // 2, R, 128), bf16),
-            shape((H, R, W), bf16),
-            shape((H, R, W), bf16),
-            shape((H, B, D, 3 * hw), bf16),
-            shape((H, D, 3 * F), bf16),
-            shape((H, A, 2, D, W), bf16),
-            shape((8, W), f32),
-            shape((H, R, 128), f32),
-            shape((H, R, 128), f32),
-        ],
-        scratch_shapes=[
-            buffer(R, W),
-            buffer(*w_in.shape),
-            buffer(*w_down.shape),
-            buffer(*w_out.shape),
-            buffer(H, R, W),
-            buffer(H, B, D, 3 * hw),
-            pltpu.VMEM((H, R, 128), f32),
-            pltpu.VMEM((H, R, 128), f32),
-            buffer(H, D, 3 * hw),
-            buffer(H, D, 3 * F),
-            buffer(A, H, R, 128),
-            buffer(A, H // 2, R, 128),
-            pltpu.VMEM((H, R, hw), f32),
-            pltpu.VMEM((H, R, W), f32),
-            pltpu.VMEM((8, 128), f32),
-            pltpu.VMEM((H - 1, 8, 128), f32),
-            pltpu.VMEM((8, 128), f32),
-            pltpu.VMEM((B, 8, 128), f32),
-            dma(8),
-            dma(4),
-            dma(3),
-            dma(H),
-            dma(H // 2),
-            *[dma(H - 1)] * 8,
-            *[dma(B - 1)] * 2,
-            *[dma(4)] * 2,
-            *[dma(H - 1)] * 2,
-            *[dma(4)] * 2,
-            *[dma(A - 1)] * 4,
-            *[dma(A)] * 2,
-            *line_sems(A) * 3,
-        ],
-        compiler_params=params(0),
-        cost_estimate=pl.CostEstimate(flops=10**9, bytes_accessed=10**7, transcendentals=10**6),
-        name="project",
-    )(tokens, cotangent, w_qkv, gain_one, gain_two, w_in, w_down, w_out, lengths)
-
-
-class Reduce:
-    def __init__(self, term, core_in, line_out, line_in, here, sems):
-        self.term, self.core_in, self.line_out, self.line_in = term, core_in, line_out, line_in
-        self.here, self.parts = here, here.parts
-        self.core_s, self.core_r, self.line_s, self.line_r = sems
-
-    def _core(self):
-        return remote(
-            self.term.at[:, 1 - self.here.share],
-            self.core_in,
-            self.core_s.at[0],
-            self.core_r.at[0],
-            self.here.beside,
-        )
-
-    def _line(self, i):
-        return remote(
-            self.line_out[i],
-            self.line_in.at[i],
-            self.line_s.at[i],
-            self.line_r.at[i],
-            self.here.along[i],
-        )
-
-    def _sum(self, there):
-        own = self.term[there, self.here.share].astype(jnp.float32)
-        return own + self.core_in[there].astype(jnp.float32)
-
-    def start(self):
-        self._core().start()
-
-    def core_sums(self):
-        self._core().wait_recv()
-        return self._sum
-
-    def middle(self):
-        self._core().wait_recv()
-        for i, there in enumerate(self.here.there):
-            self.line_out[i][...] = self._sum(there).astype(jnp.bfloat16)
-            self._line(i).start()
-
-    def close(self):
-        total = self._sum(self.here.part)
-        for i in range(self.parts - 1):
-            self._line(i).wait_recv()
-            total += self.line_in[i].astype(jnp.float32)
-        return total
-
-    def core_finish(self):
-        self._core().wait_send()
-
-    def finish(self):
-        self.core_finish()
-        for i in range(self.parts - 1):
-            self._line(i).wait_send()
-
-
-def reduce_scratch(parts, shape):
-    return [
-        pltpu.VMEM((parts, 2, *shape), jnp.bfloat16),
-        pltpu.VMEM((parts, *shape), jnp.bfloat16),
-        pltpu.VMEM((parts - 1, *shape), jnp.bfloat16),
-        pltpu.VMEM((parts - 1, *shape), jnp.bfloat16),
-        dma(1),
-        dma(1),
-        dma(parts - 1),
-        dma(parts - 1),
-    ]
-
-
-class PairReduce:
-    def __init__(self, core_in, near_out, near_in, far_out, far_in, *sems, term, here):
-        self.term, self.core_in, self.near_out, self.near_in = term, core_in, near_out, near_in
-        self.far_out, self.far_in, self.sems, self.here = far_out, far_in, sems, here
-
-    def _copy(self, step):
-        here = self.here
-        source, target, peer = (
-            (self.term.at[:, 1 - here.share], self.core_in, here.beside),
-            (self.near_out, self.near_in, (here.h, here.near * 2 + here.share)),
-            (self.far_out, self.far_in, (here.h, here.far * 2 + here.share)),
-        )[step]
-        return remote(source, target, self.sems[2 * step].at[0], self.sems[2 * step + 1].at[0], peer)
-
-    def _sum(self, there):
-        own = self.term[there, self.here.share].astype(jnp.float32)
-        return own + self.core_in[there].astype(jnp.float32)
-
-    def start(self):
-        self._copy(0).start()
-
-    def pair(self):
-        self._copy(0).wait_recv()
-        self.near_out[0] = self._sum(self.here.near).astype(jnp.bfloat16)
-        self.near_out[1] = self._sum(self.here.over).astype(jnp.bfloat16)
-        self._copy(1).start()
-
-    def cross(self):
-        self._copy(1).wait_recv()
-        self.far_out[...] = (
-            self._sum(self.here.far) + self.near_in[1].astype(jnp.float32)
-        ).astype(jnp.bfloat16)
-        self._copy(2).start()
-
-    def close(self):
-        self._copy(2).wait_recv()
-        total = self._sum(self.here.part) + self.near_in[0].astype(jnp.float32)
-        return total + self.far_in[...].astype(jnp.float32)
-
-    def finish(self):
-        for step in range(3):
-            self._copy(step).wait_send()
-
-
-def pair_scratch(parts, shape):
-    return [
-        pltpu.VMEM((parts, *shape), jnp.bfloat16),
-        *[pltpu.VMEM((2, *shape), jnp.bfloat16)] * 2,
-        *[pltpu.VMEM(shape, jnp.bfloat16)] * 2,
-        *[dma(1)] * 6,
-    ]
-
-
-def reducer(scratch, here):
-    term, core_in, line_out, line_in, *sems = scratch
-    outs = [line_out.at[i] for i in range(here.parts - 1)]
-    return (term, Reduce(term, core_in, outs, line_in, here, sems))
-
-
-class Swap:
-    def __init__(self, out, landed, send_s, recv_s, here):
-        self.out, self.landed, self.here = out, landed, here
-        self.send_s, self.recv_s = send_s, recv_s
-
-    def start(self):
-        here = self.here
-        self.copies = [
-            send(self.out.at[peer[0]], self.landed.at[here.h], self.send_s.at[i], self.recv_s.at[i], peer)
-            for i, peer in enumerate(here.across)
-        ]
-        self.landed[here.h] = self.out[here.h]
-
-    def arrive(self):
-        for copy in self.copies:
-            copy.wait_recv()
-
-    def finish(self):
-        for copy in self.copies:
-            copy.wait_send()
-
-
-def swap_scratch(heads, shape):
-    return [
-        pltpu.VMEM((heads, *shape), jnp.bfloat16),
-        pltpu.VMEM((heads, *shape), jnp.bfloat16),
-        dma(heads - 1),
-        dma(heads - 1),
-    ]
-
-
-def run_of(here, i):
-    x, y = lax.rem(here.h, 2), here.h // 2
-    x = x + (1 - i // 2) * (1 - 2 * x)
-    y = y + (1 - i % 2) * (1 - 2 * y)
-    return y * 2 + x
-
-
-def load(pairs, sems):
-    copies = [pltpu.make_async_copy(*pair, sems.at[i]) for i, pair in enumerate(pairs)]
-    for copy in copies:
-        copy.start()
-    return copies
-
-
-def feed_kernel(
-    H, A, op, tok_in, cot_in, wo_in, wm_own, wm_before, wm_after, gain_rows,
-    out_base, out_parts, grad_middle, go, kept, up_far, near_out, over_out, far_out, mixed_own, gain_part, *rest,
-):
-    (
-        tok_all, cot_all, wo, mx_in, mixed_all, wm_all, middle, normed, act, lift,
-        g2_send, g2_in, g2_own, gm_send, in_term, in_core, in_core_s, in_core_r, down_send, down_in, pair_s, pair_r,
-        load_s, mx_s, mx_r, ma_s, ma_r, g2_s, g2_r, gm_s, gm_r, *more,
-    ) = rest
-    f32, bf16 = jnp.float32, jnp.bfloat16
-    R, W = tok_all.shape[1:]
-    B = 2 * A
-    hw = W // H
-    D = wm_own.shape[1]
-    F = wm_own.shape[2] // 3
-    here = Place(A)
-    h, b, part, share = here.h, here.b, here.part, here.share
-    across, along = here.across, here.along
-    line, (down_term, down_core, *down_sems) = more[:5], more[5:9]
-    down_sum = Reduce(down_term, down_core, None, None, here, [*down_sems, None, None])
-    in_sum = Reduce(in_term, in_core, None, None, here, [in_core_s, in_core_r, None, None])
-    near, over, far = here.near, here.over, here.far
-    slot = lambda block: wm_all.at[:, block * 2 + share]
-    own_loads = load(
-        [(wm_own, slot(part)), (tok_in, tok_all), (wo_in, wo), (cot_in, cot_all)], load_s
-    )
-    near_loads = [
-        pltpu.make_async_copy(wm_before, slot(part - 1), load_s.at[4]),
-        pltpu.make_async_copy(wm_after, slot(part + 1), load_s.at[5]),
-    ]
-
-    @pl.when(part > 0)
-    def _():
-        near_loads[0].start()
-
-    @pl.when(part < A - 1)
-    def _():
-        near_loads[1].start()
-
-    others = [
-        (run_of(here, i), lax.rem(part + j, A) * 2 + share)
-        for i in range(H)
-        for j in range(A)
-        if i < H - 1 or j
-    ]
-    meet([*others, here.beside])
-
-    mx_copies = [
-        send(op.at[here.there[i]], mx_in.at[part], mx_s.at[i], mx_r.at[i], peer)
-        for i, peer in enumerate(along)
-    ]
-    gather = LineGather(lambda block, side: wm_all.at[:, block * 2 + side], wm_own, here, line)
-    gather.start_from({1: wm_before, -1: wm_after})
-    mx_in[part] = op[part]
-    for copy in own_loads[:3]:
-        copy.wait()
-    for copy in mx_copies:
-        copy.wait_recv()
-    for run in range(H):
-        side, at = run // (H // 2), run % (H // 2)
-        for slab in range(hw // 128):
-            left, right = mx_in[2 * slab, at].astype(f32), mx_in[2 * slab + 1, at].astype(f32)
-            mixed_own[run, :, slab * 128 : (slab + 1) * 128] = join(left, side, right, side).astype(bf16)
-    ma_copies = [
-        send(mixed_own, mixed_all.at[h], ma_s.at[i], ma_r.at[i], peer) for i, peer in enumerate(across)
-    ]
-    mixed_all[h] = mixed_own[...]
-
-    def project_out(source, first):
-        def one(run, carried):
-            before = tok_all[run].astype(f32) if first else middle[run]
-            middle[run] = before + mm(mixed_all[source, run], wo[source])
-            return carried
-
-        lax.fori_loop(0, H, one, 0)
-
-    project_out(h, True)
-    gather.step(2)
-    for i in (1, 2, 0):
-        ma_copies[i].wait_recv()
-        project_out(here.places[i], False)
-
-    def norm_run(run, carried):
+    kc_copies[last].wait_recv()
+    early, late = (0, H // 2), (1, H // 2 + 1)
+    project_own(early)
+    assemble(1, mx_late)
+    stores.append(local(mixed_own, mixed_out, store_s.at[7]))
+    project_own(late)
+    wm_lines[1].step(2)
+    project_others(early)
+    wm_lines[0].step(3)
+    project_others(late)
+
+    def norm_two(run, carried):
         hat, unused = standardize(middle[run])
         normed[run] = (hat * gain_rows[1:2, :]).astype(bf16)
         return carried
 
-    lax.fori_loop(0, H, norm_run, 0)
-    own_loads[3].wait()
-
-    @pl.when(part > 0)
-    def _():
-        near_loads[0].wait()
-
-    @pl.when(part < A - 1)
-    def _():
-        near_loads[1].wait()
-
-    gather.step(3)
-    gather.arrive()
+    lax.fori_loop(0, H, norm_two, 0)
+    wm_lines[1].step(3)
+    for item in wm_lines:
+        item.arrive()
+    down_sum = Reduce(down_term, down_core, None, None, here, [down_core_s, down_core_r, None, None])
+    in_sum = Reduce(in_term, in_core, None, None, here, [in_core_s, in_core_r, None, None])
+    near, over, far = here.near, here.over, here.far
 
     def block(chunk):
         return wm_all[chunk].reshape(B * D, 3 * F)
@@ -1507,11 +1491,12 @@
     gain_part[...] = jnp.broadcast_to(jnp.sum(grad * hat, axis=0, keepdims=True), gain_part.shape)
     total = cot_all[h].astype(f32) + norm_back(grad, hat, scale, gain_rows[1:2, :])
     grad_middle[...] = total
+    stores.append(local(grad_middle, middle_out, store_s.at[8]))
     branch = total.astype(bf16)
     gm_copies = []
     for i in range(H):
         place = run_of(here, i)
-        mixed_grad = mm(branch, wo[place], NT)
+        mixed_grad = mm(branch, wo_rows(place), NT)
         for a in range(A):
             slab = mixed_grad[:, a // 2 * 128 : a // 2 * 128 + 128]
             gm_send[i, a] = join(slab[: R // 2], a % 2, slab[R // 2 :], a % 2).astype(bf16)
@@ -1523,7 +1508,7 @@
                     send(gm_send.at[i, there], go.at[part, h], gm_s.at[n], gm_r.at[n], (place, there * 2 + share))
                 )
             else:
-                go[part, h] = gm_send[i, part]
+                stores.append(local(gm_send.at[i, part], go.at[part, h], own_s.at[1]))
 
     in_of = in_sum.core_sums()
     near_out[0] = in_of(near)[:, :, :F].astype(bf16)
@@ -1534,9 +1519,15 @@
     up_far[...] = in_of(far)[:, :, F:].astype(bf16)
     kept[0] = in_of(part)[:, :, :F]
     kept[1] = in_of(part)[:, :, F:]
+    stores += [
+        local(near_out, near_to, store_s.at[9]),
+        local(over_out, over_to, store_s.at[10]),
+        local(up_far, up_out, store_s.at[11]),
+    ]
     pair_copy.wait_recv()
     kept[2] = down_of(part) + down_in[0].astype(f32)
     far_out[1] = (down_of(far) + down_in[1].astype(f32)).astype(bf16)
+    stores += [local(far_out, far_to, store_s.at[12]), local(kept, kept_out, store_s.at[13])]
 
     def out_run(i, carried):
         run = run_of(here, i)
@@ -1552,76 +1543,137 @@
 
     lax.fori_loop(0, H, out_run, 0)
     out_base[...] += middle[h]
+    stores += [local(out_parts, parts_out, store_s.at[14]), local(out_base, base_out, store_s.at[15])]
     for copy in gm_copies:
         copy.wait_recv()
-    for copy in [*mx_copies, *ma_copies, *gm_copies, pair_copy]:
+    for copy in [
+        *kc_copies, *q_copies, *wm_copies, *wq_copies, *gain_copies, *tok_copies, *kv_copies,
+        *mx_copies, *mx_late, *ma_copies.values(), *gm_copies, pair_copy,
+    ]:
         copy.wait_send()
     for i in range(H - 1):
         part_of(here.places[i], i).wait_send()
-    gather.finish()
+    for copy in stores[1:]:
+        copy.wait()
+    for item in (spread, cot_gather, wo_line, *wq_lines, *wm_lines):
+        item.finish()
     in_sum.core_finish()
     down_sum.core_finish()
 
 
-def feed(op, tok_all, cot_all, wo, wm_own, wm_before, wm_after, gain_rows):
-    A, half, R, lanes = op.shape
-    H = 2 * half
-    W = tok_all.shape[-1]
-    B = 2 * A
+def forward(tokens, cotangent, w_qkv, gain_one, gain_two, w_in, w_down, w_out, lengths):
+    R, W = tokens.shape
+    H, B = lax.axis_size("head"), lax.axis_size("blk")
+    A = B // 2
     hw = W // H
-    D = wm_own.shape[1]
-    F = wm_own.shape[2] // 3
+    D = w_qkv.shape[0]
+    F = w_down.shape[1] // H
     f32, bf16 = jnp.float32, jnp.bfloat16
     shape = jax.ShapeDtypeStruct
+    buffer = lambda *sizes: pltpu.VMEM(sizes, bf16)
+    wide = lambda *sizes: pltpu.VMEM(sizes, f32)
+    outs = [
+        shape((H, B, R, 128), bf16),
+        shape((A, H // 2, R, 128), bf16),
+        shape((A, H // 2, R, 128), bf16),
+        shape((H * A // 2, 1, 2 * R), f32),
+        shape((A, H, R // 2, 128), bf16),
+        shape((H, R, W), bf16),
+        shape((H, B, D, 3 * hw), bf16),
+        shape((H, R, 128), f32),
+        shape((H, R, 128), f32),
+        shape((8, W), f32),
+        shape((8, W), f32),
+        shape((H, R, hw), bf16),
+        shape((R, W), f32),
+        shape((R, W), f32),
+        shape((H - 1, R, W), bf16),
+        shape((3, H, D, F), f32),
+        shape((H, D, F), bf16),
+        shape((3, H, D, F), bf16),
+        shape((H, D, F), bf16),
+        shape((2, H, D, F), bf16),
+    ]
     return pl.pallas_call(
-        partial(feed_kernel, H, A),
-        in_specs=[in_vmem(), *[anywhere()] * 6, in_vmem()],
-        out_specs=[in_vmem()] * 11,
-        out_shape=[
-            shape((R, W), f32),
-            shape((H - 1, R, W), bf16),
-            shape((R, W), f32),
-            shape((A, H, R // 2, 128), bf16),
-            shape((3, H, D, F), f32),
-            shape((H, D, F), bf16),
-            shape((3, H, D, F), bf16),
-            shape((H, D, F), bf16),
-            shape((2, H, D, F), bf16),
-            shape((H, R, hw), bf16),
-            shape((8, W), f32),
+        partial(forward_kernel, H, A),
+        in_specs=[*[anywhere()] * 3, *[in_vmem()] * 2, *[anywhere()] * 3, in_smem()],
+        out_specs=[in_vmem() if n in (3, 9, 10) else anywhere() for n in range(len(outs))],
+        out_shape=outs,
+        scratch_shapes=[
+            buffer(R, W),
+            buffer(*w_in.shape),
+            buffer(*w_down.shape),
+            buffer(*w_out.shape),
+            buffer(H, R, W),
+            buffer(H, R, W),
+            buffer(H, B, D, 3 * hw),
+            wide(H, R, 128),
+            wide(H, R, 128),
+            buffer(H, D, 3 * hw),
+            buffer(H, D, 3 * F),
+            buffer(H, D, 3 * F),
+            buffer(H, A, 2, D, W),
+            buffer(H, B, R, 128),
+            buffer(A, H, R, 128),
+            buffer(A, H // 2, R, 128),
+            buffer(A, H // 2, R, 128),
+            wide(H, R, hw),
+            wide(H, R, W),
+            wide(8, 128),
+            wide(H - 1, 8, 128),
+            wide(8, 128),
+            wide(B, 8, 128),
+            pltpu.VMEM((H * A // 2, 8, 2 * R), jnp.int32),
+            wide(5, KEY_STEP, 2 * R),
+            buffer(H // 2, A, R, 128),
+            buffer(H // 2, A, R, 128),
+            buffer(H, R, hw),
+            *[buffer(H, 2, R, hw)] * 2,
+            buffer(H, B, D, 3 * F),
+            wide(H, R, W),
+            buffer(H, R, W),
+            buffer(H, R, F),
+            buffer(H, R, 2 * F),
+            buffer(H - 1, R, W),
+            buffer(H - 1, R, W),
+            wide(R, W),
+            buffer(H, A, R // 2, 128),
+            buffer(A, 2, H, D, 2 * F),
+            buffer(A, H, D, 2 * F),
+            buffer(A, 2, H, D, F),
+            buffer(A, H, D, F),
+            buffer(2, H, D, F),
+            buffer(2, H, D, F),
+            wide(R, W),
+            buffer(H - 1, R, W),
+            wide(R, W),
+            wide(3, H, D, F),
+            buffer(H, D, F),
+            buffer(3, H, D, F),
+            buffer(H, D, F),
+            buffer(2, H, D, F),
+            dma(8),
+            dma(16),
+            dma(2),
+            dma(H // 2),
+            *[dma(H - 1)] * 8,
+            *[dma(B - 1)] * 2,
+            *[dma(4)] * 2,
+            *[dma(H - 1)] * 2,
+            *[dma(4)] * 2,
+            *[dma(A - 1)] * 4,
+            *[dma(A)] * 2,
+            *[dma((A - 1) * (H // 2))] * 2,
+            *[dma((H - 1) * H)] * 2,
+            *[dma(H - 1)] * 2,
+            *[dma(H * A)] * 2,
+            *[dma(1)] * 6,
+            *line_sems(A) * 5,
         ],
-        scratch_shapes=[
-            pltpu.VMEM((H, R, W), bf16),
-            pltpu.VMEM((H, R, W), bf16),
-            pltpu.VMEM((H, hw, W), bf16),
-            pltpu.VMEM((A, half, R, 128), bf16),
-            pltpu.VMEM((H, H, R, hw), bf16),
-            pltpu.VMEM((H, B, D, 3 * F), bf16),
-            pltpu.VMEM((H, R, W), f32),
-            pltpu.VMEM((H, R, W), bf16),
-            pltpu.VMEM((H, R, F), bf16),
-            pltpu.VMEM((H, R, 2 * F), bf16),
-            *[pltpu.VMEM((H - 1, R, W), bf16)] * 2,
-            pltpu.VMEM((R, W), f32),
-            pltpu.VMEM((H, A, R // 2, 128), bf16),
-            pltpu.VMEM((A, 2, H, D, 2 * F), bf16),
-            pltpu.VMEM((A, H, D, 2 * F), bf16),
-            *[dma(1)] * 2,
-            *[pltpu.VMEM((2, H, D, F), bf16)] * 2,
-            *[dma(1)] * 2,
-            dma(6),
-            *[dma(A - 1)] * 2,
-            *[dma(H - 1)] * 4,
-            *[dma(H * A)] * 2,
-            *line_sems(A),
-            pltpu.VMEM((A, 2, H, D, F), bf16),
-            pltpu.VMEM((A, H, D, F), bf16),
-            *[dma(1)] * 2,
-        ],
-        compiler_params=params(1),
-        cost_estimate=pl.CostEstimate(flops=6 * 10**9, bytes_accessed=10**7, transcendentals=10**6),
-        name="feed",
-    )(op, tok_all, cot_all, wo, wm_own, wm_before, wm_after, gain_rows)
+        compiler_params=params(0),
+        cost_estimate=pl.CostEstimate(flops=10**10, bytes_accessed=10**7, transcendentals=10**6),
+        name="forward",
+    )(tokens, cotangent, w_qkv, gain_one, gain_two, w_in, w_down, w_out, lengths)
 
 
 def finish_kernel(
@@ -1684,9 +1736,6 @@
         send(branch, branch_all.at[h], br_s.at[i], br_r.at[i], peer) for i, peer in enumerate(across)
     ]
     branch_all[h] = branch[...]
-    o_copies = [
-        send(out_parts.at[i], o_in.at[i], o_s.at[i], o_r.at[i], peer) for i, peer in enumerate(across)
-    ]
     for copy in loads[2:]:
         copy.wait()
 
@@ -1698,6 +1747,9 @@
     lax.fori_loop(0, H, norm_run, 0)
     for copy in br_copies:
         copy.wait_recv()
+    o_copies = [
+        send(out_parts.at[i], o_in.at[i], o_s.at[i], o_r.at[i], peer) for i, peer in enumerate(across)
+    ]
 
     def out_tile(n, carried):
         lanes = pl.ds(pl.multiple_of(n * hw, hw), hw)
@@ -1917,17 +1969,13 @@
     A = B // 2
     hw = W // H
     T = H * B * R
-    kv, qp, tok_all, cot_all, wq, wm, wo, gain_rows, cos_all, sin_all = project(
+    (
+        kv, qp, op, lse, gp, tok_all, wq, cos_all, sin_all, gain_rows, gain_part, mixed, grad_middle,
+        out_base, out_parts, kept, up_far, near, over, far,
+    ) = forward(
         tokens, cotangent, w_qkv, attn_gain[None], mlp_gain[None], w_in, w_mlp_out.T, w_attn_out, doc_lengths
     )
     kv = kv.reshape(T, 2 * HEAD_DIM)
-    wm_before = lax.ppermute(wm, "blk", [(i, i + 2) for i in range(B - 2)])
-    wm_after = lax.ppermute(wm, "blk", [(i + 2, i) for i in range(B - 2)])
-    op, lse = attend(doc_lengths, qp, kv)
-    out_base, out_parts, grad_middle, gp, kept, up_far, *out_terms, mixed, gain_part = feed(
-        op, tok_all, cot_all, wo.reshape(H, hw, W), wm, wm_before, wm_after, gain_rows
-    )
-    near, over, far = out_terms
     flipped = lambda flip: [(p, (p // 2 ^ flip) * 2 + p % 2) for p in range(B)]
     near, far = lax.ppermute(near, "blk", flipped(1)), lax.ppermute(far, "blk", flipped(3))
     dqp, dkv = attend_back(doc_lengths, qp, gp, op, lse, kv)

time: 224 us -> 204 us (0.911)
  Pallas kernels: 209 us -> 194 us
  starting transfers between devices: 8.65 us -> 2.74 us
    pallas_call x3 -> x1, Pallas kernels: 131 us -> 117 us  [forward(): pl.pallas_call(partial(forward_kernel, H, A), in_specs=[*[anywhere()] * 3...]
    ppermute x2 -> x0, starting transfers between devices: 5.87 us -> none  [the longest x1 4.58 us: per_device_split(): wm_before = lax.ppermute(wm, 'blk', [(i, i + 2) for i in range(B - 2)])]
  transfers between devices with their start and end apart: 4 -> 2, of which waited for: 1 -> 1; matrix products, arithmetic and copies ran while one was open for 0% -> 0% of each run, Pallas kernels for 15% -> 8%
where the time goes in v6:
time: 204 us; the launch traced here: 203 us
  Pallas kernels  194 us (95%)
  waiting for transfers between devices  4.65 us (2%)
  starting transfers between devices  2.74 us (1%)
    pallas_call x1, Pallas kernels, forward(): pl.pallas_call(partial(forward_kernel, H, A), in_specs=[*[anywhere()] * 3...  117 us
    pallas_call x1, Pallas kernels, finish(): pl.pallas_call(partial(finish_kernel, H, A), in_specs=[in_vmem() if n in...  57.5 us
    pallas_call x1, Pallas kernels, attend_back(): pl.pallas_call(attend_back_kernel, grid_spec=pltpu.PrefetchScalarGridSpec...  17.1 us
    ppermute x1, waiting for transfers between devices, per_device_split(): lax.ppermute(far, 'blk', flipped(3))  4.64 us
  transfers between devices with their start and end apart: 2, of which 1 were waited for; matrix products, arithmetic and copies ran while one was open for 0% of the time, Pallas kernels for 8%

profile of v6, /device:TPU:0, one launch (start us, length us, event | category | flops | bytes accessed | tf_op | source)
XLA Modules:
  0.0 203.3 jit_solution(16821361525279466345)
XLA Ops:
  0.6 116.8 %forward.1 = (bf16[4,8,128,128]{3,2,1,0:T(8,128)(2,1)}, bf16[4,2,128,128]{3,2,1,0:T(8,128)(2,1)}, bf16[4,2,128,128]{3,2,1,0:T(8,128)(2,1)}, f32[8,1,256]{2,1,0:T...) custom-call(bf16[128,1024]{1,0:T(8,128)(2,1)} %tok_in.1, ...), custom_call_target="tpu_custom_call" | custom-call | flops 10000000000 | bytes 10000000 | tf_op jit(solution)/shard_map/forward/pallas_call | solution.py:1597
  117.4 0.9 collective-permute-start
  118.3 1.9 collective-permute-start.1
  120.2 17.1 %attend_back.1 = (bf16[4,2,128,128]{3,2,1,0:T(8,128)(2,1)}, bf16[4096,128]{1,0:T(8,128)(2,1)}) custom-call(s32[32]{0:T(128)} %lengths.3, bf16[4,2,128,128]{3,2,1,0:T(8,128)(2,1)} %get-tuple-element.46.qp, bf16[4,4,64,128]{3,2,1,0:T(8,128)(2,1)} %get-tuple-element.47.gp, bf16[4,2,128,128]{3,2,1,0:T(8,128)(2,1)} %get-tuple-element.48.op, ...), custom_call_target="tpu_custom_call" | custom-call | flops 3000000000 | bytes 60000000 | tf_op jit(solution)/shard_map/attend_back/pallas_call | solution.py:622
  137.3 4.6 %collective-permute-done.1.far_in = bf16[2,4,32,656]{3,2,1,0:T(8,128)(2,1)S(1)} collective-permute-done((bf16[2,4,32,656]{3,2,1,0:T(8,128)(2,1)}, bf16[2,4,32,656]{3,2,1,0:T(8,128)(2,1)S(1)}, u32[]{:S(2)}, u32[]{:S(2)}) %collective-permute-start.1) | collective-permute-done | bytes 335904 | tf_op jit(solution)/shard_map/ppermute | solution.py:1980
  141.9 0.0 copy-start.1
  141.9 0.0 collective-permute-done.near_in
  141.9 0.0 copy-start
  141.9 0.7 copy-done.1
  142.6 0.2 copy-done
  142.8 57.5 %finish.1 = (bf16[128,1024]{1,0:T(8,128)(2,1)}, f32[128,1024]{1,0:T(8,128)}, f32[32,3072]{1,0:T(8,128)}, f32[32,1024]{1,0:T(8,128)}, f32[32,5248]{1,0:T(8,128)},...) custom-call(bf16[4,2,128,128]{3,2,1,0:T(8,128)(2,1)} %get-tuple-element.51.dqp, ...), custom_call_target="tpu_custom_call" | custom-call | flops 2000000000 | bytes 10000000 | tf_op jit(solution)/shard_map/finish/pallas_call | solution.py:1904
  200.3 3.0 %deliver.1 = (bf16[128,1024]{1,0:T(8,128)(2,1)}, f32[128,1024]{1,0:T(8,128)}, f32[32,3072]{1,0:T(8,128)}, f32[32,1024]{1,0:T(8,128)}, f32[32,5248]{1,0:T(8,128)}...) custom-call(bf16[128,1024]{1,0:T(8,128)(2,1)} %get-tuple-element.68.refs_0_, ...), custom_call_target="tpu_custom_call" | custom-call | tf_op jit(solution)/shard_map/deliver/pallas_call | solution.py:650
Async XLA Ops:
  117.4 24.5 %collective-permute-start = (bf16[3,4,32,656]{3,2,1,0:T(8,128)(2,1)}, bf16[3,4,32,656]{3,2,1,0:T(8,128)(2,1)S(1)}, u32[]{:S(2)}, u32[]{:S(2)}) collective-permute-start(bf16[3,4,32,656]{3,2,1,0:T(8,128)(2,1)} %get-tuple-element.65), channel_id=1, source_target_pairs={{0,2},{1,3},{2,0},{3,1},{4,6},{5,7},{6,4},{7,5},{8,10},{9,11},{10,... | collective-permute-start | bytes 1511432 | tf_op jit(solution)/shard_map/ppermute | solution.py:1980
  118.3 23.6 %collective-permute-start.1 = (bf16[2,4,32,656]{3,2,1,0:T(8,128)(2,1)}, bf16[2,4,32,656]{3,2,1,0:T(8,128)(2,1)S(1)}, u32[]{:S(2)}, u32[]{:S(2)}) collective-permute-start(bf16[2,4,32,656]{3,2,1,0:T(8,128)(2,1)} %get-tuple-element.67), channel_id=1, source_target_pairs={{0,6},{1,7},{2,4},{3,5},{4,2},{5,3},{6,0},{7,1},{8,14},{9,15},{10,... | collective-permute-start | bytes 1007624 | tf_op jit(solution)/shard_map/ppermute | solution.py:1980
  141.9 0.7 copy-start.1
  141.9 0.9 copy-start

commit v7 on v6

--- a/solution.py
+++ b/solution.py
@@ -1030,20 +1030,25 @@
     return copies
 
 
-def forward_kernel(
-    H, A, tok_in, cot_in, wq_in, gain_one, gain_two, w_in_in, w_down_in, w_out_in, lengths,
-    kv_out, q_out, op_out, lse, go, tok_out, wq_out, cos_out, sin_out, gain_rows, gain_part, mixed_out, middle_out,
-    base_out, parts_out, kept_out, up_out, near_to, over_to, far_to,
+def layer_kernel(
+    H, A, tok_in, cot_in, wq_in, gain_one_in, gain_two_in, w_in_in, w_down_in, w_out_in, lengths,
+    output, input_grad, qkv_grad, out_grad, in_grad, down_grad, gain_one, gain_two,
     cot, w_in, w_down, w_out, tok_all, cot_all, wq_all, cos_all, sin_all,
     wq_st, wm_src, wm_own, wo_all, kv, kv_send, q_all, q_send, q_runs, hats, gain_src, gain_st, gain_tile, gain_all,
     bounds, s_scr, op, mx_in, mixed_own, mixed_early, mixed_late, wm_all, middle, normed, act, lift,
     g2_send, g2_in, g2_own, gm_send, in_term, in_core, down_term, down_core, down_send, down_in,
-    out_base, out_parts, grad_middle, kept, up_far, near_out, over_out, far_out,
-    load_s, store_s, own_s, o_s,
+    out_base, out_parts, grad_middle, near_out, far_out,
+    lse, go, gain_rows, gain_part, branch_own, branch_all, o_in, from_near, from_far, in_send, in_last,
+    dkv_sum, dq_send, dq_in, dk_send, dk_in, dkv_send, dkv_in, gp, g1_send, g1_in, g1_own,
+    term_out, term_qkv_low, term_qkv_high,
+    load_s, own_s,
     tok_s, tok_r, wq_s, wq_r, wm_s, wm_r, ga_s, ga_r, gb_s, gb_r, wx_s, wx_r, wf_s, wf_r, cot_s, cot_r,
     q_s, q_r, kv_s, kv_r, kc_s, kc_r, mx_s, mx_r, ma_s, ma_r, g2_s, g2_r, gm_s, gm_r,
-    in_core_s, in_core_r, down_core_s, down_core_r, pair_s, pair_r, *line,
+    in_core_s, in_core_r, down_core_s, down_core_r, pair_s, pair_r,
+    br_s, br_r, o_s, o_r, g1_s, g1_r, nr_s, nr_r, dq_s, dq_r, dz_s, dz_r, dk_s, dk_r, *more,
 ):
+    line, more = more[:25], more[25:]
+    term_qkv = (term_qkv_low, term_qkv_high)
     f32, bf16 = jnp.float32, jnp.bfloat16
     R, W = tok_all.shape[1:]
     B = 2 * A
@@ -1075,8 +1080,8 @@
     row = lax.broadcasted_iota(jnp.int32, (8, 128), 0)
     lane = lax.broadcasted_iota(jnp.int32, (8, 128), 1)
     gain_src[...] = jnp.zeros((8, 128), f32)
-    gain_src[0:1, :D] = gain_one[...].astype(f32)
-    gain_src[1:2, :D] = gain_two[...].astype(f32)
+    gain_src[0:1, :D] = gain_one_in[...].astype(f32)
+    gain_src[1:2, :D] = gain_two_in[...].astype(f32)
     gain_src[...] = pltpu.roll(gain_src[...], h * D, 1)
     others = [
         (run_of(here, i), lax.rem(part + j, A) * 2 + share)
@@ -1099,7 +1104,7 @@
     wo_line = LineGather(lambda block, side: wo_all.at[h, block, side], w_out, here, line[:5])
     loads[0].wait()
     wo_line.start()
-    stores = [local(w_out, wo_all.at[h, part, share], own_s.at[0])]
+    own_copy = local(w_out, wo_all.at[h, part, share], own_s.at[0])
     for copy in loads[1:]:
         copy.wait()
     for place in range(H):
@@ -1172,8 +1177,7 @@
         here,
         (wx_s, wx_r),
     )
-    for copy in stores[:1]:
-        copy.wait()
+    own_copy.wait()
     spread.start()
     wm_copies = [
         send(wm_src.at[peer[0]], wm_own.at[h], wm_s.at[i], wm_r.at[i], peer)
@@ -1188,10 +1192,8 @@
     )
     cot_gather.start()
     tables(3)
-    stores += [local(cos_all, cos_out, store_s.at[0]), local(sin_all, sin_out, store_s.at[1])]
     for copy in tok_copies:
         copy.wait_recv()
-    stores.append(local(tok_all, tok_out, store_s.at[2]))
 
     def norm_run(run, carried):
         hat, unused = standardize(tok_all[run].astype(f32))
@@ -1217,7 +1219,6 @@
     wq_lines[1].step(3)
     wq_lines[0].arrive()
     wq_lines[1].arrive()
-    stores.append(local(wq_all, wq_out, store_s.at[3]))
 
     for run in [run for low in range(H // 2) for run in (low, low + H // 2)]:
         rounded = (hats[run] * gain_rows[0:1, :]).astype(bf16)
@@ -1303,7 +1304,6 @@
     wm_all[:, b] = wm_own[...]
     for copy in [*kc_copies, *q_copies]:
         copy.wait_recv()
-    stores += [local(kv, kv_out, store_s.at[4]), local(q_all, q_out, store_s.at[5])]
     spread.arrive()
     last = len(kc_copies)
     pass_on(0)
@@ -1397,14 +1397,12 @@
     assemble(0, mx_copies)
     attend_pair(1, 1)
     mx_late = mixed_out_copies(1)
-    stores += [local(op.at[hh], op_out.at[:, hh], o_s.at[hh]) for hh in range(H // 2)]
     wm_lines[0].step(2)
     cot_gather.arrive()
     kc_copies[last].wait_recv()
     early, late = (0, H // 2), (1, H // 2 + 1)
     project_own(early)
     assemble(1, mx_late)
-    stores.append(local(mixed_own, mixed_out, store_s.at[7]))
     project_own(late)
     wm_lines[1].step(2)
     project_others(early)
@@ -1491,8 +1489,8 @@
     gain_part[...] = jnp.broadcast_to(jnp.sum(grad * hat, axis=0, keepdims=True), gain_part.shape)
     total = cot_all[h].astype(f32) + norm_back(grad, hat, scale, gain_rows[1:2, :])
     grad_middle[...] = total
-    stores.append(local(grad_middle, middle_out, store_s.at[8]))
     branch = total.astype(bf16)
+    branch_own[...] = branch
     gm_copies = []
     for i in range(H):
         place = run_of(here, i)
@@ -1508,26 +1506,18 @@
                     send(gm_send.at[i, there], go.at[part, h], gm_s.at[n], gm_r.at[n], (place, there * 2 + share))
                 )
             else:
-                stores.append(local(gm_send.at[i, part], go.at[part, h], own_s.at[1]))
-
+                go[part, h] = gm_send[i, part]
+
+    br_copies = [
+        send(branch_own, branch_all.at[h], br_s.at[i], br_r.at[i], peer) for i, peer in enumerate(across)
+    ]
+    branch_all[h] = branch
     in_of = in_sum.core_sums()
-    near_out[0] = in_of(near)[:, :, :F].astype(bf16)
-    near_out[1] = in_of(near)[:, :, F:].astype(bf16)
-    near_out[2] = in_of(over)[:, :, F:].astype(bf16)
-    over_out[...] = in_of(over)[:, :, :F].astype(bf16)
-    far_out[0] = in_of(far)[:, :, :F].astype(bf16)
-    up_far[...] = in_of(far)[:, :, F:].astype(bf16)
-    kept[0] = in_of(part)[:, :, :F]
-    kept[1] = in_of(part)[:, :, F:]
-    stores += [
-        local(near_out, near_to, store_s.at[9]),
-        local(over_out, over_to, store_s.at[10]),
-        local(up_far, up_out, store_s.at[11]),
-    ]
+    near_out[0] = in_of(near).astype(bf16)
+    near_out[1] = in_of(over).astype(bf16)
+    near_copy = send(near_out, from_near, nr_s.at[0], nr_r.at[0], (h, near * 2 + share))
     pair_copy.wait_recv()
-    kept[2] = down_of(part) + down_in[0].astype(f32)
-    far_out[1] = (down_of(far) + down_in[1].astype(f32)).astype(bf16)
-    stores += [local(far_out, far_to, store_s.at[12]), local(kept, kept_out, store_s.at[13])]
+    far_out[...] = (down_of(far) + down_in[1].astype(f32)).astype(bf16)
 
     def out_run(i, carried):
         run = run_of(here, i)
@@ -1543,25 +1533,267 @@
 
     lax.fori_loop(0, H, out_run, 0)
     out_base[...] += middle[h]
-    stores += [local(out_parts, parts_out, store_s.at[14]), local(out_base, base_out, store_s.at[15])]
+    o_copies = [
+        send(out_parts.at[i], o_in.at[i], o_s.at[i], o_r.at[i], peer) for i, peer in enumerate(across)
+    ]
+    dkv_sum[...] = jnp.zeros_like(dkv_sum)
     for copy in gm_copies:
         copy.wait_recv()
+    far_copy = send(far_out, from_far, nr_s.at[1], nr_r.at[1], (h, far * 2 + share))
+
+    wide_lane = lax.broadcasted_iota(jnp.int32, (2 * R, 128), 1)
+
+    def attend_back_tile(tile):
+        run, u = tile // (A // 2), tile % (A // 2)
+        side, hh = run // (H // 2), run % (H // 2)
+        low, high = max(tile - 2, 0), min(tile + 3, steps)
+        begin, stop = bounds[tile, 0:1], bounds[tile, 1:2]
+        pair = q_all[2 * u : 2 * u + 2, hh].reshape(2 * R, 128)
+        query = (halves(pair, side) * HEAD_DIM**-0.5).astype(bf16)
+        pieces = []
+        for a in (2 * u, 2 * u + 1):
+            piece = go[a, run].astype(f32)
+            pieces += [pltpu.roll(piece, HEAD_DIM, 1), piece]
+        grad = jnp.where(wide_lane < HEAD_DIM, 0.0, jnp.concatenate(pieces, axis=0))
+        mixed = op[hh, 2 * u : 2 * u + 2].reshape(2 * R, 128).astype(f32)
+        if not side:
+            mixed = pltpu.roll(mixed, HEAD_DIM, 1)
+        delta = jnp.sum((grad * mixed).T, axis=0, keepdims=True)
+        both = jnp.concatenate([query, grad.astype(bf16)], axis=0)
+        logs = lse[tile]
+
+        def step(n, dq):
+            keys = kv[n * spans // B, pl.ds(lax.rem(n * spans, B), spans)].reshape(KEY_STEP, 128)
+            same = (at >= begin - n * KEY_STEP) & (at < stop - n * KEY_STEP)
+            products = mm(keys, both, NT)
+            probs = jnp.where(same, jnp.exp(products[:, : 2 * R] - logs), 0.0)
+            grad_scores = (probs * (products[:, 2 * R :] - delta)).astype(bf16)
+            left = jnp.concatenate([grad_scores, probs.astype(bf16)], axis=1)
+            dkv_sum[n] += mm(left, both)
+            return dq + mm(keys, grad_scores, TN)
+
+        dq = lax.fori_loop(low, high, step, jnp.zeros((128, 2 * R), f32))
+        dq = (dq * HEAD_DIM**-0.5).T
+        for k, a in enumerate((2 * u, 2 * u + 1)):
+            rows = dq[k * R : (k + 1) * R]
+            dq_send[a, run] = join(rows[: R // 2], 0, rows[R // 2 :], 0).astype(bf16)
+
+            @pl.when(part == a)
+            def _(a=a):
+                dq_in[a, run] = dq_send[a, run]
+
+            @pl.when(part != a)
+            def _(a=a):
+                n = part * H + run
+                remote(
+                    dq_send.at[a, run], dq_in.at[part, run], dq_s.at[a * H + run], dq_r.at[n], (h, a * 2 + share)
+                ).start()
+
+    def dk_copy(k):
+        return remote(dk_send.at[k], dk_in.at[k], dk_s.at[k], dk_r.at[k], beside)
+
+    def keys_done(k):
+        for n in range(2):
+            first = pl.multiple_of((2 * n + 1 - share) * R, R)
+            dk_send[k, n] = dkv_sum[k, pl.ds(first, R), :].astype(bf16)
+        dk_copy(k).start()
+
+    def keys_sum(k):
+        dk_copy(k).wait_recv()
+        run = k * spans // B
+        for n in range(2):
+            a = k * spans % B // 2 + n
+            first = pl.multiple_of((2 * n + share) * R, R)
+            summed = dkv_sum[k, pl.ds(first, R), :] + dk_in[k, n].astype(f32)
+            dkv_send[a, run] = summed.astype(bf16)
+
+            @pl.when(part == a)
+            def _(a=a):
+                dkv_in[a, run] = dkv_send[a, run]
+
+            @pl.when(part != a)
+            def _(a=a):
+                n = part * H + run
+                remote(
+                    dkv_send.at[a, run], dkv_in.at[part, run], dz_s.at[a * H + run], dz_r.at[n], (h, a * 2 + share)
+                ).start()
+
+    out_sum, *qkv_sums = (
+        PairReduce(*more[11 * n : 11 * n + 11], term=term, here=here)
+        for n, term in enumerate((term_out, *term_qkv))
+    )
+    gain_scratch, swaps = more[33:41], more[41:]
+    term_gain, gain_sum = reducer(gain_scratch, here)
+    in_swap, qkv_swap, gain_swap = (Swap(*swaps[4 * n : 4 * n + 4], here) for n in range(3))
+
+    def out_tile(n, carried):
+        lanes = pl.ds(pl.multiple_of(n * hw, hw), hw)
+        grads = mm(mixed_own[...].reshape(H * R, hw), branch_all[:, :, lanes].reshape(H * R, hw), TN)
+        term_out[:, :, :, lanes] = grads.astype(bf16).reshape(A, 2, D, hw)
+        return carried
+
+    for tile in range(tiles):
+        attend_back_tile(tile)
+        if tile >= 2:
+            keys_done(tile - 2)
+        if tile >= 3:
+            keys_sum(tile - 3)
+        if tile == 3:
+            for copy in br_copies:
+                copy.wait_recv()
+            lax.fori_loop(0, W // hw, out_tile, 0)
+            out_sum.start()
+        if tile == 4:
+            out_sum.pair()
+        if tile == 6:
+            near_copy.wait_recv()
+            in_send[...] = (in_of(far) + from_near[1].astype(f32)).astype(bf16)
+    for k in (tiles - 2, tiles - 1):
+        keys_done(k)
+    for k in (tiles - 3, tiles - 2, tiles - 1):
+        keys_sum(k)
+    out_sum.cross()
+    last_copy = send(in_send, in_last, nr_s.at[2], nr_r.at[2], (h, far * 2 + share))
+    for source in here.back:
+        for run in range(H):
+            n = source * H + run
+            remote(dq_send.at[0, 0], dq_in.at[0, 0], dq_s.at[n], dq_r.at[n], beside).wait_recv()
+            remote(dkv_send.at[0, 0], dkv_in.at[0, 0], dz_s.at[n], dz_r.at[n], beside).wait_recv()
+    for run in range(H):
+        cosine, sine = cos_all[run], sin_all[run]
+        for slab in range(hw // 128):
+            lanes = slab * 128
+            left, right = dq_in[2 * slab, run].astype(f32), dq_in[2 * slab + 1, run].astype(f32)
+            both = jnp.concatenate([join(left, 0, right, 0), join(left, 1, right, 1)], axis=0)
+            gp[run, :, lanes : lanes + 128] = turn(both, cosine, sine, True).astype(bf16)
+            left, right = dkv_in[2 * slab, run].astype(f32), dkv_in[2 * slab + 1, run].astype(f32)
+            gp[run, :, hw + lanes : hw + lanes + 128] = turn(
+                join(left, 0, right, 0), cosine, sine, True
+            ).astype(bf16)
+            gp[run, :, 2 * hw + lanes : 2 * hw + lanes + 128] = join(left, 1, right, 1).astype(bf16)
+
+    def qkv_block(chunk):
+        return wq_all[chunk].reshape(B * D, 3 * hw)
+
+    for half, (term, item) in enumerate(zip(term_qkv, qkv_sums)):
+
+        def term_chunk(n, carried, half=half, term=term):
+            lanes = pl.ds(pl.multiple_of((half * (H // 2) + n) * hw, hw), hw)
+            left = (hats[:, :, lanes] * gain_rows[0:1, lanes]).astype(bf16).reshape(H * R, hw)
+            grads = mm(left, gp[...].reshape(H * R, 3 * hw), TN).astype(bf16)
+            term[:, :, n] = grads.reshape(A, 2, D, 3 * hw)
+            return carried
+
+        lax.fori_loop(0, H // 2, term_chunk, 0)
+        item.start()
+        if half:
+            qkv_sums[0].pair()
+
+    def part_one(run, i):
+        return remote(g1_send.at[i], g1_in.at[i], g1_s.at[i], g1_r.at[i], (run, b))
+
+    def one_run(i, carried):
+        run = run_of(here, i)
+        for chunk in range(H):
+            lanes = slice(chunk * hw, (chunk + 1) * hw)
+            g1_own[:, lanes] = mm(gp[run], qkv_block(chunk), NT)
+
+        @pl.when(i < H - 1)
+        def _():
+            g1_send[i] = g1_own[...].astype(bf16)
+            part_one(run, i).start()
+
+        return carried
+
+    lax.fori_loop(0, 1, one_run, 0)
+    qkv_sums[1].pair()
+    lax.fori_loop(1, H, one_run, 0)
+    qkv_sums[0].cross()
+    far_copy.wait_recv()
+    down = down_of(part) + down_in[0].astype(f32) + from_far[...].astype(f32)
+    in_swap.out[:, :, 2 * F :] = down.astype(bf16)
+    last_copy.wait_recv()
+    total = in_of(part) + from_near[0].astype(f32) + in_last[...].astype(f32)
+    in_swap.out[:, :, : 2 * F] = total.astype(bf16)
+    in_swap.start()
+    qkv_sums[1].cross()
+
+    grad = g1_own[...]
+    hat, scale = standardize(tok_all[h].astype(f32))
+    for i in (1, 2, 0):
+        part_one(here.places[i], i).wait_recv()
+        grad += g1_in[i].astype(f32)
+    row = lax.broadcasted_iota(jnp.int32, (8, W), 0)
+    rows = jnp.where(
+        row == 0,
+        jnp.sum(grad * hat, axis=0, keepdims=True),
+        jnp.where(row == 1, gain_part[...], 0.0),
+    )
+    pick = (
+        lax.broadcasted_iota(jnp.int32, (8, 128), 0) == lax.broadcasted_iota(jnp.int32, (8, 128), 1)
+    ).astype(bf16)
+    for chunk in range(H):
+        gain_columns = mm(rows[:, chunk * hw : (chunk + 1) * hw].astype(bf16), pick, TN)
+        term_gain[:, :, chunk] = gain_columns.astype(bf16).reshape(A, 2, D, 128)
+    gain_sum.start()
+    input_grad[...] = grad_middle[...] + norm_back(grad, hat, scale, gain_rows[0:1, :])
+    gain_sum.middle()
+    result = out_base[...]
+    for i, copy in enumerate(o_copies):
+        copy.wait_recv()
+        result += o_in[i].astype(f32)
+    output[...] = result.astype(bf16)
+    in_swap.arrive()
+    for place in range(H):
+        in_grad[:, place * F : (place + 1) * F] = in_swap.landed[place, :, :F].astype(f32)
+        in_grad[:, (H + place) * F : (H + place + 1) * F] = in_swap.landed[
+            place, :, F : 2 * F
+        ].astype(f32)
+        down_grad[:, place * F : (place + 1) * F] = in_swap.landed[place, :, 2 * F :].astype(f32)
+    for half, item in enumerate(qkv_sums):
+        qkv_swap.out[half * (H // 2) : (half + 1) * (H // 2)] = item.close().astype(bf16)
+    qkv_swap.start()
+    gain_swap.out[...] = gain_sum.close().astype(bf16)
+    gain_swap.start()
+    out_grad[...] = out_sum.close()
+    qkv_swap.arrive()
+    for place in range(H):
+        for j in range(3):
+            qkv_grad[:, j * W + place * hw : j * W + (place + 1) * hw] = qkv_swap.landed[
+                place, :, j * hw : (j + 1) * hw
+            ].astype(f32)
+    gain_swap.arrive()
+    total = gain_swap.landed[0].astype(f32)
+    for place in range(1, H):
+        total += gain_swap.landed[place].astype(f32)
+    rows = total.T
+    gain_one[...] = rows[0:1, :]
+    gain_two[...] = rows[1:2, :]
     for copy in [
         *kc_copies, *q_copies, *wm_copies, *wq_copies, *gain_copies, *tok_copies, *kv_copies,
         *mx_copies, *mx_late, *ma_copies.values(), *gm_copies, pair_copy,
+        *br_copies, *o_copies, near_copy, far_copy, last_copy,
     ]:
         copy.wait_send()
+    for k in range(tiles):
+        dk_copy(k).wait_send()
+    for there in here.there:
+        for run in range(H):
+            n = there * H + run
+            remote(dq_send.at[0, 0], dq_in.at[0, 0], dq_s.at[n], dq_r.at[n], beside).wait_send()
+            remote(dkv_send.at[0, 0], dkv_in.at[0, 0], dz_s.at[n], dz_r.at[n], beside).wait_send()
     for i in range(H - 1):
         part_of(here.places[i], i).wait_send()
-    for copy in stores[1:]:
-        copy.wait()
+        part_one(here.places[i], i).wait_send()
     for item in (spread, cot_gather, wo_line, *wq_lines, *wm_lines):
         item.finish()
     in_sum.core_finish()
     down_sum.core_finish()
-
-
-def forward(tokens, cotangent, w_qkv, gain_one, gain_two, w_in, w_down, w_out, lengths):
+    for item in (out_sum, *qkv_sums, gain_sum, in_swap, qkv_swap, gain_swap):
+        item.finish()
+
+
+def layer(tokens, cotangent, w_qkv, gain_one, gain_two, w_in, w_down, w_out, lengths):
     R, W = tokens.shape
     H, B = lax.axis_size("head"), lax.axis_size("blk")
     A = B // 2
@@ -1573,31 +1805,19 @@
     buffer = lambda *sizes: pltpu.VMEM(sizes, bf16)
     wide = lambda *sizes: pltpu.VMEM(sizes, f32)
     outs = [
-        shape((H, B, R, 128), bf16),
-        shape((A, H // 2, R, 128), bf16),
-        shape((A, H // 2, R, 128), bf16),
-        shape((H * A // 2, 1, 2 * R), f32),
-        shape((A, H, R // 2, 128), bf16),
-        shape((H, R, W), bf16),
-        shape((H, B, D, 3 * hw), bf16),
-        shape((H, R, 128), f32),
-        shape((H, R, 128), f32),
-        shape((8, W), f32),
-        shape((8, W), f32),
-        shape((H, R, hw), bf16),
+        shape((R, W), bf16),
         shape((R, W), f32),
-        shape((R, W), f32),
-        shape((H - 1, R, W), bf16),
-        shape((3, H, D, F), f32),
-        shape((H, D, F), bf16),
-        shape((3, H, D, F), bf16),
-        shape((H, D, F), bf16),
-        shape((2, H, D, F), bf16),
+        shape((D, 3 * W), f32),
+        shape((D, W), f32),
+        shape((D, 2 * H * F), f32),
+        shape((D, H * F), f32),
+        shape((1, D), f32),
+        shape((1, D), f32),
     ]
     return pl.pallas_call(
-        partial(forward_kernel, H, A),
+        partial(layer_kernel, H, A),
         in_specs=[*[anywhere()] * 3, *[in_vmem()] * 2, *[anywhere()] * 3, in_smem()],
-        out_specs=[in_vmem() if n in (3, 9, 10) else anywhere() for n in range(len(outs))],
+        out_specs=[in_vmem()] * len(outs),
         out_shape=outs,
         scratch_shapes=[
             buffer(R, W),
@@ -1647,15 +1867,29 @@
             wide(R, W),
             buffer(H - 1, R, W),
             wide(R, W),
-            wide(3, H, D, F),
+            buffer(2, H, D, 2 * F),
             buffer(H, D, F),
-            buffer(3, H, D, F),
+            wide(H * A // 2, 1, 2 * R),
+            buffer(A, H, R // 2, 128),
+            wide(8, W),
+            wide(8, W),
+            buffer(R, W),
+            buffer(H, R, W),
+            buffer(H - 1, R, W),
+            buffer(2, H, D, 2 * F),
             buffer(H, D, F),
-            buffer(2, H, D, F),
+            *[buffer(H, D, 2 * F)] * 2,
+            wide(H * B * R // KEY_STEP, KEY_STEP, 128),
+            *[buffer(A, H, R // 2, 128)] * 2,
+            *[buffer(H * B * R // KEY_STEP, 2, R, 128)] * 2,
+            *[buffer(A, H, R, 128)] * 2,
+            buffer(H, R, 3 * hw),
+            *[buffer(H - 1, R, W)] * 2,
+            wide(R, W),
+            buffer(A, 2, D, W),
+            *[buffer(A, 2, H // 2, D, 3 * hw)] * 2,
             dma(8),
-            dma(16),
-            dma(2),
-            dma(H // 2),
+            dma(1),
             *[dma(H - 1)] * 8,
             *[dma(B - 1)] * 2,
             *[dma(4)] * 2,
@@ -1668,321 +1902,31 @@
             *[dma(H - 1)] * 2,
             *[dma(H * A)] * 2,
             *[dma(1)] * 6,
+            *[dma(H - 1)] * 6,
+            *[dma(4)] * 2,
+            *[dma(A * H)] * 4,
+            *[dma(H * B * R // KEY_STEP)] * 2,
             *line_sems(A) * 5,
-        ],
-        compiler_params=params(0),
-        cost_estimate=pl.CostEstimate(flops=10**10, bytes_accessed=10**7, transcendentals=10**6),
-        name="forward",
-    )(tokens, cotangent, w_qkv, gain_one, gain_two, w_in, w_down, w_out, lengths)
-
-
-def finish_kernel(
-    H, A, dqp, dkv, tok_in, wq_in, cos_in, sin_in, gain_rows, mixed_in, middle_in, gain_part, base_in, out_parts, kept_in, up_in, near_in, over_in, far_in,
-    output, input_grad, qkv_grad, out_grad, in_grad, down_grad, gain_one, gain_two,
-    dkv_own, tok_all, wq_all, cos_all, sin_all, mixed_own, grad_middle, out_base, o_in, kept, up_far, from_near, from_over, from_far, up_send, up_last,
-    dk_in, dkv_send, dkv_in, dq_in, branch, branch_all, gp, normed, g1_send, g1_in, g1_own,
-    load_s, up_s, up_r, o_s, o_r, dk_s, dk_r, dz_s, dz_r, dq_s, dq_r, br_s, br_r, g1_s, g1_r, *rest,
-):
-    f32, bf16 = jnp.float32, jnp.bfloat16
-    R, W = tok_all.shape[1:]
-    B = 2 * A
-    hw = W // H
-    D, F = kept_in.shape[2:]
-    here = Place(A)
-    h, b, part, share = here.h, here.b, here.part, here.share
-    across, along, beside = here.across, here.along, here.beside
-    term_gain, gain_sum = reducer(rest[:8], here)
-    in_swap, qkv_swap, gain_swap = (Swap(*rest[8 + 4 * n : 12 + 4 * n], here) for n in range(3))
-    term_out, *term_qkv = rest[20:23]
-    out_sum, *qkv_sums = (
-        PairReduce(*rest[23 + 11 * n : 34 + 11 * n], term=term, here=here)
-        for n, term in enumerate((term_out, *term_qkv))
-    )
-    loads = load(
-        [
-            (dkv, dkv_own), (middle_in, grad_middle), (tok_in, tok_all), (mixed_in, mixed_own), (cos_in, cos_all),
-            (sin_in, sin_all), (wq_in, wq_all), (kept_in, kept), (up_in, up_far), (near_in, from_near),
-            (far_in, from_far), (base_in, out_base),
-        ],
-        load_s,
-    )
-    meet([*across, *along, beside])
-
-    order = [*here.there, part]
-    dk_copies = [
-        send(dkv.at[:, there * 2 + 1 - share], dk_in.at[i], dk_s.at[i], dk_r.at[i], beside)
-        for i, there in enumerate(order)
-    ]
-    dq_copies = [
-        send(dqp.at[here.there[i]], dq_in.at[part], dq_s.at[i], dq_r.at[i], peer)
-        for i, peer in enumerate(along)
-    ]
-    loads[0].wait()
-    dz_copies = []
-    for i, there in enumerate(order):
-        dk_copies[i].wait_recv()
-        summed = dkv_own[:, there * 2 + share].astype(f32) + dk_in[i].astype(f32)
-        if i < A - 1:
-            dkv_send[i] = summed.astype(bf16)
-            dz_copies.append(
-                send(dkv_send.at[i], dkv_in.at[part], dz_s.at[i], dz_r.at[i], along[i])
-            )
-        else:
-            dkv_in[part] = summed.astype(bf16)
-    dq_in[part] = dqp[part]
-    loads[1].wait()
-    branch[...] = grad_middle[...].astype(bf16)
-    br_copies = [
-        send(branch, branch_all.at[h], br_s.at[i], br_r.at[i], peer) for i, peer in enumerate(across)
-    ]
-    branch_all[h] = branch[...]
-    for copy in loads[2:]:
-        copy.wait()
-
-    def norm_run(run, carried):
-        hat, unused = standardize(tok_all[run].astype(f32))
-        normed[run] = (hat * gain_rows[0:1, :]).astype(bf16)
-        return carried
-
-    lax.fori_loop(0, H, norm_run, 0)
-    for copy in br_copies:
-        copy.wait_recv()
-    o_copies = [
-        send(out_parts.at[i], o_in.at[i], o_s.at[i], o_r.at[i], peer) for i, peer in enumerate(across)
-    ]
-
-    def out_tile(n, carried):
-        lanes = pl.ds(pl.multiple_of(n * hw, hw), hw)
-        grads = mm(mixed_own[...].reshape(H * R, hw), branch_all[:, :, lanes].reshape(H * R, hw), TN)
-        term_out[:, :, :, lanes] = grads.astype(bf16).reshape(A, 2, D, hw)
-        return carried
-
-    lax.fori_loop(0, W // hw, out_tile, 0)
-    out_sum.start()
-    up_send[...] = (up_far[...].astype(f32) + from_near[2].astype(f32)).astype(bf16)
-    for copy in [*dq_copies, *dz_copies]:
-        copy.wait_recv()
-    out_sum.pair()
-    up_copy = send(up_send, up_last, up_s.at[0], up_r.at[0], (h, here.far * 2 + share))
-    over_copy = send(over_in, from_over, up_s.at[1], up_r.at[1], (h, here.over * 2 + share))
-    for run in range(H):
-        side, at = run // (H // 2), run % (H // 2)
-        cosine, sine = cos_all[run], sin_all[run]
-        for slab in range(hw // 128):
-            lanes = slab * 128
-            left, right = dq_in[2 * slab, at].astype(f32), dq_in[2 * slab + 1, at].astype(f32)
-            gp[run, :, lanes : lanes + 128] = turn(
-                join(left, side, right, side), cosine, sine, True
-            ).astype(bf16)
-            left, right = dkv_in[2 * slab, run].astype(f32), dkv_in[2 * slab + 1, run].astype(f32)
-            gp[run, :, hw + lanes : hw + lanes + 128] = turn(
-                join(left, 0, right, 0), cosine, sine, True
-            ).astype(bf16)
-            gp[run, :, 2 * hw + lanes : 2 * hw + lanes + 128] = join(left, 1, right, 1).astype(bf16)
-
-    def block(chunk):
-        return wq_all[chunk].reshape(B * D, 3 * hw)
-
-    for half, (term, item) in enumerate(zip(term_qkv, qkv_sums)):
-
-        def term_chunk(n, carried, half=half, term=term):
-            lanes = pl.ds(pl.multiple_of((half * (H // 2) + n) * hw, hw), hw)
-            left = normed[:, :, lanes].reshape(H * R, hw)
-            grads = mm(left, gp[...].reshape(H * R, 3 * hw), TN).astype(bf16)
-            term[:, :, n] = grads.reshape(A, 2, D, 3 * hw)
-            return carried
-
-        lax.fori_loop(0, H // 2, term_chunk, 0)
-        item.start()
-        if half:
-            qkv_sums[0].pair()
-
-    def part_of(run, i):
-        return remote(g1_send.at[i], g1_in.at[i], g1_s.at[i], g1_r.at[i], (run, b))
-
-    def one_run(i, carried):
-        run = run_of(here, i)
-        for chunk in range(H):
-            lanes = slice(chunk * hw, (chunk + 1) * hw)
-            g1_own[:, lanes] = mm(gp[run], block(chunk), NT)
-
-        @pl.when(i < H - 1)
-        def _():
-            g1_send[i] = g1_own[...].astype(bf16)
-            part_of(run, i).start()
-
-        return carried
-
-    lax.fori_loop(0, 1, one_run, 0)
-    qkv_sums[1].pair()
-    out_sum.cross()
-    lax.fori_loop(1, H, one_run, 0)
-    qkv_sums[0].cross()
-    over_copy.wait_recv()
-    gate = kept[0] + from_near[0].astype(f32) + from_over[...].astype(f32) + from_far[0].astype(f32)
-    in_swap.out[:, :, :F] = gate.astype(bf16)
-    in_swap.out[:, :, 2 * F :] = (kept[2] + from_far[1].astype(f32)).astype(bf16)
-    up_copy.wait_recv()
-    up = kept[1] + from_near[1].astype(f32) + up_last[...].astype(f32)
-    in_swap.out[:, :, F : 2 * F] = up.astype(bf16)
-    in_swap.start()
-    qkv_sums[1].cross()
-
-    grad = g1_own[...]
-    hat, scale = standardize(tok_all[h].astype(f32))
-    for i in (1, 2, 0):
-        part_of(here.places[i], i).wait_recv()
-        grad += g1_in[i].astype(f32)
-    row = lax.broadcasted_iota(jnp.int32, (8, W), 0)
-    rows = jnp.where(
-        row == 0,
-        jnp.sum(grad * hat, axis=0, keepdims=True),
-        jnp.where(row == 1, gain_part[...], 0.0),
-    )
-    pick = (
-        lax.broadcasted_iota(jnp.int32, (8, 128), 0) == lax.broadcasted_iota(jnp.int32, (8, 128), 1)
-    ).astype(bf16)
-    for chunk in range(H):
-        gain_columns = mm(rows[:, chunk * hw : (chunk + 1) * hw].astype(bf16), pick, TN)
-        term_gain[:, :, chunk] = gain_columns.astype(bf16).reshape(A, 2, D, 128)
-    gain_sum.start()
-    input_grad[...] = grad_middle[...] + norm_back(grad, hat, scale, gain_rows[0:1, :])
-    gain_sum.middle()
-    result = out_base[...]
-    for i, copy in enumerate(o_copies):
-        copy.wait_recv()
-        result += o_in[i].astype(f32)
-    output[...] = result.astype(bf16)
-    in_swap.arrive()
-    for place in range(H):
-        in_grad[:, place * F : (place + 1) * F] = in_swap.landed[place, :, :F].astype(f32)
-        in_grad[:, (H + place) * F : (H + place + 1) * F] = in_swap.landed[
-            place, :, F : 2 * F
-        ].astype(f32)
-        down_grad[:, place * F : (place + 1) * F] = in_swap.landed[place, :, 2 * F :].astype(f32)
-    for half, item in enumerate(qkv_sums):
-        qkv_swap.out[half * (H // 2) : (half + 1) * (H // 2)] = item.close().astype(bf16)
-    qkv_swap.start()
-    gain_swap.out[...] = gain_sum.close().astype(bf16)
-    gain_swap.start()
-    out_grad[...] = out_sum.close()
-    qkv_swap.arrive()
-    for place in range(H):
-        for j in range(3):
-            qkv_grad[:, j * W + place * hw : j * W + (place + 1) * hw] = qkv_swap.landed[
-                place, :, j * hw : (j + 1) * hw
-            ].astype(f32)
-    gain_swap.arrive()
-    total = gain_swap.landed[0].astype(f32)
-    for place in range(1, H):
-        total += gain_swap.landed[place].astype(f32)
-    rows = total.T
-    gain_one[...] = rows[0:1, :]
-    gain_two[...] = rows[1:2, :]
-    for copy in [*dk_copies, *dq_copies, *br_copies, *dz_copies, *o_copies, up_copy, over_copy]:
-        copy.wait_send()
-    for i in range(H - 1):
-        part_of(here.places[i], i).wait_send()
-    for item in (out_sum, *qkv_sums, gain_sum, in_swap, qkv_swap, gain_swap):
-        item.finish()
-
-
-def finish(dqp, dkv, tok_all, wq_all, cos_all, sin_all, gain_rows, mixed, grad_middle, gain_part, out_base, out_parts, kept, *terms):
-    A, half, R, lanes = dqp.shape
-    H = 2 * half
-    W = tok_all.shape[-1]
-    B = 2 * A
-    hw = W // H
-    D, F = kept.shape[2:]
-    f32, bf16 = jnp.float32, jnp.bfloat16
-    shape = jax.ShapeDtypeStruct
-    buffer = lambda *sizes: pltpu.VMEM(sizes, bf16)
-    arrays = [
-        dqp, dkv, tok_all, wq_all, cos_all, sin_all, gain_rows, mixed, grad_middle, gain_part, out_base, out_parts,
-        kept, *terms,
-    ]
-    return pl.pallas_call(
-        partial(finish_kernel, H, A),
-        in_specs=[in_vmem() if n in (0, 6, 9) else anywhere() for n in range(len(arrays))],
-        out_specs=[in_vmem()] * 8,
-        out_shape=[
-            shape((R, W), bf16),
-            shape((R, W), f32),
-            shape((D, 3 * W), f32),
-            shape((D, W), f32),
-            shape((D, 2 * H * F), f32),
-            shape((D, H * F), f32),
-            shape((1, D), f32),
-            shape((1, D), f32),
-        ],
-        scratch_shapes=[
-            buffer(*dkv.shape),
-            buffer(*tok_all.shape),
-            buffer(*wq_all.shape),
-            pltpu.VMEM(cos_all.shape, f32),
-            pltpu.VMEM(sin_all.shape, f32),
-            buffer(*mixed.shape),
-            pltpu.VMEM(grad_middle.shape, f32),
-            pltpu.VMEM(out_base.shape, f32),
-            buffer(*out_parts.shape),
-            pltpu.VMEM(kept.shape, f32),
-            *[buffer(*term.shape) for term in terms],
-            *[buffer(H, D, F)] * 2,
-            buffer(A, H, R, 128),
-            buffer(A - 1, H, R, 128),
-            buffer(A, H, R, 128),
-            buffer(A, half, R, 128),
-            buffer(R, W),
-            buffer(H, R, W),
-            buffer(H, R, 3 * hw),
-            buffer(H, R, W),
-            buffer(H - 1, R, W),
-            buffer(H - 1, R, W),
-            pltpu.VMEM((R, W), f32),
-            dma(12),
-            *[dma(2)] * 2,
-            *[dma(H - 1)] * 2,
-            *[dma(A)] * 2,
-            *[dma(A - 1)] * 4,
-            *[dma(H - 1)] * 4,
+            *pair_scratch(A, (D, W)),
+            *pair_scratch(A, (H // 2, D, 3 * hw)),
+            *pair_scratch(A, (H // 2, D, 3 * hw)),
             *reduce_scratch(A, (H, D, 128)),
             *swap_scratch(H, (D, 3 * F)),
             *swap_scratch(H, (D, 3 * hw)),
             *swap_scratch(H, (D, 128)),
-            buffer(A, 2, D, W),
-            *[buffer(A, 2, H // 2, D, 3 * hw)] * 2,
-            *pair_scratch(A, (D, W)),
-            *pair_scratch(A, (H // 2, D, 3 * hw)),
-            *pair_scratch(A, (H // 2, D, 3 * hw)),
         ],
-        compiler_params=params(2),
-        cost_estimate=pl.CostEstimate(flops=2 * 10**9, bytes_accessed=10**7, transcendentals=10**5),
-        name="finish",
-    )(*arrays)
+        compiler_params=params(0),
+        cost_estimate=pl.CostEstimate(flops=10**10, bytes_accessed=10**7, transcendentals=10**6),
+        name="layer",
+    )(tokens, cotangent, w_qkv, gain_one, gain_two, w_in, w_down, w_out, lengths)
 
 
 def per_device_split(
     tokens, attn_gain, w_qkv, w_attn_out, mlp_gain, w_in, w_mlp_out, doc_lengths, cotangent
 ):
-    R, W = tokens.shape
-    H, B = lax.axis_size("head"), lax.axis_size("blk")
-    A = B // 2
-    hw = W // H
-    T = H * B * R
-    (
-        kv, qp, op, lse, gp, tok_all, wq, cos_all, sin_all, gain_rows, gain_part, mixed, grad_middle,
-        out_base, out_parts, kept, up_far, near, over, far,
-    ) = forward(
-        tokens, cotangent, w_qkv, attn_gain[None], mlp_gain[None], w_in, w_mlp_out.T, w_attn_out, doc_lengths
-    )
-    kv = kv.reshape(T, 2 * HEAD_DIM)
-    flipped = lambda flip: [(p, (p // 2 ^ flip) * 2 + p % 2) for p in range(B)]
-    near, far = lax.ppermute(near, "blk", flipped(1)), lax.ppermute(far, "blk", flipped(3))
-    dqp, dkv = attend_back(doc_lengths, qp, gp, op, lse, kv)
     output, input_grad, qkv_grad, out_grad, in_grad, down_grad, gain_one, gain_two = deliver(
-        *finish(
-            dqp, dkv.reshape(H, B, R, 128), tok_all, wq, cos_all, sin_all, gain_rows, mixed, grad_middle, gain_part,
-            out_base, out_parts, kept, up_far, near, over, far,
+        *layer(
+            tokens, cotangent, w_qkv, attn_gain[None], mlp_gain[None], w_in, w_mlp_out.T, w_attn_out, doc_lengths
         )
     )
     return (

time: 204 us -> 196 us (0.961)
  waiting for transfers between devices: 4.65 us -> 0 us
  starting transfers between devices: 2.74 us -> 0 us
    ppermute x2 -> x0, waiting for transfers between devices: 4.65 us -> none  [the longest x1 4.64 us: per_device_split(): lax.ppermute(far, 'blk', flipped(3))]
    ppermute x2 -> x0, starting transfers between devices: 2.74 us -> none  [the longest x1 1.88 us: per_device_split(): lax.ppermute(far, 'blk', flipped(3))]
    pallas_call x3 -> x1, Pallas kernels: 191 us -> 192 us  [layer(): pl.pallas_call(partial(layer_kernel, H, A), in_specs=[*[anywhere()] * 3,...]
  transfers between devices with their start and end apart: 2 -> 0, of which waited for: 1 -> 0; matrix products, arithmetic and copies ran while one was open for 0% -> 0% of each run, Pallas kernels for 8% -> 0%
where the time goes in v7:
time: 196 us
  Pallas kernels  195 us (99%)
    pallas_call x1, Pallas kernels, layer(): pl.pallas_call(partial(layer_kernel, H, A), in_specs=[*[anywhere()] * 3,...  192 us

profile of v7, /device:TPU:0, one launch (start us, length us, event | category | flops | bytes accessed | tf_op | source)
XLA Modules:
  0.0 196.0 jit_solution(16216525010975195640)
XLA Ops:
  0.6 192.4 %layer.1 = (bf16[128,1024]{1,0:T(8,128)(2,1)}, f32[128,1024]{1,0:T(8,128)}, f32[32,3072]{1,0:T(8,128)}, f32[32,1024]{1,0:T(8,128)}, f32[32,5248]{1,0:T(8,128)}, ...) custom-call(bf16[128,1024]{1,0:T(8,128)(2,1)} %tok_in.1, bf16[128,1024]{1,0:T(8,128)(2,1)} %cot_in.1, ...), custom_call_target="tpu_custom_call" | custom-call | flops 10000000000 | bytes 10000000 | tf_op jit(solution)/shard_map/layer/pallas_call | solution.py:1817
  193.0 3.0 %deliver.1 = (bf16[128,1024]{1,0:T(8,128)(2,1)}, f32[128,1024]{1,0:T(8,128)}, f32[32,3072]{1,0:T(8,128)}, f32[32,1024]{1,0:T(8,128)}, f32[32,5248]{1,0:T(8,128)}...) custom-call(bf16[128,1024]{1,0:T(8,128)(2,1)} %get-tuple-element.24.refs_0_, ...), custom_call_target="tpu_custom_call" | custom-call | tf_op jit(solution)/shard_map/deliver/pallas_call | solution.py:650

commit v8 on v7

--- a/solution.py
+++ b/solution.py
@@ -1533,9 +1533,6 @@
 
     lax.fori_loop(0, H, out_run, 0)
     out_base[...] += middle[h]
-    o_copies = [
-        send(out_parts.at[i], o_in.at[i], o_s.at[i], o_r.at[i], peer) for i, peer in enumerate(across)
-    ]
     dkv_sum[...] = jnp.zeros_like(dkv_sum)
     for copy in gm_copies:
         copy.wait_recv()
@@ -1638,13 +1635,15 @@
             keys_done(tile - 2)
         if tile >= 3:
             keys_sum(tile - 3)
-        if tile == 3:
+        if tile == 5:
             for copy in br_copies:
                 copy.wait_recv()
+            o_copies = [
+                send(out_parts.at[i], o_in.at[i], o_s.at[i], o_r.at[i], peer)
+                for i, peer in enumerate(across)
+            ]
             lax.fori_loop(0, W // hw, out_tile, 0)
             out_sum.start()
-        if tile == 4:
-            out_sum.pair()
         if tile == 6:
             near_copy.wait_recv()
             in_send[...] = (in_of(far) + from_near[1].astype(f32)).astype(bf16)
@@ -1652,7 +1651,7 @@
         keys_done(k)
     for k in (tiles - 3, tiles - 2, tiles - 1):
         keys_sum(k)
-    out_sum.cross()
+    out_sum.pair()
     last_copy = send(in_send, in_last, nr_s.at[2], nr_r.at[2], (h, far * 2 + share))
     for source in here.back:
         for run in range(H):
@@ -1671,6 +1670,8 @@
                 join(left, 0, right, 0), cosine, sine, True
             ).astype(bf16)
             gp[run, :, 2 * hw + lanes : 2 * hw + lanes + 128] = join(left, 1, right, 1).astype(bf16)
+
+    out_sum.cross()
 
     def qkv_block(chunk):
         return wq_all[chunk].reshape(B * D, 3 * hw)

time: 196 us -> 189 us (0.964)
  Pallas kernels: 195 us -> 188 us
    pallas_call x1, Pallas kernels: 192 us -> 185 us  [layer(): pl.pallas_call(partial(layer_kernel, H, A), in_specs=[*[anywhere()] * 3,...]
where the time goes in v8:
time: 189 us
  Pallas kernels  188 us (99%)
    pallas_call x1, Pallas kernels, layer(): pl.pallas_call(partial(layer_kernel, H, A), in_specs=[*[anywhere()] * 3,...  185 us

profile of v8, /device:TPU:0, one launch (start us, length us, event | category | flops | bytes accessed | tf_op | source)
XLA Modules:
  0.0 188.7 jit_solution(14288165819684275504)
XLA Ops:
  0.6 185.0 %layer.1 = (bf16[128,1024]{1,0:T(8,128)(2,1)}, f32[128,1024]{1,0:T(8,128)}, f32[32,3072]{1,0:T(8,128)}, f32[32,1024]{1,0:T(8,128)}, f32[32,5248]{1,0:T(8,128)}, ...) custom-call(bf16[128,1024]{1,0:T(8,128)(2,1)} %tok_in.1, bf16[128,1024]{1,0:T(8,128)(2,1)} %cot_in.1, ...), custom_call_target="tpu_custom_call" | custom-call | flops 10000000000 | bytes 10000000 | tf_op jit(solution)/shard_map/layer/pallas_call | solution.py:1818
  185.7 3.0 %deliver.1 = (bf16[128,1024]{1,0:T(8,128)(2,1)}, f32[128,1024]{1,0:T(8,128)}, f32[32,3072]{1,0:T(8,128)}, f32[32,1024]{1,0:T(8,128)}, f32[32,5248]{1,0:T(8,128)}...) custom-call(bf16[128,1024]{1,0:T(8,128)(2,1)} %get-tuple-element.24.refs_0_, ...), custom_call_target="tpu_custom_call" | custom-call | tf_op jit(solution)/shard_map/deliver/pallas_call | solution.py:650

commit v9 on v8

--- a/solution.py
+++ b/solution.py
@@ -640,18 +640,28 @@
     )(lengths, qp, gp, op, lse, kv)
 
 
-def deliver_kernel(*refs):
-    count = len(refs) // 2
-    for source, target in zip(refs[:count], refs[count:]):
-        target[...] = source[...]
+def deliver_kernel(count, *refs):
+    sources, targets, held = refs[:count], refs[count : 2 * count], refs[2 * count : 3 * count]
+    into, out = refs[3 * count :]
+    first = [pltpu.make_async_copy(sources[n], held[n], into.at[n]) for n in range(count)]
+    second = [pltpu.make_async_copy(held[n], targets[n], out.at[n]) for n in range(count)]
+    for copy in first:
+        copy.start()
+    for arrived, leaving in zip(first, second):
+        arrived.wait()
+        leaving.start()
+    for copy in second:
+        copy.wait()
 
 
 def deliver(*arrays):
+    count = len(arrays)
     return pl.pallas_call(
-        deliver_kernel,
-        in_specs=[in_vmem()] * len(arrays),
-        out_specs=[in_vmem()] * len(arrays),
+        partial(deliver_kernel, count),
+        in_specs=[anywhere()] * count,
+        out_specs=[anywhere()] * count,
         out_shape=[jax.ShapeDtypeStruct(a.shape, a.dtype) for a in arrays],
+        scratch_shapes=[*[pltpu.VMEM(a.shape, a.dtype) for a in arrays], dma(count), dma(count)],
         compiler_params=params(),
         name="deliver",
     )(*arrays)
@@ -1032,7 +1042,7 @@
 
 def layer_kernel(
     H, A, tok_in, cot_in, wq_in, gain_one_in, gain_two_in, w_in_in, w_down_in, w_out_in, lengths,
-    output, input_grad, qkv_grad, out_grad, in_grad, down_grad, gain_one, gain_two,
+    output_to, input_to, qkv_grad, out_grad, in_to, down_to, gain_one, gain_two,
     cot, w_in, w_down, w_out, tok_all, cot_all, wq_all, cos_all, sin_all,
     wq_st, wm_src, wm_own, wo_all, kv, kv_send, q_all, q_send, q_runs, hats, gain_src, gain_st, gain_tile, gain_all,
     bounds, s_scr, op, mx_in, mixed_own, mixed_early, mixed_late, wm_all, middle, normed, act, lift,
@@ -1040,8 +1050,8 @@
     out_base, out_parts, grad_middle, near_out, far_out,
     lse, go, gain_rows, gain_part, branch_own, branch_all, o_in, from_near, from_far, in_send, in_last,
     dkv_sum, dq_send, dq_in, dk_send, dk_in, dkv_send, dkv_in, gp, g1_send, g1_in, g1_own,
-    term_out, term_qkv_low, term_qkv_high,
-    load_s, own_s,
+    term_out, term_qkv_low, term_qkv_high, output, input_grad, in_grad, down_grad,
+    load_s, own_s, result_s,
     tok_s, tok_r, wq_s, wq_r, wm_s, wm_r, ga_s, ga_r, gb_s, gb_r, wx_s, wx_r, wf_s, wf_r, cot_s, cot_r,
     q_s, q_r, kv_s, kv_r, kc_s, kc_r, mx_s, mx_r, ma_s, ma_r, g2_s, g2_r, gm_s, gm_r,
     in_core_s, in_core_r, down_core_s, down_core_r, pair_s, pair_r,
@@ -1744,6 +1754,7 @@
         copy.wait_recv()
         result += o_in[i].astype(f32)
     output[...] = result.astype(bf16)
+    results = [local(output, output_to, result_s.at[0]), local(input_grad, input_to, result_s.at[1])]
     in_swap.arrive()
     for place in range(H):
         in_grad[:, place * F : (place + 1) * F] = in_swap.landed[place, :, :F].astype(f32)
@@ -1751,6 +1762,7 @@
             place, :, F : 2 * F
         ].astype(f32)
         down_grad[:, place * F : (place + 1) * F] = in_swap.landed[place, :, 2 * F :].astype(f32)
+    results += [local(in_grad, in_to, result_s.at[2]), local(down_grad, down_to, result_s.at[3])]
     for half, item in enumerate(qkv_sums):
         qkv_swap.out[half * (H // 2) : (half + 1) * (H // 2)] = item.close().astype(bf16)
     qkv_swap.start()
@@ -1790,6 +1802,8 @@
         item.finish()
     in_sum.core_finish()
     down_sum.core_finish()
+    for copy in results:
+        copy.wait()
     for item in (out_sum, *qkv_sums, gain_sum, in_swap, qkv_swap, gain_swap):
         item.finish()
 
@@ -1818,7 +1832,7 @@
     return pl.pallas_call(
         partial(layer_kernel, H, A),
         in_specs=[*[anywhere()] * 3, *[in_vmem()] * 2, *[anywhere()] * 3, in_smem()],
-        out_specs=[in_vmem()] * len(outs),
+        out_specs=[anywhere() if n in (0, 1, 4, 5) else in_vmem() for n in range(len(outs))],
         out_shape=outs,
         scratch_shapes=[
             buffer(R, W),
@@ -1889,8 +1903,10 @@
             wide(R, W),
             buffer(A, 2, D, W),
             *[buffer(A, 2, H // 2, D, 3 * hw)] * 2,
+            *[pltpu.VMEM(outs[n].shape, outs[n].dtype) for n in (0, 1, 4, 5)],
             dma(8),
             dma(1),
+            dma(4),
             *[dma(H - 1)] * 8,
             *[dma(B - 1)] * 2,
             *[dma(4)] * 2,

time: 189 us -> 188 us (level)
  no operation moved by 1% of the time
where the time goes in v9:
time: 188 us
  Pallas kernels  187 us (99%)
    pallas_call x1, Pallas kernels, layer(): pl.pallas_call(partial(layer_kernel, H, A), in_specs=[*[anywhere()] * 3,...  184 us

profile of v9, /device:TPU:0, one launch (start us, length us, event | category | flops | bytes accessed | tf_op | source)
XLA Modules:
  0.0 187.9 jit_solution(13319739555898109522)
XLA Ops:
  0.6 184.5 %layer.1 = (bf16[128,1024]{1,0:T(8,128)(2,1)}, f32[128,1024]{1,0:T(8,128)}, f32[32,3072]{1,0:T(8,128)}, f32[32,1024]{1,0:T(8,128)}, f32[32,5248]{1,0:T(8,128)}, ...) custom-call(bf16[128,1024]{1,0:T(8,128)(2,1)} %tok_in.1, bf16[128,1024]{1,0:T(8,128)(2,1)} %cot_in.1, ...), custom_call_target="tpu_custom_call" | custom-call | flops 10000000000 | bytes 10000000 | tf_op jit(solution)/shard_map/layer/pallas_call | solution.py:1832
  185.1 2.6 %deliver.1 = (bf16[128,1024]{1,0:T(8,128)(2,1)}, f32[128,1024]{1,0:T(8,128)}, f32[32,3072]{1,0:T(8,128)}, f32[32,1024]{1,0:T(8,128)}, f32[32,5248]{1,0:T(8,128)}...) custom-call(bf16[128,1024]{1,0:T(8,128)(2,1)} %get-tuple-element.24.refs_0_, ...), custom_call_target="tpu_custom_call" | custom-call | tf_op jit(solution)/shard_map/deliver/pallas_call | solution.py:659
